TPU v7x, 32 devices: a whole 2x2x4 slice. The times are simulated.
32 devices in a mesh: groups: 2 (over y), row: 4 (over z), col: 2 (over x), half: 2 (over core).
Axes of the slice: x: 2, y: 2, z: 4, core: 2. Of those that a mesh axis runs over, the one named last changes fastest.
Arguments:
- log_derivs: bfloat16 [2048, 16384], P(('groups', 'row'), ('col', 'half')), parts along dimension 0, may hold values from -40 to 40
- shift: float32 [2], P('groups'), parts along dimension 0, may hold values from 0.5 to 2
Outputs:
- gram: float32 [2048, 1024], P(('groups', 'row'), ('col', 'half')), parts along dimension 0
There are 2 independent parts, one for each index of `groups`. A program takes and returns all parts, laid end to end along the dimension named above; each array names one. Nothing has to cross between parts.
All inputs are finite; a program needn't handle non-finite values.
Results may differ from a plain program's by a relative error of at most 0.0003.
Values may be sent and summed in bfloat16 or wider, within the bound.
No kernel may reach another device: no remote copies, remote signals or barrier semaphores. Data moves between devices by JAX's collectives and lax.ppermute only.
A program may use at most 64 MiB of HBM per device.

v0:
```python
import jax
import jax.numpy as jnp
from jax import lax
from jax.sharding import PartitionSpec as P


def broadcast(value, axis, source):
    kept = jnp.where(lax.axis_index(axis) == source, value, 0).astype(value.dtype)
    return lax.psum(kept, axis)


def pair_product(left, right):
    return jnp.einsum("ip,jp->ij", left, right, preferred_element_type=jnp.float32)


def on_device(log_derivs, shift):
    local_rows = log_derivs.shape[0]
    samples = local_rows * lax.axis_size("row")
    sub_blocks = lax.axis_size("row") // lax.axis_size("col")
    column_index = lax.axis_index("col")
    values = log_derivs.astype(jnp.float32)
    column_sums = lax.psum(jnp.sum(values, axis=0), "row")
    mean = column_sums / samples
    centered = (values - mean[None, :]).astype(jnp.bfloat16)
    own_rows = lax.all_gather(centered, "col", axis=1, tiled=True)
    products = []
    for offset in range(sub_blocks):
        other_rows = broadcast(own_rows, "row", column_index * sub_blocks + offset)
        products.append(pair_product(own_rows, other_rows))
    tile = jnp.concatenate(products, axis=1)
    summed = lax.psum_scatter(tile, "half", scatter_dimension=1, tiled=True)
    width = summed.shape[1]
    first_row = lax.axis_index("row") * local_rows
    first_column = (column_index * lax.axis_size("half") + lax.axis_index("half")) * width
    row_ids = first_row + lax.broadcasted_iota(jnp.int32, (local_rows, width), 0)
    column_ids = first_column + lax.broadcasted_iota(jnp.int32, (local_rows, width), 1)
    identity = jnp.where(row_ids == column_ids, 1.0, 0.0).astype(jnp.float32)
    return summed / samples + shift[0] * identity


def solution(mesh):
    placed = (P(("groups", "row"), ("col", "half")), P("groups"))
    return jax.shard_map(
        on_device,
        mesh=mesh,
        in_specs=placed,
        out_specs=P(("groups", "row"), ("col", "half")),
        check_vma=False,
    )
```

profile of v0, /device:TPU:8, one launch (start us, length us, event | category | flops | bytes accessed | tf_op | source)
XLA Modules:
  0.0 407.4 jit_solution(9346421414770680822)
XLA Ops:
  6.5 0.0 all-gather.2.cloned.1.call-start
  6.5 1.9 convert_reduce_fusion
  8.5 15.4 %psum.21 = f32[4096]{0:T(1024)S(1)} all-reduce(f32[4096]{0:T(1024)S(1)} %convert_reduce_fusion), channel_id=1, replica_groups=mesh['groups'=2,'row'=4,'col'=2,'half'=2] {'row'}, use_global_device_ids=true, to_apply=%region_1.0 | all-reduce | flops 4096 | bytes 32768 | tf_op jit(solution)/shard_map/psum | solution.py:22
  23.9 3.4 fusion
  27.3 0.0 all-gather.2.cloned.1.call-update
  27.3 0.0 all-reduce.3.cloned.1.call-start
  27.4 58.6 %all-gather.2.cloned.1.call-done = bf16[256,8192]{1,0:T(8,128)(2,1)} async-done(((bf16[256,4096]{1,0:T(8,128)(2,1)}), bf16[256,8192]{1,0:T(8,128)(2,1)}) %all-gather.2.cloned.1.call-update) | async-done | bytes 4194320 | tf_op jit(solution)/shard_map/all_gather | solution.py:25
  85.9 5.9 %broadcast_select_fusion.1 = (bf16[256,8192]{1,0:T(8,128)(2,1)}, bf16[256,8192]{1,0:T(8,128)(2,1)}) fusion(bf16[256,8192]{1,0:T(8,128)(2,1)} %all-gather.2.cloned.1.call-done, pred[]{:T(512)S(6)} %eq.9, pred[]{:T(512)S(6)} %eq.10), kind=kLoop, calls=%fused_computation.4 | loop fusion | flops 4194304 | bytes 12582914 | tf_op jit(solution)/shard_map/jit(_where)/select_n | solution.py:8
  91.9 0.0 all-reduce.3.cloned.1.call-update
  91.9 0.0 reduce-scatter.2.cloned.1.call-start
  91.9 289.5 %all-reduce.3.cloned.1.call-done = (bf16[256,8192]{1,0:T(8,128)(2,1)}, bf16[256,8192]{1,0:T(8,128)(2,1)}) async-done(((bf16[256,8192]{1,0:T(8,128)(2,1)}, bf16[256,8192]{1,0:T(8,128)(2,1)}), (bf16[256,8192]{1,0:T(8,128)(2,1)}, bf16[256,8192]{1,0:T(8,128)(2,1)})) %all-reduce.3.cloned.1.call-update) | async-done | bytes 8388624 | tf_op jit(solution)/shard_map/psum | solution.py:9
  381.4 0.0 copy-start
  381.4 0.0 copy-start.1
  381.4 4.9 %fusion.1 = f32[256,256]{0,1:T(8,128)S(1)} fusion(bf16[256,8192]{1,0:T(8,128)(2,1)} %all-gather.2.cloned.1.call-done, bf16[256,8192]{1,0:T(8,128)(2,1)} %get-tuple-element.6), kind=kOutput, calls=%fused_computation.10 | convolution fusion | flops 1073741824 | bytes 8650752 | tf_op jit(solution)/shard_map/ip,jp->ij/dot_general | solution.py:13
  386.3 0.0 copy-done
  386.3 1.0 copy-done.1
  387.4 1.3 fusion.2
  388.6 0.8 pad_maximum_fusion
  389.5 0.0 reduce-scatter.2.cloned.1.call-update
  390.2 8.8 %reduce-scatter.2.cloned.1.call-done = f32[256,256]{0,1:T(8,128)} async-done(((f32[256,512]{0,1:T(8,128)}), f32[256,256]{0,1:T(8,128)}) %reduce-scatter.2.cloned.1.call-update) | async-done | bytes 262160 | tf_op jit(solution)/shard_map/reduce_scatter | solution.py:31
  399.0 1.1 multiply_add_fusion
  400.1 0.8 copy.3
  (3 shorter events, 0.0 us)
Async XLA Ops:
  6.5 79.4 %all-gather.2.cloned.1.call-start = ((), (), s32[]{:S(2)}) async-start(), calls=%async_computation.1 | async-start | bytes 6291456 | tf_op jit(solution)/shard_map/all_gather | solution.py:25
  27.3 354.1 %all-reduce.3.cloned.1.call-start = ((), (), s32[]{:S(2)}) async-start(), calls=%async_computation.3 | async-start | bytes 16777216 | tf_op jit(solution)/shard_map/psum | solution.py:9
  91.9 307.1 %reduce-scatter.2.cloned.1.call-start = ((), (), s32[]{:S(2)}) async-start(), calls=%async_computation.2 | async-start | bytes 786432 | tf_op jit(solution)/shard_map/reduce_scatter | solution.py:31
  381.4 4.9 %copy-start = (bf16[256,8192]{1,0:T(8,128)(2,1)S(1)}, bf16[256,8192]{1,0:T(8,128)(2,1)}, u32[]{:S(2)}) copy-start(bf16[256,8192]{1,0:T(8,128)(2,1)} %all-gather.2.cloned.1.call-done) | copy-start | bytes 12582916
  381.4 5.9 %copy-start.1 = (bf16[256,8192]{1,0:T(8,128)(2,1)S(1)}, bf16[256,8192]{1,0:T(8,128)(2,1)}, u32[]{:S(2)}) copy-start(bf16[256,8192]{1,0:T(8,128)(2,1)} %get-tuple-element.5) | copy-start | bytes 12582916
Sparse Core Ops, SparseCore 0:
  27.4 58.4 all-gather.1
  92.0 289.3 all-reduce.2
  389.6 9.3 reduce-scatter.1
where the time goes:
time: 409 us; the launch traced here: 407 us
  waiting for transfers between devices  357 us (87%)
  blocking collectives  15.4 us (4%)
  between operations  13.8 us (3%)
  other arithmetic  13.1 us (3%)
  matrix products  6.15 us (2%)
    psum x1, waiting for transfers between devices, broadcast(): return lax.psum(kept, axis)  289 us
    all_gather x1, waiting for transfers between devices, on_device(): own_rows = lax.all_gather(centered, 'col', axis=1, tiled=True)  58.6 us
    psum x1, blocking collectives, on_device(): column_sums = lax.psum(jnp.sum(values, axis=0), 'row')  15.4 us
    reduce_scatter x1, waiting for transfers between devices, on_device(): summed = lax.psum_scatter(tile, 'half', scatter_dimension=1, tiled=True)  8.82 us
  transfers between devices with their start and end apart: 3, of which 3 were waited for; matrix products, arithmetic and copies ran while one was open for 0% of the time, Pallas kernels for 0%

commit v1 on v0

v1 whole, which is shorter than its diff:
```python
import jax
import jax.numpy as jnp
from jax import lax
from jax.sharding import PartitionSpec as P


def pair_product(left, right):
    return jnp.einsum("ip,jp->ij", left, right, preferred_element_type=jnp.float32)


def add_shift(summed, samples, shift, local_rows):
    width = summed.shape[1]
    first_row = lax.axis_index("row") * local_rows
    block = lax.axis_index("col") * lax.axis_size("half") + lax.axis_index("half")
    row_ids = first_row + lax.broadcasted_iota(jnp.int32, (local_rows, width), 0)
    column_ids = block * width + lax.broadcasted_iota(jnp.int32, (local_rows, width), 1)
    return summed / samples + jnp.where(row_ids == column_ids, shift[0], 0.0)


def gathered(log_derivs, shift):
    local_rows = log_derivs.shape[0]
    samples = local_rows * lax.axis_size("row")
    rows = lax.all_gather(log_derivs, "row", axis=0, tiled=True).astype(jnp.float32)
    mean = jnp.sum(rows, axis=0) / samples
    centered = (rows - mean[None, :]).astype(jnp.bfloat16)
    own = (log_derivs.astype(jnp.float32) - mean[None, :]).astype(jnp.bfloat16)
    tile = pair_product(own, centered)
    summed = lax.psum_scatter(tile, ("col", "half"), scatter_dimension=1, tiled=True)
    return add_shift(summed, samples, shift, local_rows)


def two_centres(log_derivs, shift):
    local_rows, local_params = log_derivs.shape
    samples = local_rows * 4
    half_params = local_params // 2
    row, col, half = (lax.axis_index(name) for name in ("row", "col", "half"))
    upper = (row >= 2).astype(jnp.int32)
    near = lax.dynamic_slice_in_dim(log_derivs, (1 - upper) * half_params, half_params, 1)
    far = lax.dynamic_slice_in_dim(log_derivs, upper * half_params, half_params, 1)

    from_centre = lax.ppermute(far, "row", [(1, 2), (2, 1)])
    from_edge = lax.ppermute(near, "row", [(0, 1), (3, 2)])
    from_far_edge = lax.ppermute(far, "row", [(0, 2), (3, 1)])

    blocks = jnp.stack([from_edge, near, from_centre, from_far_edge]).astype(jnp.float32)
    mean = jnp.sum(blocks, axis=(0, 1)) / samples
    centered = (blocks - mean).astype(jnp.bfloat16)
    rows = centered.reshape(4 * local_rows, half_params)

    def place(c, h):
        k = c * 2 + h
        return jnp.where(upper == 1, 3 - k, k)

    def columns(c, h):
        right = lax.dynamic_index_in_dim(centered, place(c, h), 0, keepdims=False)
        return pair_product(rows, right)

    def swap(value, axis):
        return lax.ppermute(value, axis, [(0, 1), (1, 0)])

    other_both = swap(columns(1 - col, 1 - half), "half")
    other_col = columns(1 - col, half) + other_both
    crossed = swap(other_col, "col")
    other_half = swap(columns(col, 1 - half), "half")
    mine = columns(col, half) + other_half + crossed
    keep, send = mine[: 2 * local_rows], mine[2 * local_rows :]
    arrived = lax.ppermute(send, "row", [(1, 2), (2, 1)])
    centre = keep[local_rows:] + arrived[:local_rows]
    edge = keep[:local_rows] + arrived[local_rows:]
    delivered = lax.ppermute(edge, "row", [(1, 0), (2, 3)])
    is_centre = jnp.logical_or(row == 1, row == 2)
    summed = jnp.where(is_centre, centre, delivered)
    return add_shift(summed, samples, shift, local_rows)


def solution(mesh):
    shape = mesh.shape
    small = shape["row"] == 4 and shape["col"] == 2 and shape["half"] == 2
    return jax.shard_map(
        two_centres if small else gathered,
        mesh=mesh,
        in_specs=(P(("groups", "row"), ("col", "half")), P("groups")),
        out_specs=P(("groups", "row"), ("col", "half")),
        check_vma=False,
    )
```

time: 409 us -> 122 us (0.30)
  the two profiles are of different devices: /device:TPU:8 before, /device:TPU:0 now
where the time goes in v1:
time: 122 us; the launch traced here: 121 us
  waiting for transfers between devices  85 us (70%)
  starting transfers between devices  14.7 us (12%)
  matrix products  11.3 us (9%)
  other arithmetic  4.77 us (4%)
  local copies, waits for them, and re-layouts  4.67 us (4%)
    ppermute x3, waiting for transfers between devices, swap(): return lax.ppermute(value, axis, [(0, 1), (1, 0)])  23.6 us
    ppermute x1, waiting for transfers between devices, two_centres(): delivered = lax.ppermute(edge, 'row', [(1, 0), (2, 3)])  22.1 us
    ppermute x1, waiting for transfers between devices, two_centres(): from_far_edge = lax.ppermute(far, 'row', [(0, 2), (3, 1)])  21.5 us
    ppermute x1, waiting for transfers between devices, two_centres(): from_edge = lax.ppermute(near, 'row', [(0, 1), (3, 2)])  17.8 us
    dot_general x4, matrix products, pair_product(): jnp.einsum('ip,jp->ij', left, right, preferred_element_type=jnp.float32)  11.3 us
    ppermute x1, starting transfers between devices, two_centres(): from_edge = lax.ppermute(near, 'row', [(0, 1), (3, 2)])  4.98 us
    ppermute x1, starting transfers between devices, two_centres(): from_far_edge = lax.ppermute(far, 'row', [(0, 2), (3, 1)])  4.9 us
    dynamic_slice x1, local copies, waits for them, and re-layouts, two_centres(): lax.dynamic_slice_in_dim(log_derivs, (1 - upper) * half_params, half_para...  2.69 us
  transfers between devices with their start and end apart: 8, of which 4 were waited for; matrix products, arithmetic and copies ran while one was open for 5% of the time, Pallas kernels for 0%

profile of v1, /device:TPU:0, one launch (start us, length us, event | category | flops | bytes accessed | tf_op | source)
XLA Modules:
  0.0 121.3 jit_solution(14992317219048162363)
XLA Ops:
  0.0 2.7 %constant_dynamic-slice_fusion.1 = (bf16[256,2048]{1,0:T(8,128)(2,1)S(1)}, bf16[256,2048]{1,0:T(8,128)(2,1)}) fusion(bf16[256,4096]{1,0:T(8,128)(2,1)} %param.2, s32[]{:T(128)S(6)} %select_n.43, s32[]{:T(128)S(6)} %mul.22), kind=kLoop, calls=%fused_computation.28 | loop fusion | bytes 4194312 | tf_op jit(solution)/shard_map/dynamic_slice | solution.py:38
  2.7 5.0 %collective-permute-start = (bf16[256,2048]{1,0:T(8,128)(2,1)S(1)}, bf16[256,2048]{1,0:T(8,128)(2,1)S(1)}, u32[]{:S(2)}, u32[]{:S(2)}) collective-permute-start(bf16[256,2048]{1,0:T(8,128)(2,1)S(1)} %get-tuple-element.5), channel_id=1, source_target_pairs={{0,4},{12,8},{1,5},{13,9},{2,6},{14,10},{3,7},{15,11},{16,20},{28,... | collective-permute-start | bytes 3145736 | tf_op jit(solution)/shard_map/ppermute | solution.py:42
  7.7 0.7 collective-permute-start.1
  8.4 4.9 %collective-permute-start.2 = (bf16[256,2048]{1,0:T(8,128)(2,1)}, bf16[256,2048]{1,0:T(8,128)(2,1)}, u32[]{:S(2)}, u32[]{:S(2)}) collective-permute-start(bf16[256,2048]{1,0:T(8,128)(2,1)} %get-tuple-element.6), channel_id=1, source_target_pairs={{0,8},{12,4},{1,9},{13,5},{2,10},{14,6},{3,11},{15,7},{16,24},{28,... | collective-permute-start | bytes 3145736 | tf_op jit(solution)/shard_map/ppermute | solution.py:43
  13.3 17.8 %collective-permute-done = bf16[256,2048]{1,0:T(8,128)(2,1)S(1)} collective-permute-done((bf16[256,2048]{1,0:T(8,128)(2,1)S(1)}, bf16[256,2048]{1,0:T(8,128)(2,1)S(1)}, u32[]{:S(2)}, u32[]{:S(2)}) %collective-permute-start) | collective-permute-done | bytes 1048608 | tf_op jit(solution)/shard_map/ppermute | solution.py:42
  31.2 0.0 collective-permute-done.1
  31.2 21.5 %collective-permute-done.2 = bf16[256,2048]{1,0:T(8,128)(2,1)} collective-permute-done((bf16[256,2048]{1,0:T(8,128)(2,1)}, bf16[256,2048]{1,0:T(8,128)(2,1)}, u32[]{:S(2)}, u32[]{:S(2)}) %collective-permute-start.2) | collective-permute-done | bytes 1048608 | tf_op jit(solution)/shard_map/ppermute | solution.py:43
  52.6 1.8 %convert_reduce_fusion = f32[2048]{0:T(1024)S(1)} fusion(bf16[1,256,2048]{2,1,0:T(8,128)(2,1)} %bitcast.3, bf16[1,256,2048]{2,1,0:T(8,128)(2,1)S(1)} %bitcast.31, bf16[1,256,2048]{2,1,0:T(8,128)(2,1)S(1)} %bitcast.23, bf16[1,256,2048]{2,1,0:T(8,128)(2,1)S(1)} %bitcast.29), kind=kLoop, calls=%fused_computation.1 | loop fusion | flops 10483712 | bytes 4202496 | tf_op jit(solution)/shard_map/reduce_sum | solution.py:46
  54.5 2.1 %fusion = bf16[4,256,2048]{2,1,0:T(8,128)(2,1)S(1)} fusion(f32[2048]{0:T(1024)S(1)} %broadcast_multiply_fusion, bf16[1,256,2048]{2,1,0:T(8,128)(2,1)} %bitcast.3, bf16[1,256,2048]{2,1,0:T(8,128)(2,1)S(1)} %bitcast.32, bf16[1,256,2048]{2,1,0:T(8,128)(2,1)S(1)} %bitcast.24, bf16[1,256,2048]{2,1,0:T(8,128)(2,1)S(1)} %bitcast.30), kind=kLoop, calls=%fused_computation.2 | loop fusion | flops 12582912 | bytes 8396800 | tf_op jit(solution)/shard_map/convert_element_type | solution.py:47
  56.6 1.9 %copy-done = bf16[4,256,2048]{2,1,0:T(8,128)(2,1)} copy-done((bf16[4,256,2048]{2,1,0:T(8,128)(2,1)}, bf16[4,256,2048]{2,1,0:T(8,128)(2,1)S(1)}, u32[]{:S(2)}) %copy-start) | copy-done | bytes 4194328
  58.5 1.3 %fusion.2 = f32[1024,256]{1,0:T(8,128)S(1)} fusion(bf16[1024,2048]{1,0:T(8,128)(2,1)S(1)} %bitcast.25, bf16[4,256,2048]{2,1,0:T(8,128)(2,1)S(1)} %fusion, s32[]{:T(128)S(6)} %select_n.51), kind=kOutput, calls=%fused_computation.7 | convolution fusion | flops 1073741824 | bytes 6291460 | tf_op jit(solution)/shard_map/ip,jp->ij/dot_general | solution.py:8
  59.8 0.1 collective-permute-start.4
  59.9 4.9 %fusion.5 = f32[1024,256]{1,0:T(8,128)} fusion(bf16[1024,2048]{1,0:T(8,128)(2,1)} %bitcast.26, bf16[4,256,2048]{2,1,0:T(8,128)(2,1)} %copy-done, s32[]{:T(128)S(6)} %select_n.47), kind=kOutput, calls=%fused_computation.10 | convolution fusion | flops 1073741824 | bytes 6291460 | tf_op jit(solution)/shard_map/ip,jp->ij/dot_general | solution.py:8
  64.8 0.5 collective-permute-start.3
  65.3 0.0 collective-permute-done.4
  65.3 1.3 %convolution_add_fusion = f32[1024,256]{1,0:T(8,128)S(1)} fusion(f32[1024,256]{1,0:T(8,128)S(1)} %collective-permute-done.4, bf16[1024,2048]{1,0:T(8,128)(2,1)S(1)} %bitcast.28, bf16[4,256,2048]{2,1,0:T(8,128)(2,1)S(1)} %copy-done.1, s32[]{:T(128)S(6)} %select_n.49), kind=kOutput, calls=%fused_computation.4 | convolution fusion | flops 1074003968 | bytes 7340036 | tf_op jit(solution)/shard_map/ip,jp->ij/dot_general | solution.py:8
  66.6 1.6 %collective-permute-start.5 = (f32[1024,256]{1,0:T(8,128)S(1)}, f32[1024,256]{1,0:T(8,128)S(1)}, u32[]{:S(2)}, u32[]{:S(2)}) collective-permute-start(f32[1024,256]{1,0:T(8,128)S(1)} %convolution_add_fusion), channel_id=1, source_target_pairs={{0,2},{2,0},{1,3},{3,1},{4,6},{6,4},{5,7},{7,5},{8,10},{10,8},{9,1... | collective-permute-start | bytes 3145736 | tf_op jit(solution)/shard_map/ppermute | solution.py:59
  68.2 0.0 collective-permute-done.3
  68.2 23.6 %collective-permute-done.5 = f32[1024,256]{1,0:T(8,128)S(1)} collective-permute-done((f32[1024,256]{1,0:T(8,128)S(1)}, f32[1024,256]{1,0:T(8,128)S(1)}, u32[]{:S(2)}, u32[]{:S(2)}) %collective-permute-start.5) | collective-permute-done | bytes 1048608 | tf_op jit(solution)/shard_map/ppermute | solution.py:59
  91.8 3.8 %fusion.1 = f32[1024,256]{1,0:T(8,128)S(1)} fusion(f32[1024,256]{1,0:T(8,128)S(1)} %collective-permute-done.5, f32[1024,256]{1,0:T(8,128)S(1)} %collective-permute-done.3, bf16[1024,2048]{1,0:T(8,128)(2,1)} %bitcast.27, bf16[4,256,2048]{2,1,0:T(8,128)(2,1)} %copy-done, s32[]{:T(128)S(6)} %select_n.45), kind=kOutput, calls=%fused_computation.6 | convolution fusion | flops 1074266112 | bytes 8388612 | tf_op jit(solution)/shard_map/ip,jp->ij/dot_general | solution.py:8
  95.6 0.7 collective-permute-start.6
  96.4 1.3 %collective-permute-start.7 = (f32[256,256]{1,0:T(8,128)S(1)}, f32[256,256]{1,0:T(8,128)S(1)}, u32[]{:S(2)}, u32[]{:S(2)}) collective-permute-start(f32[256,256]{1,0:T(8,128)S(1)} %slice_add_fusion), channel_id=1, source_target_pairs={{4,0},{8,12},{5,1},{9,13},{6,2},{10,14},{7,3},{11,15},{20,16},{24,... | collective-permute-start | bytes 786440 | tf_op jit(solution)/shard_map/ppermute | solution.py:70
  98.3 22.1 %collective-permute-done.7 = f32[256,256]{1,0:T(8,128)S(1)} collective-permute-done((f32[256,256]{1,0:T(8,128)S(1)}, f32[256,256]{1,0:T(8,128)S(1)}, u32[]{:S(2)}, u32[]{:S(2)}) %collective-permute-start.7) | collective-permute-done | bytes 262176 | tf_op jit(solution)/shard_map/ppermute | solution.py:70
  120.5 0.8 fusion.14
  (8 shorter events, 0.1 us)
Async XLA Ops:
  2.7 28.5 %collective-permute-start = (bf16[256,2048]{1,0:T(8,128)(2,1)S(1)}, bf16[256,2048]{1,0:T(8,128)(2,1)S(1)}, u32[]{:S(2)}, u32[]{:S(2)}) collective-permute-start(bf16[256,2048]{1,0:T(8,128)(2,1)S(1)} %get-tuple-element.5), channel_id=1, source_target_pairs={{0,4},{12,8},{1,5},{13,9},{2,6},{14,10},{3,7},{15,11},{16,20},{28,... | collective-permute-start | bytes 3145736 | tf_op jit(solution)/shard_map/ppermute | solution.py:42
  7.7 23.5 %collective-permute-start.1 = (bf16[256,2048]{1,0:T(8,128)(2,1)}, bf16[256,2048]{1,0:T(8,128)(2,1)S(1)}, u32[]{:S(2)}, u32[]{:S(2)}) collective-permute-start(bf16[256,2048]{1,0:T(8,128)(2,1)} %get-tuple-element.6), channel_id=1, source_target_pairs={{4,8},{8,4},{5,9},{9,5},{6,10},{10,6},{7,11},{11,7},{20,24},{24,20... | collective-permute-start | bytes 3145736 | tf_op jit(solution)/shard_map/ppermute | solution.py:41
  8.4 44.2 %collective-permute-start.2 = (bf16[256,2048]{1,0:T(8,128)(2,1)}, bf16[256,2048]{1,0:T(8,128)(2,1)}, u32[]{:S(2)}, u32[]{:S(2)}) collective-permute-start(bf16[256,2048]{1,0:T(8,128)(2,1)} %get-tuple-element.6), channel_id=1, source_target_pairs={{0,8},{12,4},{1,9},{13,5},{2,10},{14,6},{3,11},{15,7},{16,24},{28,... | collective-permute-start | bytes 3145736 | tf_op jit(solution)/shard_map/ppermute | solution.py:43
  56.6 1.9 %copy-start = (bf16[4,256,2048]{2,1,0:T(8,128)(2,1)}, bf16[4,256,2048]{2,1,0:T(8,128)(2,1)S(1)}, u32[]{:S(2)}) copy-start(bf16[4,256,2048]{2,1,0:T(8,128)(2,1)S(1)} %fusion) | copy-start | bytes 12582916
  59.8 5.5 %collective-permute-start.4 = (f32[1024,256]{1,0:T(8,128)S(1)}, f32[1024,256]{1,0:T(8,128)S(1)}, u32[]{:S(2)}, u32[]{:S(2)}) collective-permute-start(f32[1024,256]{1,0:T(8,128)S(1)} %fusion.2), channel_id=1, source_target_pairs={{0,1},{1,0},{2,3},{3,2},{4,5},{5,4},{6,7},{7,6},{8,9},{9,8},{10,11... | collective-permute-start | bytes 3145736 | tf_op jit(solution)/shard_map/ppermute | solution.py:59
  59.9 5.4 %copy-start.1 = (bf16[4,256,2048]{2,1,0:T(8,128)(2,1)S(1)}, bf16[4,256,2048]{2,1,0:T(8,128)(2,1)}, u32[]{:S(2)}) copy-start(bf16[4,256,2048]{2,1,0:T(8,128)(2,1)} %copy-done) | copy-start | bytes 12582916
  64.8 3.4 %collective-permute-start.3 = (f32[1024,256]{1,0:T(8,128)}, f32[1024,256]{1,0:T(8,128)S(1)}, u32[]{:S(2)}, u32[]{:S(2)}) collective-permute-start(f32[1024,256]{1,0:T(8,128)} %fusion.5), channel_id=1, source_target_pairs={{0,1},{1,0},{2,3},{3,2},{4,5},{5,4},{6,7},{7,6},{8,9},{9,8},{10,11... | collective-permute-start | bytes 3145736 | tf_op jit(solution)/shard_map/ppermute | solution.py:59
  66.6 25.2 %collective-permute-start.5 = (f32[1024,256]{1,0:T(8,128)S(1)}, f32[1024,256]{1,0:T(8,128)S(1)}, u32[]{:S(2)}, u32[]{:S(2)}) collective-permute-start(f32[1024,256]{1,0:T(8,128)S(1)} %convolution_add_fusion), channel_id=1, source_target_pairs={{0,2},{2,0},{1,3},{3,1},{4,6},{6,4},{5,7},{7,5},{8,10},{10,8},{9,1... | collective-permute-start | bytes 3145736 | tf_op jit(solution)/shard_map/ppermute | solution.py:59
  95.6 0.7 collective-permute-start.6
  96.4 24.1 %collective-permute-start.7 = (f32[256,256]{1,0:T(8,128)S(1)}, f32[256,256]{1,0:T(8,128)S(1)}, u32[]{:S(2)}, u32[]{:S(2)}) collective-permute-start(f32[256,256]{1,0:T(8,128)S(1)} %slice_add_fusion), channel_id=1, source_target_pairs={{4,0},{8,12},{5,1},{9,13},{6,2},{10,14},{7,3},{11,15},{20,16},{24,... | collective-permute-start | bytes 786440 | tf_op jit(solution)/shard_map/ppermute | solution.py:70

commit v2 on v1

v2 whole, which is shorter than its diff:
```python
import jax
import jax.numpy as jnp
from jax import lax
from jax.sharding import PartitionSpec as P


def pair_product(left, right):
    return jnp.einsum("ip,jp->ij", left, right, preferred_element_type=jnp.float32)


def add_shift(summed, samples, shift, local_rows):
    width = summed.shape[1]
    first_row = lax.axis_index("row") * local_rows
    block = lax.axis_index("col") * lax.axis_size("half") + lax.axis_index("half")
    row_ids = first_row + lax.broadcasted_iota(jnp.int32, (local_rows, width), 0)
    column_ids = block * width + lax.broadcasted_iota(jnp.int32, (local_rows, width), 1)
    return summed / samples + jnp.where(row_ids == column_ids, shift[0], 0.0)


def gathered(log_derivs, shift):
    local_rows = log_derivs.shape[0]
    samples = local_rows * lax.axis_size("row")
    rows = lax.all_gather(log_derivs, "row", axis=0, tiled=True).astype(jnp.float32)
    mean = jnp.sum(rows, axis=0) / samples
    centered = (rows - mean[None, :]).astype(jnp.bfloat16)
    own = (log_derivs.astype(jnp.float32) - mean[None, :]).astype(jnp.bfloat16)
    tile = pair_product(own, centered)
    summed = lax.psum_scatter(tile, ("col", "half"), scatter_dimension=1, tiled=True)
    return add_shift(summed, samples, shift, local_rows)


EARLY = (
    (((0, 0), (0, 1)), ((0, 2), (1, 2))),
    (((0, 1), (0, 0)), ((1, 2), (2, 2))),
    (((1, 0), (1, 1)), ((2, 0), (0, 2))),
    (((1, 1), (1, 0)), ((2, 1), (2, 0))),
    ((None, None), ((2, 2), (2, 1))),
)
LATE = (
    (((3, 0), (3, 1)), ((3, 2), (3, 3))),
    (((3, 1), (3, 0)), ((3, 3), (3, 2))),
    (((0, 3), (1, 3)), ((2, 3), None)),
    (((1, 3), (0, 3)), (None, (2, 3))),
)


def device_index(row, col, half):
    return (row * 2 + col) * 2 + half


def round_pairs(blocks):
    pairs = []
    for side in (0, 1):
        for turn in (0, 1):
            for half in (0, 1):
                block = blocks[half][turn]
                if block is None:
                    continue
                i, j = (3 - b if side else b for b in block)
                source = device_index(1 + side, turn ^ side, half)
                pairs.append((source, device_index(i, j // 2, j % 2)))
    return pairs


def two_centres(log_derivs, shift):
    local_rows, local_params = log_derivs.shape
    samples = local_rows * 4
    part = local_params // 2
    everyone = ("row", "col", "half")
    row, col, half = (lax.axis_index(name) for name in everyone)
    side = (row >= 2).astype(jnp.int32)
    turn = jnp.bitwise_xor(col, side)
    near = lax.dynamic_slice_in_dim(log_derivs, (1 - side) * part, part, 1)
    far = lax.dynamic_slice_in_dim(log_derivs, side * part, part, 1)

    to_centre = [(1, 2), (2, 1)]
    to_own = [(0, 1), (3, 2)]
    to_far = [(0, 2), (3, 1)]
    centres = [(r * 2 + h, r * 2 + 1 - h) for r in (1, 2) for h in (0, 1)]

    def swap(value):
        return lax.ppermute(value, ("row", "half"), centres)

    def sums(value):
        return jnp.sum(value.astype(jnp.float32), axis=0, keepdims=True)

    from_centre = lax.ppermute(far, "row", to_centre)
    from_edge = lax.ppermute(near, "row", to_own)
    near_sum, far_sum = sums(near), sums(far)
    total = near_sum + lax.ppermute(near_sum, "row", to_own)
    total = total + lax.ppermute(far_sum, "row", to_centre)
    total = total + lax.ppermute(far_sum, "row", to_far)
    mean = total / samples
    mean = jnp.concatenate([mean, swap(mean)], axis=1)
    from_far_edge = lax.ppermute(far, "row", to_far)

    def centred(own):
        both = jnp.concatenate([own, swap(own)], axis=1).astype(jnp.float32)
        return (both - mean).astype(jnp.bfloat16)

    def scaled(product):
        return (product / samples).astype(jnp.float16)

    edge, centre, other_centre = centred(from_edge), centred(near), centred(from_centre)
    early = jnp.concatenate([edge, centre, other_centre], axis=0)
    early_tile = scaled(pair_product(early, early))

    def pick(blocks):
        table = jnp.array([[b or (0, 0) for b in pair] for pair in blocks], jnp.int32)
        place = table[half, turn] * local_rows
        return lax.dynamic_slice(early_tile, (place[0], place[1]), (local_rows, local_rows))

    def send(value, blocks):
        return lax.ppermute(value, everyone, round_pairs(blocks))

    arrived = [send(pick(blocks), blocks) for blocks in EARLY]

    last = centred(from_far_edge)
    lower = jnp.concatenate([edge, centre], axis=0)
    upper = jnp.concatenate([other_centre, last], axis=0)
    held = jnp.where(half == 0, lower, upper)
    wide = scaled(pair_product(last, held)).reshape(local_rows, 2, local_rows)
    tall = scaled(pair_product(held, last)).reshape(2, local_rows, local_rows)
    flip = (1 - half) * turn
    keep = (1 - half) * (1 - turn)
    late = [
        lax.dynamic_index_in_dim(wide, turn, 1, keepdims=False),
        lax.dynamic_index_in_dim(wide, 1 - turn, 1, keepdims=False),
        lax.dynamic_index_in_dim(tall, flip, 0, keepdims=False),
        lax.dynamic_index_in_dim(tall, keep, 0, keepdims=False),
    ]
    arrived += [send(value, blocks) for value, blocks in zip(late, LATE)]
    summed = sum(block.astype(jnp.float32) for block in arrived)
    return add_shift(summed, 1, shift, local_rows)


def solution(mesh):
    shape = mesh.shape
    small = shape["row"] == 4 and shape["col"] == 2 and shape["half"] == 2
    return jax.shard_map(
        two_centres if small else gathered,
        mesh=mesh,
        in_specs=(P(("groups", "row"), ("col", "half")), P("groups")),
        out_specs=P(("groups", "row"), ("col", "half")),
        check_vma=False,
    )
```

time: 122 us -> 127 us (1.041)
  the two profiles are of different devices: /device:TPU:0 before, /device:TPU:8 now
where the time goes in v2:
time: 127 us; the launch traced here: 125 us
  starting transfers between devices  41.5 us (33%)
  waiting for transfers between devices  39.2 us (31%)
  between operations  19.8 us (16%)
  other arithmetic  10.2 us (8%)
  matrix products  8.72 us (7%)
  local copies, waits for them, and re-layouts  5.4 us (4%)
    ppermute x1, waiting for transfers between devices, two_centres(): total = near_sum + lax.ppermute(near_sum, 'row', to_own)  35.8 us
    ppermute x9, starting transfers between devices, send(): return lax.ppermute(value, everyone, round_pairs(blocks))  19.9 us
    ppermute x5, starting transfers between devices, swap(): return lax.ppermute(value, ('row', 'half'), centres)  10.6 us
    dot_general x3, matrix products, pair_product(): jnp.einsum('ip,jp->ij', left, right, preferred_element_type=jnp.float32)  8.72 us
    convert_element_type x1, other arithmetic, centred(): return (both - mean).astype(jnp.bfloat16)  4 us
    ppermute x1, starting transfers between devices, two_centres(): from_centre = lax.ppermute(far, 'row', to_centre)  3.49 us
    reduce_sum x1, other arithmetic, sums(): return jnp.sum(value.astype(jnp.float32), axis=0, keepdims=True)  3.17 us
    slice x5, local copies, waits for them, and re-layouts, pick(): place[1]  3.11 us
  transfers between devices with their start and end apart: 20, of which 4 were waited for; matrix products, arithmetic and copies ran while one was open for 5% of the time, Pallas kernels for 0%

profile of v2, /device:TPU:8, one launch (start us, length us, event | category | flops | bytes accessed | tf_op | source)
XLA Modules:
  0.0 124.8 jit_solution(15275303769650817189)
XLA Ops:
  0.0 3.2 %convert_reduce_fusion.1 = (f32[2048]{0:T(1024)S(1)}, bf16[256,2048]{1,0:T(8,128)(2,1)S(1)}, f32[2048]{0:T(1024)S(1)}, bf16[256,2048]{1,0:T(8,128)(2,1)}) fusion(bf16[256,4096]{1,0:T(8,128)(2,1)} %param.7, s32[]{:T(128)S(6)} %select_n.72, s32[]{:T(128)S(6)} %mul.42), kind=kLoop, calls=%fused_computation.13 | loop fusion | flops 2093056 | bytes 4210696 | tf_op jit(solution)/shard_map/reduce_sum | solution.py:85
  4.5 1.3 %collective-permute-start.14 = (bf16[256,2048]{1,0:T(8,128)(2,1)}, bf16[256,2048]{1,0:T(8,128)(2,1)}, u32[]{:S(2)}, u32[]{:S(2)}) collective-permute-start(bf16[256,2048]{1,0:T(8,128)(2,1)} %get-tuple-element.10), channel_id=1, source_target_pairs={{0,8},{12,4},{1,9},{13,5},{2,10},{14,6},{3,11},{15,7},{16,24},{28,... | collective-permute-start | bytes 3145736 | tf_op jit(solution)/shard_map/ppermute | solution.py:95
  5.8 3.5 %collective-permute-start.7 = (bf16[256,2048]{1,0:T(8,128)(2,1)}, bf16[256,2048]{1,0:T(8,128)(2,1)}, u32[]{:S(2)}, u32[]{:S(2)}) collective-permute-start(bf16[256,2048]{1,0:T(8,128)(2,1)} %get-tuple-element.10), channel_id=1, source_target_pairs={{4,8},{8,4},{5,9},{9,5},{6,10},{10,6},{7,11},{11,7},{20,24},{24,20... | collective-permute-start | bytes 3145736 | tf_op jit(solution)/shard_map/ppermute | solution.py:87
  9.3 1.3 %collective-permute-start.2 = (f32[1,2048]{1,0:T(1,128)S(1)}, f32[1,2048]{1,0:T(1,128)S(1)}, u32[]{:S(2)}, u32[]{:S(2)}) collective-permute-start(f32[1,2048]{1,0:T(1,128)S(1)} %bitcast.32), channel_id=1, source_target_pairs={{0,4},{12,8},{1,5},{13,9},{2,6},{14,10},{3,7},{15,11},{16,20},{28,... | collective-permute-start | bytes 24584 | tf_op jit(solution)/shard_map/ppermute | solution.py:90
  10.6 2.4 %collective-permute-start.3 = (f32[1,2048]{1,0:T(1,128)S(1)}, f32[1,2048]{1,0:T(1,128)S(1)}, u32[]{:S(2)}, u32[]{:S(2)}) collective-permute-start(f32[1,2048]{1,0:T(1,128)S(1)} %bitcast.34), channel_id=1, source_target_pairs={{4,8},{8,4},{5,9},{9,5},{6,10},{10,6},{7,11},{11,7},{20,24},{24,20... | collective-permute-start | bytes 24584 | tf_op jit(solution)/shard_map/ppermute | solution.py:91
  16.8 35.8 %collective-permute-done.2 = f32[1,2048]{1,0:T(1,128)S(1)} collective-permute-done((f32[1,2048]{1,0:T(1,128)S(1)}, f32[1,2048]{1,0:T(1,128)S(1)}, u32[]{:S(2)}, u32[]{:S(2)}) %collective-permute-start.2) | collective-permute-done | bytes 8224 | tf_op jit(solution)/shard_map/ppermute | solution.py:90
  53.9 1.5 %collective-permute-done.3 = f32[1,2048]{1,0:T(1,128)S(1)} collective-permute-done((f32[1,2048]{1,0:T(1,128)S(1)}, f32[1,2048]{1,0:T(1,128)S(1)}, u32[]{:S(2)}, u32[]{:S(2)}) %collective-permute-start.3) | collective-permute-done | bytes 8224 | tf_op jit(solution)/shard_map/ppermute | solution.py:91
  55.4 1.9 %collective-permute-start.6 = (bf16[256,2048]{1,0:T(8,128)(2,1)S(1)}, bf16[256,2048]{1,0:T(8,128)(2,1)}, u32[]{:S(2)}, u32[]{:S(2)}) collective-permute-start(bf16[256,2048]{1,0:T(8,128)(2,1)S(1)} %get-tuple-element.6), channel_id=1, source_target_pairs={{4,5},{5,4},{8,9},{9,8},{6,7},{7,6},{10,11},{11,10},{20,21},{21,20... | collective-permute-start | bytes 3145736 | tf_op jit(solution)/shard_map/ppermute | solution.py:82
  57.4 2.4 %collective-permute-start.1 = (bf16[256,2048]{1,0:T(8,128)(2,1)S(1)}, bf16[256,2048]{1,0:T(8,128)(2,1)S(1)}, u32[]{:S(2)}, u32[]{:S(2)}) collective-permute-start(bf16[256,2048]{1,0:T(8,128)(2,1)S(1)} %collective-permute-done), channel_id=1, source_target_pairs={{4,5},{5,4},{8,9},{9,8},{6,7},{7,6},{10,11},{11,10},{20,21},{21,20... | collective-permute-start | bytes 3145736 | tf_op jit(solution)/shard_map/ppermute | solution.py:82
  59.8 1.9 %collective-permute-start.15 = (bf16[256,2048]{1,0:T(8,128)(2,1)}, bf16[256,2048]{1,0:T(8,128)(2,1)}, u32[]{:S(2)}, u32[]{:S(2)}) collective-permute-start(bf16[256,2048]{1,0:T(8,128)(2,1)} %collective-permute-done.14), channel_id=1, source_target_pairs={{4,5},{5,4},{8,9},{9,8},{6,7},{7,6},{10,11},{11,10},{20,21},{21,20... | collective-permute-start | bytes 3145736 | tf_op jit(solution)/shard_map/ppermute | solution.py:82
  61.7 2.4 %collective-permute-start.8 = (bf16[256,2048]{1,0:T(8,128)(2,1)}, bf16[256,2048]{1,0:T(8,128)(2,1)}, u32[]{:S(2)}, u32[]{:S(2)}) collective-permute-start(bf16[256,2048]{1,0:T(8,128)(2,1)} %collective-permute-done.7), channel_id=1, source_target_pairs={{4,5},{5,4},{8,9},{9,8},{6,7},{7,6},{10,11},{11,10},{20,21},{21,20... | collective-permute-start | bytes 3145736 | tf_op jit(solution)/shard_map/ppermute | solution.py:82
  64.9 1.9 %collective-permute-start.5 = (f32[1,2048]{1,0:T(1,128)S(1)}, f32[1,2048]{1,0:T(1,128)S(1)}, u32[]{:S(2)}, u32[]{:S(2)}) collective-permute-start(f32[1,2048]{1,0:T(1,128)S(1)} %add_multiply_fusion), channel_id=1, source_target_pairs={{4,5},{5,4},{8,9},{9,8},{6,7},{7,6},{10,11},{11,10},{20,21},{21,20... | collective-permute-start | bytes 24584 | tf_op jit(solution)/shard_map/ppermute | solution.py:82
  87.2 4.0 %subtract_convert_fusion.1 = (bf16[256,4096]{1,0:T(8,128)(2,1)S(1)}, bf16[256,4096]{1,0:T(8,128)(2,1)S(1)}, bf16[256,4096]{1,0:T(8,128)(2,1)S(1)}, bf16[256,4096]{1,0:T(8,128)(2,1)S(1)}) fusion(bf16[256,2048]{1,0:T(8,128)(2,1)} %collective-permute-done.8, bf16[256,2048]{1,0:T(8,128)(2,1)} %collective-permute-done.7, f32[4096]{0:T(1024)S(1)} %bitcast.31, ...), kind=kLoop, calls=%fused_computation.8 | loop fusion | flops 25165824 | bytes 16793600 | tf_op jit(solution)/shard_map/convert_element_type | solution.py:99
  91.2 6.1 %multiply_convert_fusion = f16[768,768]{1,0:T(8,128)(2,1)} fusion(bf16[256,4096]{1,0:T(8,128)(2,1)S(1)} %get-tuple-element.20, bf16[256,4096]{1,0:T(8,128)(2,1)S(1)} %get-tuple-element.21, bf16[256,4096]{1,0:T(8,128)(2,1)S(1)} %get-tuple-element.23), kind=kOutput, calls=%fused_computation.11 | convolution fusion | flops 4851892224 | bytes 7471104 | tf_op jit(solution)/shard_map/ip,jp->ij/dot_general | solution.py:8
  97.3 1.3 %fusion.6 = f16[256,512]{1,0:T(8,128)(2,1)S(1)} fusion(bf16[256,4096]{1,0:T(8,128)(2,1)S(1)} %get-tuple-element.22, bf16[256,4096]{1,0:T(8,128)(2,1)S(1)} %get-tuple-element.21, bf16[256,4096]{1,0:T(8,128)(2,1)S(1)} %get-tuple-element.23, bf16[256,4096]{1,0:T(8,128)(2,1)S(1)} %get-tuple-element.20, pred[]{:T(512)S(6)} %eq.6), kind=kOutput, calls=%fused_computation.16 | convolution fusion | flops 1092878336 | bytes 8650753 | tf_op jit(solution)/shard_map/ip,jp->ij/dot_general | solution.py:8
  98.7 1.3 %fusion.7 = f16[512,256]{1,0:T(8,128)(2,1)S(1)} fusion(bf16[256,4096]{1,0:T(8,128)(2,1)S(1)} %get-tuple-element.22, bf16[256,4096]{1,0:T(8,128)(2,1)S(1)} %get-tuple-element.21, bf16[256,4096]{1,0:T(8,128)(2,1)S(1)} %get-tuple-element.23, bf16[256,4096]{1,0:T(8,128)(2,1)S(1)} %get-tuple-element.20, pred[]{:T(512)S(6)} %eq.6), kind=kOutput, calls=%fused_computation.17 | convolution fusion | flops 1092878336 | bytes 8650753 | tf_op jit(solution)/shard_map/ip,jp->ij/dot_general | solution.py:8
  100.4 1.3 %collective-permute-start.10 = (f16[256,256]{1,0:T(8,128)(2,1)S(1)}, f16[256,256]{1,0:T(8,128)(2,1)S(1)}, u32[]{:S(2)}, u32[]{:S(2)}) collective-permute-start(f16[256,256]{1,0:T(8,128)(2,1)S(1)} %get-tuple-element.15), channel_id=1, source_target_pairs={{4,1},{5,6},{6,0},{7,10},{10,14},{11,9},{8,15},{9,5},{20,17},{21,2... | collective-permute-start | bytes 393224 | tf_op jit(solution)/shard_map/ppermute | solution.py:114
  102.4 5.4 %collective-permute-start.12 = (f16[256,256]{1,0:T(8,128)(2,1)S(1)}, f16[256,256]{1,0:T(8,128)(2,1)S(1)}, u32[]{:S(2)}, u32[]{:S(2)}) collective-permute-start(f16[256,256]{1,0:T(8,128)(2,1)S(1)} %get-tuple-element.13), channel_id=1, source_target_pairs={{4,5},{5,9},{6,4},{7,8},{10,10},{11,6},{8,11},{9,7},{20,21},{21,25... | collective-permute-start | bytes 393224 | tf_op jit(solution)/shard_map/ppermute | solution.py:114
  108.5 1.3 %collective-permute-start.9 = (f16[256,256]{1,0:T(8,128)(2,1)S(1)}, f16[256,256]{1,0:T(8,128)(2,1)S(1)}, u32[]{:S(2)}, u32[]{:S(2)}) collective-permute-start(f16[256,256]{1,0:T(8,128)(2,1)S(1)} %get-tuple-element.11), channel_id=1, source_target_pairs={{4,0},{5,2},{6,1},{7,6},{10,15},{11,13},{8,14},{9,9},{20,16},{21,1... | collective-permute-start | bytes 393224 | tf_op jit(solution)/shard_map/ppermute | solution.py:114
  110.7 1.3 %collective-permute-start.16 = (f16[256,256]{1,0:T(8,128)(2,1)S(1)}, f16[256,256]{1,0:T(8,128)(2,1)S(1)}, u32[]{:S(2)}, u32[]{:S(2)}) collective-permute-start(f16[256,256]{1,0:T(8,128)(2,1)S(1)} %bitcast.30), channel_id=1, source_target_pairs={{4,12},{5,14},{6,13},{7,15},{10,3},{11,1},{8,2},{9,0},{20,28},{21,... | collective-permute-start | bytes 393224 | tf_op jit(solution)/shard_map/ppermute | solution.py:114
  112.0 1.3 %collective-permute-start.17 = (f16[256,256]{1,0:T(8,128)(2,1)S(1)}, f16[256,256]{1,0:T(8,128)(2,1)S(1)}, u32[]{:S(2)}, u32[]{:S(2)}) collective-permute-start(f16[256,256]{1,0:T(8,128)(2,1)S(1)} %bitcast.29), channel_id=1, source_target_pairs={{4,13},{5,15},{6,12},{7,14},{10,2},{11,0},{8,3},{9,1},{20,29},{21,... | collective-permute-start | bytes 393224 | tf_op jit(solution)/shard_map/ppermute | solution.py:114
  113.4 1.9 %collective-permute-start.18 = (f16[256,256]{1,0:T(8,128)(2,1)S(1)}, f16[256,256]{1,0:T(8,128)(2,1)S(1)}, u32[]{:S(2)}, u32[]{:S(2)}) collective-permute-start(f16[256,256]{1,0:T(8,128)(2,1)S(1)} %get-tuple-element.18), channel_id=1, source_target_pairs={{4,3},{5,11},{6,7},{10,12},{11,4},{8,8},{20,19},{21,27},{22,23},{2... | collective-permute-start | bytes 393224 | tf_op jit(solution)/shard_map/ppermute | solution.py:114
  115.3 6.1 %collective-permute-start.19 = (f16[256,256]{1,0:T(8,128)(2,1)S(1)}, f16[256,256]{1,0:T(8,128)(2,1)S(1)}, u32[]{:S(2)}, u32[]{:S(2)}) collective-permute-start(f16[256,256]{1,0:T(8,128)(2,1)S(1)} %get-tuple-element.19), channel_id=1, source_target_pairs={{4,7},{6,3},{7,11},{10,8},{8,12},{9,4},{20,23},{22,19},{23,27},{26... | collective-permute-start | bytes 393224 | tf_op jit(solution)/shard_map/ppermute | solution.py:114
  122.5 1.4 %collective-permute-done.19 = f16[256,256]{1,0:T(8,128)(2,1)S(1)} collective-permute-done((f16[256,256]{1,0:T(8,128)(2,1)S(1)}, f16[256,256]{1,0:T(8,128)(2,1)S(1)}, u32[]{:S(2)}, u32[]{:S(2)}) %collective-permute-start.19) | collective-permute-done | bytes 131104 | tf_op jit(solution)/shard_map/ppermute | solution.py:114
  (45 shorter events, 12.7 us)
Async XLA Ops:
  3.2 54.2 %collective-permute-start = (bf16[256,2048]{1,0:T(8,128)(2,1)S(1)}, bf16[256,2048]{1,0:T(8,128)(2,1)S(1)}, u32[]{:S(2)}, u32[]{:S(2)}) collective-permute-start(bf16[256,2048]{1,0:T(8,128)(2,1)S(1)} %get-tuple-element.6), channel_id=1, source_target_pairs={{0,4},{12,8},{1,5},{13,9},{2,6},{14,10},{3,7},{15,11},{16,20},{28,... | collective-permute-start | bytes 3145736 | tf_op jit(solution)/shard_map/ppermute | solution.py:88
  4.5 55.3 %collective-permute-start.14 = (bf16[256,2048]{1,0:T(8,128)(2,1)}, bf16[256,2048]{1,0:T(8,128)(2,1)}, u32[]{:S(2)}, u32[]{:S(2)}) collective-permute-start(bf16[256,2048]{1,0:T(8,128)(2,1)} %get-tuple-element.10), channel_id=1, source_target_pairs={{0,8},{12,4},{1,9},{13,5},{2,10},{14,6},{3,11},{15,7},{16,24},{28,... | collective-permute-start | bytes 3145736 | tf_op jit(solution)/shard_map/ppermute | solution.py:95
  5.8 56.0 %collective-permute-start.7 = (bf16[256,2048]{1,0:T(8,128)(2,1)}, bf16[256,2048]{1,0:T(8,128)(2,1)}, u32[]{:S(2)}, u32[]{:S(2)}) collective-permute-start(bf16[256,2048]{1,0:T(8,128)(2,1)} %get-tuple-element.10), channel_id=1, source_target_pairs={{4,8},{8,4},{5,9},{9,5},{6,10},{10,6},{7,11},{11,7},{20,24},{24,20... | collective-permute-start | bytes 3145736 | tf_op jit(solution)/shard_map/ppermute | solution.py:87
  9.3 43.4 %collective-permute-start.2 = (f32[1,2048]{1,0:T(1,128)S(1)}, f32[1,2048]{1,0:T(1,128)S(1)}, u32[]{:S(2)}, u32[]{:S(2)}) collective-permute-start(f32[1,2048]{1,0:T(1,128)S(1)} %bitcast.32), channel_id=1, source_target_pairs={{0,4},{12,8},{1,5},{13,9},{2,6},{14,10},{3,7},{15,11},{16,20},{28,... | collective-permute-start | bytes 24584 | tf_op jit(solution)/shard_map/ppermute | solution.py:90
  10.6 44.9 %collective-permute-start.3 = (f32[1,2048]{1,0:T(1,128)S(1)}, f32[1,2048]{1,0:T(1,128)S(1)}, u32[]{:S(2)}, u32[]{:S(2)}) collective-permute-start(f32[1,2048]{1,0:T(1,128)S(1)} %bitcast.34), channel_id=1, source_target_pairs={{4,8},{8,4},{5,9},{9,5},{6,10},{10,6},{7,11},{11,7},{20,24},{24,20... | collective-permute-start | bytes 24584 | tf_op jit(solution)/shard_map/ppermute | solution.py:91
  52.6 12.2 %collective-permute-start.4 = (f32[1,2048]{1,0:T(1,128)S(1)}, f32[1,2048]{1,0:T(1,128)S(1)}, u32[]{:S(2)}, u32[]{:S(2)}) collective-permute-start(f32[1,2048]{1,0:T(1,128)S(1)} %bitcast.35), channel_id=1, source_target_pairs={{0,8},{12,4},{1,9},{13,5},{2,10},{14,6},{3,11},{15,7},{16,24},{28,... | collective-permute-start | bytes 24584 | tf_op jit(solution)/shard_map/ppermute | solution.py:92
  55.4 30.8 %collective-permute-start.6 = (bf16[256,2048]{1,0:T(8,128)(2,1)S(1)}, bf16[256,2048]{1,0:T(8,128)(2,1)}, u32[]{:S(2)}, u32[]{:S(2)}) collective-permute-start(bf16[256,2048]{1,0:T(8,128)(2,1)S(1)} %get-tuple-element.6), channel_id=1, source_target_pairs={{4,5},{5,4},{8,9},{9,8},{6,7},{7,6},{10,11},{11,10},{20,21},{21,20... | collective-permute-start | bytes 3145736 | tf_op jit(solution)/shard_map/ppermute | solution.py:82
  57.4 28.9 %copy-start = (bf16[256,2048]{1,0:T(8,128)(2,1)}, bf16[256,2048]{1,0:T(8,128)(2,1)S(1)}, u32[]{:S(2)}) copy-start(bf16[256,2048]{1,0:T(8,128)(2,1)S(1)} %collective-permute-done) | copy-start | bytes 3145732
  57.4 28.9 %collective-permute-start.1 = (bf16[256,2048]{1,0:T(8,128)(2,1)S(1)}, bf16[256,2048]{1,0:T(8,128)(2,1)S(1)}, u32[]{:S(2)}, u32[]{:S(2)}) collective-permute-start(bf16[256,2048]{1,0:T(8,128)(2,1)S(1)} %collective-permute-done), channel_id=1, source_target_pairs={{4,5},{5,4},{8,9},{9,8},{6,7},{7,6},{10,11},{11,10},{20,21},{21,20... | collective-permute-start | bytes 3145736 | tf_op jit(solution)/shard_map/ppermute | solution.py:82
  59.8 26.5 %collective-permute-start.15 = (bf16[256,2048]{1,0:T(8,128)(2,1)}, bf16[256,2048]{1,0:T(8,128)(2,1)}, u32[]{:S(2)}, u32[]{:S(2)}) collective-permute-start(bf16[256,2048]{1,0:T(8,128)(2,1)} %collective-permute-done.14), channel_id=1, source_target_pairs={{4,5},{5,4},{8,9},{9,8},{6,7},{7,6},{10,11},{11,10},{20,21},{21,20... | collective-permute-start | bytes 3145736 | tf_op jit(solution)/shard_map/ppermute | solution.py:82
  61.7 24.5 %collective-permute-start.8 = (bf16[256,2048]{1,0:T(8,128)(2,1)}, bf16[256,2048]{1,0:T(8,128)(2,1)}, u32[]{:S(2)}, u32[]{:S(2)}) collective-permute-start(bf16[256,2048]{1,0:T(8,128)(2,1)} %collective-permute-done.7), channel_id=1, source_target_pairs={{4,5},{5,4},{8,9},{9,8},{6,7},{7,6},{10,11},{11,10},{20,21},{21,20... | collective-permute-start | bytes 3145736 | tf_op jit(solution)/shard_map/ppermute | solution.py:82
  64.9 21.3 %collective-permute-start.5 = (f32[1,2048]{1,0:T(1,128)S(1)}, f32[1,2048]{1,0:T(1,128)S(1)}, u32[]{:S(2)}, u32[]{:S(2)}) collective-permute-start(f32[1,2048]{1,0:T(1,128)S(1)} %add_multiply_fusion), channel_id=1, source_target_pairs={{4,5},{5,4},{8,9},{9,8},{6,7},{7,6},{10,11},{11,10},{20,21},{21,20... | collective-permute-start | bytes 24584 | tf_op jit(solution)/shard_map/ppermute | solution.py:82
  86.3 1.0 copy-start.1
  98.6 1.3 %copy-start.2 = (f16[768,768]{1,0:T(8,128)(2,1)S(1)}, f16[768,768]{1,0:T(8,128)(2,1)}, u32[]{:S(2)}) copy-start(f16[768,768]{1,0:T(8,128)(2,1)} %multiply_convert_fusion) | copy-start | bytes 3538948
  100.4 10.3 %collective-permute-start.10 = (f16[256,256]{1,0:T(8,128)(2,1)S(1)}, f16[256,256]{1,0:T(8,128)(2,1)S(1)}, u32[]{:S(2)}, u32[]{:S(2)}) collective-permute-start(f16[256,256]{1,0:T(8,128)(2,1)S(1)} %get-tuple-element.15), channel_id=1, source_target_pairs={{4,1},{5,6},{6,0},{7,10},{10,14},{11,9},{8,15},{9,5},{20,17},{21,2... | collective-permute-start | bytes 393224 | tf_op jit(solution)/shard_map/ppermute | solution.py:114
  101.8 10.3 %collective-permute-start.11 = (f16[256,256]{1,0:T(8,128)(2,1)S(1)}, f16[256,256]{1,0:T(8,128)(2,1)S(1)}, u32[]{:S(2)}, u32[]{:S(2)}) collective-permute-start(f16[256,256]{1,0:T(8,128)(2,1)S(1)} %get-tuple-element.14), channel_id=1, source_target_pairs={{4,4},{5,8},{6,5},{7,2},{10,11},{11,7},{8,10},{9,13},{20,20},{21,2... | collective-permute-start | bytes 393224 | tf_op jit(solution)/shard_map/ppermute | solution.py:114
  102.4 10.9 %collective-permute-start.12 = (f16[256,256]{1,0:T(8,128)(2,1)S(1)}, f16[256,256]{1,0:T(8,128)(2,1)S(1)}, u32[]{:S(2)}, u32[]{:S(2)}) collective-permute-start(f16[256,256]{1,0:T(8,128)(2,1)S(1)} %get-tuple-element.13), channel_id=1, source_target_pairs={{4,5},{5,9},{6,4},{7,8},{10,10},{11,6},{8,11},{9,7},{20,21},{21,25... | collective-permute-start | bytes 393224 | tf_op jit(solution)/shard_map/ppermute | solution.py:114
  107.8 7.5 %collective-permute-start.13 = (f16[256,256]{1,0:T(8,128)(2,1)S(1)}, f16[256,256]{1,0:T(8,128)(2,1)S(1)}, u32[]{:S(2)}, u32[]{:S(2)}) collective-permute-start(f16[256,256]{1,0:T(8,128)(2,1)S(1)} %get-tuple-element.12), channel_id=1, source_target_pairs={{5,10},{7,9},{11,5},{9,6},{21,26},{23,25},{27,21},{25,22}} | collective-permute-start | bytes 393224 | tf_op jit(solution)/shard_map/ppermute | solution.py:114
  108.5 13.6 %collective-permute-start.9 = (f16[256,256]{1,0:T(8,128)(2,1)S(1)}, f16[256,256]{1,0:T(8,128)(2,1)S(1)}, u32[]{:S(2)}, u32[]{:S(2)}) collective-permute-start(f16[256,256]{1,0:T(8,128)(2,1)S(1)} %get-tuple-element.11), channel_id=1, source_target_pairs={{4,0},{5,2},{6,1},{7,6},{10,15},{11,13},{8,14},{9,9},{20,16},{21,1... | collective-permute-start | bytes 393224 | tf_op jit(solution)/shard_map/ppermute | solution.py:114
  110.7 11.3 %collective-permute-start.16 = (f16[256,256]{1,0:T(8,128)(2,1)S(1)}, f16[256,256]{1,0:T(8,128)(2,1)S(1)}, u32[]{:S(2)}, u32[]{:S(2)}) collective-permute-start(f16[256,256]{1,0:T(8,128)(2,1)S(1)} %bitcast.30), channel_id=1, source_target_pairs={{4,12},{5,14},{6,13},{7,15},{10,3},{11,1},{8,2},{9,0},{20,28},{21,... | collective-permute-start | bytes 393224 | tf_op jit(solution)/shard_map/ppermute | solution.py:114
  112.0 10.0 %collective-permute-start.17 = (f16[256,256]{1,0:T(8,128)(2,1)S(1)}, f16[256,256]{1,0:T(8,128)(2,1)S(1)}, u32[]{:S(2)}, u32[]{:S(2)}) collective-permute-start(f16[256,256]{1,0:T(8,128)(2,1)S(1)} %bitcast.29), channel_id=1, source_target_pairs={{4,13},{5,15},{6,12},{7,14},{10,2},{11,0},{8,3},{9,1},{20,29},{21,... | collective-permute-start | bytes 393224 | tf_op jit(solution)/shard_map/ppermute | solution.py:114
  113.4 9.1 %collective-permute-start.18 = (f16[256,256]{1,0:T(8,128)(2,1)S(1)}, f16[256,256]{1,0:T(8,128)(2,1)S(1)}, u32[]{:S(2)}, u32[]{:S(2)}) collective-permute-start(f16[256,256]{1,0:T(8,128)(2,1)S(1)} %get-tuple-element.18), channel_id=1, source_target_pairs={{4,3},{5,11},{6,7},{10,12},{11,4},{8,8},{20,19},{21,27},{22,23},{2... | collective-permute-start | bytes 393224 | tf_op jit(solution)/shard_map/ppermute | solution.py:114
  115.3 8.6 %collective-permute-start.19 = (f16[256,256]{1,0:T(8,128)(2,1)S(1)}, f16[256,256]{1,0:T(8,128)(2,1)S(1)}, u32[]{:S(2)}, u32[]{:S(2)}) collective-permute-start(f16[256,256]{1,0:T(8,128)(2,1)S(1)} %get-tuple-element.19), channel_id=1, source_target_pairs={{4,7},{6,3},{7,11},{10,8},{8,12},{9,4},{20,23},{22,19},{23,27},{26... | collective-permute-start | bytes 393224 | tf_op jit(solution)/shard_map/ppermute | solution.py:114

commit v3 on v2

v3 whole, which is shorter than its diff:
```python
import functools

import jax
import jax.numpy as jnp
from jax import lax
from jax.experimental import pallas as pl
from jax.experimental.pallas import tpu as pltpu
from jax.sharding import PartitionSpec as P


def pair_product(left, right):
    return jnp.einsum("ip,jp->ij", left, right, preferred_element_type=jnp.float32)


def add_shift(summed, samples, shift, local_rows):
    width = summed.shape[1]
    first_row = lax.axis_index("row") * local_rows
    block = lax.axis_index("col") * lax.axis_size("half") + lax.axis_index("half")
    row_ids = first_row + lax.broadcasted_iota(jnp.int32, (local_rows, width), 0)
    column_ids = block * width + lax.broadcasted_iota(jnp.int32, (local_rows, width), 1)
    return summed / samples + jnp.where(row_ids == column_ids, shift[0], 0.0)


def gathered(log_derivs, shift):
    local_rows = log_derivs.shape[0]
    samples = local_rows * lax.axis_size("row")
    rows = lax.all_gather(log_derivs, "row", axis=0, tiled=True).astype(jnp.float32)
    mean = jnp.sum(rows, axis=0) / samples
    centered = (rows - mean[None, :]).astype(jnp.bfloat16)
    own = (log_derivs.astype(jnp.float32) - mean[None, :]).astype(jnp.bfloat16)
    tile = pair_product(own, centered)
    summed = lax.psum_scatter(tile, ("col", "half"), scatter_dimension=1, tiled=True)
    return add_shift(summed, samples, shift, local_rows)


EARLY = (
    (((0, 0), (0, 1)), ((0, 2), (1, 2))),
    (((0, 1), (0, 0)), ((1, 2), (2, 2))),
    (((1, 0), (1, 1)), ((2, 0), (0, 2))),
    (((1, 1), (1, 0)), ((2, 1), (2, 0))),
    ((None, None), ((2, 2), (2, 1))),
)
LATE = (
    (((3, 0), (3, 1)), ((3, 2), (3, 3))),
    (((3, 1), (3, 0)), ((3, 3), (3, 2))),
    (((0, 3), (1, 3)), ((2, 3), None)),
    (((1, 3), (0, 3)), (None, (2, 3))),
)
EARLY_SUMS = (((0, 0), (0, 1), (1, 1)), ((2, 2), (2, 0), (2, 1)))
EARLY_HELD = (
    ((0, 0), (0, 1), (1, 1), (1, 0), (1, 1)),
    ((2, 2), (2, 0), (2, 1), (0, 2), (1, 2)),
)
LATE_SUMS = (((3, 0), (3, 1)), ((3, 2), (3, 3)))
LATE_HELD = (
    ((3, 0), (3, 1), (0, 3), (1, 3)),
    ((3, 2), (3, 3), (2, 3), (3, 3)),
)
EXTRA = 16
HEAD = 64
VMEM = pl.BlockSpec(memory_space=pltpu.VMEM)
SMEM = pl.BlockSpec(memory_space=pltpu.SMEM)
ANY = pl.BlockSpec(memory_space=pl.ANY)
LIMIT = pltpu.CompilerParams(vmem_limit_bytes=40 * 2**20)


def device_index(row, col, half):
    return (row * 2 + col) * 2 + half


def round_pairs(blocks):
    pairs = []
    for side in (0, 1):
        for turn in (0, 1):
            for half in (0, 1):
                block = blocks[half][turn]
                if block is None:
                    continue
                i, j = (3 - b if side else b for b in block)
                source = device_index(1 + side, turn ^ side, half)
                pairs.append((source, device_index(i, j // 2, j % 2)))
    return pairs


def held_place(held, rounds):
    return [
        [[0 if b is None else held[half].index(b) for b in rounds_[half]] for half in (0, 1)]
        for rounds_ in rounds
    ]


def far_kernel(bits, values, far, head, tail, sems):
    part = far.shape[1]
    columns = pl.ds(pl.multiple_of(bits[0] * part, 128), part)
    copies = [
        pltpu.make_async_copy(values.at[:, columns], far, sems.at[0]),
        pltpu.make_async_copy(values.at[pl.ds(0, HEAD), columns], head, sems.at[1]),
        pltpu.make_async_copy(values.at[pl.ds(HEAD, tail.shape[0]), columns], tail, sems.at[2]),
    ]
    for copy in copies:
        copy.start()
    for copy in copies:
        copy.wait()


def near_kernel(bits, values, near, sums):
    rows, part = values.shape[0], values.shape[1] // 2
    step = 512

    @pl.loop(0, part // step)
    def _(i):
        out = pl.ds(pl.multiple_of(i * step, step), step)
        near_columns = pl.ds(pl.multiple_of((1 - bits[0]) * part + i * step, step), step)
        far_columns = pl.ds(pl.multiple_of(bits[0] * part + i * step, step), step)
        block = values[:, near_columns]
        near[pl.ds(0, rows), out] = block
        near_sum = jnp.sum(block.astype(jnp.float32), axis=0, keepdims=True)
        far_sum = jnp.sum(values[:, far_columns].astype(jnp.float32), axis=0, keepdims=True)
        sums[pl.ds(0, 1), out] = near_sum
        sums[pl.ds(1, 1), out] = far_sum
        pieces = []
        for left in (near_sum, far_sum):
            for _ in range(3):
                piece = left.astype(jnp.bfloat16).astype(jnp.float32)
                pieces.append(piece)
                left = left - piece
        pieces.append(jnp.zeros((EXTRA - len(pieces), step), jnp.float32))
        near[pl.ds(rows, EXTRA), out] = jnp.concatenate(pieces, axis=0).astype(jnp.bfloat16)


def block_product(left, right):
    return lax.dot_general(left, right, (((1,), (1,)), ((), ())), preferred_element_type=jnp.float32)


def early_kernel(bits, edge, near, other, sums, arrived, centred, mean, own, send, both):
    rows = other.shape[0]
    pieces = edge[pl.ds(rows, EXTRA), :].astype(jnp.float32)
    edge_sum = pieces[0:1] + pieces[1:2] + pieces[2:3]
    average = (sums[pl.ds(0, 1), :] + edge_sum + arrived[...]) * (1.0 / (4 * rows))
    mean[...] = average
    for i, block in enumerate((edge, near, other)):
        values = block[pl.ds(0, rows), :].astype(jnp.float32)
        centred[i] = (values - average).astype(jnp.bfloat16)
    for core in (0, 1):
        for place, (i, j) in enumerate(EARLY_SUMS[core]):
            both[core, place] = block_product(centred[i], centred[j])
    own[...] = both[bits[1]]
    send[...] = both[1 - bits[1]]


def late_kernel(bits, head, tail, mean, centred, *rest):
    passed = (len(rest) - 4) // 2
    own, send = rest[passed], rest[passed + 1]
    last, both = rest[-2:]
    average = mean[...]
    last[pl.ds(0, HEAD), :] = (head[...].astype(jnp.float32) - average).astype(jnp.bfloat16)
    last[pl.ds(HEAD, tail.shape[0]), :] = (tail[...].astype(jnp.float32) - average).astype(jnp.bfloat16)
    for core in (0, 1):
        for place, (_, j) in enumerate(LATE_SUMS[core]):
            both[core, place] = block_product(last[...], last[...] if j == 3 else centred[j])
    own[...] = both[bits[1]]
    send[...] = both[1 - bits[1]]


def combine_kernel(flips, scale, bits, places, own, other, *rest):
    held = rest[-1]
    count = own.shape[0]
    for i in range(count):
        held[i] = (own[i] + other[i]) * scale
    for n, i in enumerate(flips):
        held[count + n] = held[i].T
    for r, out in enumerate(rest[:-1]):
        out[...] = held[places[r, bits[1], bits[2]]]


def shape_of(shape, dtype):
    return jax.ShapeDtypeStruct(shape, dtype)


def combine(bits, own, other, flips, held, rounds, samples):
    rows = own.shape[1]
    places = jnp.array(held_place(held, rounds), jnp.int32)
    return pl.pallas_call(
        functools.partial(combine_kernel, flips, 1.0 / samples),
        out_shape=[shape_of((rows, rows), jnp.float32)] * len(rounds),
        in_specs=[SMEM, SMEM, VMEM, VMEM],
        out_specs=[VMEM] * len(rounds),
        scratch_shapes=[pltpu.VMEM((len(held[0]), rows, rows), jnp.float32)],
        compiler_params=LIMIT,
    )(bits, places, own, other)


def two_centres(log_derivs, shift):
    local_rows, local_params = log_derivs.shape
    samples = local_rows * 4
    part = local_params // 2
    everyone = ("row", "col", "half")
    row, col, half = (lax.axis_index(name) for name in everyone)
    side = (row >= 2).astype(jnp.int32)
    bits = jnp.stack([side, half, jnp.bitwise_xor(col, side)]).astype(jnp.int32)

    to_centre = [(1, 2), (2, 1)]
    to_own = [(0, 1), (3, 2)]
    to_far = [(0, 2), (3, 1)]
    centres = [(r * 2 + h, r * 2 + 1 - h) for r in (1, 2) for h in (0, 1)]

    def swap(value):
        return lax.ppermute(value, ("row", "half"), centres)

    def send(value, blocks):
        return lax.ppermute(value.astype(jnp.float16), everyone, round_pairs(blocks))

    far, head, tail = pl.pallas_call(
        far_kernel,
        out_shape=[
            shape_of((local_rows, part), jnp.bfloat16),
            shape_of((HEAD, part), jnp.bfloat16),
            shape_of((local_rows - HEAD, part), jnp.bfloat16),
        ],
        in_specs=[SMEM, ANY],
        out_specs=[ANY] * 3,
        scratch_shapes=[pltpu.SemaphoreType.DMA((3,))],
        compiler_params=LIMIT,
    )(bits, log_derivs)
    from_centre = lax.ppermute(far, "row", to_centre)
    from_head = lax.ppermute(head, "row", to_far)
    near, sums = pl.pallas_call(
        near_kernel,
        out_shape=[
            shape_of((local_rows + EXTRA, part), jnp.bfloat16),
            shape_of((2, part), jnp.float32),
        ],
        in_specs=[SMEM, VMEM],
        out_specs=[VMEM] * 2,
        compiler_params=LIMIT,
    )(bits, log_derivs)
    from_edge = lax.ppermute(near, "row", to_own)
    from_tail = lax.ppermute(tail, "row", to_far)
    pieces = from_edge[local_rows : local_rows + EXTRA].astype(jnp.float32)
    passed_on = sums[1:2] + pieces[3:4] + pieces[4:5] + pieces[5:6]
    arrived_sum = lax.ppermute(passed_on, "row", to_centre)

    early_blocks = (3, local_rows, local_rows)
    centred, mean, own, other = pl.pallas_call(
        early_kernel,
        out_shape=[
            shape_of((3, local_rows, part), jnp.bfloat16),
            shape_of((1, part), jnp.float32),
            shape_of(early_blocks, jnp.float32),
            shape_of(early_blocks, jnp.float32),
        ],
        in_specs=[SMEM] + [VMEM] * 5,
        out_specs=[VMEM] * 4,
        scratch_shapes=[pltpu.VMEM((2,) + early_blocks, jnp.float32)],
        compiler_params=LIMIT,
    )(bits, from_edge, near, from_centre, sums, arrived_sum)
    early = combine(bits, own, swap(other), (1, 2), EARLY_HELD, EARLY, samples)
    arrived = [send(early[0], EARLY[0])]

    late_blocks = (2, local_rows, local_rows)
    waiting = early[1:]
    own, other, *waiting = pl.pallas_call(
        late_kernel,
        out_shape=[
            shape_of(late_blocks, jnp.float32),
            shape_of(late_blocks, jnp.float32),
        ]
        + [shape_of(value.shape, value.dtype) for value in waiting],
        in_specs=[SMEM] + [VMEM] * 4 + [ANY] * len(waiting),
        out_specs=[VMEM] * 2 + [ANY] * len(waiting),
        scratch_shapes=[
            pltpu.VMEM((local_rows, part), jnp.bfloat16),
            pltpu.VMEM((2,) + late_blocks, jnp.float32),
        ],
        input_output_aliases={5 + i: 2 + i for i in range(len(waiting))},
        compiler_params=LIMIT,
    )(bits, from_head, from_tail, mean, centred, *waiting)
    other = swap(other)
    arrived += [send(value, blocks) for value, blocks in zip(waiting, EARLY[1:])]
    late = combine(bits, own, other, (0, 1), LATE_HELD, LATE, samples)
    arrived += [send(value, blocks) for value, blocks in zip(late, LATE)]
    summed = sum(block.astype(jnp.float32) for block in arrived)
    return add_shift(summed, 1, shift, local_rows)


def solution(mesh):
    shape = mesh.shape
    small = shape["row"] == 4 and shape["col"] == 2 and shape["half"] == 2
    return jax.shard_map(
        two_centres if small else gathered,
        mesh=mesh,
        in_specs=(P(("groups", "row"), ("col", "half")), P("groups")),
        out_specs=P(("groups", "row"), ("col", "half")),
        check_vma=False,
    )
```

time: 127 us -> 104 us (0.82)
  the two profiles are of different devices: /device:TPU:8 before, /device:TPU:1 now
where the time goes in v3:
time: 104 us; the launch traced here: 103 us
  waiting for transfers between devices  62 us (60%)
  starting transfers between devices  29.5 us (28%)
  Pallas kernels  8.06 us (8%)
  local copies, waits for them, and re-layouts  1.61 us (2%)
  other arithmetic  1.15 us (1%)
    ppermute x1, waiting for transfers between devices, two_centres(): from_edge = lax.ppermute(near, 'row', to_own)  21.6 us
    ppermute x1, waiting for transfers between devices, two_centres(): from_head = lax.ppermute(head, 'row', to_far)  20.3 us
    ppermute x9, waiting for transfers between devices, send(): lax.ppermute(value.astype(jnp.float16), everyone, round_pairs(blocks))  20.1 us
    ppermute x1, starting transfers between devices, two_centres(): from_tail = lax.ppermute(tail, 'row', to_far)  12.8 us
    ppermute x9, starting transfers between devices, send(): lax.ppermute(value.astype(jnp.float16), everyone, round_pairs(blocks))  8.5 us
    ppermute x1, starting transfers between devices, two_centres(): from_edge = lax.ppermute(near, 'row', to_own)  4.1 us
    pallas_call x1, Pallas kernels, two_centres(): pl.pallas_call(early_kernel, out_shape=[shape_of((3, local_rows, part), j...  2.63 us
  transfers between devices with their start and end apart: 16, of which 6 were waited for; matrix products, arithmetic and copies ran while one was open for 0% of the time, Pallas kernels for 2%

profile of v3, /device:TPU:1, one launch (start us, length us, event | category | flops | bytes accessed | tf_op | source)
XLA Modules:
  0.0 103.3 jit_solution(16347533526878964298)
XLA Ops:
  0.1 1.6 %copy-done = bf16[256,4096]{1,0:T(8,128)(2,1)S(1)} copy-done((bf16[256,4096]{1,0:T(8,128)(2,1)S(1)}, bf16[256,4096]{1,0:T(8,128)(2,1)}, u32[]{:S(2)}) %copy-start) | copy-done | bytes 2097176
  1.7 1.0 shard_map.46
  2.6 4.1 %collective-permute-start = (bf16[272,2048]{1,0:T(8,128)(2,1)S(1)}, bf16[272,2048]{1,0:T(8,128)(2,1)S(1)}, u32[]{:S(2)}, u32[]{:S(2)}) collective-permute-start(bf16[272,2048]{1,0:T(8,128)(2,1)S(1)} %get-tuple-element.29.near), channel_id=1, source_target_pairs={{0,4},{12,8},{1,5},{13,9},{2,6},{14,10},{3,7},{15,11},{16,20},{28,... | collective-permute-start | bytes 3342344 | tf_op jit(solution)/shard_map/ppermute | solution.py:237
  6.8 0.8 shard_map.47
  7.5 0.7 collective-permute-start.1
  8.2 21.6 %collective-permute-done.edge = bf16[272,2048]{1,0:T(8,128)(2,1)S(1)} collective-permute-done((bf16[272,2048]{1,0:T(8,128)(2,1)S(1)}, bf16[272,2048]{1,0:T(8,128)(2,1)S(1)}, u32[]{:S(2)}, u32[]{:S(2)}) %collective-permute-start) | collective-permute-done | bytes 1114144 | tf_op jit(solution)/shard_map/ppermute | solution.py:237
  30.6 2.6 %shard_map.48 = (bf16[3,256,2048]{2,1,0:T(8,128)(2,1)S(1)}, f32[1,2048]{1,0:T(1,128)S(1)}, f32[3,256,256]{2,1,0:T(8,128)S(1)}, f32[3,256,256]{2,1,0:T(8,128)S(1)}) custom-call(s32[3]{0:T(128)S(1)} %pad_add_fusion.bits, bf16[272,2048]{1,0:T(8,128)(2,1)S(1)} %collective-permute-done.edge, bf16[272,2048]{1,0:T(8,128)(2,1)S(1)} %get-tuple-element.29.near, ...), custom_call_target="tpu_custom_call" | custom-call | tf_op jit(solution)/shard_map/pallas_call | solution.py:244
  33.3 0.7 collective-permute-start.3
  34.0 12.8 %collective-permute-start.6 = (bf16[192,2048]{1,0:T(8,128)(2,1)S(1)}, bf16[192,2048]{1,0:T(8,128)(2,1)S(1)}, u32[]{:S(2)}, u32[]{:S(2)}) collective-permute-start(bf16[192,2048]{1,0:T(8,128)(2,1)S(1)} %get-tuple-element.36), channel_id=1, source_target_pairs={{0,8},{12,4},{1,9},{13,5},{2,10},{14,6},{3,11},{15,7},{16,24},{28,... | collective-permute-start | bytes 2359304 | tf_op jit(solution)/shard_map/ppermute | solution.py:238
  46.8 1.3 %collective-permute-start.5 = (bf16[64,2048]{1,0:T(8,128)(2,1)S(1)}, bf16[64,2048]{1,0:T(8,128)(2,1)S(1)}, u32[]{:S(2)}, u32[]{:S(2)}) collective-permute-start(bf16[64,2048]{1,0:T(8,128)(2,1)S(1)} %get-tuple-element.35), channel_id=1, source_target_pairs={{0,8},{12,4},{1,9},{13,5},{2,10},{14,6},{3,11},{15,7},{16,24},{28,... | collective-permute-start | bytes 786440 | tf_op jit(solution)/shard_map/ppermute | solution.py:226
  48.1 0.9 shard_map.49
  49.0 20.3 %collective-permute-done.5.head = bf16[64,2048]{1,0:T(8,128)(2,1)S(1)} collective-permute-done((bf16[64,2048]{1,0:T(8,128)(2,1)S(1)}, bf16[64,2048]{1,0:T(8,128)(2,1)S(1)}, u32[]{:S(2)}, u32[]{:S(2)}) %collective-permute-start.5) | collective-permute-done | bytes 262176 | tf_op jit(solution)/shard_map/ppermute | solution.py:226
  69.3 1.9 %shard_map.50 = (f32[2,256,256]{2,1,0:T(8,128)S(1)}, f32[2,256,256]{2,1,0:T(8,128)S(1)}, f32[256,256]{1,0:T(8,128)S(1)}, f32[256,256]{1,0:T(8,128)S(1)}, f32[256,256]{1,0:T(8,128)S(1)}, /*index=5*/f32[256,256]{1,0:T(8,128)S(1)}) custom-call(s32[3]{0:T(128)S(1)} %pad_add_fusion.bits, ...), custom_call_target="tpu_custom_call", output_to_operand_aliasing={{2}: (5, {}), {3}: (6, {}), {4}: (7, {}), {5}: (8, {})} | custom-call | tf_op jit(solution)/shard_map/pallas_call | solution.py:262
  71.2 0.7 collective-permute-start.11
  74.0 1.3 %collective-permute-start.7 = (f16[256,256]{1,0:T(8,128)(2,1)S(1)}, f16[256,256]{1,0:T(8,128)(2,1)S(1)}, u32[]{:S(2)}, u32[]{:S(2)}) collective-permute-start(f16[256,256]{1,0:T(8,128)(2,1)S(1)} %convert_element_type.64), channel_id=1, source_target_pairs={{4,1},{5,6},{6,0},{7,10},{10,14},{11,9},{8,15},{9,5},{20,17},{21,2... | collective-permute-start | bytes 393224 | tf_op jit(solution)/shard_map/ppermute | solution.py:211
  75.4 1.3 %collective-permute-start.4 = (f16[256,256]{1,0:T(8,128)(2,1)S(1)}, f16[256,256]{1,0:T(8,128)(2,1)S(1)}, u32[]{:S(2)}, u32[]{:S(2)}) collective-permute-start(f16[256,256]{1,0:T(8,128)(2,1)S(1)} %convert_element_type.62), channel_id=1, source_target_pairs={{4,0},{5,2},{6,1},{7,6},{10,15},{11,13},{8,14},{9,9},{20,16},{21,1... | collective-permute-start | bytes 393224 | tf_op jit(solution)/shard_map/ppermute | solution.py:211
  76.7 0.9 shard_map.51
  79.1 1.3 %collective-permute-start.13 = (f16[256,256]{1,0:T(8,128)(2,1)S(1)}, f16[256,256]{1,0:T(8,128)(2,1)S(1)}, u32[]{:S(2)}, u32[]{:S(2)}) collective-permute-start(f16[256,256]{1,0:T(8,128)(2,1)S(1)} %convert_element_type.74), channel_id=1, source_target_pairs={{4,13},{5,15},{6,12},{7,14},{10,2},{11,0},{8,3},{9,1},{20,29},{21,... | collective-permute-start | bytes 393224 | tf_op jit(solution)/shard_map/ppermute | solution.py:211
  80.4 6.7 %collective-permute-done.7 = f16[256,256]{1,0:T(8,128)(2,1)S(1)} collective-permute-done((f16[256,256]{1,0:T(8,128)(2,1)S(1)}, f16[256,256]{1,0:T(8,128)(2,1)S(1)}, u32[]{:S(2)}, u32[]{:S(2)}) %collective-permute-start.7) | collective-permute-done | bytes 131104 | tf_op jit(solution)/shard_map/ppermute | solution.py:211
  87.1 1.3 %collective-permute-start.12 = (f16[256,256]{1,0:T(8,128)(2,1)S(1)}, f16[256,256]{1,0:T(8,128)(2,1)S(1)}, u32[]{:S(2)}, u32[]{:S(2)}) collective-permute-start(f16[256,256]{1,0:T(8,128)(2,1)S(1)} %convert_element_type.72), channel_id=1, source_target_pairs={{4,12},{5,14},{6,13},{7,15},{10,3},{11,1},{8,2},{9,0},{20,28},{21,... | collective-permute-start | bytes 393224 | tf_op jit(solution)/shard_map/ppermute | solution.py:211
  89.0 3.1 %collective-permute-done.4 = f16[256,256]{1,0:T(8,128)(2,1)S(1)} collective-permute-done((f16[256,256]{1,0:T(8,128)(2,1)S(1)}, f16[256,256]{1,0:T(8,128)(2,1)S(1)}, u32[]{:S(2)}, u32[]{:S(2)}) %collective-permute-start.4) | collective-permute-done | bytes 131104 | tf_op jit(solution)/shard_map/ppermute | solution.py:211
  92.1 4.5 %collective-permute-done.13 = f16[256,256]{1,0:T(8,128)(2,1)S(1)} collective-permute-done((f16[256,256]{1,0:T(8,128)(2,1)S(1)}, f16[256,256]{1,0:T(8,128)(2,1)S(1)}, u32[]{:S(2)}, u32[]{:S(2)}) %collective-permute-start.13) | collective-permute-done | bytes 131104 | tf_op jit(solution)/shard_map/ppermute | solution.py:211
  96.6 5.8 %collective-permute-done.12 = f16[256,256]{1,0:T(8,128)(2,1)S(1)} collective-permute-done((f16[256,256]{1,0:T(8,128)(2,1)S(1)}, f16[256,256]{1,0:T(8,128)(2,1)S(1)}, u32[]{:S(2)}, u32[]{:S(2)}) %collective-permute-start.12) | collective-permute-done | bytes 131104 | tf_op jit(solution)/shard_map/ppermute | solution.py:211
  102.4 0.9 select_add_fusion
  (34 shorter events, 4.3 us)
Async XLA Ops:
  0.1 1.6 %copy-start = (bf16[256,4096]{1,0:T(8,128)(2,1)S(1)}, bf16[256,4096]{1,0:T(8,128)(2,1)}, u32[]{:S(2)}) copy-start(bf16[256,4096]{1,0:T(8,128)(2,1)} %values.3) | copy-start | bytes 6291460
  2.6 27.3 %collective-permute-start = (bf16[272,2048]{1,0:T(8,128)(2,1)S(1)}, bf16[272,2048]{1,0:T(8,128)(2,1)S(1)}, u32[]{:S(2)}, u32[]{:S(2)}) collective-permute-start(bf16[272,2048]{1,0:T(8,128)(2,1)S(1)} %get-tuple-element.29.near), channel_id=1, source_target_pairs={{0,4},{12,8},{1,5},{13,9},{2,6},{14,10},{3,7},{15,11},{16,20},{28,... | collective-permute-start | bytes 3342344 | tf_op jit(solution)/shard_map/ppermute | solution.py:237
  7.5 23.1 %collective-permute-start.1 = (bf16[256,2048]{1,0:T(8,128)(2,1)S(1)}, bf16[256,2048]{1,0:T(8,128)(2,1)S(1)}, u32[]{:S(2)}, u32[]{:S(2)}) collective-permute-start(bf16[256,2048]{1,0:T(8,128)(2,1)S(1)} %get-tuple-element.30), channel_id=1, source_target_pairs={{4,8},{8,4},{5,9},{9,5},{6,10},{10,6},{7,11},{11,7},{20,24},{24,20... | collective-permute-start | bytes 3145736 | tf_op jit(solution)/shard_map/ppermute | solution.py:225
  29.9 18.2 %copy-start.1 = (s32[5,2,2]{2,1,0:T(2,128)S(1)}, s32[5,2,2]{2,1,0:T(2,128)}, u32[]{:S(2)}) copy-start(s32[5,2,2]{2,1,0:T(2,128)} %constant.22.clone.places) | copy-start | bytes 244
  30.0 0.7 collective-permute-start.2
  33.3 14.8 %collective-permute-start.3 = (f32[3,256,256]{2,1,0:T(8,128)S(1)}, f32[3,256,256]{2,1,0:T(8,128)S(1)}, u32[]{:S(2)}, u32[]{:S(2)}) collective-permute-start(f32[3,256,256]{2,1,0:T(8,128)S(1)} %get-tuple-element.33), channel_id=1, source_target_pairs={{4,5},{5,4},{8,9},{9,8},{6,7},{7,6},{10,11},{11,10},{20,21},{21,20... | collective-permute-start | bytes 2359304 | tf_op jit(solution)/shard_map/ppermute | solution.py:208
  34.0 35.3 %collective-permute-start.6 = (bf16[192,2048]{1,0:T(8,128)(2,1)S(1)}, bf16[192,2048]{1,0:T(8,128)(2,1)S(1)}, u32[]{:S(2)}, u32[]{:S(2)}) collective-permute-start(bf16[192,2048]{1,0:T(8,128)(2,1)S(1)} %get-tuple-element.36), channel_id=1, source_target_pairs={{0,8},{12,4},{1,9},{13,5},{2,10},{14,6},{3,11},{15,7},{16,24},{28,... | collective-permute-start | bytes 2359304 | tf_op jit(solution)/shard_map/ppermute | solution.py:238
  46.8 22.5 %collective-permute-start.5 = (bf16[64,2048]{1,0:T(8,128)(2,1)S(1)}, bf16[64,2048]{1,0:T(8,128)(2,1)S(1)}, u32[]{:S(2)}, u32[]{:S(2)}) collective-permute-start(bf16[64,2048]{1,0:T(8,128)(2,1)S(1)} %get-tuple-element.35), channel_id=1, source_target_pairs={{0,8},{12,4},{1,9},{13,5},{2,10},{14,6},{3,11},{15,7},{16,24},{28,... | collective-permute-start | bytes 786440 | tf_op jit(solution)/shard_map/ppermute | solution.py:226
  71.2 5.5 %copy-start.2 = (s32[4,2,2]{2,1,0:T(2,128)S(1)}, s32[4,2,2]{2,1,0:T(2,128)}, u32[]{:S(2)}) copy-start(s32[4,2,2]{2,1,0:T(2,128)} %constant.23.clone.places) | copy-start | bytes 196
  71.2 4.2 %collective-permute-start.11 = (f32[2,256,256]{2,1,0:T(8,128)S(1)}, f32[2,256,256]{2,1,0:T(8,128)S(1)}, u32[]{:S(2)}, u32[]{:S(2)}) collective-permute-start(f32[2,256,256]{2,1,0:T(8,128)S(1)} %get-tuple-element.48), channel_id=1, source_target_pairs={{4,5},{5,4},{8,9},{9,8},{6,7},{7,6},{10,11},{11,10},{20,21},{21,20... | collective-permute-start | bytes 1572872 | tf_op jit(solution)/shard_map/ppermute | solution.py:208
  71.9 5.8 %collective-permute-start.10 = (f16[256,256]{1,0:T(8,128)(2,1)S(1)}, f16[256,256]{1,0:T(8,128)(2,1)S(1)}, u32[]{:S(2)}, u32[]{:S(2)}) collective-permute-start(f16[256,256]{1,0:T(8,128)(2,1)S(1)} %convert_element_type.70), channel_id=1, source_target_pairs={{5,10},{7,9},{11,5},{9,6},{21,26},{23,25},{27,21},{25,22}} | collective-permute-start | bytes 393224 | tf_op jit(solution)/shard_map/ppermute | solution.py:211
  72.6 5.7 %collective-permute-start.9 = (f16[256,256]{1,0:T(8,128)(2,1)S(1)}, f16[256,256]{1,0:T(8,128)(2,1)S(1)}, u32[]{:S(2)}, u32[]{:S(2)}) collective-permute-start(f16[256,256]{1,0:T(8,128)(2,1)S(1)} %convert_element_type.68), channel_id=1, source_target_pairs={{4,5},{5,9},{6,4},{7,8},{10,10},{11,6},{8,11},{9,7},{20,21},{21,25... | collective-permute-start | bytes 393224 | tf_op jit(solution)/shard_map/ppermute | solution.py:211
  73.3 5.7 %collective-permute-start.8 = (f16[256,256]{1,0:T(8,128)(2,1)S(1)}, f16[256,256]{1,0:T(8,128)(2,1)S(1)}, u32[]{:S(2)}, u32[]{:S(2)}) collective-permute-start(f16[256,256]{1,0:T(8,128)(2,1)S(1)} %convert_element_type.66), channel_id=1, source_target_pairs={{4,4},{5,8},{6,5},{7,2},{10,11},{11,7},{8,10},{9,13},{20,20},{21,2... | collective-permute-start | bytes 393224 | tf_op jit(solution)/shard_map/ppermute | solution.py:211
  74.0 13.0 %collective-permute-start.7 = (f16[256,256]{1,0:T(8,128)(2,1)S(1)}, f16[256,256]{1,0:T(8,128)(2,1)S(1)}, u32[]{:S(2)}, u32[]{:S(2)}) collective-permute-start(f16[256,256]{1,0:T(8,128)(2,1)S(1)} %convert_element_type.64), channel_id=1, source_target_pairs={{4,1},{5,6},{6,0},{7,10},{10,14},{11,9},{8,15},{9,5},{20,17},{21,2... | collective-permute-start | bytes 393224 | tf_op jit(solution)/shard_map/ppermute | solution.py:211
  75.4 16.8 %collective-permute-start.4 = (f16[256,256]{1,0:T(8,128)(2,1)S(1)}, f16[256,256]{1,0:T(8,128)(2,1)S(1)}, u32[]{:S(2)}, u32[]{:S(2)}) collective-permute-start(f16[256,256]{1,0:T(8,128)(2,1)S(1)} %convert_element_type.62), channel_id=1, source_target_pairs={{4,0},{5,2},{6,1},{7,6},{10,15},{11,13},{8,14},{9,9},{20,16},{21,1... | collective-permute-start | bytes 393224 | tf_op jit(solution)/shard_map/ppermute | solution.py:211
  77.7 14.4 %collective-permute-start.15 = (f16[256,256]{1,0:T(8,128)(2,1)S(1)}, f16[256,256]{1,0:T(8,128)(2,1)S(1)}, u32[]{:S(2)}, u32[]{:S(2)}) collective-permute-start(f16[256,256]{1,0:T(8,128)(2,1)S(1)} %convert_element_type.78), channel_id=1, source_target_pairs={{4,7},{6,3},{7,11},{10,8},{8,12},{9,4},{20,23},{22,19},{23,27},{26... | collective-permute-start | bytes 393224 | tf_op jit(solution)/shard_map/ppermute | solution.py:211
  78.4 13.8 %collective-permute-start.14 = (f16[256,256]{1,0:T(8,128)(2,1)S(1)}, f16[256,256]{1,0:T(8,128)(2,1)S(1)}, u32[]{:S(2)}, u32[]{:S(2)}) collective-permute-start(f16[256,256]{1,0:T(8,128)(2,1)S(1)} %convert_element_type.76), channel_id=1, source_target_pairs={{4,3},{5,11},{6,7},{10,12},{11,4},{8,8},{20,19},{21,27},{22,23},{2... | collective-permute-start | bytes 393224 | tf_op jit(solution)/shard_map/ppermute | solution.py:211
  79.1 17.5 %collective-permute-start.13 = (f16[256,256]{1,0:T(8,128)(2,1)S(1)}, f16[256,256]{1,0:T(8,128)(2,1)S(1)}, u32[]{:S(2)}, u32[]{:S(2)}) collective-permute-start(f16[256,256]{1,0:T(8,128)(2,1)S(1)} %convert_element_type.74), channel_id=1, source_target_pairs={{4,13},{5,15},{6,12},{7,14},{10,2},{11,0},{8,3},{9,1},{20,29},{21,... | collective-permute-start | bytes 393224 | tf_op jit(solution)/shard_map/ppermute | solution.py:211
  87.1 15.4 %collective-permute-start.12 = (f16[256,256]{1,0:T(8,128)(2,1)S(1)}, f16[256,256]{1,0:T(8,128)(2,1)S(1)}, u32[]{:S(2)}, u32[]{:S(2)}) collective-permute-start(f16[256,256]{1,0:T(8,128)(2,1)S(1)} %convert_element_type.72), channel_id=1, source_target_pairs={{4,12},{5,14},{6,13},{7,15},{10,3},{11,1},{8,2},{9,0},{20,28},{21,... | collective-permute-start | bytes 393224 | tf_op jit(solution)/shard_map/ppermute | solution.py:211

commit v4 on v3

v4 whole, which is shorter than its diff:
```python
import functools

import jax
import jax.numpy as jnp
from jax import lax
from jax.experimental import pallas as pl
from jax.experimental.pallas import tpu as pltpu
from jax.sharding import PartitionSpec as P


def pair_product(left, right):
    return jnp.einsum("ip,jp->ij", left, right, preferred_element_type=jnp.float32)


def add_shift(summed, samples, shift, local_rows):
    width = summed.shape[1]
    first_row = lax.axis_index("row") * local_rows
    block = lax.axis_index("col") * lax.axis_size("half") + lax.axis_index("half")
    row_ids = first_row + lax.broadcasted_iota(jnp.int32, (local_rows, width), 0)
    column_ids = block * width + lax.broadcasted_iota(jnp.int32, (local_rows, width), 1)
    return summed / samples + jnp.where(row_ids == column_ids, shift[0], 0.0)


def gathered(log_derivs, shift):
    local_rows = log_derivs.shape[0]
    samples = local_rows * lax.axis_size("row")
    rows = lax.all_gather(log_derivs, "row", axis=0, tiled=True).astype(jnp.float32)
    mean = jnp.sum(rows, axis=0) / samples
    centered = (rows - mean[None, :]).astype(jnp.bfloat16)
    own = (log_derivs.astype(jnp.float32) - mean[None, :]).astype(jnp.bfloat16)
    tile = pair_product(own, centered)
    summed = lax.psum_scatter(tile, ("col", "half"), scatter_dimension=1, tiled=True)
    return add_shift(summed, samples, shift, local_rows)


NEAR_ROUNDS = (
    (((0, 0), (0, 1)), ((0, 2), (1, 2))),
    (((0, 1), (0, 0)), ((1, 2), (0, 2))),
    (((1, 0), (1, 1)), (None, None)),
    (((1, 1), (1, 0)), (None, None)),
)
FAR_ROUNDS = (
    ((None, None), ((2, 0), (2, 2))),
    ((None, None), ((2, 2), (2, 0))),
)
LATE_ROUNDS = (
    (((3, 0), (3, 1)), ((3, 2), (3, 3))),
    (((3, 1), (3, 0)), ((3, 3), (3, 2))),
    (((0, 3), (1, 3)), ((2, 3), (2, 1))),
    (((1, 3), (0, 3)), ((2, 1), (2, 3))),
)
EARLY_SUMS = (((0, 0), (0, 1), (1, 1)), ((2, 2), (2, 0), (2, 1)))
EARLY_HELD = (
    ((0, 0), (0, 1), (1, 1), (1, 0), (1, 1)),
    ((2, 2), (2, 0), (2, 1), (0, 2), (1, 2)),
)
SPARE = 2
LATE_SUMS = (((3, 0), (3, 1)), ((3, 2), (3, 3)))
LATE_HELD = (
    ((3, 0), (3, 1), (0, 3), (1, 3), (1, 1)),
    ((3, 2), (3, 3), (2, 3), (3, 3), (2, 1)),
)
EXTRA = 16
VMEM = pl.BlockSpec(memory_space=pltpu.VMEM)
SMEM = pl.BlockSpec(memory_space=pltpu.SMEM)
ANY = pl.BlockSpec(memory_space=pl.ANY)
LIMIT = pltpu.CompilerParams(vmem_limit_bytes=40 * 2**20)
BRIEF = pl.CostEstimate(flops=1024, bytes_accessed=1024, transcendentals=0)


def device_index(row, col, half):
    return (row * 2 + col) * 2 + half


def round_pairs(blocks):
    pairs = []
    for side in (0, 1):
        for turn in (0, 1):
            for half in (0, 1):
                block = blocks[half][turn]
                if block is None:
                    continue
                i, j = (3 - b if side else b for b in block)
                source = device_index(1 + side, turn ^ side, half)
                pairs.append((source, device_index(i, j // 2, j % 2)))
    return pairs


def held_place(held, rounds):
    return [
        [[0 if b is None else held[half].index(b) for b in rounds_[half]] for half in (0, 1)]
        for rounds_ in rounds
    ]


def split_kernel(bits, values, near, far, sums, sems):
    rows, part = far.shape
    step = 512
    copies = []
    for i, (out, start) in enumerate(((near, 1 - bits[0]), (far, bits[0]))):
        columns = pl.ds(pl.multiple_of(start * part, 128), part)
        copies.append(
            pltpu.make_async_copy(values.at[:, columns], out.at[pl.ds(0, rows), :], sems.at[i])
        )
    for copy in copies:
        copy.start()
    for i, (copy, out) in enumerate(zip(copies, (near, far))):
        copy.wait()

        @pl.loop(0, part // step)
        def _(j):
            columns = pl.ds(pl.multiple_of(j * step, step), step)
            block = out[pl.ds(0, rows), columns].astype(jnp.float32)
            sums[pl.ds(i, 1), columns] = jnp.sum(block, axis=0, keepdims=True)

    pieces = []
    for i in (0, 1):
        left = sums[pl.ds(i, 1), :]
        for _ in range(3):
            piece = left.astype(jnp.bfloat16).astype(jnp.float32)
            pieces.append(piece)
            left = left - piece
    pieces.append(jnp.zeros((EXTRA - len(pieces), part), jnp.float32))
    near[pl.ds(rows, EXTRA), :] = jnp.concatenate(pieces, axis=0).astype(jnp.bfloat16)


def block_product(left, right):
    return lax.dot_general(left, right, (((1,), (1,)), ((), ())), preferred_element_type=jnp.float32)


def early_kernel(bits, edge, near, other, sums, arrived, centred, mean, own, *rest):
    sends, both = rest[:-1], rest[-1]
    rows = other.shape[0]
    pieces = edge[pl.ds(rows, EXTRA), :].astype(jnp.float32)
    edge_sum = pieces[0:1] + pieces[1:2] + pieces[2:3]
    average = (sums[pl.ds(0, 1), :] + edge_sum + arrived[...]) * (1.0 / (4 * rows))
    mean[...] = average
    for i, block in enumerate((edge, near, other)):
        values = block[pl.ds(0, rows), :].astype(jnp.float32)
        centred[i] = (values - average).astype(jnp.bfloat16)
    for core in (0, 1):
        for place, (i, j) in enumerate(EARLY_SUMS[core]):
            both[core, place] = block_product(centred[i], centred[j])
    own[...] = both[bits[1]]
    for place, send in enumerate(sends):
        send[...] = both[1 - bits[1], place]


def late_kernel(bits, far_edge, mean, centred, *rest):
    handed = (len(rest) - 5) // 2
    own, *sends = rest[handed : handed + 3]
    last, both = rest[-2:]
    last[...] = (far_edge[...].astype(jnp.float32) - mean[...]).astype(jnp.bfloat16)
    for core in (0, 1):
        for place, (_, j) in enumerate(LATE_SUMS[core]):
            both[core, place] = block_product(last[...], last[...] if j == 3 else centred[j])
    own[...] = both[bits[1]]
    for place, send in enumerate(sends):
        send[...] = both[1 - bits[1], place]


def combine_kernel(flips, scale, spares, bits, places, own, *rest):
    held = rest[-1]
    count = own.shape[0]
    for i in range(count):
        held[i] = (own[i] + rest[i][...]) * scale
    rest = rest[count:]
    for n, i in enumerate(flips):
        held[count + n] = held[i].T
    for i in range(spares):
        held[count + len(flips) + i] = rest[i][...]
    for r, out in enumerate(rest[spares:-1]):
        out[...] = held[places[r, bits[1], bits[2]]]


def shape_of(shape, dtype):
    return jax.ShapeDtypeStruct(shape, dtype)


def combine(bits, own, others, flips, spares, held, places, samples):
    rows = own.shape[1]
    return pl.pallas_call(
        functools.partial(combine_kernel, flips, 1.0 / samples, len(spares)),
        out_shape=[shape_of((rows, rows), jnp.float32)] * len(places),
        in_specs=[SMEM, SMEM] + [VMEM] * (1 + len(others) + len(spares)),
        out_specs=[VMEM] * len(places),
        scratch_shapes=[pltpu.VMEM((len(held[0]), rows, rows), jnp.float32)],
        compiler_params=LIMIT,
        cost_estimate=BRIEF,
    )(bits, jnp.array(places, jnp.int32), own, *others, *spares)


def two_centres(log_derivs, shift):
    local_rows, local_params = log_derivs.shape
    samples = local_rows * 4
    part = local_params // 2
    everyone = ("row", "col", "half")
    row, col, half = (lax.axis_index(name) for name in everyone)
    side = (row >= 2).astype(jnp.int32)
    bits = jnp.stack([side, half, jnp.bitwise_xor(col, side)]).astype(jnp.int32)

    to_centre = [(1, 2), (2, 1)]
    to_own = [(0, 1), (3, 2)]
    to_far = [(0, 2), (3, 1)]
    centres = [(r * 2 + h, r * 2 + 1 - h) for r in (1, 2) for h in (0, 1)]

    def swap(value):
        return lax.ppermute(value, ("row", "half"), centres)

    def send(value, blocks):
        return lax.ppermute(value.astype(jnp.float16), everyone, round_pairs(blocks))

    near, far, sums = pl.pallas_call(
        split_kernel,
        out_shape=[
            shape_of((local_rows + EXTRA, part), jnp.bfloat16),
            shape_of((local_rows, part), jnp.bfloat16),
            shape_of((2, part), jnp.float32),
        ],
        in_specs=[SMEM, ANY],
        out_specs=[VMEM] * 3,
        scratch_shapes=[pltpu.SemaphoreType.DMA((2,))],
        compiler_params=LIMIT,
        cost_estimate=BRIEF,
    )(bits, log_derivs)
    from_centre = lax.ppermute(far, "row", to_centre)
    from_edge = lax.ppermute(near, "row", to_own)
    from_far_edge = lax.ppermute(far, "row", to_far)
    pieces = from_edge[local_rows : local_rows + EXTRA].astype(jnp.float32)
    passed_on = sums[1:2] + pieces[3:4] + pieces[4:5] + pieces[5:6]
    arrived_sum = lax.ppermute(passed_on, "row", to_centre)

    block = shape_of((local_rows, local_rows), jnp.float32)
    early_blocks = (3, local_rows, local_rows)
    centred, mean, own, *others = pl.pallas_call(
        early_kernel,
        out_shape=[
            shape_of((3, local_rows, part), jnp.bfloat16),
            shape_of((1, part), jnp.float32),
            shape_of(early_blocks, jnp.float32),
        ]
        + [block] * 3,
        in_specs=[SMEM] + [VMEM] * 5,
        out_specs=[VMEM] * 6,
        scratch_shapes=[pltpu.VMEM((2,) + early_blocks, jnp.float32)],
        compiler_params=LIMIT,
        cost_estimate=BRIEF,
    )(bits, from_edge, near, from_centre, sums, arrived_sum)
    places = held_place(EARLY_HELD, NEAR_ROUNDS + FAR_ROUNDS) + [[[SPARE] * 2] * 2]
    others = [swap(other) for other in others]
    *early, spare = combine(bits, own, others, (1, 2), (), EARLY_HELD, places, samples)
    near_blocks, far_blocks = early[: len(NEAR_ROUNDS)], early[len(NEAR_ROUNDS) :]
    arrived = [send(value, blocks) for value, blocks in zip(near_blocks, NEAR_ROUNDS)]
    summed = sum(block.astype(jnp.float32) for block in arrived)

    late_blocks = (2, local_rows, local_rows)
    handed = [summed] + far_blocks
    own, *others, summed, first, second = pl.pallas_call(
        late_kernel,
        out_shape=[shape_of(late_blocks, jnp.float32)]
        + [block] * 2
        + [shape_of(value.shape, value.dtype) for value in handed],
        in_specs=[SMEM] + [VMEM] * 3 + [ANY] * len(handed),
        out_specs=[VMEM] * 3 + [ANY] * len(handed),
        scratch_shapes=[
            pltpu.VMEM((local_rows, part), jnp.bfloat16),
            pltpu.VMEM((2,) + late_blocks, jnp.float32),
        ],
        input_output_aliases={4 + i: 3 + i for i in range(len(handed))},
        compiler_params=LIMIT,
        cost_estimate=BRIEF,
    )(bits, from_far_edge, mean, centred, *handed)
    others = [swap(other) for other in others]
    arrived = [send(value, blocks) for value, blocks in zip((first, second), FAR_ROUNDS)]
    places = held_place(LATE_HELD, LATE_ROUNDS)
    late = combine(bits, own, others, (0, 1), (spare,), LATE_HELD, places, samples)
    arrived += [send(value, blocks) for value, blocks in zip(late, LATE_ROUNDS)]
    summed = summed + sum(block.astype(jnp.float32) for block in arrived)
    return add_shift(summed, 1, shift, local_rows)


def solution(mesh):
    shape = mesh.shape
    small = shape["row"] == 4 and shape["col"] == 2 and shape["half"] == 2
    return jax.shard_map(
        two_centres if small else gathered,
        mesh=mesh,
        in_specs=(P(("groups", "row"), ("col", "half")), P("groups")),
        out_specs=P(("groups", "row"), ("col", "half")),
        check_vma=False,
    )
```

time: 104 us -> 105 us (level)
  the two profiles are of different devices: /device:TPU:1 before, /device:TPU:8 now
where the time goes in v4:
time: 105 us; the launch traced here: 103 us
  waiting for transfers between devices  47.5 us (45%)
  starting transfers between devices  44.4 us (42%)
  Pallas kernels  7.56 us (7%)
  local copies, waits for them, and re-layouts  1.61 us (2%)
  other arithmetic  1.21 us (1%)
    ppermute x1, waiting for transfers between devices, two_centres(): from_edge = lax.ppermute(near, 'row', to_own)  23.3 us
    ppermute x1, waiting for transfers between devices, two_centres(): arrived_sum = lax.ppermute(passed_on, 'row', to_centre)  18.9 us
    ppermute x10, starting transfers between devices, send(): lax.ppermute(value.astype(jnp.float16), everyone, round_pairs(blocks))  17.9 us
    ppermute x5, starting transfers between devices, swap(): return lax.ppermute(value, ('row', 'half'), centres)  17 us
    ppermute x10, waiting for transfers between devices, send(): lax.ppermute(value.astype(jnp.float16), everyone, round_pairs(blocks))  3.74 us
    ppermute x1, starting transfers between devices, two_centres(): from_centre = lax.ppermute(far, 'row', to_centre)  3.48 us
    ppermute x1, starting transfers between devices, two_centres(): arrived_sum = lax.ppermute(passed_on, 'row', to_centre)  3.48 us
    pallas_call x1, Pallas kernels, two_centres(): pl.pallas_call(early_kernel, out_shape=[shape_of((3, local_rows, part), j...  2.6 us
  transfers between devices with their start and end apart: 19, of which 8 were waited for; matrix products, arithmetic and copies ran while one was open for 0% of the time, Pallas kernels for 4%

profile of v4, /device:TPU:8, one launch (start us, length us, event | category | flops | bytes accessed | tf_op | source)
XLA Modules:
  0.0 103.4 jit_solution(14321956729306687851)
XLA Ops:
  0.1 1.6 %copy-done = bf16[256,4096]{1,0:T(8,128)(2,1)S(1)} copy-done((bf16[256,4096]{1,0:T(8,128)(2,1)S(1)}, bf16[256,4096]{1,0:T(8,128)(2,1)}, u32[]{:S(2)}) %copy-start) | copy-done | bytes 2097176
  2.9 1.3 %collective-permute-start.1 = (bf16[272,2048]{1,0:T(8,128)(2,1)S(1)}, bf16[272,2048]{1,0:T(8,128)(2,1)S(1)}, u32[]{:S(2)}, u32[]{:S(2)}) collective-permute-start(bf16[272,2048]{1,0:T(8,128)(2,1)S(1)} %get-tuple-element.32.near), channel_id=1, source_target_pairs={{0,4},{12,8},{1,5},{13,9},{2,6},{14,10},{3,7},{15,11},{16,20},{28,... | collective-permute-start | bytes 3342344 | tf_op jit(solution)/shard_map/ppermute | solution.py:227
  4.2 3.5 %collective-permute-start.2 = (bf16[256,2048]{1,0:T(8,128)(2,1)S(1)}, bf16[256,2048]{1,0:T(8,128)(2,1)S(1)}, u32[]{:S(2)}, u32[]{:S(2)}) collective-permute-start(bf16[256,2048]{1,0:T(8,128)(2,1)S(1)} %get-tuple-element.31), channel_id=1, source_target_pairs={{4,8},{8,4},{5,9},{9,5},{6,10},{10,6},{7,11},{11,7},{20,24},{24,20... | collective-permute-start | bytes 3145736 | tf_op jit(solution)/shard_map/ppermute | solution.py:226
  7.7 1.3 %collective-permute-start = (bf16[256,2048]{1,0:T(8,128)(2,1)S(1)}, bf16[256,2048]{1,0:T(8,128)(2,1)S(1)}, u32[]{:S(2)}, u32[]{:S(2)}) collective-permute-start(bf16[256,2048]{1,0:T(8,128)(2,1)S(1)} %get-tuple-element.31), channel_id=1, source_target_pairs={{0,8},{12,4},{1,9},{13,5},{2,10},{14,6},{3,11},{15,7},{16,24},{28,... | collective-permute-start | bytes 3145736 | tf_op jit(solution)/shard_map/ppermute | solution.py:228
  9.0 23.3 %collective-permute-done.1.edge = bf16[272,2048]{1,0:T(8,128)(2,1)S(1)} collective-permute-done((bf16[272,2048]{1,0:T(8,128)(2,1)S(1)}, bf16[272,2048]{1,0:T(8,128)(2,1)S(1)}, u32[]{:S(2)}, u32[]{:S(2)}) %collective-permute-start.1) | collective-permute-done | bytes 1114144 | tf_op jit(solution)/shard_map/ppermute | solution.py:227
  32.3 3.5 %collective-permute-start.3 = (f32[1,2048]{1,0:T(1,128)S(1)}, f32[1,2048]{1,0:T(1,128)S(1)}, u32[]{:S(2)}, u32[]{:S(2)}) collective-permute-start(f32[1,2048]{1,0:T(1,128)S(1)} %slice_add_fusion), channel_id=1, source_target_pairs={{4,8},{8,4},{5,9},{9,5},{6,10},{10,6},{7,11},{11,7},{20,24},{24,20... | collective-permute-start | bytes 24584 | tf_op jit(solution)/shard_map/ppermute | solution.py:231
  35.8 18.9 %collective-permute-done.3.arrived = f32[1,2048]{1,0:T(1,128)S(1)} collective-permute-done((f32[1,2048]{1,0:T(1,128)S(1)}, f32[1,2048]{1,0:T(1,128)S(1)}, u32[]{:S(2)}, u32[]{:S(2)}) %collective-permute-start.3) | collective-permute-done | bytes 8224 | tf_op jit(solution)/shard_map/ppermute | solution.py:231
  54.7 2.6 %shard_map.47 = (bf16[3,256,2048]{2,1,0:T(8,128)(2,1)S(1)}, f32[1,2048]{1,0:T(1,128)S(1)}, f32[3,256,256]{2,1,0:T(8,128)S(1)}, f32[256,256]{1,0:T(8,128)S(1)}, f...) custom-call(s32[3]{0:T(128)S(1)} %pad_add_fusion.bits, bf16[272,2048]{1,0:T(8,128)(2,1)S(1)} %collective-permute-done.1.edge, ...), custom_call_target="tpu_custom_call" | custom-call | flops 1024 | bytes 1024 | tf_op jit(solution)/shard_map/pallas_call | solution.py:235
  57.3 1.9 %collective-permute-start.4 = (f32[256,256]{1,0:T(8,128)S(1)}, f32[256,256]{1,0:T(8,128)S(1)}, u32[]{:S(2)}, u32[]{:S(2)}) collective-permute-start(f32[256,256]{1,0:T(8,128)S(1)} %get-tuple-element.37), channel_id=1, source_target_pairs={{4,5},{5,4},{8,9},{9,8},{6,7},{7,6},{10,11},{11,10},{20,21},{21,20... | collective-permute-start | bytes 786440 | tf_op jit(solution)/shard_map/ppermute | solution.py:208
  59.3 2.4 %collective-permute-start.5 = (f32[256,256]{1,0:T(8,128)S(1)}, f32[256,256]{1,0:T(8,128)S(1)}, u32[]{:S(2)}, u32[]{:S(2)}) collective-permute-start(f32[256,256]{1,0:T(8,128)S(1)} %get-tuple-element.38), channel_id=1, source_target_pairs={{4,5},{5,4},{8,9},{9,8},{6,7},{7,6},{10,11},{11,10},{20,21},{21,20... | collective-permute-start | bytes 786440 | tf_op jit(solution)/shard_map/ppermute | solution.py:208
  61.7 1.9 %collective-permute-start.6 = (f32[256,256]{1,0:T(8,128)S(1)}, f32[256,256]{1,0:T(8,128)S(1)}, u32[]{:S(2)}, u32[]{:S(2)}) collective-permute-start(f32[256,256]{1,0:T(8,128)S(1)} %get-tuple-element.39), channel_id=1, source_target_pairs={{4,5},{5,4},{8,9},{9,8},{6,7},{7,6},{10,11},{11,10},{20,21},{21,20... | collective-permute-start | bytes 786440 | tf_op jit(solution)/shard_map/ppermute | solution.py:208
  63.6 1.5 %collective-permute-done.6.rest_2_ = f32[256,256]{1,0:T(8,128)S(1)} collective-permute-done((f32[256,256]{1,0:T(8,128)S(1)}, f32[256,256]{1,0:T(8,128)S(1)}, u32[]{:S(2)}, u32[]{:S(2)}) %collective-permute-start.6) | collective-permute-done | bytes 262176 | tf_op jit(solution)/shard_map/ppermute | solution.py:208
  66.1 2.0 %collective-permute-start.10 = (f16[256,256]{1,0:T(8,128)(2,1)S(1)}, f16[256,256]{1,0:T(8,128)(2,1)S(1)}, u32[]{:S(2)}, u32[]{:S(2)}) collective-permute-start(f16[256,256]{1,0:T(8,128)(2,1)S(1)} %convert_element_type.74), channel_id=1, source_target_pairs={{4,5},{6,4},{10,10},{8,11},{20,21},{22,20},{26,26},{24,27}} | collective-permute-start | bytes 393224 | tf_op jit(solution)/shard_map/ppermute | solution.py:211
  68.2 1.3 %collective-permute-start.7 = (f16[256,256]{1,0:T(8,128)(2,1)S(1)}, f16[256,256]{1,0:T(8,128)(2,1)S(1)}, u32[]{:S(2)}, u32[]{:S(2)}) collective-permute-start(f16[256,256]{1,0:T(8,128)(2,1)S(1)} %convert_element_type.68), channel_id=1, source_target_pairs={{4,0},{5,2},{6,1},{7,6},{10,15},{11,13},{8,14},{9,9},{20,16},{21,1... | collective-permute-start | bytes 393224 | tf_op jit(solution)/shard_map/ppermute | solution.py:211
  69.5 1.3 %collective-permute-start.8 = (f16[256,256]{1,0:T(8,128)(2,1)S(1)}, f16[256,256]{1,0:T(8,128)(2,1)S(1)}, u32[]{:S(2)}, u32[]{:S(2)}) collective-permute-start(f16[256,256]{1,0:T(8,128)(2,1)S(1)} %convert_element_type.70), channel_id=1, source_target_pairs={{4,1},{5,6},{6,0},{7,2},{10,14},{11,9},{8,15},{9,13},{20,17},{21,2... | collective-permute-start | bytes 393224 | tf_op jit(solution)/shard_map/ppermute | solution.py:211
  71.5 1.4 %collective-permute-done.10 = f16[256,256]{1,0:T(8,128)(2,1)S(1)} collective-permute-done((f16[256,256]{1,0:T(8,128)(2,1)S(1)}, f16[256,256]{1,0:T(8,128)(2,1)S(1)}, u32[]{:S(2)}, u32[]{:S(2)}) %collective-permute-start.10) | collective-permute-done | bytes 131104 | tf_op jit(solution)/shard_map/ppermute | solution.py:211
  73.6 1.9 %shard_map.49 = (f32[2,256,256]{2,1,0:T(8,128)S(1)}, f32[256,256]{1,0:T(8,128)S(1)}, f32[256,256]{1,0:T(8,128)S(1)}, f32[256,256]{1,0:T(8,128)S(1)}, f32[256,256]{1,0:T(8,128)S(1)}, /*index=5*/f32[256,256]{1,0:T(8,128)S(1)}) custom-call(s32[3]{0:T(128)S(1)} %pad_add_fusion.bits, ...), custom_call_target="tpu_custom_call", output_to_operand_aliasing={{3}: (4, {}), {4}: (5, {}), {5}: (6, {})} | custom-call | flops 1024 | bytes 1024 | tf_op jit(solution)/shard_map/pallas_call | solution.py:258
  75.5 8.8 %collective-permute-start.13 = (f32[256,256]{1,0:T(8,128)S(1)}, f32[256,256]{1,0:T(8,128)S(1)}, u32[]{:S(2)}, u32[]{:S(2)}) collective-permute-start(f32[256,256]{1,0:T(8,128)S(1)} %get-tuple-element.50), channel_id=1, source_target_pairs={{4,5},{5,4},{8,9},{9,8},{6,7},{7,6},{10,11},{11,10},{20,21},{21,20... | collective-permute-start | bytes 786440 | tf_op jit(solution)/shard_map/ppermute | solution.py:208
  84.3 1.9 %collective-permute-start.14 = (f32[256,256]{1,0:T(8,128)S(1)}, f32[256,256]{1,0:T(8,128)S(1)}, u32[]{:S(2)}, u32[]{:S(2)}) collective-permute-start(f32[256,256]{1,0:T(8,128)S(1)} %get-tuple-element.51), channel_id=1, source_target_pairs={{4,5},{5,4},{8,9},{9,8},{6,7},{7,6},{10,11},{11,10},{20,21},{21,20... | collective-permute-start | bytes 786440 | tf_op jit(solution)/shard_map/ppermute | solution.py:208
  88.7 1.3 %collective-permute-start.15 = (f16[256,256]{1,0:T(8,128)(2,1)S(1)}, f16[256,256]{1,0:T(8,128)(2,1)S(1)}, u32[]{:S(2)}, u32[]{:S(2)}) collective-permute-start(f16[256,256]{1,0:T(8,128)(2,1)S(1)} %convert_element_type.80), channel_id=1, source_target_pairs={{4,12},{5,14},{6,13},{7,15},{10,3},{11,1},{8,2},{9,0},{20,28},{21,... | collective-permute-start | bytes 393224 | tf_op jit(solution)/shard_map/ppermute | solution.py:211
  90.0 1.3 %collective-permute-start.16 = (f16[256,256]{1,0:T(8,128)(2,1)S(1)}, f16[256,256]{1,0:T(8,128)(2,1)S(1)}, u32[]{:S(2)}, u32[]{:S(2)}) collective-permute-start(f16[256,256]{1,0:T(8,128)(2,1)S(1)} %convert_element_type.82), channel_id=1, source_target_pairs={{4,13},{5,15},{6,12},{7,14},{10,2},{11,0},{8,3},{9,1},{20,29},{21,... | collective-permute-start | bytes 393224 | tf_op jit(solution)/shard_map/ppermute | solution.py:211
  91.3 1.9 %collective-permute-start.17 = (f16[256,256]{1,0:T(8,128)(2,1)S(1)}, f16[256,256]{1,0:T(8,128)(2,1)S(1)}, u32[]{:S(2)}, u32[]{:S(2)}) collective-permute-start(f16[256,256]{1,0:T(8,128)(2,1)S(1)} %convert_element_type.84), channel_id=1, source_target_pairs={{4,3},{5,11},{6,7},{7,9},{10,12},{11,4},{8,8},{9,6},{20,19},{21,27... | collective-permute-start | bytes 393224 | tf_op jit(solution)/shard_map/ppermute | solution.py:211
  93.3 6.7 %collective-permute-start.18 = (f16[256,256]{1,0:T(8,128)(2,1)S(1)}, f16[256,256]{1,0:T(8,128)(2,1)S(1)}, u32[]{:S(2)}, u32[]{:S(2)}) collective-permute-start(f16[256,256]{1,0:T(8,128)(2,1)S(1)} %convert_element_type.86), channel_id=1, source_target_pairs={{4,7},{5,9},{6,3},{7,11},{10,8},{11,6},{8,12},{9,4},{20,23},{21,25... | collective-permute-start | bytes 393224 | tf_op jit(solution)/shard_map/ppermute | solution.py:211
  101.1 1.5 %collective-permute-done.18 = f16[256,256]{1,0:T(8,128)(2,1)S(1)} collective-permute-done((f16[256,256]{1,0:T(8,128)(2,1)S(1)}, f16[256,256]{1,0:T(8,128)(2,1)S(1)}, u32[]{:S(2)}, u32[]{:S(2)}) %collective-permute-start.18) | collective-permute-done | bytes 131104 | tf_op jit(solution)/shard_map/ppermute | solution.py:211
  (41 shorter events, 7.2 us)
Async XLA Ops:
  0.1 1.6 %copy-start = (bf16[256,4096]{1,0:T(8,128)(2,1)S(1)}, bf16[256,4096]{1,0:T(8,128)(2,1)}, u32[]{:S(2)}) copy-start(bf16[256,4096]{1,0:T(8,128)(2,1)} %values.1) | copy-start | bytes 6291460
  2.9 29.3 %collective-permute-start.1 = (bf16[272,2048]{1,0:T(8,128)(2,1)S(1)}, bf16[272,2048]{1,0:T(8,128)(2,1)S(1)}, u32[]{:S(2)}, u32[]{:S(2)}) collective-permute-start(bf16[272,2048]{1,0:T(8,128)(2,1)S(1)} %get-tuple-element.32.near), channel_id=1, source_target_pairs={{0,4},{12,8},{1,5},{13,9},{2,6},{14,10},{3,7},{15,11},{16,20},{28,... | collective-permute-start | bytes 3342344 | tf_op jit(solution)/shard_map/ppermute | solution.py:227
  4.2 31.6 %collective-permute-start.2 = (bf16[256,2048]{1,0:T(8,128)(2,1)S(1)}, bf16[256,2048]{1,0:T(8,128)(2,1)S(1)}, u32[]{:S(2)}, u32[]{:S(2)}) collective-permute-start(bf16[256,2048]{1,0:T(8,128)(2,1)S(1)} %get-tuple-element.31), channel_id=1, source_target_pairs={{4,8},{8,4},{5,9},{9,5},{6,10},{10,6},{7,11},{11,7},{20,24},{24,20... | collective-permute-start | bytes 3145736 | tf_op jit(solution)/shard_map/ppermute | solution.py:226
  7.7 65.9 %collective-permute-start = (bf16[256,2048]{1,0:T(8,128)(2,1)S(1)}, bf16[256,2048]{1,0:T(8,128)(2,1)S(1)}, u32[]{:S(2)}, u32[]{:S(2)}) collective-permute-start(bf16[256,2048]{1,0:T(8,128)(2,1)S(1)} %get-tuple-element.31), channel_id=1, source_target_pairs={{0,8},{12,4},{1,9},{13,5},{2,10},{14,6},{3,11},{15,7},{16,24},{28,... | collective-permute-start | bytes 3145736 | tf_op jit(solution)/shard_map/ppermute | solution.py:228
  32.3 32.8 %copy-start.1 = (s32[7,2,2]{2,1,0:T(2,128)S(1)}, s32[7,2,2]{2,1,0:T(2,128)}, u32[]{:S(2)}) copy-start(s32[7,2,2]{2,1,0:T(2,128)} %constant.22.clone.places) | copy-start | bytes 340
  32.3 22.4 %collective-permute-start.3 = (f32[1,2048]{1,0:T(1,128)S(1)}, f32[1,2048]{1,0:T(1,128)S(1)}, u32[]{:S(2)}, u32[]{:S(2)}) collective-permute-start(f32[1,2048]{1,0:T(1,128)S(1)} %slice_add_fusion), channel_id=1, source_target_pairs={{4,8},{8,4},{5,9},{9,5},{6,10},{10,6},{7,11},{11,7},{20,24},{24,20... | collective-permute-start | bytes 24584 | tf_op jit(solution)/shard_map/ppermute | solution.py:231
  57.3 6.3 %collective-permute-start.4 = (f32[256,256]{1,0:T(8,128)S(1)}, f32[256,256]{1,0:T(8,128)S(1)}, u32[]{:S(2)}, u32[]{:S(2)}) collective-permute-start(f32[256,256]{1,0:T(8,128)S(1)} %get-tuple-element.37), channel_id=1, source_target_pairs={{4,5},{5,4},{8,9},{9,8},{6,7},{7,6},{10,11},{11,10},{20,21},{21,20... | collective-permute-start | bytes 786440 | tf_op jit(solution)/shard_map/ppermute | solution.py:208
  59.3 4.4 %collective-permute-start.5 = (f32[256,256]{1,0:T(8,128)S(1)}, f32[256,256]{1,0:T(8,128)S(1)}, u32[]{:S(2)}, u32[]{:S(2)}) collective-permute-start(f32[256,256]{1,0:T(8,128)S(1)} %get-tuple-element.38), channel_id=1, source_target_pairs={{4,5},{5,4},{8,9},{9,8},{6,7},{7,6},{10,11},{11,10},{20,21},{21,20... | collective-permute-start | bytes 786440 | tf_op jit(solution)/shard_map/ppermute | solution.py:208
  61.7 3.4 %collective-permute-start.6 = (f32[256,256]{1,0:T(8,128)S(1)}, f32[256,256]{1,0:T(8,128)S(1)}, u32[]{:S(2)}, u32[]{:S(2)}) collective-permute-start(f32[256,256]{1,0:T(8,128)S(1)} %get-tuple-element.39), channel_id=1, source_target_pairs={{4,5},{5,4},{8,9},{9,8},{6,7},{7,6},{10,11},{11,10},{20,21},{21,20... | collective-permute-start | bytes 786440 | tf_op jit(solution)/shard_map/ppermute | solution.py:208
  66.1 6.9 %collective-permute-start.10 = (f16[256,256]{1,0:T(8,128)(2,1)S(1)}, f16[256,256]{1,0:T(8,128)(2,1)S(1)}, u32[]{:S(2)}, u32[]{:S(2)}) collective-permute-start(f16[256,256]{1,0:T(8,128)(2,1)S(1)} %convert_element_type.74), channel_id=1, source_target_pairs={{4,5},{6,4},{10,10},{8,11},{20,21},{22,20},{26,26},{24,27}} | collective-permute-start | bytes 393224 | tf_op jit(solution)/shard_map/ppermute | solution.py:211
  68.2 4.8 %collective-permute-start.7 = (f16[256,256]{1,0:T(8,128)(2,1)S(1)}, f16[256,256]{1,0:T(8,128)(2,1)S(1)}, u32[]{:S(2)}, u32[]{:S(2)}) collective-permute-start(f16[256,256]{1,0:T(8,128)(2,1)S(1)} %convert_element_type.68), channel_id=1, source_target_pairs={{4,0},{5,2},{6,1},{7,6},{10,15},{11,13},{8,14},{9,9},{20,16},{21,1... | collective-permute-start | bytes 393224 | tf_op jit(solution)/shard_map/ppermute | solution.py:211
  69.5 3.9 %collective-permute-start.8 = (f16[256,256]{1,0:T(8,128)(2,1)S(1)}, f16[256,256]{1,0:T(8,128)(2,1)S(1)}, u32[]{:S(2)}, u32[]{:S(2)}) collective-permute-start(f16[256,256]{1,0:T(8,128)(2,1)S(1)} %convert_element_type.70), channel_id=1, source_target_pairs={{4,1},{5,6},{6,0},{7,2},{10,14},{11,9},{8,15},{9,13},{20,17},{21,2... | collective-permute-start | bytes 393224 | tf_op jit(solution)/shard_map/ppermute | solution.py:211
  70.9 2.6 %collective-permute-start.9 = (f16[256,256]{1,0:T(8,128)(2,1)S(1)}, f16[256,256]{1,0:T(8,128)(2,1)S(1)}, u32[]{:S(2)}, u32[]{:S(2)}) collective-permute-start(f16[256,256]{1,0:T(8,128)(2,1)S(1)} %convert_element_type.72), channel_id=1, source_target_pairs={{4,4},{6,5},{10,11},{8,10},{20,20},{22,21},{26,27},{24,26}} | collective-permute-start | bytes 393224 | tf_op jit(solution)/shard_map/ppermute | solution.py:211
  73.6 14.2 %copy-start.2 = (s32[4,2,2]{2,1,0:T(2,128)S(1)}, s32[4,2,2]{2,1,0:T(2,128)}, u32[]{:S(2)}) copy-start(s32[4,2,2]{2,1,0:T(2,128)} %constant.23.clone.places) | copy-start | bytes 196
  75.5 12.2 %collective-permute-start.13 = (f32[256,256]{1,0:T(8,128)S(1)}, f32[256,256]{1,0:T(8,128)S(1)}, u32[]{:S(2)}, u32[]{:S(2)}) collective-permute-start(f32[256,256]{1,0:T(8,128)S(1)} %get-tuple-element.50), channel_id=1, source_target_pairs={{4,5},{5,4},{8,9},{9,8},{6,7},{7,6},{10,11},{11,10},{20,21},{21,20... | collective-permute-start | bytes 786440 | tf_op jit(solution)/shard_map/ppermute | solution.py:208
  84.3 3.4 %collective-permute-start.14 = (f32[256,256]{1,0:T(8,128)S(1)}, f32[256,256]{1,0:T(8,128)S(1)}, u32[]{:S(2)}, u32[]{:S(2)}) collective-permute-start(f32[256,256]{1,0:T(8,128)S(1)} %get-tuple-element.51), channel_id=1, source_target_pairs={{4,5},{5,4},{8,9},{9,8},{6,7},{7,6},{10,11},{11,10},{20,21},{21,20... | collective-permute-start | bytes 786440 | tf_op jit(solution)/shard_map/ppermute | solution.py:208
  86.3 7.0 %collective-permute-start.11 = (f16[256,256]{1,0:T(8,128)(2,1)S(1)}, f16[256,256]{1,0:T(8,128)(2,1)S(1)}, u32[]{:S(2)}, u32[]{:S(2)}) collective-permute-start(f16[256,256]{1,0:T(8,128)(2,1)S(1)} %convert_element_type.76), channel_id=1, source_target_pairs={{5,8},{7,10},{11,7},{9,5},{21,24},{23,26},{27,23},{25,21}} | collective-permute-start | bytes 393224 | tf_op jit(solution)/shard_map/ppermute | solution.py:211
  87.0 13.7 %collective-permute-start.12 = (f16[256,256]{1,0:T(8,128)(2,1)S(1)}, f16[256,256]{1,0:T(8,128)(2,1)S(1)}, u32[]{:S(2)}, u32[]{:S(2)}) collective-permute-start(f16[256,256]{1,0:T(8,128)(2,1)S(1)} %convert_element_type.78), channel_id=1, source_target_pairs={{5,10},{7,8},{11,5},{9,7},{21,26},{23,24},{27,21},{25,23}} | collective-permute-start | bytes 393224 | tf_op jit(solution)/shard_map/ppermute | solution.py:211
  88.7 12.1 %collective-permute-start.15 = (f16[256,256]{1,0:T(8,128)(2,1)S(1)}, f16[256,256]{1,0:T(8,128)(2,1)S(1)}, u32[]{:S(2)}, u32[]{:S(2)}) collective-permute-start(f16[256,256]{1,0:T(8,128)(2,1)S(1)} %convert_element_type.80), channel_id=1, source_target_pairs={{4,12},{5,14},{6,13},{7,15},{10,3},{11,1},{8,2},{9,0},{20,28},{21,... | collective-permute-start | bytes 393224 | tf_op jit(solution)/shard_map/ppermute | solution.py:211
  90.0 10.7 %collective-permute-start.16 = (f16[256,256]{1,0:T(8,128)(2,1)S(1)}, f16[256,256]{1,0:T(8,128)(2,1)S(1)}, u32[]{:S(2)}, u32[]{:S(2)}) collective-permute-start(f16[256,256]{1,0:T(8,128)(2,1)S(1)} %convert_element_type.82), channel_id=1, source_target_pairs={{4,13},{5,15},{6,12},{7,14},{10,2},{11,0},{8,3},{9,1},{20,29},{21,... | collective-permute-start | bytes 393224 | tf_op jit(solution)/shard_map/ppermute | solution.py:211
  91.3 9.7 %collective-permute-start.17 = (f16[256,256]{1,0:T(8,128)(2,1)S(1)}, f16[256,256]{1,0:T(8,128)(2,1)S(1)}, u32[]{:S(2)}, u32[]{:S(2)}) collective-permute-start(f16[256,256]{1,0:T(8,128)(2,1)S(1)} %convert_element_type.84), channel_id=1, source_target_pairs={{4,3},{5,11},{6,7},{7,9},{10,12},{11,4},{8,8},{9,6},{20,19},{21,27... | collective-permute-start | bytes 393224 | tf_op jit(solution)/shard_map/ppermute | solution.py:211
  93.3 9.2 %collective-permute-start.18 = (f16[256,256]{1,0:T(8,128)(2,1)S(1)}, f16[256,256]{1,0:T(8,128)(2,1)S(1)}, u32[]{:S(2)}, u32[]{:S(2)}) collective-permute-start(f16[256,256]{1,0:T(8,128)(2,1)S(1)} %convert_element_type.86), channel_id=1, source_target_pairs={{4,7},{5,9},{6,3},{7,11},{10,8},{11,6},{8,12},{9,4},{20,23},{21,25... | collective-permute-start | bytes 393224 | tf_op jit(solution)/shard_map/ppermute | solution.py:211

commit v5 on v4

--- a/solution.py
+++ b/solution.py
@@ -61,9 +61,11 @@
     ((3, 2), (3, 3), (2, 3), (3, 3), (2, 1)),
 )
 EXTRA = 16
+HEAD = 64
 VMEM = pl.BlockSpec(memory_space=pltpu.VMEM)
 SMEM = pl.BlockSpec(memory_space=pltpu.SMEM)
 ANY = pl.BlockSpec(memory_space=pl.ANY)
+HBM = pl.BlockSpec(memory_space=pltpu.HBM)
 LIMIT = pltpu.CompilerParams(vmem_limit_bytes=40 * 2**20)
 BRIEF = pl.CostEstimate(flops=1024, bytes_accessed=1024, transcendentals=0)
 
@@ -93,51 +95,59 @@
     ]
 
 
-def split_kernel(bits, values, near, far, sums, sems):
+def split_kernel(bits, values, near, far, head, tail, sums, sems):
     rows, part = far.shape
     step = 512
-    copies = []
-    for i, (out, start) in enumerate(((near, 1 - bits[0]), (far, bits[0]))):
-        columns = pl.ds(pl.multiple_of(start * part, 128), part)
-        copies.append(
-            pltpu.make_async_copy(values.at[:, columns], out.at[pl.ds(0, rows), :], sems.at[i])
-        )
+    near_columns = pl.ds(pl.multiple_of((1 - bits[0]) * part, 128), part)
+    far_columns = pl.ds(pl.multiple_of(bits[0] * part, 128), part)
+    first, rest = pl.ds(0, HEAD), pl.ds(HEAD, rows - HEAD)
+    copies = [
+        pltpu.make_async_copy(values.at[:, far_columns], far, sems.at[0]),
+        pltpu.make_async_copy(values.at[:, near_columns], near, sems.at[1]),
+        pltpu.make_async_copy(
+            values.at[first, far_columns], head.at[pl.ds(EXTRA, HEAD), :], sems.at[2]
+        ),
+        pltpu.make_async_copy(values.at[rest, far_columns], tail, sems.at[3]),
+    ]
     for copy in copies:
         copy.start()
-    for i, (copy, out) in enumerate(zip(copies, (near, far))):
+    copies[0].wait()
+
+    @pl.loop(0, part // step)
+    def _(j):
+        columns = pl.ds(pl.multiple_of(j * step, step), step)
+        left = jnp.sum(far[:, columns].astype(jnp.float32), axis=0, keepdims=True)
+        for i in range(3):
+            piece = left.astype(jnp.bfloat16).astype(jnp.float32)
+            sums[pl.ds(i, 1), columns] = piece
+            left = left - piece
+        sums[pl.ds(3, EXTRA - 3), columns] = jnp.zeros((EXTRA - 3, step), jnp.float32)
+
+    head[pl.ds(0, EXTRA), :] = sums[...].astype(jnp.bfloat16)
+    for copy in copies[1:]:
         copy.wait()
-
-        @pl.loop(0, part // step)
-        def _(j):
-            columns = pl.ds(pl.multiple_of(j * step, step), step)
-            block = out[pl.ds(0, rows), columns].astype(jnp.float32)
-            sums[pl.ds(i, 1), columns] = jnp.sum(block, axis=0, keepdims=True)
-
-    pieces = []
-    for i in (0, 1):
-        left = sums[pl.ds(i, 1), :]
-        for _ in range(3):
-            piece = left.astype(jnp.bfloat16).astype(jnp.float32)
-            pieces.append(piece)
-            left = left - piece
-    pieces.append(jnp.zeros((EXTRA - len(pieces), part), jnp.float32))
-    near[pl.ds(rows, EXTRA), :] = jnp.concatenate(pieces, axis=0).astype(jnp.bfloat16)
 
 
 def block_product(left, right):
     return lax.dot_general(left, right, (((1,), (1,)), ((), ())), preferred_element_type=jnp.float32)
 
 
-def early_kernel(bits, edge, near, other, sums, arrived, centred, mean, own, *rest):
+def early_kernel(bits, edge, near, other, head, centred, mean, own, *rest):
     sends, both = rest[:-1], rest[-1]
-    rows = other.shape[0]
-    pieces = edge[pl.ds(rows, EXTRA), :].astype(jnp.float32)
-    edge_sum = pieces[0:1] + pieces[1:2] + pieces[2:3]
-    average = (sums[pl.ds(0, 1), :] + edge_sum + arrived[...]) * (1.0 / (4 * rows))
-    mean[...] = average
-    for i, block in enumerate((edge, near, other)):
-        values = block[pl.ds(0, rows), :].astype(jnp.float32)
-        centred[i] = (values - average).astype(jnp.bfloat16)
+    rows, part = near.shape
+    step = 512
+
+    @pl.loop(0, part // step)
+    def _(n):
+        columns = pl.ds(pl.multiple_of(n * step, step), step)
+        values = [block[:, columns].astype(jnp.float32) for block in (edge, near, other)]
+        total = jnp.sum(head[pl.ds(0, EXTRA), columns].astype(jnp.float32), axis=0, keepdims=True)
+        total = total + jnp.sum(values[0] + values[1] + values[2], axis=0, keepdims=True)
+        average = total * (1.0 / (4 * rows))
+        mean[:, columns] = average
+        for i in range(3):
+            centred[i, :, columns] = (values[i] - average).astype(jnp.bfloat16)
+
     for core in (0, 1):
         for place, (i, j) in enumerate(EARLY_SUMS[core]):
             both[core, place] = block_product(centred[i], centred[j])
@@ -146,11 +156,15 @@
         send[...] = both[1 - bits[1], place]
 
 
-def late_kernel(bits, far_edge, mean, centred, *rest):
+def late_kernel(bits, head, tail, mean, centred, *rest):
     handed = (len(rest) - 5) // 2
     own, *sends = rest[handed : handed + 3]
     last, both = rest[-2:]
-    last[...] = (far_edge[...].astype(jnp.float32) - mean[...]).astype(jnp.bfloat16)
+    rows = last.shape[0]
+    first = head[pl.ds(EXTRA, HEAD), :].astype(jnp.float32) - mean[...]
+    last[pl.ds(0, HEAD), :] = first.astype(jnp.bfloat16)
+    second = tail[...].astype(jnp.float32) - mean[...]
+    last[pl.ds(HEAD, rows - HEAD), :] = second.astype(jnp.bfloat16)
     for core in (0, 1):
         for place, (_, j) in enumerate(LATE_SUMS[core]):
             both[core, place] = block_product(last[...], last[...] if j == 3 else centred[j])
@@ -210,25 +224,24 @@
     def send(value, blocks):
         return lax.ppermute(value.astype(jnp.float16), everyone, round_pairs(blocks))
 
-    near, far, sums = pl.pallas_call(
+    near, far, head, tail = pl.pallas_call(
         split_kernel,
         out_shape=[
-            shape_of((local_rows + EXTRA, part), jnp.bfloat16),
             shape_of((local_rows, part), jnp.bfloat16),
-            shape_of((2, part), jnp.float32),
+            shape_of((local_rows, part), jnp.bfloat16),
+            shape_of((EXTRA + HEAD, part), jnp.bfloat16),
+            shape_of((local_rows - HEAD, part), jnp.bfloat16),
         ],
-        in_specs=[SMEM, ANY],
-        out_specs=[VMEM] * 3,
-        scratch_shapes=[pltpu.SemaphoreType.DMA((2,))],
+        in_specs=[SMEM, HBM],
+        out_specs=[VMEM] * 4,
+        scratch_shapes=[pltpu.VMEM((EXTRA, part), jnp.float32), pltpu.SemaphoreType.DMA((4,))],
         compiler_params=LIMIT,
         cost_estimate=BRIEF,
     )(bits, log_derivs)
     from_centre = lax.ppermute(far, "row", to_centre)
     from_edge = lax.ppermute(near, "row", to_own)
-    from_far_edge = lax.ppermute(far, "row", to_far)
-    pieces = from_edge[local_rows : local_rows + EXTRA].astype(jnp.float32)
-    passed_on = sums[1:2] + pieces[3:4] + pieces[4:5] + pieces[5:6]
-    arrived_sum = lax.ppermute(passed_on, "row", to_centre)
+    from_head = lax.ppermute(head, "row", to_far)
+    from_tail = lax.ppermute(tail, "row", to_far)
 
     block = shape_of((local_rows, local_rows), jnp.float32)
     early_blocks = (3, local_rows, local_rows)
@@ -240,12 +253,12 @@
             shape_of(early_blocks, jnp.float32),
         ]
         + [block] * 3,
-        in_specs=[SMEM] + [VMEM] * 5,
+        in_specs=[SMEM] + [VMEM] * 4,
         out_specs=[VMEM] * 6,
         scratch_shapes=[pltpu.VMEM((2,) + early_blocks, jnp.float32)],
         compiler_params=LIMIT,
         cost_estimate=BRIEF,
-    )(bits, from_edge, near, from_centre, sums, arrived_sum)
+    )(bits, from_edge, near, from_centre, from_head)
     places = held_place(EARLY_HELD, NEAR_ROUNDS + FAR_ROUNDS) + [[[SPARE] * 2] * 2]
     others = [swap(other) for other in others]
     *early, spare = combine(bits, own, others, (1, 2), (), EARLY_HELD, places, samples)
@@ -260,16 +273,16 @@
         out_shape=[shape_of(late_blocks, jnp.float32)]
         + [block] * 2
         + [shape_of(value.shape, value.dtype) for value in handed],
-        in_specs=[SMEM] + [VMEM] * 3 + [ANY] * len(handed),
+        in_specs=[SMEM] + [VMEM] * 4 + [ANY] * len(handed),
         out_specs=[VMEM] * 3 + [ANY] * len(handed),
         scratch_shapes=[
             pltpu.VMEM((local_rows, part), jnp.bfloat16),
             pltpu.VMEM((2,) + late_blocks, jnp.float32),
         ],
-        input_output_aliases={4 + i: 3 + i for i in range(len(handed))},
+        input_output_aliases={5 + i: 3 + i for i in range(len(handed))},
         compiler_params=LIMIT,
         cost_estimate=BRIEF,
-    )(bits, from_far_edge, mean, centred, *handed)
+    )(bits, from_head, from_tail, mean, centred, *handed)
     others = [swap(other) for other in others]
     arrived = [send(value, blocks) for value, blocks in zip((first, second), FAR_ROUNDS)]
     places = held_place(LATE_HELD, LATE_ROUNDS)

time: 105 us -> 107 us (1.019)
  the two profiles are of different devices: /device:TPU:8 before, /device:TPU:1 now
where the time goes in v5:
time: 107 us; the launch traced here: 106 us
  waiting for transfers between devices  71.5 us (67%)
  starting transfers between devices  22.3 us (21%)
  Pallas kernels  8.57 us (8%)
  local copies, waits for them, and re-layouts  1.6 us (1%)
  other arithmetic  1.17 us (1%)
    ppermute x10, waiting for transfers between devices, send(): lax.ppermute(value.astype(jnp.float16), everyone, round_pairs(blocks))  48.4 us
    ppermute x1, waiting for transfers between devices, two_centres(): from_head = lax.ppermute(head, 'row', to_far)  23.1 us
    ppermute x10, starting transfers between devices, send(): lax.ppermute(value.astype(jnp.float16), everyone, round_pairs(blocks))  9.18 us
    ppermute x1, starting transfers between devices, two_centres(): from_edge = lax.ppermute(near, 'row', to_own)  4.1 us
    pallas_call x1, Pallas kernels, two_centres(): pl.pallas_call(early_kernel, out_shape=[shape_of((3, local_rows, part), j...  3.73 us
    ppermute x1, starting transfers between devices, two_centres(): from_head = lax.ppermute(head, 'row', to_far)  3.61 us
    ppermute x5, starting transfers between devices, swap(): return lax.ppermute(value, ('row', 'half'), centres)  3.39 us
  transfers between devices with their start and end apart: 19, of which 5 were waited for; matrix products, arithmetic and copies ran while one was open for 0% of the time, Pallas kernels for 5%

profile of v5, /device:TPU:1, one launch (start us, length us, event | category | flops | bytes accessed | tf_op | source)
XLA Modules:
  0.0 106.3 jit_solution(1801849108387702045)
XLA Ops:
  0.1 1.6 %copy-done = bf16[256,4096]{1,0:T(8,128)(2,1)S(1)} copy-done((bf16[256,4096]{1,0:T(8,128)(2,1)S(1)}, bf16[256,4096]{1,0:T(8,128)(2,1)}, u32[]{:S(2)}) %copy-start) | copy-done | bytes 2097176
  1.7 1.1 %shard_map.46 = (bf16[256,2048]{1,0:T(8,128)(2,1)S(1)}, bf16[256,2048]{1,0:T(8,128)(2,1)S(1)}, bf16[80,2048]{1,0:T(8,128)(2,1)S(1)}, bf16[192,2048]{1,0:T(8,128)(2,1)S(1)}) custom-call(s32[3]{0:T(128)S(1)} %pad_add_fusion.bits, bf16[256,4096]{1,0:T(8,128)(2,1)S(1)} %copy-done), custom_call_target="tpu_custom_call" | custom-call | flops 1024 | bytes 1024 | tf_op jit(solution)/shard_map/pallas_call | solution.py:227
  2.7 4.1 %collective-permute-start.2 = (bf16[256,2048]{1,0:T(8,128)(2,1)S(1)}, bf16[256,2048]{1,0:T(8,128)(2,1)S(1)}, u32[]{:S(2)}, u32[]{:S(2)}) collective-permute-start(bf16[256,2048]{1,0:T(8,128)(2,1)S(1)} %get-tuple-element.34.near), channel_id=1, source_target_pairs={{0,4},{12,8},{1,5},{13,9},{2,6},{14,10},{3,7},{15,11},{16,20},{28,... | collective-permute-start | bytes 3145736 | tf_op jit(solution)/shard_map/ppermute | solution.py:242
  6.8 0.7 collective-permute-start.3
  7.6 3.6 %collective-permute-start = (bf16[80,2048]{1,0:T(8,128)(2,1)S(1)}, bf16[80,2048]{1,0:T(8,128)(2,1)S(1)}, u32[]{:S(2)}, u32[]{:S(2)}) collective-permute-start(bf16[80,2048]{1,0:T(8,128)(2,1)S(1)} %get-tuple-element.32), channel_id=1, source_target_pairs={{0,8},{12,4},{1,9},{13,5},{2,10},{14,6},{3,11},{15,7},{16,24},{28,... | collective-permute-start | bytes 983048 | tf_op jit(solution)/shard_map/ppermute | solution.py:243
  11.2 1.3 %collective-permute-start.1 = (bf16[192,2048]{1,0:T(8,128)(2,1)S(1)}, bf16[192,2048]{1,0:T(8,128)(2,1)S(1)}, u32[]{:S(2)}, u32[]{:S(2)}) collective-permute-start(bf16[192,2048]{1,0:T(8,128)(2,1)S(1)} %get-tuple-element.33), channel_id=1, source_target_pairs={{0,8},{12,4},{1,9},{13,5},{2,10},{14,6},{3,11},{15,7},{16,24},{28,... | collective-permute-start | bytes 2359304 | tf_op jit(solution)/shard_map/ppermute | solution.py:244
  12.5 23.1 %collective-permute-done.head = bf16[80,2048]{1,0:T(8,128)(2,1)S(1)} collective-permute-done((bf16[80,2048]{1,0:T(8,128)(2,1)S(1)}, bf16[80,2048]{1,0:T(8,128)(2,1)S(1)}, u32[]{:S(2)}, u32[]{:S(2)}) %collective-permute-start) | collective-permute-done | bytes 327712 | tf_op jit(solution)/shard_map/ppermute | solution.py:243
  35.7 3.7 %shard_map.47 = (bf16[3,256,2048]{2,1,0:T(8,128)(2,1)S(1)}, f32[1,2048]{1,0:T(1,128)S(1)}, f32[3,256,256]{2,1,0:T(8,128)S(1)}, f32[256,256]{1,0:T(8,128)S(1)}, f...) custom-call(s32[3]{0:T(128)S(1)} %pad_add_fusion.bits, bf16[256,2048]{1,0:T(8,128)(2,1)S(1)} %collective-permute-done.2.edge, ...), custom_call_target="tpu_custom_call" | custom-call | flops 1024 | bytes 1024 | tf_op jit(solution)/shard_map/pallas_call | solution.py:248
  39.4 0.7 collective-permute-start.4
  40.1 0.7 collective-permute-start.5
  40.8 0.7 collective-permute-start.6
  41.5 1.0 shard_map.48
  43.9 1.3 %collective-permute-start.8 = (f16[256,256]{1,0:T(8,128)(2,1)S(1)}, f16[256,256]{1,0:T(8,128)(2,1)S(1)}, u32[]{:S(2)}, u32[]{:S(2)}) collective-permute-start(f16[256,256]{1,0:T(8,128)(2,1)S(1)} %convert_element_type.66), channel_id=1, source_target_pairs={{4,1},{5,6},{6,0},{7,2},{10,14},{11,9},{8,15},{9,13},{20,17},{21,2... | collective-permute-start | bytes 393224 | tf_op jit(solution)/shard_map/ppermute | solution.py:225
  45.3 1.3 %collective-permute-start.7 = (f16[256,256]{1,0:T(8,128)(2,1)S(1)}, f16[256,256]{1,0:T(8,128)(2,1)S(1)}, u32[]{:S(2)}, u32[]{:S(2)}) collective-permute-start(f16[256,256]{1,0:T(8,128)(2,1)S(1)} %convert_element_type.64), channel_id=1, source_target_pairs={{4,0},{5,2},{6,1},{7,6},{10,15},{11,13},{8,14},{9,9},{20,16},{21,1... | collective-permute-start | bytes 393224 | tf_op jit(solution)/shard_map/ppermute | solution.py:225
  46.6 30.0 %collective-permute-done.8 = f16[256,256]{1,0:T(8,128)(2,1)S(1)} collective-permute-done((f16[256,256]{1,0:T(8,128)(2,1)S(1)}, f16[256,256]{1,0:T(8,128)(2,1)S(1)}, u32[]{:S(2)}, u32[]{:S(2)}) %collective-permute-start.8) | collective-permute-done | bytes 131104 | tf_op jit(solution)/shard_map/ppermute | solution.py:225
  76.6 4.5 %collective-permute-done.7 = f16[256,256]{1,0:T(8,128)(2,1)S(1)} collective-permute-done((f16[256,256]{1,0:T(8,128)(2,1)S(1)}, f16[256,256]{1,0:T(8,128)(2,1)S(1)}, u32[]{:S(2)}, u32[]{:S(2)}) %collective-permute-start.7) | collective-permute-done | bytes 131104 | tf_op jit(solution)/shard_map/ppermute | solution.py:225
  81.3 1.9 %shard_map.49 = (f32[2,256,256]{2,1,0:T(8,128)S(1)}, f32[256,256]{1,0:T(8,128)S(1)}, f32[256,256]{1,0:T(8,128)S(1)}, f32[256,256]{1,0:T(8,128)S(1)}, f32[256,256]{1,0:T(8,128)S(1)}, /*index=5*/f32[256,256]{1,0:T(8,128)S(1)}) custom-call(s32[3]{0:T(128)S(1)} %pad_add_fusion.bits, ...), custom_call_target="tpu_custom_call", output_to_operand_aliasing={{3}: (5, {}), {4}: (6, {}), {5}: (7, {})} | custom-call | flops 1024 | bytes 1024 | tf_op jit(solution)/shard_map/pallas_call | solution.py:271
  83.2 0.7 collective-permute-start.13
  86.0 0.9 shard_map.50
  88.3 1.3 %collective-permute-start.16 = (f16[256,256]{1,0:T(8,128)(2,1)S(1)}, f16[256,256]{1,0:T(8,128)(2,1)S(1)}, u32[]{:S(2)}, u32[]{:S(2)}) collective-permute-start(f16[256,256]{1,0:T(8,128)(2,1)S(1)} %convert_element_type.78), channel_id=1, source_target_pairs={{4,13},{5,15},{6,12},{7,14},{10,2},{11,0},{8,3},{9,1},{20,29},{21,... | collective-permute-start | bytes 393224 | tf_op jit(solution)/shard_map/ppermute | solution.py:225
  89.7 1.3 %collective-permute-start.15 = (f16[256,256]{1,0:T(8,128)(2,1)S(1)}, f16[256,256]{1,0:T(8,128)(2,1)S(1)}, u32[]{:S(2)}, u32[]{:S(2)}) collective-permute-start(f16[256,256]{1,0:T(8,128)(2,1)S(1)} %convert_element_type.76), channel_id=1, source_target_pairs={{4,12},{5,14},{6,13},{7,15},{10,3},{11,1},{8,2},{9,0},{20,28},{21,... | collective-permute-start | bytes 393224 | tf_op jit(solution)/shard_map/ppermute | solution.py:225
  91.7 11.5 %collective-permute-done.16 = f16[256,256]{1,0:T(8,128)(2,1)S(1)} collective-permute-done((f16[256,256]{1,0:T(8,128)(2,1)S(1)}, f16[256,256]{1,0:T(8,128)(2,1)S(1)}, u32[]{:S(2)}, u32[]{:S(2)}) %collective-permute-start.16) | collective-permute-done | bytes 131104 | tf_op jit(solution)/shard_map/ppermute | solution.py:225
  103.2 2.3 %collective-permute-done.15 = f16[256,256]{1,0:T(8,128)(2,1)S(1)} collective-permute-done((f16[256,256]{1,0:T(8,128)(2,1)S(1)}, f16[256,256]{1,0:T(8,128)(2,1)S(1)}, u32[]{:S(2)}, u32[]{:S(2)}) %collective-permute-start.15) | collective-permute-done | bytes 131104 | tf_op jit(solution)/shard_map/ppermute | solution.py:225
  105.4 0.8 select_add_fusion
  (39 shorter events, 5.1 us)
Async XLA Ops:
  0.0 41.5 %copy-start.1 = (s32[7,2,2]{2,1,0:T(2,128)S(1)}, s32[7,2,2]{2,1,0:T(2,128)}, u32[]{:S(2)}) copy-start(s32[7,2,2]{2,1,0:T(2,128)} %constant.22.clone.places) | copy-start | bytes 340
  0.1 1.6 %copy-start = (bf16[256,4096]{1,0:T(8,128)(2,1)S(1)}, bf16[256,4096]{1,0:T(8,128)(2,1)}, u32[]{:S(2)}) copy-start(bf16[256,4096]{1,0:T(8,128)(2,1)} %values.1) | copy-start | bytes 6291460
  2.7 32.9 %collective-permute-start.2 = (bf16[256,2048]{1,0:T(8,128)(2,1)S(1)}, bf16[256,2048]{1,0:T(8,128)(2,1)S(1)}, u32[]{:S(2)}, u32[]{:S(2)}) collective-permute-start(bf16[256,2048]{1,0:T(8,128)(2,1)S(1)} %get-tuple-element.34.near), channel_id=1, source_target_pairs={{0,4},{12,8},{1,5},{13,9},{2,6},{14,10},{3,7},{15,11},{16,20},{28,... | collective-permute-start | bytes 3145736 | tf_op jit(solution)/shard_map/ppermute | solution.py:242
  6.8 28.8 %collective-permute-start.3 = (bf16[256,2048]{1,0:T(8,128)(2,1)S(1)}, bf16[256,2048]{1,0:T(8,128)(2,1)S(1)}, u32[]{:S(2)}, u32[]{:S(2)}) collective-permute-start(bf16[256,2048]{1,0:T(8,128)(2,1)S(1)} %get-tuple-element.35), channel_id=1, source_target_pairs={{4,8},{8,4},{5,9},{9,5},{6,10},{10,6},{7,11},{11,7},{20,24},{24,20... | collective-permute-start | bytes 3145736 | tf_op jit(solution)/shard_map/ppermute | solution.py:241
  7.6 28.1 %collective-permute-start = (bf16[80,2048]{1,0:T(8,128)(2,1)S(1)}, bf16[80,2048]{1,0:T(8,128)(2,1)S(1)}, u32[]{:S(2)}, u32[]{:S(2)}) collective-permute-start(bf16[80,2048]{1,0:T(8,128)(2,1)S(1)} %get-tuple-element.32), channel_id=1, source_target_pairs={{0,8},{12,4},{1,9},{13,5},{2,10},{14,6},{3,11},{15,7},{16,24},{28,... | collective-permute-start | bytes 983048 | tf_op jit(solution)/shard_map/ppermute | solution.py:243
  11.2 70.1 %collective-permute-start.1 = (bf16[192,2048]{1,0:T(8,128)(2,1)S(1)}, bf16[192,2048]{1,0:T(8,128)(2,1)S(1)}, u32[]{:S(2)}, u32[]{:S(2)}) collective-permute-start(bf16[192,2048]{1,0:T(8,128)(2,1)S(1)} %get-tuple-element.33), channel_id=1, source_target_pairs={{0,8},{12,4},{1,9},{13,5},{2,10},{14,6},{3,11},{15,7},{16,24},{28,... | collective-permute-start | bytes 2359304 | tf_op jit(solution)/shard_map/ppermute | solution.py:244
  39.4 2.1 %collective-permute-start.4 = (f32[256,256]{1,0:T(8,128)S(1)}, f32[256,256]{1,0:T(8,128)S(1)}, u32[]{:S(2)}, u32[]{:S(2)}) collective-permute-start(f32[256,256]{1,0:T(8,128)S(1)} %get-tuple-element.39), channel_id=1, source_target_pairs={{4,5},{5,4},{8,9},{9,8},{6,7},{7,6},{10,11},{11,10},{20,21},{21,20... | collective-permute-start | bytes 786440 | tf_op jit(solution)/shard_map/ppermute | solution.py:222
  40.1 1.4 %collective-permute-start.5 = (f32[256,256]{1,0:T(8,128)S(1)}, f32[256,256]{1,0:T(8,128)S(1)}, u32[]{:S(2)}, u32[]{:S(2)}) collective-permute-start(f32[256,256]{1,0:T(8,128)S(1)} %get-tuple-element.40), channel_id=1, source_target_pairs={{4,5},{5,4},{8,9},{9,8},{6,7},{7,6},{10,11},{11,10},{20,21},{21,20... | collective-permute-start | bytes 786440 | tf_op jit(solution)/shard_map/ppermute | solution.py:222
  40.8 0.7 collective-permute-start.6
  42.5 4.0 %collective-permute-start.10 = (f16[256,256]{1,0:T(8,128)(2,1)S(1)}, f16[256,256]{1,0:T(8,128)(2,1)S(1)}, u32[]{:S(2)}, u32[]{:S(2)}) collective-permute-start(f16[256,256]{1,0:T(8,128)(2,1)S(1)} %convert_element_type.70), channel_id=1, source_target_pairs={{4,5},{6,4},{10,10},{8,11},{20,21},{22,20},{26,26},{24,27}} | collective-permute-start | bytes 393224 | tf_op jit(solution)/shard_map/ppermute | solution.py:225
  43.2 3.4 %collective-permute-start.9 = (f16[256,256]{1,0:T(8,128)(2,1)S(1)}, f16[256,256]{1,0:T(8,128)(2,1)S(1)}, u32[]{:S(2)}, u32[]{:S(2)}) collective-permute-start(f16[256,256]{1,0:T(8,128)(2,1)S(1)} %convert_element_type.68), channel_id=1, source_target_pairs={{4,4},{6,5},{10,11},{8,10},{20,20},{22,21},{26,27},{24,26}} | collective-permute-start | bytes 393224 | tf_op jit(solution)/shard_map/ppermute | solution.py:225
  43.9 32.7 %collective-permute-start.8 = (f16[256,256]{1,0:T(8,128)(2,1)S(1)}, f16[256,256]{1,0:T(8,128)(2,1)S(1)}, u32[]{:S(2)}, u32[]{:S(2)}) collective-permute-start(f16[256,256]{1,0:T(8,128)(2,1)S(1)} %convert_element_type.66), channel_id=1, source_target_pairs={{4,1},{5,6},{6,0},{7,2},{10,14},{11,9},{8,15},{9,13},{20,17},{21,2... | collective-permute-start | bytes 393224 | tf_op jit(solution)/shard_map/ppermute | solution.py:225
  45.3 40.7 %copy-start.2 = (s32[4,2,2]{2,1,0:T(2,128)S(1)}, s32[4,2,2]{2,1,0:T(2,128)}, u32[]{:S(2)}) copy-start(s32[4,2,2]{2,1,0:T(2,128)} %constant.23.clone.places) | copy-start | bytes 196
  45.3 35.9 %collective-permute-start.7 = (f16[256,256]{1,0:T(8,128)(2,1)S(1)}, f16[256,256]{1,0:T(8,128)(2,1)S(1)}, u32[]{:S(2)}, u32[]{:S(2)}) collective-permute-start(f16[256,256]{1,0:T(8,128)(2,1)S(1)} %convert_element_type.64), channel_id=1, source_target_pairs={{4,0},{5,2},{6,1},{7,6},{10,15},{11,13},{8,14},{9,9},{20,16},{21,1... | collective-permute-start | bytes 393224 | tf_op jit(solution)/shard_map/ppermute | solution.py:225
  83.2 2.8 %collective-permute-start.13 = (f32[256,256]{1,0:T(8,128)S(1)}, f32[256,256]{1,0:T(8,128)S(1)}, u32[]{:S(2)}, u32[]{:S(2)}) collective-permute-start(f32[256,256]{1,0:T(8,128)S(1)} %get-tuple-element.52), channel_id=1, source_target_pairs={{4,5},{5,4},{8,9},{9,8},{6,7},{7,6},{10,11},{11,10},{20,21},{21,20... | collective-permute-start | bytes 786440 | tf_op jit(solution)/shard_map/ppermute | solution.py:222
  83.9 2.1 %collective-permute-start.14 = (f32[256,256]{1,0:T(8,128)S(1)}, f32[256,256]{1,0:T(8,128)S(1)}, u32[]{:S(2)}, u32[]{:S(2)}) collective-permute-start(f32[256,256]{1,0:T(8,128)S(1)} %get-tuple-element.53), channel_id=1, source_target_pairs={{4,5},{5,4},{8,9},{9,8},{6,7},{7,6},{10,11},{11,10},{20,21},{21,20... | collective-permute-start | bytes 786440 | tf_op jit(solution)/shard_map/ppermute | solution.py:222
  84.6 5.1 %collective-permute-start.12 = (f16[256,256]{1,0:T(8,128)(2,1)S(1)}, f16[256,256]{1,0:T(8,128)(2,1)S(1)}, u32[]{:S(2)}, u32[]{:S(2)}) collective-permute-start(f16[256,256]{1,0:T(8,128)(2,1)S(1)} %convert_element_type.74), channel_id=1, source_target_pairs={{5,10},{7,8},{11,5},{9,7},{21,26},{23,24},{27,21},{25,23}} | collective-permute-start | bytes 393224 | tf_op jit(solution)/shard_map/ppermute | solution.py:225
  85.3 6.3 %collective-permute-start.11 = (f16[256,256]{1,0:T(8,128)(2,1)S(1)}, f16[256,256]{1,0:T(8,128)(2,1)S(1)}, u32[]{:S(2)}, u32[]{:S(2)}) collective-permute-start(f16[256,256]{1,0:T(8,128)(2,1)S(1)} %convert_element_type.72), channel_id=1, source_target_pairs={{5,8},{7,10},{11,7},{9,5},{21,24},{23,26},{27,23},{25,21}} | collective-permute-start | bytes 393224 | tf_op jit(solution)/shard_map/ppermute | solution.py:225
  86.9 4.7 %collective-permute-start.18 = (f16[256,256]{1,0:T(8,128)(2,1)S(1)}, f16[256,256]{1,0:T(8,128)(2,1)S(1)}, u32[]{:S(2)}, u32[]{:S(2)}) collective-permute-start(f16[256,256]{1,0:T(8,128)(2,1)S(1)} %convert_element_type.82), channel_id=1, source_target_pairs={{4,7},{5,9},{6,3},{7,11},{10,8},{11,6},{8,12},{9,4},{20,23},{21,25... | collective-permute-start | bytes 393224 | tf_op jit(solution)/shard_map/ppermute | solution.py:225
  87.6 4.0 %collective-permute-start.17 = (f16[256,256]{1,0:T(8,128)(2,1)S(1)}, f16[256,256]{1,0:T(8,128)(2,1)S(1)}, u32[]{:S(2)}, u32[]{:S(2)}) collective-permute-start(f16[256,256]{1,0:T(8,128)(2,1)S(1)} %convert_element_type.80), channel_id=1, source_target_pairs={{4,3},{5,11},{6,7},{7,9},{10,12},{11,4},{8,8},{9,6},{20,19},{21,27... | collective-permute-start | bytes 393224 | tf_op jit(solution)/shard_map/ppermute | solution.py:225
  88.3 14.9 %collective-permute-start.16 = (f16[256,256]{1,0:T(8,128)(2,1)S(1)}, f16[256,256]{1,0:T(8,128)(2,1)S(1)}, u32[]{:S(2)}, u32[]{:S(2)}) collective-permute-start(f16[256,256]{1,0:T(8,128)(2,1)S(1)} %convert_element_type.78), channel_id=1, source_target_pairs={{4,13},{5,15},{6,12},{7,14},{10,2},{11,0},{8,3},{9,1},{20,29},{21,... | collective-permute-start | bytes 393224 | tf_op jit(solution)/shard_map/ppermute | solution.py:225
  89.7 15.8 %collective-permute-start.15 = (f16[256,256]{1,0:T(8,128)(2,1)S(1)}, f16[256,256]{1,0:T(8,128)(2,1)S(1)}, u32[]{:S(2)}, u32[]{:S(2)}) collective-permute-start(f16[256,256]{1,0:T(8,128)(2,1)S(1)} %convert_element_type.76), channel_id=1, source_target_pairs={{4,12},{5,14},{6,13},{7,15},{10,3},{11,1},{8,2},{9,0},{20,28},{21,... | collective-permute-start | bytes 393224 | tf_op jit(solution)/shard_map/ppermute | solution.py:225

commit v6 on v5

--- a/solution.py
+++ b/solution.py
@@ -54,11 +54,10 @@
     ((0, 0), (0, 1), (1, 1), (1, 0), (1, 1)),
     ((2, 2), (2, 0), (2, 1), (0, 2), (1, 2)),
 )
-SPARE = 2
 LATE_SUMS = (((3, 0), (3, 1)), ((3, 2), (3, 3)))
 LATE_HELD = (
-    ((3, 0), (3, 1), (0, 3), (1, 3), (1, 1)),
-    ((3, 2), (3, 3), (2, 3), (3, 3), (2, 1)),
+    ((3, 0), (3, 1), (0, 3), (1, 3)) + EARLY_SUMS[0],
+    ((3, 2), (3, 3), (2, 3), (3, 3)) + EARLY_SUMS[1],
 )
 EXTRA = 16
 HEAD = 64
@@ -132,7 +131,7 @@
     return lax.dot_general(left, right, (((1,), (1,)), ((), ())), preferred_element_type=jnp.float32)
 
 
-def early_kernel(bits, edge, near, other, head, centred, mean, own, *rest):
+def early_kernel(bits, other, edge, head, near, centred, mean, own, *rest):
     sends, both = rest[:-1], rest[-1]
     rows, part = near.shape
     step = 512
@@ -156,10 +155,7 @@
         send[...] = both[1 - bits[1], place]
 
 
-def late_kernel(bits, head, tail, mean, centred, *rest):
-    handed = (len(rest) - 5) // 2
-    own, *sends = rest[handed : handed + 3]
-    last, both = rest[-2:]
+def late_kernel(bits, head, tail, mean, centred, summed, own, send, summed_out, last, both):
     rows = last.shape[0]
     first = head[pl.ds(EXTRA, HEAD), :].astype(jnp.float32) - mean[...]
     last[pl.ds(0, HEAD), :] = first.astype(jnp.bfloat16)
@@ -169,21 +165,21 @@
         for place, (_, j) in enumerate(LATE_SUMS[core]):
             both[core, place] = block_product(last[...], last[...] if j == 3 else centred[j])
     own[...] = both[bits[1]]
-    for place, send in enumerate(sends):
-        send[...] = both[1 - bits[1], place]
-
-
-def combine_kernel(flips, scale, spares, bits, places, own, *rest):
-    held = rest[-1]
+    send[...] = both[1 - bits[1]]
+
+
+def combine_kernel(flips, scale, pieces, spares, bits, places, own, *rest):
+    others, spare = rest[:pieces], rest[pieces : pieces + spares]
+    outs, held = rest[pieces + spares : -1], rest[-1]
     count = own.shape[0]
     for i in range(count):
-        held[i] = (own[i] + rest[i][...]) * scale
-    rest = rest[count:]
+        other = others[0][i] if pieces == 1 else others[i][...]
+        held[i] = (own[i] + other) * scale
     for n, i in enumerate(flips):
         held[count + n] = held[i].T
     for i in range(spares):
-        held[count + len(flips) + i] = rest[i][...]
-    for r, out in enumerate(rest[spares:-1]):
+        held[count + len(flips) + i] = spare[i][...]
+    for r, out in enumerate(outs):
         out[...] = held[places[r, bits[1], bits[2]]]
 
 
@@ -194,7 +190,7 @@
 def combine(bits, own, others, flips, spares, held, places, samples):
     rows = own.shape[1]
     return pl.pallas_call(
-        functools.partial(combine_kernel, flips, 1.0 / samples, len(spares)),
+        functools.partial(combine_kernel, flips, 1.0 / samples, len(others), len(spares)),
         out_shape=[shape_of((rows, rows), jnp.float32)] * len(places),
         in_specs=[SMEM, SMEM] + [VMEM] * (1 + len(others) + len(spares)),
         out_specs=[VMEM] * len(places),
@@ -258,37 +254,33 @@
         scratch_shapes=[pltpu.VMEM((2,) + early_blocks, jnp.float32)],
         compiler_params=LIMIT,
         cost_estimate=BRIEF,
-    )(bits, from_edge, near, from_centre, from_head)
-    places = held_place(EARLY_HELD, NEAR_ROUNDS + FAR_ROUNDS) + [[[SPARE] * 2] * 2]
+    )(bits, from_centre, from_edge, from_head, near)
     others = [swap(other) for other in others]
-    *early, spare = combine(bits, own, others, (1, 2), (), EARLY_HELD, places, samples)
-    near_blocks, far_blocks = early[: len(NEAR_ROUNDS)], early[len(NEAR_ROUNDS) :]
+    places = held_place(EARLY_HELD, NEAR_ROUNDS) + [[[i] * 2] * 2 for i in range(3)]
+    early = combine(bits, own, others, (1, 2), (), EARLY_HELD, places, samples)
+    near_blocks, spares = early[: len(NEAR_ROUNDS)], early[len(NEAR_ROUNDS) :]
     arrived = [send(value, blocks) for value, blocks in zip(near_blocks, NEAR_ROUNDS)]
     summed = sum(block.astype(jnp.float32) for block in arrived)
 
-    late_blocks = (2, local_rows, local_rows)
-    handed = [summed] + far_blocks
-    own, *others, summed, first, second = pl.pallas_call(
+    late_blocks = shape_of((2, local_rows, local_rows), jnp.float32)
+    own, other, summed = pl.pallas_call(
         late_kernel,
-        out_shape=[shape_of(late_blocks, jnp.float32)]
-        + [block] * 2
-        + [shape_of(value.shape, value.dtype) for value in handed],
-        in_specs=[SMEM] + [VMEM] * 4 + [ANY] * len(handed),
-        out_specs=[VMEM] * 3 + [ANY] * len(handed),
+        out_shape=[late_blocks, late_blocks, shape_of(summed.shape, summed.dtype)],
+        in_specs=[SMEM] + [VMEM] * 4 + [ANY],
+        out_specs=[VMEM] * 2 + [ANY],
         scratch_shapes=[
             pltpu.VMEM((local_rows, part), jnp.bfloat16),
-            pltpu.VMEM((2,) + late_blocks, jnp.float32),
+            pltpu.VMEM((2,) + late_blocks.shape, jnp.float32),
         ],
-        input_output_aliases={5 + i: 3 + i for i in range(len(handed))},
-        compiler_params=LIMIT,
-        cost_estimate=BRIEF,
-    )(bits, from_head, from_tail, mean, centred, *handed)
-    others = [swap(other) for other in others]
-    arrived = [send(value, blocks) for value, blocks in zip((first, second), FAR_ROUNDS)]
-    places = held_place(LATE_HELD, LATE_ROUNDS)
-    late = combine(bits, own, others, (0, 1), (spare,), LATE_HELD, places, samples)
-    arrived += [send(value, blocks) for value, blocks in zip(late, LATE_ROUNDS)]
-    summed = summed + sum(block.astype(jnp.float32) for block in arrived)
+        input_output_aliases={5: 2},
+        compiler_params=LIMIT,
+        cost_estimate=BRIEF,
+    )(bits, from_head, from_tail, mean, centred, summed)
+    rounds = LATE_ROUNDS + FAR_ROUNDS
+    places = held_place(LATE_HELD, rounds)
+    late = combine(bits, own, [swap(other)], (0, 1), spares, LATE_HELD, places, samples)
+    arrived = [send(value, blocks) for value, blocks in zip(late, rounds)]
+    summed = summed + sum(block.astype(jnp.float32) for block in reversed(arrived))
     return add_shift(summed, 1, shift, local_rows)
 
 

time: 107 us -> 90.1 us (0.84)
  the two profiles are of different devices: /device:TPU:1 before, /device:TPU:9 now
where the time goes in v6:
time: 90.1 us; the launch traced here: 89.6 us
  starting transfers between devices  39.6 us (44%)
  waiting for transfers between devices  37.5 us (42%)
  Pallas kernels  8.67 us (10%)
  local copies, waits for them, and re-layouts  1.6 us (2%)
  other arithmetic  1.17 us (1%)
  between operations  1.01 us (1%)
    ppermute x1, waiting for transfers between devices, two_centres(): from_head = lax.ppermute(head, 'row', to_far)  28.6 us
    ppermute x10, starting transfers between devices, send(): lax.ppermute(value.astype(jnp.float16), everyone, round_pairs(blocks))  21.1 us
    ppermute x4, starting transfers between devices, swap(): return lax.ppermute(value, ('row', 'half'), centres)  11.5 us
    ppermute x10, waiting for transfers between devices, send(): lax.ppermute(value.astype(jnp.float16), everyone, round_pairs(blocks))  5.9 us
    pallas_call x1, Pallas kernels, two_centres(): pl.pallas_call(early_kernel, out_shape=[shape_of((3, local_rows, part), j...  3.73 us
    ppermute x1, starting transfers between devices, two_centres(): from_centre = lax.ppermute(far, 'row', to_centre)  3.2 us
    ppermute x4, waiting for transfers between devices, swap(): return lax.ppermute(value, ('row', 'half'), centres)  3 us
    pallas_call x2, Pallas kernels, combine(): pl.pallas_call(functools.partial(combine_kernel, flips, 1.0 / samples, le...  1.94 us
  transfers between devices with their start and end apart: 18, of which 7 were waited for; matrix products, arithmetic and copies ran while one was open for 0% of the time, Pallas kernels for 5%

profile of v6, /device:TPU:9, one launch (start us, length us, event | category | flops | bytes accessed | tf_op | source)
XLA Modules:
  0.0 89.6 jit_solution(6561342506211860690)
XLA Ops:
  0.1 1.6 %copy-done = bf16[256,4096]{1,0:T(8,128)(2,1)S(1)} copy-done((bf16[256,4096]{1,0:T(8,128)(2,1)S(1)}, bf16[256,4096]{1,0:T(8,128)(2,1)}, u32[]{:S(2)}) %copy-start) | copy-done | bytes 2097176
  2.8 3.2 %collective-permute-start.2 = (bf16[256,2048]{1,0:T(8,128)(2,1)S(1)}, bf16[256,2048]{1,0:T(8,128)(2,1)S(1)}, u32[]{:S(2)}, u32[]{:S(2)}) collective-permute-start(bf16[256,2048]{1,0:T(8,128)(2,1)S(1)} %get-tuple-element.33), channel_id=1, source_target_pairs={{4,8},{8,4},{5,9},{9,5},{6,10},{10,6},{7,11},{11,7},{20,24},{24,20... | collective-permute-start | bytes 3145736 | tf_op jit(solution)/shard_map/ppermute | solution.py:237
  6.0 1.3 %collective-permute-start.3 = (bf16[256,2048]{1,0:T(8,128)(2,1)S(1)}, bf16[256,2048]{1,0:T(8,128)(2,1)S(1)}, u32[]{:S(2)}, u32[]{:S(2)}) collective-permute-start(bf16[256,2048]{1,0:T(8,128)(2,1)S(1)} %get-tuple-element.34.near), channel_id=1, source_target_pairs={{0,4},{12,8},{1,5},{13,9},{2,6},{14,10},{3,7},{15,11},{16,20},{28,... | collective-permute-start | bytes 3145736 | tf_op jit(solution)/shard_map/ppermute | solution.py:238
  7.3 1.3 %collective-permute-start = (bf16[80,2048]{1,0:T(8,128)(2,1)S(1)}, bf16[80,2048]{1,0:T(8,128)(2,1)S(1)}, u32[]{:S(2)}, u32[]{:S(2)}) collective-permute-start(bf16[80,2048]{1,0:T(8,128)(2,1)S(1)} %get-tuple-element.31), channel_id=1, source_target_pairs={{0,8},{12,4},{1,9},{13,5},{2,10},{14,6},{3,11},{15,7},{16,24},{28,... | collective-permute-start | bytes 983048 | tf_op jit(solution)/shard_map/ppermute | solution.py:239
  8.6 1.3 %collective-permute-start.1 = (bf16[192,2048]{1,0:T(8,128)(2,1)S(1)}, bf16[192,2048]{1,0:T(8,128)(2,1)S(1)}, u32[]{:S(2)}, u32[]{:S(2)}) collective-permute-start(bf16[192,2048]{1,0:T(8,128)(2,1)S(1)} %get-tuple-element.32), channel_id=1, source_target_pairs={{0,8},{12,4},{1,9},{13,5},{2,10},{14,6},{3,11},{15,7},{16,24},{28,... | collective-permute-start | bytes 2359304 | tf_op jit(solution)/shard_map/ppermute | solution.py:240
  9.9 28.6 %collective-permute-done.head = bf16[80,2048]{1,0:T(8,128)(2,1)S(1)} collective-permute-done((bf16[80,2048]{1,0:T(8,128)(2,1)S(1)}, bf16[80,2048]{1,0:T(8,128)(2,1)S(1)}, u32[]{:S(2)}, u32[]{:S(2)}) %collective-permute-start) | collective-permute-done | bytes 327712 | tf_op jit(solution)/shard_map/ppermute | solution.py:239
  38.5 3.7 %shard_map.47 = (bf16[3,256,2048]{2,1,0:T(8,128)(2,1)S(1)}, f32[1,2048]{1,0:T(1,128)S(1)}, f32[3,256,256]{2,1,0:T(8,128)S(1)}, f32[256,256]{1,0:T(8,128)S(1)}, f...) custom-call(s32[3]{0:T(128)S(1)} %pad_add_fusion.bits, bf16[256,2048]{1,0:T(8,128)(2,1)S(1)} %collective-permute-done.2.other, ...), custom_call_target="tpu_custom_call" | custom-call | flops 1024 | bytes 1024 | tf_op jit(solution)/shard_map/pallas_call | solution.py:244
  42.2 5.2 %collective-permute-start.4 = (f32[256,256]{1,0:T(8,128)S(1)}, f32[256,256]{1,0:T(8,128)S(1)}, u32[]{:S(2)}, u32[]{:S(2)}) collective-permute-start(f32[256,256]{1,0:T(8,128)S(1)} %get-tuple-element.38), channel_id=1, source_target_pairs={{4,5},{5,4},{8,9},{9,8},{6,7},{7,6},{10,11},{11,10},{20,21},{21,20... | collective-permute-start | bytes 786440 | tf_op jit(solution)/shard_map/ppermute | solution.py:218
  47.5 1.9 %collective-permute-start.5 = (f32[256,256]{1,0:T(8,128)S(1)}, f32[256,256]{1,0:T(8,128)S(1)}, u32[]{:S(2)}, u32[]{:S(2)}) collective-permute-start(f32[256,256]{1,0:T(8,128)S(1)} %get-tuple-element.39), channel_id=1, source_target_pairs={{4,5},{5,4},{8,9},{9,8},{6,7},{7,6},{10,11},{11,10},{20,21},{21,20... | collective-permute-start | bytes 786440 | tf_op jit(solution)/shard_map/ppermute | solution.py:218
  49.4 2.4 %collective-permute-start.6 = (f32[256,256]{1,0:T(8,128)S(1)}, f32[256,256]{1,0:T(8,128)S(1)}, u32[]{:S(2)}, u32[]{:S(2)}) collective-permute-start(f32[256,256]{1,0:T(8,128)S(1)} %get-tuple-element.40), channel_id=1, source_target_pairs={{4,5},{5,4},{8,9},{9,8},{6,7},{7,6},{10,11},{11,10},{20,21},{21,20... | collective-permute-start | bytes 786440 | tf_op jit(solution)/shard_map/ppermute | solution.py:218
  54.0 1.3 %collective-permute-start.10 = (f16[256,256]{1,0:T(8,128)(2,1)S(1)}, f16[256,256]{1,0:T(8,128)(2,1)S(1)}, u32[]{:S(2)}, u32[]{:S(2)}) collective-permute-start(f16[256,256]{1,0:T(8,128)(2,1)S(1)} %convert_element_type.70), channel_id=1, source_target_pairs={{4,5},{6,4},{10,10},{8,11},{20,21},{22,20},{26,26},{24,27}} | collective-permute-start | bytes 393224 | tf_op jit(solution)/shard_map/ppermute | solution.py:221
  56.6 4.5 %collective-permute-start.8 = (f16[256,256]{1,0:T(8,128)(2,1)S(1)}, f16[256,256]{1,0:T(8,128)(2,1)S(1)}, u32[]{:S(2)}, u32[]{:S(2)}) collective-permute-start(f16[256,256]{1,0:T(8,128)(2,1)S(1)} %convert_element_type.66), channel_id=1, source_target_pairs={{4,1},{5,6},{6,0},{7,2},{10,14},{11,9},{8,15},{9,13},{20,17},{21,2... | collective-permute-start | bytes 393224 | tf_op jit(solution)/shard_map/ppermute | solution.py:221
  61.2 1.3 %collective-permute-start.7 = (f16[256,256]{1,0:T(8,128)(2,1)S(1)}, f16[256,256]{1,0:T(8,128)(2,1)S(1)}, u32[]{:S(2)}, u32[]{:S(2)}) collective-permute-start(f16[256,256]{1,0:T(8,128)(2,1)S(1)} %convert_element_type.64), channel_id=1, source_target_pairs={{4,0},{5,2},{6,1},{7,6},{10,15},{11,13},{8,14},{9,9},{20,16},{21,1... | collective-permute-start | bytes 393224 | tf_op jit(solution)/shard_map/ppermute | solution.py:221
  63.1 1.3 %collective-permute-done.7 = f16[256,256]{1,0:T(8,128)(2,1)S(1)} collective-permute-done((f16[256,256]{1,0:T(8,128)(2,1)S(1)}, f16[256,256]{1,0:T(8,128)(2,1)S(1)}, u32[]{:S(2)}, u32[]{:S(2)}) %collective-permute-start.7) | collective-permute-done | bytes 131104 | tf_op jit(solution)/shard_map/ppermute | solution.py:221
  64.5 1.9 %shard_map.49 = (f32[2,256,256]{2,1,0:T(8,128)S(1)}, f32[2,256,256]{2,1,0:T(8,128)S(1)}, f32[256,256]{1,0:T(8,128)S(1)}) custom-call(s32[3]{0:T(128)S(1)} %pad_add_fusion.bits, bf16[80,2048]{1,0:T(8,128)(2,1)S(1)} %collective-permute-done.head, bf16[192,2048]{1,0:T(8,128)(2,1)S(1)} %collective-permute-done.1.tail, ...), custom_call_target="tpu_custom_call", output_to_operand_aliasing={{2}: (5, {})} | custom-call | flops 1024 | bytes 1024 | tf_op jit(solution)/shard_map/pallas_call | solution.py:266
  66.5 1.9 %collective-permute-start.11 = (f32[2,256,256]{2,1,0:T(8,128)S(1)}, f32[2,256,256]{2,1,0:T(8,128)S(1)}, u32[]{:S(2)}, u32[]{:S(2)}) collective-permute-start(f32[2,256,256]{2,1,0:T(8,128)S(1)} %get-tuple-element.47), channel_id=1, source_target_pairs={{4,5},{5,4},{8,9},{9,8},{6,7},{7,6},{10,11},{11,10},{20,21},{21,20... | collective-permute-start | bytes 1572872 | tf_op jit(solution)/shard_map/ppermute | solution.py:218
  68.4 1.9 %collective-permute-done.11.rest_0_ = f32[2,256,256]{2,1,0:T(8,128)S(1)} collective-permute-done((f32[2,256,256]{2,1,0:T(8,128)S(1)}, f32[2,256,256]{2,1,0:T(8,128)S(1)}, u32[]{:S(2)}, u32[]{:S(2)}) %collective-permute-start.11) | collective-permute-done | bytes 524320 | tf_op jit(solution)/shard_map/ppermute | solution.py:218
  71.3 2.4 %collective-permute-start.17 = (f16[256,256]{1,0:T(8,128)(2,1)S(1)}, f16[256,256]{1,0:T(8,128)(2,1)S(1)}, u32[]{:S(2)}, u32[]{:S(2)}) collective-permute-start(f16[256,256]{1,0:T(8,128)(2,1)S(1)} %convert_element_type.82), channel_id=1, source_target_pairs={{4,12},{5,14},{6,13},{7,15},{10,3},{11,1},{8,2},{9,0},{20,28},{21,... | collective-permute-start | bytes 393224 | tf_op jit(solution)/shard_map/ppermute | solution.py:221
  73.7 1.3 %collective-permute-start.16 = (f16[256,256]{1,0:T(8,128)(2,1)S(1)}, f16[256,256]{1,0:T(8,128)(2,1)S(1)}, u32[]{:S(2)}, u32[]{:S(2)}) collective-permute-start(f16[256,256]{1,0:T(8,128)(2,1)S(1)} %convert_element_type.80), channel_id=1, source_target_pairs={{4,13},{5,15},{6,12},{7,14},{10,2},{11,0},{8,3},{9,1},{20,29},{21,... | collective-permute-start | bytes 393224 | tf_op jit(solution)/shard_map/ppermute | solution.py:221
  75.0 2.9 %collective-permute-start.15 = (f16[256,256]{1,0:T(8,128)(2,1)S(1)}, f16[256,256]{1,0:T(8,128)(2,1)S(1)}, u32[]{:S(2)}, u32[]{:S(2)}) collective-permute-start(f16[256,256]{1,0:T(8,128)(2,1)S(1)} %convert_element_type.78), channel_id=1, source_target_pairs={{4,3},{5,11},{6,7},{7,9},{10,12},{11,4},{8,8},{9,6},{20,19},{21,27... | collective-permute-start | bytes 393224 | tf_op jit(solution)/shard_map/ppermute | solution.py:221
  78.0 2.2 %collective-permute-start.14 = (f16[256,256]{1,0:T(8,128)(2,1)S(1)}, f16[256,256]{1,0:T(8,128)(2,1)S(1)}, u32[]{:S(2)}, u32[]{:S(2)}) collective-permute-start(f16[256,256]{1,0:T(8,128)(2,1)S(1)} %convert_element_type.76), channel_id=1, source_target_pairs={{4,7},{5,9},{6,3},{7,11},{10,8},{11,6},{8,12},{9,4},{20,23},{21,25... | collective-permute-start | bytes 393224 | tf_op jit(solution)/shard_map/ppermute | solution.py:221
  80.2 1.9 %collective-permute-start.13 = (f16[256,256]{1,0:T(8,128)(2,1)S(1)}, f16[256,256]{1,0:T(8,128)(2,1)S(1)}, u32[]{:S(2)}, u32[]{:S(2)}) collective-permute-start(f16[256,256]{1,0:T(8,128)(2,1)S(1)} %convert_element_type.74), channel_id=1, source_target_pairs={{5,8},{7,10},{11,7},{9,5},{21,24},{23,26},{27,23},{25,21}} | collective-permute-start | bytes 393224 | tf_op jit(solution)/shard_map/ppermute | solution.py:221
  82.2 1.9 %collective-permute-start.12 = (f16[256,256]{1,0:T(8,128)(2,1)S(1)}, f16[256,256]{1,0:T(8,128)(2,1)S(1)}, u32[]{:S(2)}, u32[]{:S(2)}) collective-permute-start(f16[256,256]{1,0:T(8,128)(2,1)S(1)} %convert_element_type.72), channel_id=1, source_target_pairs={{5,10},{7,8},{11,5},{9,7},{21,26},{23,24},{27,21},{25,23}} | collective-permute-start | bytes 393224 | tf_op jit(solution)/shard_map/ppermute | solution.py:221
  85.9 2.9 %collective-permute-done.12 = f16[256,256]{1,0:T(8,128)(2,1)S(1)} collective-permute-done((f16[256,256]{1,0:T(8,128)(2,1)S(1)}, f16[256,256]{1,0:T(8,128)(2,1)S(1)}, u32[]{:S(2)}, u32[]{:S(2)}) %collective-permute-start.12) | collective-permute-done | bytes 131104 | tf_op jit(solution)/shard_map/ppermute | solution.py:221
  (37 shorter events, 8.3 us)
Async XLA Ops:
  0.0 53.0 %copy-start.1 = (s32[7,2,2]{2,1,0:T(2,128)S(1)}, s32[7,2,2]{2,1,0:T(2,128)}, u32[]{:S(2)}) copy-start(s32[7,2,2]{2,1,0:T(2,128)} %constant.22.clone.places) | copy-start | bytes 340
  0.1 1.6 %copy-start = (bf16[256,4096]{1,0:T(8,128)(2,1)S(1)}, bf16[256,4096]{1,0:T(8,128)(2,1)}, u32[]{:S(2)}) copy-start(bf16[256,4096]{1,0:T(8,128)(2,1)} %values.1) | copy-start | bytes 6291460
  2.8 35.7 %collective-permute-start.2 = (bf16[256,2048]{1,0:T(8,128)(2,1)S(1)}, bf16[256,2048]{1,0:T(8,128)(2,1)S(1)}, u32[]{:S(2)}, u32[]{:S(2)}) collective-permute-start(bf16[256,2048]{1,0:T(8,128)(2,1)S(1)} %get-tuple-element.33), channel_id=1, source_target_pairs={{4,8},{8,4},{5,9},{9,5},{6,10},{10,6},{7,11},{11,7},{20,24},{24,20... | collective-permute-start | bytes 3145736 | tf_op jit(solution)/shard_map/ppermute | solution.py:237
  6.0 32.5 %collective-permute-start.3 = (bf16[256,2048]{1,0:T(8,128)(2,1)S(1)}, bf16[256,2048]{1,0:T(8,128)(2,1)S(1)}, u32[]{:S(2)}, u32[]{:S(2)}) collective-permute-start(bf16[256,2048]{1,0:T(8,128)(2,1)S(1)} %get-tuple-element.34.near), channel_id=1, source_target_pairs={{0,4},{12,8},{1,5},{13,9},{2,6},{14,10},{3,7},{15,11},{16,20},{28,... | collective-permute-start | bytes 3145736 | tf_op jit(solution)/shard_map/ppermute | solution.py:238
  7.3 31.2 %collective-permute-start = (bf16[80,2048]{1,0:T(8,128)(2,1)S(1)}, bf16[80,2048]{1,0:T(8,128)(2,1)S(1)}, u32[]{:S(2)}, u32[]{:S(2)}) collective-permute-start(bf16[80,2048]{1,0:T(8,128)(2,1)S(1)} %get-tuple-element.31), channel_id=1, source_target_pairs={{0,8},{12,4},{1,9},{13,5},{2,10},{14,6},{3,11},{15,7},{16,24},{28,... | collective-permute-start | bytes 983048 | tf_op jit(solution)/shard_map/ppermute | solution.py:239
  8.6 56.0 %collective-permute-start.1 = (bf16[192,2048]{1,0:T(8,128)(2,1)S(1)}, bf16[192,2048]{1,0:T(8,128)(2,1)S(1)}, u32[]{:S(2)}, u32[]{:S(2)}) collective-permute-start(bf16[192,2048]{1,0:T(8,128)(2,1)S(1)} %get-tuple-element.32), channel_id=1, source_target_pairs={{0,8},{12,4},{1,9},{13,5},{2,10},{14,6},{3,11},{15,7},{16,24},{28,... | collective-permute-start | bytes 2359304 | tf_op jit(solution)/shard_map/ppermute | solution.py:240
  42.2 9.6 %collective-permute-start.4 = (f32[256,256]{1,0:T(8,128)S(1)}, f32[256,256]{1,0:T(8,128)S(1)}, u32[]{:S(2)}, u32[]{:S(2)}) collective-permute-start(f32[256,256]{1,0:T(8,128)S(1)} %get-tuple-element.38), channel_id=1, source_target_pairs={{4,5},{5,4},{8,9},{9,8},{6,7},{7,6},{10,11},{11,10},{20,21},{21,20... | collective-permute-start | bytes 786440 | tf_op jit(solution)/shard_map/ppermute | solution.py:218
  47.5 4.4 %collective-permute-start.5 = (f32[256,256]{1,0:T(8,128)S(1)}, f32[256,256]{1,0:T(8,128)S(1)}, u32[]{:S(2)}, u32[]{:S(2)}) collective-permute-start(f32[256,256]{1,0:T(8,128)S(1)} %get-tuple-element.39), channel_id=1, source_target_pairs={{4,5},{5,4},{8,9},{9,8},{6,7},{7,6},{10,11},{11,10},{20,21},{21,20... | collective-permute-start | bytes 786440 | tf_op jit(solution)/shard_map/ppermute | solution.py:218
  49.4 3.6 %collective-permute-start.6 = (f32[256,256]{1,0:T(8,128)S(1)}, f32[256,256]{1,0:T(8,128)S(1)}, u32[]{:S(2)}, u32[]{:S(2)}) collective-permute-start(f32[256,256]{1,0:T(8,128)S(1)} %get-tuple-element.40), channel_id=1, source_target_pairs={{4,5},{5,4},{8,9},{9,8},{6,7},{7,6},{10,11},{11,10},{20,21},{21,20... | collective-permute-start | bytes 786440 | tf_op jit(solution)/shard_map/ppermute | solution.py:218
  54.0 8.5 %collective-permute-start.10 = (f16[256,256]{1,0:T(8,128)(2,1)S(1)}, f16[256,256]{1,0:T(8,128)(2,1)S(1)}, u32[]{:S(2)}, u32[]{:S(2)}) collective-permute-start(f16[256,256]{1,0:T(8,128)(2,1)S(1)} %convert_element_type.70), channel_id=1, source_target_pairs={{4,5},{6,4},{10,10},{8,11},{20,21},{22,20},{26,26},{24,27}} | collective-permute-start | bytes 393224 | tf_op jit(solution)/shard_map/ppermute | solution.py:221
  55.3 14.9 %copy-start.2 = (s32[6,2,2]{2,1,0:T(2,128)S(1)}, s32[6,2,2]{2,1,0:T(2,128)}, u32[]{:S(2)}) copy-start(s32[6,2,2]{2,1,0:T(2,128)} %constant.23.clone.places) | copy-start | bytes 292
  55.3 7.2 %collective-permute-start.9 = (f16[256,256]{1,0:T(8,128)(2,1)S(1)}, f16[256,256]{1,0:T(8,128)(2,1)S(1)}, u32[]{:S(2)}, u32[]{:S(2)}) collective-permute-start(f16[256,256]{1,0:T(8,128)(2,1)S(1)} %convert_element_type.68), channel_id=1, source_target_pairs={{4,4},{6,5},{10,11},{8,10},{20,20},{22,21},{26,27},{24,26}} | collective-permute-start | bytes 393224 | tf_op jit(solution)/shard_map/ppermute | solution.py:221
  56.6 6.5 %collective-permute-start.8 = (f16[256,256]{1,0:T(8,128)(2,1)S(1)}, f16[256,256]{1,0:T(8,128)(2,1)S(1)}, u32[]{:S(2)}, u32[]{:S(2)}) collective-permute-start(f16[256,256]{1,0:T(8,128)(2,1)S(1)} %convert_element_type.66), channel_id=1, source_target_pairs={{4,1},{5,6},{6,0},{7,2},{10,14},{11,9},{8,15},{9,13},{20,17},{21,2... | collective-permute-start | bytes 393224 | tf_op jit(solution)/shard_map/ppermute | solution.py:221
  61.2 3.2 %collective-permute-start.7 = (f16[256,256]{1,0:T(8,128)(2,1)S(1)}, f16[256,256]{1,0:T(8,128)(2,1)S(1)}, u32[]{:S(2)}, u32[]{:S(2)}) collective-permute-start(f16[256,256]{1,0:T(8,128)(2,1)S(1)} %convert_element_type.64), channel_id=1, source_target_pairs={{4,0},{5,2},{6,1},{7,6},{10,15},{11,13},{8,14},{9,9},{20,16},{21,1... | collective-permute-start | bytes 393224 | tf_op jit(solution)/shard_map/ppermute | solution.py:221
  66.5 3.8 %collective-permute-start.11 = (f32[2,256,256]{2,1,0:T(8,128)S(1)}, f32[2,256,256]{2,1,0:T(8,128)S(1)}, u32[]{:S(2)}, u32[]{:S(2)}) collective-permute-start(f32[2,256,256]{2,1,0:T(8,128)S(1)} %get-tuple-element.47), channel_id=1, source_target_pairs={{4,5},{5,4},{8,9},{9,8},{6,7},{7,6},{10,11},{11,10},{20,21},{21,20... | collective-permute-start | bytes 1572872 | tf_op jit(solution)/shard_map/ppermute | solution.py:218
  71.3 10.9 %collective-permute-start.17 = (f16[256,256]{1,0:T(8,128)(2,1)S(1)}, f16[256,256]{1,0:T(8,128)(2,1)S(1)}, u32[]{:S(2)}, u32[]{:S(2)}) collective-permute-start(f16[256,256]{1,0:T(8,128)(2,1)S(1)} %convert_element_type.82), channel_id=1, source_target_pairs={{4,12},{5,14},{6,13},{7,15},{10,3},{11,1},{8,2},{9,0},{20,28},{21,... | collective-permute-start | bytes 393224 | tf_op jit(solution)/shard_map/ppermute | solution.py:221
  73.7 11.0 %collective-permute-start.16 = (f16[256,256]{1,0:T(8,128)(2,1)S(1)}, f16[256,256]{1,0:T(8,128)(2,1)S(1)}, u32[]{:S(2)}, u32[]{:S(2)}) collective-permute-start(f16[256,256]{1,0:T(8,128)(2,1)S(1)} %convert_element_type.80), channel_id=1, source_target_pairs={{4,13},{5,15},{6,12},{7,14},{10,2},{11,0},{8,3},{9,1},{20,29},{21,... | collective-permute-start | bytes 393224 | tf_op jit(solution)/shard_map/ppermute | solution.py:221
  75.0 9.7 %collective-permute-start.15 = (f16[256,256]{1,0:T(8,128)(2,1)S(1)}, f16[256,256]{1,0:T(8,128)(2,1)S(1)}, u32[]{:S(2)}, u32[]{:S(2)}) collective-permute-start(f16[256,256]{1,0:T(8,128)(2,1)S(1)} %convert_element_type.78), channel_id=1, source_target_pairs={{4,3},{5,11},{6,7},{7,9},{10,12},{11,4},{8,8},{9,6},{20,19},{21,27... | collective-permute-start | bytes 393224 | tf_op jit(solution)/shard_map/ppermute | solution.py:221
  78.0 6.8 %collective-permute-start.14 = (f16[256,256]{1,0:T(8,128)(2,1)S(1)}, f16[256,256]{1,0:T(8,128)(2,1)S(1)}, u32[]{:S(2)}, u32[]{:S(2)}) collective-permute-start(f16[256,256]{1,0:T(8,128)(2,1)S(1)} %convert_element_type.76), channel_id=1, source_target_pairs={{4,7},{5,9},{6,3},{7,11},{10,8},{11,6},{8,12},{9,4},{20,23},{21,25... | collective-permute-start | bytes 393224 | tf_op jit(solution)/shard_map/ppermute | solution.py:221
  80.2 5.7 %collective-permute-start.13 = (f16[256,256]{1,0:T(8,128)(2,1)S(1)}, f16[256,256]{1,0:T(8,128)(2,1)S(1)}, u32[]{:S(2)}, u32[]{:S(2)}) collective-permute-start(f16[256,256]{1,0:T(8,128)(2,1)S(1)} %convert_element_type.74), channel_id=1, source_target_pairs={{5,8},{7,10},{11,7},{9,5},{21,24},{23,26},{27,23},{25,21}} | collective-permute-start | bytes 393224 | tf_op jit(solution)/shard_map/ppermute | solution.py:221
  82.2 6.6 %collective-permute-start.12 = (f16[256,256]{1,0:T(8,128)(2,1)S(1)}, f16[256,256]{1,0:T(8,128)(2,1)S(1)}, u32[]{:S(2)}, u32[]{:S(2)}) collective-permute-start(f16[256,256]{1,0:T(8,128)(2,1)S(1)} %convert_element_type.72), channel_id=1, source_target_pairs={{5,10},{7,8},{11,5},{9,7},{21,26},{23,24},{27,21},{25,23}} | collective-permute-start | bytes 393224 | tf_op jit(solution)/shard_map/ppermute | solution.py:221

commit v7 on v6

--- a/solution.py
+++ b/solution.py
@@ -33,15 +33,11 @@
     return add_shift(summed, samples, shift, local_rows)
 
 
-NEAR_ROUNDS = (
-    (((0, 0), (0, 1)), ((0, 2), (1, 2))),
-    (((0, 1), (0, 0)), ((1, 2), (0, 2))),
-    (((1, 0), (1, 1)), (None, None)),
-    (((1, 1), (1, 0)), (None, None)),
-)
-FAR_ROUNDS = (
-    ((None, None), ((2, 0), (2, 2))),
-    ((None, None), ((2, 2), (2, 0))),
+EARLY_ROUNDS = (
+    (((0, 0), (0, 1)), ((2, 2), (2, 0))),
+    (((0, 1), (0, 0)), ((2, 0), (2, 2))),
+    (((1, 0), (1, 1)), ((0, 2), (1, 2))),
+    (((1, 1), (1, 0)), ((1, 2), (0, 2))),
 )
 LATE_ROUNDS = (
     (((3, 0), (3, 1)), ((3, 2), (3, 3))),
@@ -54,17 +50,17 @@
     ((0, 0), (0, 1), (1, 1), (1, 0), (1, 1)),
     ((2, 2), (2, 0), (2, 1), (0, 2), (1, 2)),
 )
+SPARE = 2
 LATE_SUMS = (((3, 0), (3, 1)), ((3, 2), (3, 3)))
 LATE_HELD = (
-    ((3, 0), (3, 1), (0, 3), (1, 3)) + EARLY_SUMS[0],
-    ((3, 2), (3, 3), (2, 3), (3, 3)) + EARLY_SUMS[1],
+    ((3, 0), (3, 1), (0, 3), (1, 3), (1, 1)),
+    ((3, 2), (3, 3), (2, 3), (3, 3), (2, 1)),
 )
 EXTRA = 16
-HEAD = 64
+HEAD = 32
 VMEM = pl.BlockSpec(memory_space=pltpu.VMEM)
 SMEM = pl.BlockSpec(memory_space=pltpu.SMEM)
 ANY = pl.BlockSpec(memory_space=pl.ANY)
-HBM = pl.BlockSpec(memory_space=pltpu.HBM)
 LIMIT = pltpu.CompilerParams(vmem_limit_bytes=40 * 2**20)
 BRIEF = pl.CostEstimate(flops=1024, bytes_accessed=1024, transcendentals=0)
 
@@ -94,23 +90,34 @@
     ]
 
 
-def split_kernel(bits, values, near, far, head, tail, sums, sems):
+def tail_places(rows):
+    return HEAD, HEAD + (rows - HEAD) // 2
+
+
+def far_kernel(bits, values, far, sem):
+    part = far.shape[1]
+    columns = pl.ds(pl.multiple_of(bits[0] * part, 128), part)
+    copy = pltpu.make_async_copy(values.at[:, columns], far, sem)
+    copy.start()
+    copy.wait()
+
+
+def near_kernel(bits, values, far, near, head, *rest):
+    tails, (sums, sems) = rest[:-2], rest[-2:]
     rows, part = far.shape
     step = 512
     near_columns = pl.ds(pl.multiple_of((1 - bits[0]) * part, 128), part)
-    far_columns = pl.ds(pl.multiple_of(bits[0] * part, 128), part)
-    first, rest = pl.ds(0, HEAD), pl.ds(HEAD, rows - HEAD)
     copies = [
-        pltpu.make_async_copy(values.at[:, far_columns], far, sems.at[0]),
-        pltpu.make_async_copy(values.at[:, near_columns], near, sems.at[1]),
+        pltpu.make_async_copy(values.at[:, near_columns], near, sems.at[0]),
         pltpu.make_async_copy(
-            values.at[first, far_columns], head.at[pl.ds(EXTRA, HEAD), :], sems.at[2]
+            far.at[pl.ds(0, HEAD), :], head.at[pl.ds(EXTRA, HEAD), :], sems.at[1]
         ),
-        pltpu.make_async_copy(values.at[rest, far_columns], tail, sems.at[3]),
     ]
+    for i, (first, tail) in enumerate(zip(tail_places(rows), tails)):
+        from_rows = far.at[pl.ds(first, tail.shape[0]), :]
+        copies.append(pltpu.make_async_copy(from_rows, tail, sems.at[2 + i]))
     for copy in copies:
         copy.start()
-    copies[0].wait()
 
     @pl.loop(0, part // step)
     def _(j):
@@ -123,7 +130,7 @@
         sums[pl.ds(3, EXTRA - 3), columns] = jnp.zeros((EXTRA - 3, step), jnp.float32)
 
     head[pl.ds(0, EXTRA), :] = sums[...].astype(jnp.bfloat16)
-    for copy in copies[1:]:
+    for copy in copies:
         copy.wait()
 
 
@@ -131,7 +138,17 @@
     return lax.dot_general(left, right, (((1,), (1,)), ((), ())), preferred_element_type=jnp.float32)
 
 
-def early_kernel(bits, other, edge, head, near, centred, mean, own, *rest):
+def sum_kernel(other, near, partial):
+    step = 512
+
+    @pl.loop(0, near.shape[1] // step)
+    def _(n):
+        columns = pl.ds(pl.multiple_of(n * step, step), step)
+        rows = other[:, columns].astype(jnp.float32) + near[:, columns].astype(jnp.float32)
+        partial[:, columns] = jnp.sum(rows, axis=0, keepdims=True)
+
+
+def early_kernel(bits, other, edge, head, near, partial, centred, mean, own, *rest):
     sends, both = rest[:-1], rest[-1]
     rows, part = near.shape
     step = 512
@@ -140,8 +157,9 @@
     def _(n):
         columns = pl.ds(pl.multiple_of(n * step, step), step)
         values = [block[:, columns].astype(jnp.float32) for block in (edge, near, other)]
-        total = jnp.sum(head[pl.ds(0, EXTRA), columns].astype(jnp.float32), axis=0, keepdims=True)
-        total = total + jnp.sum(values[0] + values[1] + values[2], axis=0, keepdims=True)
+        pieces = head[pl.ds(0, EXTRA), columns].astype(jnp.float32)
+        total = partial[:, columns] + jnp.sum(pieces, axis=0, keepdims=True)
+        total = total + jnp.sum(values[0], axis=0, keepdims=True)
         average = total * (1.0 / (4 * rows))
         mean[:, columns] = average
         for i in range(3):
@@ -152,15 +170,17 @@
             both[core, place] = block_product(centred[i], centred[j])
     own[...] = both[bits[1]]
     for place, send in enumerate(sends):
-        send[...] = both[1 - bits[1], place]
-
-
-def late_kernel(bits, head, tail, mean, centred, summed, own, send, summed_out, last, both):
+        first = place * send.shape[1]
+        send[...] = both[1 - bits[1], :, pl.ds(first, send.shape[1]), :]
+
+
+def late_kernel(bits, head, tail, end, mean, centred, spare, own, send, handed, last, both):
     rows = last.shape[0]
     first = head[pl.ds(EXTRA, HEAD), :].astype(jnp.float32) - mean[...]
     last[pl.ds(0, HEAD), :] = first.astype(jnp.bfloat16)
-    second = tail[...].astype(jnp.float32) - mean[...]
-    last[pl.ds(HEAD, rows - HEAD), :] = second.astype(jnp.bfloat16)
+    for place, block in zip(tail_places(rows), (tail, end)):
+        values = block[...].astype(jnp.float32) - mean[...]
+        last[pl.ds(place, block.shape[0]), :] = values.astype(jnp.bfloat16)
     for core in (0, 1):
         for place, (_, j) in enumerate(LATE_SUMS[core]):
             both[core, place] = block_product(last[...], last[...] if j == 3 else centred[j])
@@ -173,7 +193,7 @@
     outs, held = rest[pieces + spares : -1], rest[-1]
     count = own.shape[0]
     for i in range(count):
-        other = others[0][i] if pieces == 1 else others[i][...]
+        other = jnp.concatenate([piece[i] for piece in others], axis=0)
         held[i] = (own[i] + other) * scale
     for n, i in enumerate(flips):
         held[count + n] = held[i].T
@@ -220,26 +240,40 @@
     def send(value, blocks):
         return lax.ppermute(value.astype(jnp.float16), everyone, round_pairs(blocks))
 
-    near, far, head, tail = pl.pallas_call(
-        split_kernel,
+    far = pl.pallas_call(
+        far_kernel,
+        out_shape=shape_of((local_rows, part), jnp.bfloat16),
+        in_specs=[SMEM, ANY],
+        out_specs=VMEM,
+        scratch_shapes=[pltpu.SemaphoreType.DMA],
+        compiler_params=LIMIT,
+        cost_estimate=BRIEF,
+    )(bits, log_derivs)
+    near, head, *tails = pl.pallas_call(
+        near_kernel,
         out_shape=[
             shape_of((local_rows, part), jnp.bfloat16),
-            shape_of((local_rows, part), jnp.bfloat16),
             shape_of((EXTRA + HEAD, part), jnp.bfloat16),
-            shape_of((local_rows - HEAD, part), jnp.bfloat16),
-        ],
-        in_specs=[SMEM, HBM],
+        ]
+        + [shape_of(((local_rows - HEAD) // 2, part), jnp.bfloat16)] * 2,
+        in_specs=[SMEM, ANY, VMEM],
         out_specs=[VMEM] * 4,
         scratch_shapes=[pltpu.VMEM((EXTRA, part), jnp.float32), pltpu.SemaphoreType.DMA((4,))],
         compiler_params=LIMIT,
         cost_estimate=BRIEF,
-    )(bits, log_derivs)
+    )(bits, log_derivs, far)
     from_centre = lax.ppermute(far, "row", to_centre)
     from_edge = lax.ppermute(near, "row", to_own)
     from_head = lax.ppermute(head, "row", to_far)
-    from_tail = lax.ppermute(tail, "row", to_far)
-
-    block = shape_of((local_rows, local_rows), jnp.float32)
+    from_tails = [lax.ppermute(tail, "row", to_far) for tail in tails]
+
+    partial = pl.pallas_call(
+        sum_kernel,
+        out_shape=shape_of((1, part), jnp.float32),
+        in_specs=[VMEM] * 2,
+        out_specs=VMEM,
+        compiler_params=LIMIT,
+    )(from_centre, near)
     early_blocks = (3, local_rows, local_rows)
     centred, mean, own, *others = pl.pallas_call(
         early_kernel,
@@ -248,39 +282,36 @@
             shape_of((1, part), jnp.float32),
             shape_of(early_blocks, jnp.float32),
         ]
-        + [block] * 3,
-        in_specs=[SMEM] + [VMEM] * 4,
-        out_specs=[VMEM] * 6,
+        + [shape_of((3, local_rows // 2, local_rows), jnp.float32)] * 2,
+        in_specs=[SMEM] + [VMEM] * 5,
+        out_specs=[VMEM] * 5,
         scratch_shapes=[pltpu.VMEM((2,) + early_blocks, jnp.float32)],
         compiler_params=LIMIT,
         cost_estimate=BRIEF,
-    )(bits, from_centre, from_edge, from_head, near)
+    )(bits, from_centre, from_edge, from_head, near, partial)
     others = [swap(other) for other in others]
-    places = held_place(EARLY_HELD, NEAR_ROUNDS) + [[[i] * 2] * 2 for i in range(3)]
-    early = combine(bits, own, others, (1, 2), (), EARLY_HELD, places, samples)
-    near_blocks, spares = early[: len(NEAR_ROUNDS)], early[len(NEAR_ROUNDS) :]
-    arrived = [send(value, blocks) for value, blocks in zip(near_blocks, NEAR_ROUNDS)]
-    summed = sum(block.astype(jnp.float32) for block in arrived)
+    places = held_place(EARLY_HELD, EARLY_ROUNDS) + [[[SPARE] * 2] * 2]
+    *early, spare = combine(bits, own, others, (1, 2), (), EARLY_HELD, places, samples)
+    arrived = [send(value, blocks) for value, blocks in zip(early, EARLY_ROUNDS)]
 
     late_blocks = shape_of((2, local_rows, local_rows), jnp.float32)
-    own, other, summed = pl.pallas_call(
+    own, other, spare = pl.pallas_call(
         late_kernel,
-        out_shape=[late_blocks, late_blocks, shape_of(summed.shape, summed.dtype)],
-        in_specs=[SMEM] + [VMEM] * 4 + [ANY],
+        out_shape=[late_blocks, late_blocks, shape_of(spare.shape, spare.dtype)],
+        in_specs=[SMEM] + [VMEM] * 5 + [ANY],
         out_specs=[VMEM] * 2 + [ANY],
         scratch_shapes=[
             pltpu.VMEM((local_rows, part), jnp.bfloat16),
             pltpu.VMEM((2,) + late_blocks.shape, jnp.float32),
         ],
-        input_output_aliases={5: 2},
-        compiler_params=LIMIT,
-        cost_estimate=BRIEF,
-    )(bits, from_head, from_tail, mean, centred, summed)
-    rounds = LATE_ROUNDS + FAR_ROUNDS
-    places = held_place(LATE_HELD, rounds)
-    late = combine(bits, own, [swap(other)], (0, 1), spares, LATE_HELD, places, samples)
-    arrived = [send(value, blocks) for value, blocks in zip(late, rounds)]
-    summed = summed + sum(block.astype(jnp.float32) for block in reversed(arrived))
+        input_output_aliases={6: 2},
+        compiler_params=LIMIT,
+        cost_estimate=BRIEF,
+    )(bits, from_head, *from_tails, mean, centred, spare)
+    places = held_place(LATE_HELD, LATE_ROUNDS)
+    late = combine(bits, own, [swap(other)], (0, 1), (spare,), LATE_HELD, places, samples)
+    arrived += [send(value, blocks) for value, blocks in zip(late, LATE_ROUNDS)]
+    summed = sum(block.astype(jnp.float32) for block in reversed(arrived))
     return add_shift(summed, 1, shift, local_rows)
 
 

time: 90.1 us -> 87.2 us (0.968)
  the two profiles are of different devices: /device:TPU:9 before, /device:TPU:8 now
where the time goes in v7:
time: 87.2 us; the launch traced here: 86.7 us
  waiting for transfers between devices  40.6 us (47%)
  starting transfers between devices  32.7 us (38%)
  Pallas kernels  9.75 us (11%)
  local copies, waits for them, and re-layouts  1.61 us (2%)
  other arithmetic  1.08 us (1%)
  between operations  1.01 us (1%)
    ppermute x8, starting transfers between devices, send(): lax.ppermute(value.astype(jnp.float16), everyone, round_pairs(blocks))  17.8 us
    ppermute x1, waiting for transfers between devices, two_centres(): from_centre = lax.ppermute(far, 'row', to_centre)  16.5 us
    ppermute x1, waiting for transfers between devices, two_centres(): from_head = lax.ppermute(head, 'row', to_far)  9.95 us
    ppermute x2, waiting for transfers between devices, two_centres(): from_tails = [lax.ppermute(tail, 'row', to_far) for tail in tails]  8.26 us
    ppermute x3, starting transfers between devices, swap(): return lax.ppermute(value, ('row', 'half'), centres)  6.25 us
    ppermute x8, waiting for transfers between devices, send(): lax.ppermute(value.astype(jnp.float16), everyone, round_pairs(blocks))  4.57 us
    ppermute x1, starting transfers between devices, two_centres(): from_centre = lax.ppermute(far, 'row', to_centre)  3.48 us
    pallas_call x1, Pallas kernels, two_centres(): pl.pallas_call(early_kernel, out_shape=[shape_of((3, local_rows, part), j...  3.3 us
  transfers between devices with their start and end apart: 16, of which 6 were waited for; matrix products, arithmetic and copies ran while one was open for 0% of the time, Pallas kernels for 8%

profile of v7, /device:TPU:8, one launch (start us, length us, event | category | flops | bytes accessed | tf_op | source)
XLA Modules:
  0.0 86.7 jit_solution(1459174570184087826)
XLA Ops:
  0.1 1.6 %copy-done = bf16[256,4096]{1,0:T(8,128)(2,1)S(1)} copy-done((bf16[256,4096]{1,0:T(8,128)(2,1)S(1)}, bf16[256,4096]{1,0:T(8,128)(2,1)}, u32[]{:S(2)}) %copy-start) | copy-done | bytes 2097176
  2.3 3.5 %collective-permute-start.3 = (bf16[256,2048]{1,0:T(8,128)(2,1)S(1)}, bf16[256,2048]{1,0:T(8,128)(2,1)S(1)}, u32[]{:S(2)}, u32[]{:S(2)}) collective-permute-start(bf16[256,2048]{1,0:T(8,128)(2,1)S(1)} %shard_map.46.far), channel_id=1, source_target_pairs={{4,8},{8,4},{5,9},{9,5},{6,10},{10,6},{7,11},{11,7},{20,24},{24,20... | collective-permute-start | bytes 3145736 | tf_op jit(solution)/shard_map/ppermute | solution.py:265
  5.8 1.6 %shard_map.47 = (bf16[256,2048]{1,0:T(8,128)(2,1)S(1)}, bf16[48,2048]{1,0:T(8,128)(2,1)S(1)}, bf16[112,2048]{1,0:T(8,128)(2,1)S(1)}, bf16[112,2048]{1,0:T(8,128)(2,1)S(1)}) custom-call(s32[3]{0:T(128)S(1)} %pad_add_fusion.bits, bf16[256,4096]{1,0:T(8,128)(2,1)S(1)} %copy-done, bf16[256,2048]{1,0:T(8,128)(2,1)S(1)} %shard_map.46.far), custom_call_target="tpu_custom_call" | custom-call | flops 1024 | bytes 1024 | tf_op jit(solution)/shard_map/pallas_call | solution.py:252
  7.5 1.3 %collective-permute-start.4 = (bf16[256,2048]{1,0:T(8,128)(2,1)S(1)}, bf16[256,2048]{1,0:T(8,128)(2,1)S(1)}, u32[]{:S(2)}, u32[]{:S(2)}) collective-permute-start(bf16[256,2048]{1,0:T(8,128)(2,1)S(1)} %get-tuple-element.29.near), channel_id=1, source_target_pairs={{0,4},{12,8},{1,5},{13,9},{2,6},{14,10},{3,7},{15,11},{16,20},{28,... | collective-permute-start | bytes 3145736 | tf_op jit(solution)/shard_map/ppermute | solution.py:266
  8.8 1.3 %collective-permute-start = (bf16[48,2048]{1,0:T(8,128)(2,1)S(1)}, bf16[48,2048]{1,0:T(8,128)(2,1)S(1)}, u32[]{:S(2)}, u32[]{:S(2)}) collective-permute-start(bf16[48,2048]{1,0:T(8,128)(2,1)S(1)} %get-tuple-element.26), channel_id=1, source_target_pairs={{0,8},{12,4},{1,9},{13,5},{2,10},{14,6},{3,11},{15,7},{16,24},{28,... | collective-permute-start | bytes 589832 | tf_op jit(solution)/shard_map/ppermute | solution.py:267
  10.1 1.3 %collective-permute-start.1 = (bf16[112,2048]{1,0:T(8,128)(2,1)S(1)}, bf16[112,2048]{1,0:T(8,128)(2,1)S(1)}, u32[]{:S(2)}, u32[]{:S(2)}) collective-permute-start(bf16[112,2048]{1,0:T(8,128)(2,1)S(1)} %get-tuple-element.27), channel_id=1, source_target_pairs={{0,8},{12,4},{1,9},{13,5},{2,10},{14,6},{3,11},{15,7},{16,24},{28,... | collective-permute-start | bytes 1376264 | tf_op jit(solution)/shard_map/ppermute | solution.py:268
  12.7 16.5 %collective-permute-done.3.other = bf16[256,2048]{1,0:T(8,128)(2,1)S(1)} collective-permute-done((bf16[256,2048]{1,0:T(8,128)(2,1)S(1)}, bf16[256,2048]{1,0:T(8,128)(2,1)S(1)}, u32[]{:S(2)}, u32[]{:S(2)}) %collective-permute-start.3) | collective-permute-done | bytes 1048608 | tf_op jit(solution)/shard_map/ppermute | solution.py:265
  29.6 9.9 %collective-permute-done.head = bf16[48,2048]{1,0:T(8,128)(2,1)S(1)} collective-permute-done((bf16[48,2048]{1,0:T(8,128)(2,1)S(1)}, bf16[48,2048]{1,0:T(8,128)(2,1)S(1)}, u32[]{:S(2)}, u32[]{:S(2)}) %collective-permute-start) | collective-permute-done | bytes 196640 | tf_op jit(solution)/shard_map/ppermute | solution.py:267
  39.5 3.3 %shard_map.49 = (bf16[3,256,2048]{2,1,0:T(8,128)(2,1)S(1)}, f32[1,2048]{1,0:T(1,128)S(1)}, f32[3,256,256]{2,1,0:T(8,128)S(1)}, f32[3,128,256]{2,1,0:T(8,128)S(1)}, f32[3,128,256]{2,1,0:T(8,128)S(1)}) custom-call(s32[3]{0:T(128)S(1)} %pad_add_fusion.bits, bf16[256,2048]{1,0:T(8,128)(2,1)S(1)} %collective-permute-done.3.other, ...), custom_call_target="tpu_custom_call" | custom-call | flops 1024 | bytes 1024 | tf_op jit(solution)/shard_map/pallas_call | solution.py:278
  42.9 1.9 %collective-permute-start.5 = (f32[3,128,256]{2,1,0:T(8,128)S(1)}, f32[3,128,256]{2,1,0:T(8,128)S(1)}, u32[]{:S(2)}, u32[]{:S(2)}) collective-permute-start(f32[3,128,256]{2,1,0:T(8,128)S(1)} %get-tuple-element.33), channel_id=1, source_target_pairs={{4,5},{5,4},{8,9},{9,8},{6,7},{7,6},{10,11},{11,10},{20,21},{21,20... | collective-permute-start | bytes 1179656 | tf_op jit(solution)/shard_map/ppermute | solution.py:238
  44.8 2.4 %collective-permute-start.6 = (f32[3,128,256]{2,1,0:T(8,128)S(1)}, f32[3,128,256]{2,1,0:T(8,128)S(1)}, u32[]{:S(2)}, u32[]{:S(2)}) collective-permute-start(f32[3,128,256]{2,1,0:T(8,128)S(1)} %get-tuple-element.34), channel_id=1, source_target_pairs={{4,5},{5,4},{8,9},{9,8},{6,7},{7,6},{10,11},{11,10},{20,21},{21,20... | collective-permute-start | bytes 1179656 | tf_op jit(solution)/shard_map/ppermute | solution.py:238
  47.2 1.3 %collective-permute-done.6.rest_1_ = f32[3,128,256]{2,1,0:T(8,128)S(1)} collective-permute-done((f32[3,128,256]{2,1,0:T(8,128)S(1)}, f32[3,128,256]{2,1,0:T(8,128)S(1)}, u32[]{:S(2)}, u32[]{:S(2)}) %collective-permute-start.6) | collective-permute-done | bytes 393248 | tf_op jit(solution)/shard_map/ppermute | solution.py:238
  49.5 8.3 %collective-permute-done.2.end = bf16[112,2048]{1,0:T(8,128)(2,1)S(1)} collective-permute-done((bf16[112,2048]{1,0:T(8,128)(2,1)S(1)}, bf16[112,2048]{1,0:T(8,128)(2,1)S(1)}, u32[]{:S(2)}, u32[]{:S(2)}) %collective-permute-start.2) | collective-permute-done | bytes 458784 | tf_op jit(solution)/shard_map/ppermute | solution.py:268
  57.7 1.9 %shard_map.51 = (f32[2,256,256]{2,1,0:T(8,128)S(1)}, f32[2,256,256]{2,1,0:T(8,128)S(1)}, f32[256,256]{1,0:T(8,128)S(1)}) custom-call(s32[3]{0:T(128)S(1)} %pad_add_fusion.bits, bf16[48,2048]{1,0:T(8,128)(2,1)S(1)} %collective-permute-done.head, bf16[112,2048]{1,0:T(8,128)(2,1)S(1)} %collective-permute-done.1.tail, ...), custom_call_target="tpu_custom_call", output_to_operand_aliasing={{2}: (6, {})} | custom-call | flops 1024 | bytes 1024 | tf_op jit(solution)/shard_map/pallas_call | solution.py:298
  59.6 1.9 %collective-permute-start.7 = (f32[2,256,256]{2,1,0:T(8,128)S(1)}, f32[2,256,256]{2,1,0:T(8,128)S(1)}, u32[]{:S(2)}, u32[]{:S(2)}) collective-permute-start(f32[2,256,256]{2,1,0:T(8,128)S(1)} %get-tuple-element.37), channel_id=1, source_target_pairs={{4,5},{5,4},{8,9},{9,8},{6,7},{7,6},{10,11},{11,10},{20,21},{21,20... | collective-permute-start | bytes 1572872 | tf_op jit(solution)/shard_map/ppermute | solution.py:238
  61.6 2.4 %collective-permute-start.12 = (f16[256,256]{1,0:T(8,128)(2,1)S(1)}, f16[256,256]{1,0:T(8,128)(2,1)S(1)}, u32[]{:S(2)}, u32[]{:S(2)}) collective-permute-start(f16[256,256]{1,0:T(8,128)(2,1)S(1)} %convert_element_type.60), channel_id=1, source_target_pairs={{4,5},{5,6},{6,4},{7,2},{10,10},{11,9},{8,11},{9,13},{20,21},{21,2... | collective-permute-start | bytes 393224 | tf_op jit(solution)/shard_map/ppermute | solution.py:241
  64.7 1.3 %collective-permute-start.14 = (f16[256,256]{1,0:T(8,128)(2,1)S(1)}, f16[256,256]{1,0:T(8,128)(2,1)S(1)}, u32[]{:S(2)}, u32[]{:S(2)}) collective-permute-start(f16[256,256]{1,0:T(8,128)(2,1)S(1)} %convert_element_type.64), channel_id=1, source_target_pairs={{4,1},{5,8},{6,0},{7,10},{10,14},{11,7},{8,15},{9,5},{20,17},{21,2... | collective-permute-start | bytes 393224 | tf_op jit(solution)/shard_map/ppermute | solution.py:241
  66.1 1.3 %collective-permute-start.15 = (f16[256,256]{1,0:T(8,128)(2,1)S(1)}, f16[256,256]{1,0:T(8,128)(2,1)S(1)}, u32[]{:S(2)}, u32[]{:S(2)}) collective-permute-start(f16[256,256]{1,0:T(8,128)(2,1)S(1)} %convert_element_type.66), channel_id=1, source_target_pairs={{4,0},{5,10},{6,1},{7,8},{10,15},{11,5},{8,14},{9,7},{20,16},{21,2... | collective-permute-start | bytes 393224 | tf_op jit(solution)/shard_map/ppermute | solution.py:241
  68.3 1.3 %collective-permute-start.10 = (f16[256,256]{1,0:T(8,128)(2,1)S(1)}, f16[256,256]{1,0:T(8,128)(2,1)S(1)}, u32[]{:S(2)}, u32[]{:S(2)}) collective-permute-start(f16[256,256]{1,0:T(8,128)(2,1)S(1)} %convert_element_type.56), channel_id=1, source_target_pairs={{4,13},{5,15},{6,12},{7,14},{10,2},{11,0},{8,3},{9,1},{20,29},{21,... | collective-permute-start | bytes 393224 | tf_op jit(solution)/shard_map/ppermute | solution.py:241
  69.7 1.3 %collective-permute-start.11 = (f16[256,256]{1,0:T(8,128)(2,1)S(1)}, f16[256,256]{1,0:T(8,128)(2,1)S(1)}, u32[]{:S(2)}, u32[]{:S(2)}) collective-permute-start(f16[256,256]{1,0:T(8,128)(2,1)S(1)} %convert_element_type.58), channel_id=1, source_target_pairs={{4,12},{5,14},{6,13},{7,15},{10,3},{11,1},{8,2},{9,0},{20,28},{21,... | collective-permute-start | bytes 393224 | tf_op jit(solution)/shard_map/ppermute | solution.py:241
  71.0 7.6 %collective-permute-start.8 = (f16[256,256]{1,0:T(8,128)(2,1)S(1)}, f16[256,256]{1,0:T(8,128)(2,1)S(1)}, u32[]{:S(2)}, u32[]{:S(2)}) collective-permute-start(f16[256,256]{1,0:T(8,128)(2,1)S(1)} %convert_element_type.52), channel_id=1, source_target_pairs={{4,7},{5,9},{6,3},{7,11},{10,8},{11,6},{8,12},{9,4},{20,23},{21,25... | collective-permute-start | bytes 393224 | tf_op jit(solution)/shard_map/ppermute | solution.py:241
  78.7 1.9 %collective-permute-start.9 = (f16[256,256]{1,0:T(8,128)(2,1)S(1)}, f16[256,256]{1,0:T(8,128)(2,1)S(1)}, u32[]{:S(2)}, u32[]{:S(2)}) collective-permute-start(f16[256,256]{1,0:T(8,128)(2,1)S(1)} %convert_element_type.54), channel_id=1, source_target_pairs={{4,3},{5,11},{6,7},{7,9},{10,12},{11,4},{8,8},{9,6},{20,19},{21,27... | collective-permute-start | bytes 393224 | tf_op jit(solution)/shard_map/ppermute | solution.py:241
  81.3 2.4 %collective-permute-done.8 = f16[256,256]{1,0:T(8,128)(2,1)S(1)} collective-permute-done((f16[256,256]{1,0:T(8,128)(2,1)S(1)}, f16[256,256]{1,0:T(8,128)(2,1)S(1)}, u32[]{:S(2)}, u32[]{:S(2)}) %collective-permute-start.8) | collective-permute-done | bytes 131104 | tf_op jit(solution)/shard_map/ppermute | solution.py:241
  83.7 2.2 %collective-permute-done.9 = f16[256,256]{1,0:T(8,128)(2,1)S(1)} collective-permute-done((f16[256,256]{1,0:T(8,128)(2,1)S(1)}, f16[256,256]{1,0:T(8,128)(2,1)S(1)}, u32[]{:S(2)}, u32[]{:S(2)}) %collective-permute-start.9) | collective-permute-done | bytes 131104 | tf_op jit(solution)/shard_map/ppermute | solution.py:241
  (32 shorter events, 6.0 us)
Async XLA Ops:
  0.1 1.6 %copy-start = (bf16[256,4096]{1,0:T(8,128)(2,1)S(1)}, bf16[256,4096]{1,0:T(8,128)(2,1)}, u32[]{:S(2)}) copy-start(bf16[256,4096]{1,0:T(8,128)(2,1)} %values.3) | copy-start | bytes 6291460
  2.3 26.8 %collective-permute-start.3 = (bf16[256,2048]{1,0:T(8,128)(2,1)S(1)}, bf16[256,2048]{1,0:T(8,128)(2,1)S(1)}, u32[]{:S(2)}, u32[]{:S(2)}) collective-permute-start(bf16[256,2048]{1,0:T(8,128)(2,1)S(1)} %shard_map.46.far), channel_id=1, source_target_pairs={{4,8},{8,4},{5,9},{9,5},{6,10},{10,6},{7,11},{11,7},{20,24},{24,20... | collective-permute-start | bytes 3145736 | tf_op jit(solution)/shard_map/ppermute | solution.py:265
  7.5 41.1 %copy-start.1 = (s32[5,2,2]{2,1,0:T(2,128)S(1)}, s32[5,2,2]{2,1,0:T(2,128)}, u32[]{:S(2)}) copy-start(s32[5,2,2]{2,1,0:T(2,128)} %constant.22.clone.places) | copy-start | bytes 244
  7.5 32.1 %collective-permute-start.4 = (bf16[256,2048]{1,0:T(8,128)(2,1)S(1)}, bf16[256,2048]{1,0:T(8,128)(2,1)S(1)}, u32[]{:S(2)}, u32[]{:S(2)}) collective-permute-start(bf16[256,2048]{1,0:T(8,128)(2,1)S(1)} %get-tuple-element.29.near), channel_id=1, source_target_pairs={{0,4},{12,8},{1,5},{13,9},{2,6},{14,10},{3,7},{15,11},{16,20},{28,... | collective-permute-start | bytes 3145736 | tf_op jit(solution)/shard_map/ppermute | solution.py:266
  8.8 30.8 %collective-permute-start = (bf16[48,2048]{1,0:T(8,128)(2,1)S(1)}, bf16[48,2048]{1,0:T(8,128)(2,1)S(1)}, u32[]{:S(2)}, u32[]{:S(2)}) collective-permute-start(bf16[48,2048]{1,0:T(8,128)(2,1)S(1)} %get-tuple-element.26), channel_id=1, source_target_pairs={{0,8},{12,4},{1,9},{13,5},{2,10},{14,6},{3,11},{15,7},{16,24},{28,... | collective-permute-start | bytes 589832 | tf_op jit(solution)/shard_map/ppermute | solution.py:267
  10.1 39.4 %collective-permute-start.1 = (bf16[112,2048]{1,0:T(8,128)(2,1)S(1)}, bf16[112,2048]{1,0:T(8,128)(2,1)S(1)}, u32[]{:S(2)}, u32[]{:S(2)}) collective-permute-start(bf16[112,2048]{1,0:T(8,128)(2,1)S(1)} %get-tuple-element.27), channel_id=1, source_target_pairs={{0,8},{12,4},{1,9},{13,5},{2,10},{14,6},{3,11},{15,7},{16,24},{28,... | collective-permute-start | bytes 1376264 | tf_op jit(solution)/shard_map/ppermute | solution.py:268
  11.4 46.4 %collective-permute-start.2 = (bf16[112,2048]{1,0:T(8,128)(2,1)S(1)}, bf16[112,2048]{1,0:T(8,128)(2,1)S(1)}, u32[]{:S(2)}, u32[]{:S(2)}) collective-permute-start(bf16[112,2048]{1,0:T(8,128)(2,1)S(1)} %get-tuple-element.28), channel_id=1, source_target_pairs={{0,8},{12,4},{1,9},{13,5},{2,10},{14,6},{3,11},{15,7},{16,24},{28,... | collective-permute-start | bytes 1376264 | tf_op jit(solution)/shard_map/ppermute | solution.py:268
  42.9 4.3 %collective-permute-start.5 = (f32[3,128,256]{2,1,0:T(8,128)S(1)}, f32[3,128,256]{2,1,0:T(8,128)S(1)}, u32[]{:S(2)}, u32[]{:S(2)}) collective-permute-start(f32[3,128,256]{2,1,0:T(8,128)S(1)} %get-tuple-element.33), channel_id=1, source_target_pairs={{4,5},{5,4},{8,9},{9,8},{6,7},{7,6},{10,11},{11,10},{20,21},{21,20... | collective-permute-start | bytes 1179656 | tf_op jit(solution)/shard_map/ppermute | solution.py:238
  44.8 3.7 %collective-permute-start.6 = (f32[3,128,256]{2,1,0:T(8,128)S(1)}, f32[3,128,256]{2,1,0:T(8,128)S(1)}, u32[]{:S(2)}, u32[]{:S(2)}) collective-permute-start(f32[3,128,256]{2,1,0:T(8,128)S(1)} %get-tuple-element.34), channel_id=1, source_target_pairs={{4,5},{5,4},{8,9},{9,8},{6,7},{7,6},{10,11},{11,10},{20,21},{21,20... | collective-permute-start | bytes 1179656 | tf_op jit(solution)/shard_map/ppermute | solution.py:238
  49.5 17.9 %copy-start.2 = (s32[4,2,2]{2,1,0:T(2,128)S(1)}, s32[4,2,2]{2,1,0:T(2,128)}, u32[]{:S(2)}) copy-start(s32[4,2,2]{2,1,0:T(2,128)} %constant.23.clone.places) | copy-start | bytes 196
  59.6 7.7 %collective-permute-start.7 = (f32[2,256,256]{2,1,0:T(8,128)S(1)}, f32[2,256,256]{2,1,0:T(8,128)S(1)}, u32[]{:S(2)}, u32[]{:S(2)}) collective-permute-start(f32[2,256,256]{2,1,0:T(8,128)S(1)} %get-tuple-element.37), channel_id=1, source_target_pairs={{4,5},{5,4},{8,9},{9,8},{6,7},{7,6},{10,11},{11,10},{20,21},{21,20... | collective-permute-start | bytes 1572872 | tf_op jit(solution)/shard_map/ppermute | solution.py:238
  61.6 8.1 %collective-permute-start.12 = (f16[256,256]{1,0:T(8,128)(2,1)S(1)}, f16[256,256]{1,0:T(8,128)(2,1)S(1)}, u32[]{:S(2)}, u32[]{:S(2)}) collective-permute-start(f16[256,256]{1,0:T(8,128)(2,1)S(1)} %convert_element_type.60), channel_id=1, source_target_pairs={{4,5},{5,6},{6,4},{7,2},{10,10},{11,9},{8,11},{9,13},{20,21},{21,2... | collective-permute-start | bytes 393224 | tf_op jit(solution)/shard_map/ppermute | solution.py:241
  64.0 7.0 %collective-permute-start.13 = (f16[256,256]{1,0:T(8,128)(2,1)S(1)}, f16[256,256]{1,0:T(8,128)(2,1)S(1)}, u32[]{:S(2)}, u32[]{:S(2)}) collective-permute-start(f16[256,256]{1,0:T(8,128)(2,1)S(1)} %convert_element_type.62), channel_id=1, source_target_pairs={{4,4},{5,2},{6,5},{7,6},{10,11},{11,13},{8,10},{9,9},{20,20},{21,1... | collective-permute-start | bytes 393224 | tf_op jit(solution)/shard_map/ppermute | solution.py:241
  64.7 13.9 %collective-permute-start.14 = (f16[256,256]{1,0:T(8,128)(2,1)S(1)}, f16[256,256]{1,0:T(8,128)(2,1)S(1)}, u32[]{:S(2)}, u32[]{:S(2)}) collective-permute-start(f16[256,256]{1,0:T(8,128)(2,1)S(1)} %convert_element_type.64), channel_id=1, source_target_pairs={{4,1},{5,8},{6,0},{7,10},{10,14},{11,7},{8,15},{9,5},{20,17},{21,2... | collective-permute-start | bytes 393224 | tf_op jit(solution)/shard_map/ppermute | solution.py:241
  66.1 15.2 %collective-permute-start.15 = (f16[256,256]{1,0:T(8,128)(2,1)S(1)}, f16[256,256]{1,0:T(8,128)(2,1)S(1)}, u32[]{:S(2)}, u32[]{:S(2)}) collective-permute-start(f16[256,256]{1,0:T(8,128)(2,1)S(1)} %convert_element_type.66), channel_id=1, source_target_pairs={{4,0},{5,10},{6,1},{7,8},{10,15},{11,5},{8,14},{9,7},{20,16},{21,2... | collective-permute-start | bytes 393224 | tf_op jit(solution)/shard_map/ppermute | solution.py:241
  68.3 13.0 %collective-permute-start.10 = (f16[256,256]{1,0:T(8,128)(2,1)S(1)}, f16[256,256]{1,0:T(8,128)(2,1)S(1)}, u32[]{:S(2)}, u32[]{:S(2)}) collective-permute-start(f16[256,256]{1,0:T(8,128)(2,1)S(1)} %convert_element_type.56), channel_id=1, source_target_pairs={{4,13},{5,15},{6,12},{7,14},{10,2},{11,0},{8,3},{9,1},{20,29},{21,... | collective-permute-start | bytes 393224 | tf_op jit(solution)/shard_map/ppermute | solution.py:241
  69.7 11.6 %collective-permute-start.11 = (f16[256,256]{1,0:T(8,128)(2,1)S(1)}, f16[256,256]{1,0:T(8,128)(2,1)S(1)}, u32[]{:S(2)}, u32[]{:S(2)}) collective-permute-start(f16[256,256]{1,0:T(8,128)(2,1)S(1)} %convert_element_type.58), channel_id=1, source_target_pairs={{4,12},{5,14},{6,13},{7,15},{10,3},{11,1},{8,2},{9,0},{20,28},{21,... | collective-permute-start | bytes 393224 | tf_op jit(solution)/shard_map/ppermute | solution.py:241
  71.0 12.7 %collective-permute-start.8 = (f16[256,256]{1,0:T(8,128)(2,1)S(1)}, f16[256,256]{1,0:T(8,128)(2,1)S(1)}, u32[]{:S(2)}, u32[]{:S(2)}) collective-permute-start(f16[256,256]{1,0:T(8,128)(2,1)S(1)} %convert_element_type.52), channel_id=1, source_target_pairs={{4,7},{5,9},{6,3},{7,11},{10,8},{11,6},{8,12},{9,4},{20,23},{21,25... | collective-permute-start | bytes 393224 | tf_op jit(solution)/shard_map/ppermute | solution.py:241
  78.7 7.2 %collective-permute-start.9 = (f16[256,256]{1,0:T(8,128)(2,1)S(1)}, f16[256,256]{1,0:T(8,128)(2,1)S(1)}, u32[]{:S(2)}, u32[]{:S(2)}) collective-permute-start(f16[256,256]{1,0:T(8,128)(2,1)S(1)} %convert_element_type.54), channel_id=1, source_target_pairs={{4,3},{5,11},{6,7},{7,9},{10,12},{11,4},{8,8},{9,6},{20,19},{21,27... | collective-permute-start | bytes 393224 | tf_op jit(solution)/shard_map/ppermute | solution.py:241

commit v8 on v7

--- a/solution.py
+++ b/solution.py
@@ -33,11 +33,13 @@
     return add_shift(summed, samples, shift, local_rows)
 
 
-EARLY_ROUNDS = (
+NEAR_ROUNDS = (
+    (((1, 0), (1, 1)), ((0, 2), (1, 2))),
+    (((1, 1), (1, 0)), ((1, 2), (0, 2))),
+)
+FAR_ROUNDS = (
     (((0, 0), (0, 1)), ((2, 2), (2, 0))),
     (((0, 1), (0, 0)), ((2, 0), (2, 2))),
-    (((1, 0), (1, 1)), ((0, 2), (1, 2))),
-    (((1, 1), (1, 0)), ((1, 2), (0, 2))),
 )
 LATE_ROUNDS = (
     (((3, 0), (3, 1)), ((3, 2), (3, 3))),
@@ -57,7 +59,7 @@
     ((3, 2), (3, 3), (2, 3), (3, 3), (2, 1)),
 )
 EXTRA = 16
-HEAD = 32
+HEAD = 48
 VMEM = pl.BlockSpec(memory_space=pltpu.VMEM)
 SMEM = pl.BlockSpec(memory_space=pltpu.SMEM)
 ANY = pl.BlockSpec(memory_space=pl.ANY)
@@ -90,10 +92,6 @@
     ]
 
 
-def tail_places(rows):
-    return HEAD, HEAD + (rows - HEAD) // 2
-
-
 def far_kernel(bits, values, far, sem):
     part = far.shape[1]
     columns = pl.ds(pl.multiple_of(bits[0] * part, 128), part)
@@ -102,8 +100,7 @@
     copy.wait()
 
 
-def near_kernel(bits, values, far, near, head, *rest):
-    tails, (sums, sems) = rest[:-2], rest[-2:]
+def near_kernel(bits, values, far, near, head, tail, sums, sems):
     rows, part = far.shape
     step = 512
     near_columns = pl.ds(pl.multiple_of((1 - bits[0]) * part, 128), part)
@@ -113,9 +110,8 @@
             far.at[pl.ds(0, HEAD), :], head.at[pl.ds(EXTRA, HEAD), :], sems.at[1]
         ),
     ]
-    for i, (first, tail) in enumerate(zip(tail_places(rows), tails)):
-        from_rows = far.at[pl.ds(first, tail.shape[0]), :]
-        copies.append(pltpu.make_async_copy(from_rows, tail, sems.at[2 + i]))
+    from_rows = far.at[pl.ds(HEAD, rows - HEAD), :]
+    copies.append(pltpu.make_async_copy(from_rows, tail, sems.at[2]))
     for copy in copies:
         copy.start()
 
@@ -170,17 +166,17 @@
             both[core, place] = block_product(centred[i], centred[j])
     own[...] = both[bits[1]]
     for place, send in enumerate(sends):
-        first = place * send.shape[1]
-        send[...] = both[1 - bits[1], :, pl.ds(first, send.shape[1]), :]
-
-
-def late_kernel(bits, head, tail, end, mean, centred, spare, own, send, handed, last, both):
+        send[...] = both[1 - bits[1], pl.ds(place, 1), :, :]
+
+
+def late_kernel(bits, head, tail, mean, centred, *rest):
+    own, send = rest[len(rest) // 2 - 2 : len(rest) // 2]
+    last, both = rest[-2:]
     rows = last.shape[0]
     first = head[pl.ds(EXTRA, HEAD), :].astype(jnp.float32) - mean[...]
     last[pl.ds(0, HEAD), :] = first.astype(jnp.bfloat16)
-    for place, block in zip(tail_places(rows), (tail, end)):
-        values = block[...].astype(jnp.float32) - mean[...]
-        last[pl.ds(place, block.shape[0]), :] = values.astype(jnp.bfloat16)
+    second = tail[...].astype(jnp.float32) - mean[...]
+    last[pl.ds(HEAD, rows - HEAD), :] = second.astype(jnp.bfloat16)
     for core in (0, 1):
         for place, (_, j) in enumerate(LATE_SUMS[core]):
             both[core, place] = block_product(last[...], last[...] if j == 3 else centred[j])
@@ -193,7 +189,7 @@
     outs, held = rest[pieces + spares : -1], rest[-1]
     count = own.shape[0]
     for i in range(count):
-        other = jnp.concatenate([piece[i] for piece in others], axis=0)
+        other = others[0][i] if pieces == 1 else others[i][0]
         held[i] = (own[i] + other) * scale
     for n, i in enumerate(flips):
         held[count + n] = held[i].T
@@ -249,23 +245,23 @@
         compiler_params=LIMIT,
         cost_estimate=BRIEF,
     )(bits, log_derivs)
-    near, head, *tails = pl.pallas_call(
+    near, head, tail = pl.pallas_call(
         near_kernel,
         out_shape=[
             shape_of((local_rows, part), jnp.bfloat16),
             shape_of((EXTRA + HEAD, part), jnp.bfloat16),
-        ]
-        + [shape_of(((local_rows - HEAD) // 2, part), jnp.bfloat16)] * 2,
+            shape_of((local_rows - HEAD, part), jnp.bfloat16),
+        ],
         in_specs=[SMEM, ANY, VMEM],
-        out_specs=[VMEM] * 4,
-        scratch_shapes=[pltpu.VMEM((EXTRA, part), jnp.float32), pltpu.SemaphoreType.DMA((4,))],
+        out_specs=[VMEM] * 3,
+        scratch_shapes=[pltpu.VMEM((EXTRA, part), jnp.float32), pltpu.SemaphoreType.DMA((3,))],
         compiler_params=LIMIT,
         cost_estimate=BRIEF,
     )(bits, log_derivs, far)
     from_centre = lax.ppermute(far, "row", to_centre)
     from_edge = lax.ppermute(near, "row", to_own)
     from_head = lax.ppermute(head, "row", to_far)
-    from_tails = [lax.ppermute(tail, "row", to_far) for tail in tails]
+    from_tail = lax.ppermute(tail, "row", to_far)
 
     partial = pl.pallas_call(
         sum_kernel,
@@ -282,36 +278,42 @@
             shape_of((1, part), jnp.float32),
             shape_of(early_blocks, jnp.float32),
         ]
-        + [shape_of((3, local_rows // 2, local_rows), jnp.float32)] * 2,
+        + [shape_of((1, local_rows, local_rows), jnp.float32)] * 3,
         in_specs=[SMEM] + [VMEM] * 5,
-        out_specs=[VMEM] * 5,
+        out_specs=[VMEM] * 6,
         scratch_shapes=[pltpu.VMEM((2,) + early_blocks, jnp.float32)],
         compiler_params=LIMIT,
         cost_estimate=BRIEF,
     )(bits, from_centre, from_edge, from_head, near, partial)
     others = [swap(other) for other in others]
-    places = held_place(EARLY_HELD, EARLY_ROUNDS) + [[[SPARE] * 2] * 2]
+    places = held_place(EARLY_HELD, NEAR_ROUNDS + FAR_ROUNDS) + [[[SPARE] * 2] * 2]
     *early, spare = combine(bits, own, others, (1, 2), (), EARLY_HELD, places, samples)
-    arrived = [send(value, blocks) for value, blocks in zip(early, EARLY_ROUNDS)]
+    near_blocks, far_blocks = early[: len(NEAR_ROUNDS)], early[len(NEAR_ROUNDS) :]
+    arrived = [send(value, blocks) for value, blocks in zip(near_blocks, NEAR_ROUNDS)]
+    summed = sum(block.astype(jnp.float32) for block in arrived)
 
     late_blocks = shape_of((2, local_rows, local_rows), jnp.float32)
-    own, other, spare = pl.pallas_call(
+    handed = [summed] + far_blocks
+    own, other, summed, *far_blocks = pl.pallas_call(
         late_kernel,
-        out_shape=[late_blocks, late_blocks, shape_of(spare.shape, spare.dtype)],
-        in_specs=[SMEM] + [VMEM] * 5 + [ANY],
-        out_specs=[VMEM] * 2 + [ANY],
+        out_shape=[late_blocks, late_blocks]
+        + [shape_of(value.shape, value.dtype) for value in handed],
+        in_specs=[SMEM] + [VMEM] * 4 + [ANY] * len(handed),
+        out_specs=[VMEM] * 2 + [ANY] * len(handed),
         scratch_shapes=[
             pltpu.VMEM((local_rows, part), jnp.bfloat16),
             pltpu.VMEM((2,) + late_blocks.shape, jnp.float32),
         ],
-        input_output_aliases={6: 2},
-        compiler_params=LIMIT,
-        cost_estimate=BRIEF,
-    )(bits, from_head, *from_tails, mean, centred, spare)
+        input_output_aliases={5 + i: 2 + i for i in range(len(handed))},
+        compiler_params=LIMIT,
+        cost_estimate=BRIEF,
+    )(bits, from_head, from_tail, mean, centred, *handed)
+    other = swap(other)
+    arrived = [send(value, blocks) for value, blocks in zip(far_blocks, FAR_ROUNDS)]
     places = held_place(LATE_HELD, LATE_ROUNDS)
-    late = combine(bits, own, [swap(other)], (0, 1), (spare,), LATE_HELD, places, samples)
+    late = combine(bits, own, [other], (0, 1), (spare,), LATE_HELD, places, samples)
     arrived += [send(value, blocks) for value, blocks in zip(late, LATE_ROUNDS)]
-    summed = sum(block.astype(jnp.float32) for block in reversed(arrived))
+    summed = summed + sum(block.astype(jnp.float32) for block in reversed(arrived))
     return add_shift(summed, 1, shift, local_rows)
 
 

time: 87.2 us -> 85.9 us (0.985); the launches traced: 86.7 us -> 84.4 us
  waiting for transfers between devices: 40.6 us -> 36.5 us
  starting transfers between devices: 32.7 us -> 34.8 us
    ppermute x2 -> x1, waiting for transfers between devices: 8.26 us -> 0.01 us  [two_centres(): from_tail = lax.ppermute(tail, 'row', to_far)]
    ppermute x3 -> x4, starting transfers between devices: 6.25 us -> 11.1 us  [swap(): return lax.ppermute(value, ('row', 'half'), centres)]
    ppermute x1, waiting for transfers between devices: 16.5 us -> 18.1 us  [two_centres(): from_centre = lax.ppermute(far, 'row', to_centre)]
    ppermute x8, starting transfers between devices: 17.8 us -> 16.3 us  [send(): lax.ppermute(value.astype(jnp.float16), everyone, round_pairs(blocks))]
    ppermute x8, waiting for transfers between devices: 4.57 us -> 5.9 us  [send(): lax.ppermute(value.astype(jnp.float16), everyone, round_pairs(blocks))]
    ppermute x2 -> x1, starting transfers between devices: 2.58 us -> 1.29 us  [two_centres(): from_tail = lax.ppermute(tail, 'row', to_far)]
    ppermute x1, waiting for transfers between devices: 9.95 us -> 11 us  [two_centres(): from_head = lax.ppermute(head, 'row', to_far)]
  transfers between devices with their start and end apart: 16 -> 16, of which waited for: 6 -> 5; matrix products, arithmetic and copies ran while one was open for 0% -> 0% of each run, Pallas kernels for 8% -> 8%
where the time goes in v8:
time: 85.9 us; the launch traced here: 84.4 us
  waiting for transfers between devices  36.5 us (42%)
  starting transfers between devices  34.8 us (41%)
  Pallas kernels  9.41 us (11%)
  local copies, waits for them, and re-layouts  1.61 us (2%)
  other arithmetic  1.09 us (1%)
  between operations  1.01 us (1%)
    ppermute x1, waiting for transfers between devices, two_centres(): from_centre = lax.ppermute(far, 'row', to_centre)  18.1 us
    ppermute x8, starting transfers between devices, send(): lax.ppermute(value.astype(jnp.float16), everyone, round_pairs(blocks))  16.3 us
    ppermute x4, starting transfers between devices, swap(): return lax.ppermute(value, ('row', 'half'), centres)  11.1 us
    ppermute x1, waiting for transfers between devices, two_centres(): from_head = lax.ppermute(head, 'row', to_far)  11 us
    ppermute x8, waiting for transfers between devices, send(): lax.ppermute(value.astype(jnp.float16), everyone, round_pairs(blocks))  5.9 us
    ppermute x1, starting transfers between devices, two_centres(): from_centre = lax.ppermute(far, 'row', to_centre)  3.48 us
    pallas_call x1, Pallas kernels, two_centres(): pl.pallas_call(early_kernel, out_shape=[shape_of((3, local_rows, part), j...  3.3 us
    pallas_call x1, Pallas kernels, two_centres(): pl.pallas_call(late_kernel, out_shape=[late_blocks, late_blocks] + [shape...  1.9 us
  transfers between devices with their start and end apart: 16, of which 5 were waited for; matrix products, arithmetic and copies ran while one was open for 0% of the time, Pallas kernels for 8%

profile of v8, /device:TPU:8, one launch (start us, length us, event | category | flops | bytes accessed | tf_op | source)
XLA Modules:
  0.0 84.4 jit_solution(14615431059632456806)
XLA Ops:
  0.1 1.6 %copy-done = bf16[256,4096]{1,0:T(8,128)(2,1)S(1)} copy-done((bf16[256,4096]{1,0:T(8,128)(2,1)S(1)}, bf16[256,4096]{1,0:T(8,128)(2,1)}, u32[]{:S(2)}) %copy-start) | copy-done | bytes 2097176
  2.3 3.5 %collective-permute-start.2 = (bf16[256,2048]{1,0:T(8,128)(2,1)S(1)}, bf16[256,2048]{1,0:T(8,128)(2,1)S(1)}, u32[]{:S(2)}, u32[]{:S(2)}) collective-permute-start(bf16[256,2048]{1,0:T(8,128)(2,1)S(1)} %shard_map.46.far), channel_id=1, source_target_pairs={{4,8},{8,4},{5,9},{9,5},{6,10},{10,6},{7,11},{11,7},{20,24},{24,20... | collective-permute-start | bytes 3145736 | tf_op jit(solution)/shard_map/ppermute | solution.py:261
  5.8 1.3 %shard_map.47 = (bf16[256,2048]{1,0:T(8,128)(2,1)S(1)}, bf16[64,2048]{1,0:T(8,128)(2,1)S(1)}, bf16[208,2048]{1,0:T(8,128)(2,1)S(1)}) custom-call(s32[3]{0:T(128)S(1)} %pad_add_fusion.bits, bf16[256,4096]{1,0:T(8,128)(2,1)S(1)} %copy-done, bf16[256,2048]{1,0:T(8,128)(2,1)S(1)} %shard_map.46.far), custom_call_target="tpu_custom_call" | custom-call | flops 1024 | bytes 1024 | tf_op jit(solution)/shard_map/pallas_call | solution.py:248
  7.1 1.3 %collective-permute-start.3 = (bf16[256,2048]{1,0:T(8,128)(2,1)S(1)}, bf16[256,2048]{1,0:T(8,128)(2,1)S(1)}, u32[]{:S(2)}, u32[]{:S(2)}) collective-permute-start(bf16[256,2048]{1,0:T(8,128)(2,1)S(1)} %get-tuple-element.30.near), channel_id=1, source_target_pairs={{0,4},{12,8},{1,5},{13,9},{2,6},{14,10},{3,7},{15,11},{16,20},{28,... | collective-permute-start | bytes 3145736 | tf_op jit(solution)/shard_map/ppermute | solution.py:262
  8.4 1.3 %collective-permute-start = (bf16[64,2048]{1,0:T(8,128)(2,1)S(1)}, bf16[64,2048]{1,0:T(8,128)(2,1)S(1)}, u32[]{:S(2)}, u32[]{:S(2)}) collective-permute-start(bf16[64,2048]{1,0:T(8,128)(2,1)S(1)} %get-tuple-element.28), channel_id=1, source_target_pairs={{0,8},{12,4},{1,9},{13,5},{2,10},{14,6},{3,11},{15,7},{16,24},{28,... | collective-permute-start | bytes 786440 | tf_op jit(solution)/shard_map/ppermute | solution.py:263
  9.7 1.3 %collective-permute-start.1 = (bf16[208,2048]{1,0:T(8,128)(2,1)S(1)}, bf16[208,2048]{1,0:T(8,128)(2,1)S(1)}, u32[]{:S(2)}, u32[]{:S(2)}) collective-permute-start(bf16[208,2048]{1,0:T(8,128)(2,1)S(1)} %get-tuple-element.29), channel_id=1, source_target_pairs={{0,8},{12,4},{1,9},{13,5},{2,10},{14,6},{3,11},{15,7},{16,24},{28,... | collective-permute-start | bytes 2555912 | tf_op jit(solution)/shard_map/ppermute | solution.py:264
  11.0 18.1 %collective-permute-done.2.other = bf16[256,2048]{1,0:T(8,128)(2,1)S(1)} collective-permute-done((bf16[256,2048]{1,0:T(8,128)(2,1)S(1)}, bf16[256,2048]{1,0:T(8,128)(2,1)S(1)}, u32[]{:S(2)}, u32[]{:S(2)}) %collective-permute-start.2) | collective-permute-done | bytes 1048608 | tf_op jit(solution)/shard_map/ppermute | solution.py:261
  29.6 11.0 %collective-permute-done.head = bf16[64,2048]{1,0:T(8,128)(2,1)S(1)} collective-permute-done((bf16[64,2048]{1,0:T(8,128)(2,1)S(1)}, bf16[64,2048]{1,0:T(8,128)(2,1)S(1)}, u32[]{:S(2)}, u32[]{:S(2)}) %collective-permute-start) | collective-permute-done | bytes 262176 | tf_op jit(solution)/shard_map/ppermute | solution.py:263
  40.6 3.3 %shard_map.49 = (bf16[3,256,2048]{2,1,0:T(8,128)(2,1)S(1)}, f32[1,2048]{1,0:T(1,128)S(1)}, f32[3,256,256]{2,1,0:T(8,128)S(1)}, f32[1,256,256]{2,1,0:T(8,128)S(1)...) custom-call(s32[3]{0:T(128)S(1)} %pad_add_fusion.bits, bf16[256,2048]{1,0:T(8,128)(2,1)S(1)} %collective-permute-done.2.other, ...), custom_call_target="tpu_custom_call" | custom-call | flops 1024 | bytes 1024 | tf_op jit(solution)/shard_map/pallas_call | solution.py:274
  43.9 1.9 %collective-permute-start.4 = (f32[1,256,256]{2,1,0:T(8,128)S(1)}, f32[1,256,256]{2,1,0:T(8,128)S(1)}, u32[]{:S(2)}, u32[]{:S(2)}) collective-permute-start(f32[1,256,256]{2,1,0:T(8,128)S(1)} %get-tuple-element.34), channel_id=1, source_target_pairs={{4,5},{5,4},{8,9},{9,8},{6,7},{7,6},{10,11},{11,10},{20,21},{21,20... | collective-permute-start | bytes 786440 | tf_op jit(solution)/shard_map/ppermute | solution.py:234
  45.9 2.4 %collective-permute-start.5 = (f32[1,256,256]{2,1,0:T(8,128)S(1)}, f32[1,256,256]{2,1,0:T(8,128)S(1)}, u32[]{:S(2)}, u32[]{:S(2)}) collective-permute-start(f32[1,256,256]{2,1,0:T(8,128)S(1)} %get-tuple-element.35), channel_id=1, source_target_pairs={{4,5},{5,4},{8,9},{9,8},{6,7},{7,6},{10,11},{11,10},{20,21},{21,20... | collective-permute-start | bytes 786440 | tf_op jit(solution)/shard_map/ppermute | solution.py:234
  48.3 1.9 %collective-permute-start.6 = (f32[1,256,256]{2,1,0:T(8,128)S(1)}, f32[1,256,256]{2,1,0:T(8,128)S(1)}, u32[]{:S(2)}, u32[]{:S(2)}) collective-permute-start(f32[1,256,256]{2,1,0:T(8,128)S(1)} %get-tuple-element.36), channel_id=1, source_target_pairs={{4,5},{5,4},{8,9},{9,8},{6,7},{7,6},{10,11},{11,10},{20,21},{21,20... | collective-permute-start | bytes 786440 | tf_op jit(solution)/shard_map/ppermute | solution.py:234
  50.2 1.5 %collective-permute-done.6.rest_2_ = f32[1,256,256]{2,1,0:T(8,128)S(1)} collective-permute-done((f32[1,256,256]{2,1,0:T(8,128)S(1)}, f32[1,256,256]{2,1,0:T(8,128)S(1)}, u32[]{:S(2)}, u32[]{:S(2)}) %collective-permute-start.6) | collective-permute-done | bytes 262176 | tf_op jit(solution)/shard_map/ppermute | solution.py:234
  52.7 2.0 %collective-permute-start.8 = (f16[256,256]{1,0:T(8,128)(2,1)S(1)}, f16[256,256]{1,0:T(8,128)(2,1)S(1)}, u32[]{:S(2)}, u32[]{:S(2)}) collective-permute-start(f16[256,256]{1,0:T(8,128)(2,1)S(1)} %convert_element_type.54), channel_id=1, source_target_pairs={{4,5},{5,6},{6,4},{7,2},{10,10},{11,9},{8,11},{9,13},{20,21},{21,2... | collective-permute-start | bytes 393224 | tf_op jit(solution)/shard_map/ppermute | solution.py:237
  55.4 4.1 %collective-permute-done.8 = f16[256,256]{1,0:T(8,128)(2,1)S(1)} collective-permute-done((f16[256,256]{1,0:T(8,128)(2,1)S(1)}, f16[256,256]{1,0:T(8,128)(2,1)S(1)}, u32[]{:S(2)}, u32[]{:S(2)}) %collective-permute-start.8) | collective-permute-done | bytes 131104 | tf_op jit(solution)/shard_map/ppermute | solution.py:237
  59.6 1.9 %shard_map.51 = (f32[2,256,256]{2,1,0:T(8,128)S(1)}, f32[2,256,256]{2,1,0:T(8,128)S(1)}, f32[256,256]{1,0:T(8,128)S(1)}, f32[256,256]{1,0:T(8,128)S(1)}, f32[256,256]{1,0:T(8,128)S(1)}) custom-call(s32[3]{0:T(128)S(1)} %pad_add_fusion.bits, ...), custom_call_target="tpu_custom_call", output_to_operand_aliasing={{2}: (5, {}), {3}: (6, {}), {4}: (7, {})} | custom-call | flops 1024 | bytes 1024 | tf_op jit(solution)/shard_map/pallas_call | solution.py:297
  61.5 4.9 %collective-permute-start.9 = (f32[2,256,256]{2,1,0:T(8,128)S(1)}, f32[2,256,256]{2,1,0:T(8,128)S(1)}, u32[]{:S(2)}, u32[]{:S(2)}) collective-permute-start(f32[2,256,256]{2,1,0:T(8,128)S(1)} %get-tuple-element.43), channel_id=1, source_target_pairs={{4,5},{5,4},{8,9},{9,8},{6,7},{7,6},{10,11},{11,10},{20,21},{21,20... | collective-permute-start | bytes 1572872 | tf_op jit(solution)/shard_map/ppermute | solution.py:234
  66.4 1.3 %collective-permute-start.15 = (f16[256,256]{1,0:T(8,128)(2,1)S(1)}, f16[256,256]{1,0:T(8,128)(2,1)S(1)}, u32[]{:S(2)}, u32[]{:S(2)}) collective-permute-start(f16[256,256]{1,0:T(8,128)(2,1)S(1)} %convert_element_type.66), channel_id=1, source_target_pairs={{4,0},{5,10},{6,1},{7,8},{10,15},{11,5},{8,14},{9,7},{20,16},{21,2... | collective-permute-start | bytes 393224 | tf_op jit(solution)/shard_map/ppermute | solution.py:237
  67.7 1.3 %collective-permute-start.14 = (f16[256,256]{1,0:T(8,128)(2,1)S(1)}, f16[256,256]{1,0:T(8,128)(2,1)S(1)}, u32[]{:S(2)}, u32[]{:S(2)}) collective-permute-start(f16[256,256]{1,0:T(8,128)(2,1)S(1)} %convert_element_type.64), channel_id=1, source_target_pairs={{4,1},{5,8},{6,0},{7,10},{10,14},{11,7},{8,15},{9,5},{20,17},{21,2... | collective-permute-start | bytes 393224 | tf_op jit(solution)/shard_map/ppermute | solution.py:237
  70.0 1.3 %collective-permute-start.13 = (f16[256,256]{1,0:T(8,128)(2,1)S(1)}, f16[256,256]{1,0:T(8,128)(2,1)S(1)}, u32[]{:S(2)}, u32[]{:S(2)}) collective-permute-start(f16[256,256]{1,0:T(8,128)(2,1)S(1)} %convert_element_type.62), channel_id=1, source_target_pairs={{4,12},{5,14},{6,13},{7,15},{10,3},{11,1},{8,2},{9,0},{20,28},{21,... | collective-permute-start | bytes 393224 | tf_op jit(solution)/shard_map/ppermute | solution.py:237
  71.3 1.3 %collective-permute-start.12 = (f16[256,256]{1,0:T(8,128)(2,1)S(1)}, f16[256,256]{1,0:T(8,128)(2,1)S(1)}, u32[]{:S(2)}, u32[]{:S(2)}) collective-permute-start(f16[256,256]{1,0:T(8,128)(2,1)S(1)} %convert_element_type.60), channel_id=1, source_target_pairs={{4,13},{5,15},{6,12},{7,14},{10,2},{11,0},{8,3},{9,1},{20,29},{21,... | collective-permute-start | bytes 393224 | tf_op jit(solution)/shard_map/ppermute | solution.py:237
  72.6 1.9 %collective-permute-start.11 = (f16[256,256]{1,0:T(8,128)(2,1)S(1)}, f16[256,256]{1,0:T(8,128)(2,1)S(1)}, u32[]{:S(2)}, u32[]{:S(2)}) collective-permute-start(f16[256,256]{1,0:T(8,128)(2,1)S(1)} %convert_element_type.58), channel_id=1, source_target_pairs={{4,3},{5,11},{6,7},{7,9},{10,12},{11,4},{8,8},{9,6},{20,19},{21,27... | collective-permute-start | bytes 393224 | tf_op jit(solution)/shard_map/ppermute | solution.py:237
  74.6 6.5 %collective-permute-start.10 = (f16[256,256]{1,0:T(8,128)(2,1)S(1)}, f16[256,256]{1,0:T(8,128)(2,1)S(1)}, u32[]{:S(2)}, u32[]{:S(2)}) collective-permute-start(f16[256,256]{1,0:T(8,128)(2,1)S(1)} %convert_element_type.56), channel_id=1, source_target_pairs={{4,7},{5,9},{6,3},{7,11},{10,8},{11,6},{8,12},{9,4},{20,23},{21,25... | collective-permute-start | bytes 393224 | tf_op jit(solution)/shard_map/ppermute | solution.py:237
  81.8 1.8 %collective-permute-done.10 = f16[256,256]{1,0:T(8,128)(2,1)S(1)} collective-permute-done((f16[256,256]{1,0:T(8,128)(2,1)S(1)}, f16[256,256]{1,0:T(8,128)(2,1)S(1)}, u32[]{:S(2)}, u32[]{:S(2)}) %collective-permute-start.10) | collective-permute-done | bytes 131104 | tf_op jit(solution)/shard_map/ppermute | solution.py:237
  (33 shorter events, 4.7 us)
Async XLA Ops:
  0.1 1.6 %copy-start = (bf16[256,4096]{1,0:T(8,128)(2,1)S(1)}, bf16[256,4096]{1,0:T(8,128)(2,1)}, u32[]{:S(2)}) copy-start(bf16[256,4096]{1,0:T(8,128)(2,1)} %values.3) | copy-start | bytes 6291460
  2.3 26.8 %collective-permute-start.2 = (bf16[256,2048]{1,0:T(8,128)(2,1)S(1)}, bf16[256,2048]{1,0:T(8,128)(2,1)S(1)}, u32[]{:S(2)}, u32[]{:S(2)}) collective-permute-start(bf16[256,2048]{1,0:T(8,128)(2,1)S(1)} %shard_map.46.far), channel_id=1, source_target_pairs={{4,8},{8,4},{5,9},{9,5},{6,10},{10,6},{7,11},{11,7},{20,24},{24,20... | collective-permute-start | bytes 3145736 | tf_op jit(solution)/shard_map/ppermute | solution.py:261
  7.1 44.6 %copy-start.1 = (s32[5,2,2]{2,1,0:T(2,128)S(1)}, s32[5,2,2]{2,1,0:T(2,128)}, u32[]{:S(2)}) copy-start(s32[5,2,2]{2,1,0:T(2,128)} %constant.22.clone.places) | copy-start | bytes 244
  7.1 33.5 %collective-permute-start.3 = (bf16[256,2048]{1,0:T(8,128)(2,1)S(1)}, bf16[256,2048]{1,0:T(8,128)(2,1)S(1)}, u32[]{:S(2)}, u32[]{:S(2)}) collective-permute-start(bf16[256,2048]{1,0:T(8,128)(2,1)S(1)} %get-tuple-element.30.near), channel_id=1, source_target_pairs={{0,4},{12,8},{1,5},{13,9},{2,6},{14,10},{3,7},{15,11},{16,20},{28,... | collective-permute-start | bytes 3145736 | tf_op jit(solution)/shard_map/ppermute | solution.py:262
  8.4 32.2 %collective-permute-start = (bf16[64,2048]{1,0:T(8,128)(2,1)S(1)}, bf16[64,2048]{1,0:T(8,128)(2,1)S(1)}, u32[]{:S(2)}, u32[]{:S(2)}) collective-permute-start(bf16[64,2048]{1,0:T(8,128)(2,1)S(1)} %get-tuple-element.28), channel_id=1, source_target_pairs={{0,8},{12,4},{1,9},{13,5},{2,10},{14,6},{3,11},{15,7},{16,24},{28,... | collective-permute-start | bytes 786440 | tf_op jit(solution)/shard_map/ppermute | solution.py:263
  9.7 49.8 %collective-permute-start.1 = (bf16[208,2048]{1,0:T(8,128)(2,1)S(1)}, bf16[208,2048]{1,0:T(8,128)(2,1)S(1)}, u32[]{:S(2)}, u32[]{:S(2)}) collective-permute-start(bf16[208,2048]{1,0:T(8,128)(2,1)S(1)} %get-tuple-element.29), channel_id=1, source_target_pairs={{0,8},{12,4},{1,9},{13,5},{2,10},{14,6},{3,11},{15,7},{16,24},{28,... | collective-permute-start | bytes 2555912 | tf_op jit(solution)/shard_map/ppermute | solution.py:264
  43.9 6.3 %collective-permute-start.4 = (f32[1,256,256]{2,1,0:T(8,128)S(1)}, f32[1,256,256]{2,1,0:T(8,128)S(1)}, u32[]{:S(2)}, u32[]{:S(2)}) collective-permute-start(f32[1,256,256]{2,1,0:T(8,128)S(1)} %get-tuple-element.34), channel_id=1, source_target_pairs={{4,5},{5,4},{8,9},{9,8},{6,7},{7,6},{10,11},{11,10},{20,21},{21,20... | collective-permute-start | bytes 786440 | tf_op jit(solution)/shard_map/ppermute | solution.py:234
  45.9 4.4 %collective-permute-start.5 = (f32[1,256,256]{2,1,0:T(8,128)S(1)}, f32[1,256,256]{2,1,0:T(8,128)S(1)}, u32[]{:S(2)}, u32[]{:S(2)}) collective-permute-start(f32[1,256,256]{2,1,0:T(8,128)S(1)} %get-tuple-element.35), channel_id=1, source_target_pairs={{4,5},{5,4},{8,9},{9,8},{6,7},{7,6},{10,11},{11,10},{20,21},{21,20... | collective-permute-start | bytes 786440 | tf_op jit(solution)/shard_map/ppermute | solution.py:234
  48.3 3.4 %collective-permute-start.6 = (f32[1,256,256]{2,1,0:T(8,128)S(1)}, f32[1,256,256]{2,1,0:T(8,128)S(1)}, u32[]{:S(2)}, u32[]{:S(2)}) collective-permute-start(f32[1,256,256]{2,1,0:T(8,128)S(1)} %get-tuple-element.36), channel_id=1, source_target_pairs={{4,5},{5,4},{8,9},{9,8},{6,7},{7,6},{10,11},{11,10},{20,21},{21,20... | collective-permute-start | bytes 786440 | tf_op jit(solution)/shard_map/ppermute | solution.py:234
  52.7 6.9 %collective-permute-start.8 = (f16[256,256]{1,0:T(8,128)(2,1)S(1)}, f16[256,256]{1,0:T(8,128)(2,1)S(1)}, u32[]{:S(2)}, u32[]{:S(2)}) collective-permute-start(f16[256,256]{1,0:T(8,128)(2,1)S(1)} %convert_element_type.54), channel_id=1, source_target_pairs={{4,5},{5,6},{6,4},{7,2},{10,10},{11,9},{8,11},{9,13},{20,21},{21,2... | collective-permute-start | bytes 393224 | tf_op jit(solution)/shard_map/ppermute | solution.py:237
  54.7 14.3 %copy-start.2 = (s32[4,2,2]{2,1,0:T(2,128)S(1)}, s32[4,2,2]{2,1,0:T(2,128)}, u32[]{:S(2)}) copy-start(s32[4,2,2]{2,1,0:T(2,128)} %constant.23.clone.places) | copy-start | bytes 196
  54.7 4.8 %collective-permute-start.7 = (f16[256,256]{1,0:T(8,128)(2,1)S(1)}, f16[256,256]{1,0:T(8,128)(2,1)S(1)}, u32[]{:S(2)}, u32[]{:S(2)}) collective-permute-start(f16[256,256]{1,0:T(8,128)(2,1)S(1)} %convert_element_type.52), channel_id=1, source_target_pairs={{4,4},{5,2},{6,5},{7,6},{10,11},{11,13},{8,10},{9,9},{20,20},{21,1... | collective-permute-start | bytes 393224 | tf_op jit(solution)/shard_map/ppermute | solution.py:237
  61.5 7.6 %collective-permute-start.9 = (f32[2,256,256]{2,1,0:T(8,128)S(1)}, f32[2,256,256]{2,1,0:T(8,128)S(1)}, u32[]{:S(2)}, u32[]{:S(2)}) collective-permute-start(f32[2,256,256]{2,1,0:T(8,128)S(1)} %get-tuple-element.43), channel_id=1, source_target_pairs={{4,5},{5,4},{8,9},{9,8},{6,7},{7,6},{10,11},{11,10},{20,21},{21,20... | collective-permute-start | bytes 1572872 | tf_op jit(solution)/shard_map/ppermute | solution.py:234
  66.4 8.2 %collective-permute-start.15 = (f16[256,256]{1,0:T(8,128)(2,1)S(1)}, f16[256,256]{1,0:T(8,128)(2,1)S(1)}, u32[]{:S(2)}, u32[]{:S(2)}) collective-permute-start(f16[256,256]{1,0:T(8,128)(2,1)S(1)} %convert_element_type.66), channel_id=1, source_target_pairs={{4,0},{5,10},{6,1},{7,8},{10,15},{11,5},{8,14},{9,7},{20,16},{21,2... | collective-permute-start | bytes 393224 | tf_op jit(solution)/shard_map/ppermute | solution.py:237
  67.7 14.0 %collective-permute-start.14 = (f16[256,256]{1,0:T(8,128)(2,1)S(1)}, f16[256,256]{1,0:T(8,128)(2,1)S(1)}, u32[]{:S(2)}, u32[]{:S(2)}) collective-permute-start(f16[256,256]{1,0:T(8,128)(2,1)S(1)} %convert_element_type.64), channel_id=1, source_target_pairs={{4,1},{5,8},{6,0},{7,10},{10,14},{11,7},{8,15},{9,5},{20,17},{21,2... | collective-permute-start | bytes 393224 | tf_op jit(solution)/shard_map/ppermute | solution.py:237
  70.0 11.8 %collective-permute-start.13 = (f16[256,256]{1,0:T(8,128)(2,1)S(1)}, f16[256,256]{1,0:T(8,128)(2,1)S(1)}, u32[]{:S(2)}, u32[]{:S(2)}) collective-permute-start(f16[256,256]{1,0:T(8,128)(2,1)S(1)} %convert_element_type.62), channel_id=1, source_target_pairs={{4,12},{5,14},{6,13},{7,15},{10,3},{11,1},{8,2},{9,0},{20,28},{21,... | collective-permute-start | bytes 393224 | tf_op jit(solution)/shard_map/ppermute | solution.py:237
  71.3 10.4 %collective-permute-start.12 = (f16[256,256]{1,0:T(8,128)(2,1)S(1)}, f16[256,256]{1,0:T(8,128)(2,1)S(1)}, u32[]{:S(2)}, u32[]{:S(2)}) collective-permute-start(f16[256,256]{1,0:T(8,128)(2,1)S(1)} %convert_element_type.60), channel_id=1, source_target_pairs={{4,13},{5,15},{6,12},{7,14},{10,2},{11,0},{8,3},{9,1},{20,29},{21,... | collective-permute-start | bytes 393224 | tf_op jit(solution)/shard_map/ppermute | solution.py:237
  72.6 9.1 %collective-permute-start.11 = (f16[256,256]{1,0:T(8,128)(2,1)S(1)}, f16[256,256]{1,0:T(8,128)(2,1)S(1)}, u32[]{:S(2)}, u32[]{:S(2)}) collective-permute-start(f16[256,256]{1,0:T(8,128)(2,1)S(1)} %convert_element_type.58), channel_id=1, source_target_pairs={{4,3},{5,11},{6,7},{7,9},{10,12},{11,4},{8,8},{9,6},{20,19},{21,27... | collective-permute-start | bytes 393224 | tf_op jit(solution)/shard_map/ppermute | solution.py:237
  74.6 9.0 %collective-permute-start.10 = (f16[256,256]{1,0:T(8,128)(2,1)S(1)}, f16[256,256]{1,0:T(8,128)(2,1)S(1)}, u32[]{:S(2)}, u32[]{:S(2)}) collective-permute-start(f16[256,256]{1,0:T(8,128)(2,1)S(1)} %convert_element_type.56), channel_id=1, source_target_pairs={{4,7},{5,9},{6,3},{7,11},{10,8},{11,6},{8,12},{9,4},{20,23},{21,25... | collective-permute-start | bytes 393224 | tf_op jit(solution)/shard_map/ppermute | solution.py:237

commit v9 on v8

--- a/solution.py
+++ b/solution.py
@@ -34,18 +34,20 @@
 
 
 NEAR_ROUNDS = (
-    (((1, 0), (1, 1)), ((0, 2), (1, 2))),
-    (((1, 1), (1, 0)), ((1, 2), (0, 2))),
+    (((0, 0), (0, 1)), ((0, 2), (1, 2))),
+    (((0, 1), (0, 0)), ((1, 2), (0, 2))),
+    (((1, 0), (1, 1)), (None, None)),
+    (((1, 1), (1, 0)), (None, None)),
 )
 FAR_ROUNDS = (
-    (((0, 0), (0, 1)), ((2, 2), (2, 0))),
-    (((0, 1), (0, 0)), ((2, 0), (2, 2))),
+    ((None, None), ((2, 0), (2, 2))),
+    ((None, None), ((2, 2), (2, 0))),
 )
 LATE_ROUNDS = (
+    (((1, 3), (0, 3)), ((2, 1), (2, 3))),
+    (((0, 3), (1, 3)), ((2, 3), (2, 1))),
+    (((3, 1), (3, 0)), ((3, 3), (3, 2))),
     (((3, 0), (3, 1)), ((3, 2), (3, 3))),
-    (((3, 1), (3, 0)), ((3, 3), (3, 2))),
-    (((0, 3), (1, 3)), ((2, 3), (2, 1))),
-    (((1, 3), (0, 3)), ((2, 1), (2, 3))),
 )
 EARLY_SUMS = (((0, 0), (0, 1), (1, 1)), ((2, 2), (2, 0), (2, 1)))
 EARLY_HELD = (
@@ -58,13 +60,12 @@
     ((3, 0), (3, 1), (0, 3), (1, 3), (1, 1)),
     ((3, 2), (3, 3), (2, 3), (3, 3), (2, 1)),
 )
-EXTRA = 16
-HEAD = 48
 VMEM = pl.BlockSpec(memory_space=pltpu.VMEM)
 SMEM = pl.BlockSpec(memory_space=pltpu.SMEM)
 ANY = pl.BlockSpec(memory_space=pl.ANY)
 LIMIT = pltpu.CompilerParams(vmem_limit_bytes=40 * 2**20)
 BRIEF = pl.CostEstimate(flops=1024, bytes_accessed=1024, transcendentals=0)
+LONG = pl.CostEstimate(flops=3 * 2**31, bytes_accessed=1024, transcendentals=0)
 
 
 def device_index(row, col, half):
@@ -92,59 +93,41 @@
     ]
 
 
-def far_kernel(bits, values, far, sem):
+def split_kernel(bits, values, near, far, far_sum, sems):
     part = far.shape[1]
-    columns = pl.ds(pl.multiple_of(bits[0] * part, 128), part)
-    copy = pltpu.make_async_copy(values.at[:, columns], far, sem)
-    copy.start()
-    copy.wait()
-
-
-def near_kernel(bits, values, far, near, head, tail, sums, sems):
-    rows, part = far.shape
     step = 512
-    near_columns = pl.ds(pl.multiple_of((1 - bits[0]) * part, 128), part)
-    copies = [
-        pltpu.make_async_copy(values.at[:, near_columns], near, sems.at[0]),
-        pltpu.make_async_copy(
-            far.at[pl.ds(0, HEAD), :], head.at[pl.ds(EXTRA, HEAD), :], sems.at[1]
-        ),
-    ]
-    from_rows = far.at[pl.ds(HEAD, rows - HEAD), :]
-    copies.append(pltpu.make_async_copy(from_rows, tail, sems.at[2]))
+    copies = []
+    for i, (out, start) in enumerate(((far, bits[0]), (near, 1 - bits[0]))):
+        columns = pl.ds(pl.multiple_of(start * part, 128), part)
+        copies.append(pltpu.make_async_copy(values.at[:, columns], out, sems.at[i]))
     for copy in copies:
         copy.start()
+    copies[0].wait()
 
     @pl.loop(0, part // step)
     def _(j):
         columns = pl.ds(pl.multiple_of(j * step, step), step)
-        left = jnp.sum(far[:, columns].astype(jnp.float32), axis=0, keepdims=True)
-        for i in range(3):
-            piece = left.astype(jnp.bfloat16).astype(jnp.float32)
-            sums[pl.ds(i, 1), columns] = piece
-            left = left - piece
-        sums[pl.ds(3, EXTRA - 3), columns] = jnp.zeros((EXTRA - 3, step), jnp.float32)
-
-    head[pl.ds(0, EXTRA), :] = sums[...].astype(jnp.bfloat16)
-    for copy in copies:
-        copy.wait()
+        block = far[:, columns].astype(jnp.float32)
+        far_sum[:, columns] = jnp.sum(block, axis=0, keepdims=True)
+
+    copies[1].wait()
 
 
 def block_product(left, right):
     return lax.dot_general(left, right, (((1,), (1,)), ((), ())), preferred_element_type=jnp.float32)
 
 
-def sum_kernel(other, near, partial):
+def sum_kernel(other, near, far_sum, partial):
     step = 512
 
     @pl.loop(0, near.shape[1] // step)
     def _(n):
         columns = pl.ds(pl.multiple_of(n * step, step), step)
         rows = other[:, columns].astype(jnp.float32) + near[:, columns].astype(jnp.float32)
-        partial[:, columns] = jnp.sum(rows, axis=0, keepdims=True)
-
-
-def early_kernel(bits, other, edge, head, near, partial, centred, mean, own, *rest):
+        partial[:, columns] = far_sum[:, columns] + jnp.sum(rows, axis=0, keepdims=True)
+
+
+def early_kernel(bits, other, edge, near, partial, centred, mean, own, *rest):
     sends, both = rest[:-1], rest[-1]
     rows, part = near.shape
     step = 512
@@ -153,9 +136,7 @@
     def _(n):
         columns = pl.ds(pl.multiple_of(n * step, step), step)
         values = [block[:, columns].astype(jnp.float32) for block in (edge, near, other)]
-        pieces = head[pl.ds(0, EXTRA), columns].astype(jnp.float32)
-        total = partial[:, columns] + jnp.sum(pieces, axis=0, keepdims=True)
-        total = total + jnp.sum(values[0], axis=0, keepdims=True)
+        total = partial[:, columns] + jnp.sum(values[0], axis=0, keepdims=True)
         average = total * (1.0 / (4 * rows))
         mean[:, columns] = average
         for i in range(3):
@@ -169,14 +150,10 @@
         send[...] = both[1 - bits[1], pl.ds(place, 1), :, :]
 
 
-def late_kernel(bits, head, tail, mean, centred, *rest):
+def late_kernel(bits, far_edge, mean, centred, *rest):
     own, send = rest[len(rest) // 2 - 2 : len(rest) // 2]
     last, both = rest[-2:]
-    rows = last.shape[0]
-    first = head[pl.ds(EXTRA, HEAD), :].astype(jnp.float32) - mean[...]
-    last[pl.ds(0, HEAD), :] = first.astype(jnp.bfloat16)
-    second = tail[...].astype(jnp.float32) - mean[...]
-    last[pl.ds(HEAD, rows - HEAD), :] = second.astype(jnp.bfloat16)
+    last[...] = (far_edge[...].astype(jnp.float32) - mean[...]).astype(jnp.bfloat16)
     for core in (0, 1):
         for place, (_, j) in enumerate(LATE_SUMS[core]):
             both[core, place] = block_product(last[...], last[...] if j == 3 else centred[j])
@@ -236,40 +213,32 @@
     def send(value, blocks):
         return lax.ppermute(value.astype(jnp.float16), everyone, round_pairs(blocks))
 
-    far = pl.pallas_call(
-        far_kernel,
-        out_shape=shape_of((local_rows, part), jnp.bfloat16),
-        in_specs=[SMEM, ANY],
-        out_specs=VMEM,
-        scratch_shapes=[pltpu.SemaphoreType.DMA],
-        compiler_params=LIMIT,
-        cost_estimate=BRIEF,
-    )(bits, log_derivs)
-    near, head, tail = pl.pallas_call(
-        near_kernel,
+    near, far, far_sum = pl.pallas_call(
+        split_kernel,
         out_shape=[
             shape_of((local_rows, part), jnp.bfloat16),
-            shape_of((EXTRA + HEAD, part), jnp.bfloat16),
-            shape_of((local_rows - HEAD, part), jnp.bfloat16),
+            shape_of((local_rows, part), jnp.bfloat16),
+            shape_of((1, part), jnp.float32),
         ],
-        in_specs=[SMEM, ANY, VMEM],
+        in_specs=[SMEM, ANY],
         out_specs=[VMEM] * 3,
-        scratch_shapes=[pltpu.VMEM((EXTRA, part), jnp.float32), pltpu.SemaphoreType.DMA((3,))],
-        compiler_params=LIMIT,
-        cost_estimate=BRIEF,
-    )(bits, log_derivs, far)
+        scratch_shapes=[pltpu.SemaphoreType.DMA((2,))],
+        compiler_params=LIMIT,
+        cost_estimate=BRIEF,
+    )(bits, log_derivs)
     from_centre = lax.ppermute(far, "row", to_centre)
+    from_sum = lax.ppermute(far_sum, "row", to_far)
     from_edge = lax.ppermute(near, "row", to_own)
-    from_head = lax.ppermute(head, "row", to_far)
-    from_tail = lax.ppermute(tail, "row", to_far)
+    from_far_edge = lax.ppermute(far, "row", to_far)
 
     partial = pl.pallas_call(
         sum_kernel,
         out_shape=shape_of((1, part), jnp.float32),
-        in_specs=[VMEM] * 2,
+        in_specs=[VMEM] * 3,
         out_specs=VMEM,
         compiler_params=LIMIT,
-    )(from_centre, near)
+        cost_estimate=LONG,
+    )(from_centre, near, from_sum)
     early_blocks = (3, local_rows, local_rows)
     centred, mean, own, *others = pl.pallas_call(
         early_kernel,
@@ -279,12 +248,12 @@
             shape_of(early_blocks, jnp.float32),
         ]
         + [shape_of((1, local_rows, local_rows), jnp.float32)] * 3,
-        in_specs=[SMEM] + [VMEM] * 5,
+        in_specs=[SMEM] + [VMEM] * 4,
         out_specs=[VMEM] * 6,
         scratch_shapes=[pltpu.VMEM((2,) + early_blocks, jnp.float32)],
         compiler_params=LIMIT,
         cost_estimate=BRIEF,
-    )(bits, from_centre, from_edge, from_head, near, partial)
+    )(bits, from_centre, from_edge, near, partial)
     others = [swap(other) for other in others]
     places = held_place(EARLY_HELD, NEAR_ROUNDS + FAR_ROUNDS) + [[[SPARE] * 2] * 2]
     *early, spare = combine(bits, own, others, (1, 2), (), EARLY_HELD, places, samples)
@@ -298,16 +267,16 @@
         late_kernel,
         out_shape=[late_blocks, late_blocks]
         + [shape_of(value.shape, value.dtype) for value in handed],
-        in_specs=[SMEM] + [VMEM] * 4 + [ANY] * len(handed),
+        in_specs=[SMEM] + [VMEM] * 3 + [ANY] * len(handed),
         out_specs=[VMEM] * 2 + [ANY] * len(handed),
         scratch_shapes=[
             pltpu.VMEM((local_rows, part), jnp.bfloat16),
             pltpu.VMEM((2,) + late_blocks.shape, jnp.float32),
         ],
-        input_output_aliases={5 + i: 2 + i for i in range(len(handed))},
-        compiler_params=LIMIT,
-        cost_estimate=BRIEF,
-    )(bits, from_head, from_tail, mean, centred, *handed)
+        input_output_aliases={4 + i: 2 + i for i in range(len(handed))},
+        compiler_params=LIMIT,
+        cost_estimate=BRIEF,
+    )(bits, from_far_edge, mean, centred, *handed)
     other = swap(other)
     arrived = [send(value, blocks) for value, blocks in zip(far_blocks, FAR_ROUNDS)]
     places = held_place(LATE_HELD, LATE_ROUNDS)

time: 85.9 us -> 83.6 us (0.973)
  waiting for transfers between devices: 36.5 us -> 30.5 us
  starting transfers between devices: 34.8 us -> 39.5 us
  Pallas kernels: 9.41 us -> 8.43 us
    ppermute x1, waiting for transfers between devices: 18.1 us -> 0.01 us  [two_centres(): from_centre = lax.ppermute(far, 'row', to_centre)]
    ppermute x2, waiting for transfers between devices: 11 us -> 25.1 us  [the longest x1 24.1 us: two_centres(): from_sum = lax.ppermute(far_sum, 'row', to_far)]
    ppermute x4, starting transfers between devices: 11.1 us -> 14.1 us  [swap(): return lax.ppermute(value, ('row', 'half'), centres)]
    ppermute x8 -> x10, waiting for transfers between devices: 5.9 us -> 3.73 us  [send(): lax.ppermute(value.astype(jnp.float16), everyone, round_pairs(blocks))]
    ppermute x8 -> x10, starting transfers between devices: 16.3 us -> 18 us  [send(): lax.ppermute(value.astype(jnp.float16), everyone, round_pairs(blocks))]
    pallas_call x2 -> x1, Pallas kernels: 1.95 us -> 0.89 us  [two_centres(): pl.pallas_call(split_kernel, out_shape=[shape_of((local_rows, part), jnp....]
  transfers between devices with their start and end apart: 16 -> 18, of which waited for: 5 -> 8; matrix products, arithmetic and copies ran while one was open for 0% -> 0% of each run, Pallas kernels for 8% -> 7%
where the time goes in v9:
time: 83.6 us; the launch traced here: 82.1 us
  starting transfers between devices  39.5 us (47%)
  waiting for transfers between devices  30.5 us (36%)
  Pallas kernels  8.43 us (10%)
  local copies, waits for them, and re-layouts  1.61 us (2%)
  other arithmetic  1.15 us (1%)
  between operations  1.01 us (1%)
    ppermute x1, waiting for transfers between devices, two_centres(): from_sum = lax.ppermute(far_sum, 'row', to_far)  24.1 us
    ppermute x10, starting transfers between devices, send(): lax.ppermute(value.astype(jnp.float16), everyone, round_pairs(blocks))  18 us
    ppermute x4, starting transfers between devices, swap(): return lax.ppermute(value, ('row', 'half'), centres)  14.1 us
    ppermute x10, waiting for transfers between devices, send(): lax.ppermute(value.astype(jnp.float16), everyone, round_pairs(blocks))  3.73 us
    ppermute x1, starting transfers between devices, two_centres(): from_centre = lax.ppermute(far, 'row', to_centre)  3.48 us
    pallas_call x1, Pallas kernels, two_centres(): pl.pallas_call(early_kernel, out_shape=[shape_of((3, local_rows, part), j...  3.3 us
    pallas_call x2, Pallas kernels, combine(): pl.pallas_call(functools.partial(combine_kernel, flips, 1.0 / samples, le...  1.89 us
    pallas_call x1, Pallas kernels, two_centres(): pl.pallas_call(late_kernel, out_shape=[late_blocks, late_blocks] + [shape...  1.89 us
  transfers between devices with their start and end apart: 18, of which 8 were waited for; matrix products, arithmetic and copies ran while one was open for 0% of the time, Pallas kernels for 7%

profile of v9, /device:TPU:8, one launch (start us, length us, event | category | flops | bytes accessed | tf_op | source)
XLA Modules:
  0.0 82.1 jit_solution(925689339297119087)
XLA Ops:
  0.1 1.6 %copy-done = bf16[256,4096]{1,0:T(8,128)(2,1)S(1)} copy-done((bf16[256,4096]{1,0:T(8,128)(2,1)S(1)}, bf16[256,4096]{1,0:T(8,128)(2,1)}, u32[]{:S(2)}) %copy-start) | copy-done | bytes 2097176
  2.6 3.5 %collective-permute-start.1 = (bf16[256,2048]{1,0:T(8,128)(2,1)S(1)}, bf16[256,2048]{1,0:T(8,128)(2,1)S(1)}, u32[]{:S(2)}, u32[]{:S(2)}) collective-permute-start(bf16[256,2048]{1,0:T(8,128)(2,1)S(1)} %get-tuple-element.30), channel_id=1, source_target_pairs={{4,8},{8,4},{5,9},{9,5},{6,10},{10,6},{7,11},{11,7},{20,24},{24,20... | collective-permute-start | bytes 3145736 | tf_op jit(solution)/shard_map/ppermute | solution.py:229
  6.1 1.3 %collective-permute-start.2 = (bf16[256,2048]{1,0:T(8,128)(2,1)S(1)}, bf16[256,2048]{1,0:T(8,128)(2,1)S(1)}, u32[]{:S(2)}, u32[]{:S(2)}) collective-permute-start(bf16[256,2048]{1,0:T(8,128)(2,1)S(1)} %get-tuple-element.31.near), channel_id=1, source_target_pairs={{0,4},{12,8},{1,5},{13,9},{2,6},{14,10},{3,7},{15,11},{16,20},{28,... | collective-permute-start | bytes 3145736 | tf_op jit(solution)/shard_map/ppermute | solution.py:231
  7.4 1.3 %collective-permute-start.3 = (f32[1,2048]{1,0:T(1,128)S(1)}, f32[1,2048]{1,0:T(1,128)S(1)}, u32[]{:S(2)}, u32[]{:S(2)}) collective-permute-start(f32[1,2048]{1,0:T(1,128)S(1)} %get-tuple-element.32), channel_id=1, source_target_pairs={{0,8},{12,4},{1,9},{13,5},{2,10},{14,6},{3,11},{15,7},{16,24},{28,... | collective-permute-start | bytes 24584 | tf_op jit(solution)/shard_map/ppermute | solution.py:230
  8.7 1.3 %collective-permute-start = (bf16[256,2048]{1,0:T(8,128)(2,1)S(1)}, bf16[256,2048]{1,0:T(8,128)(2,1)S(1)}, u32[]{:S(2)}, u32[]{:S(2)}) collective-permute-start(bf16[256,2048]{1,0:T(8,128)(2,1)S(1)} %get-tuple-element.30), channel_id=1, source_target_pairs={{0,8},{12,4},{1,9},{13,5},{2,10},{14,6},{3,11},{15,7},{16,24},{28,... | collective-permute-start | bytes 3145736 | tf_op jit(solution)/shard_map/ppermute | solution.py:232
  10.0 24.1 %collective-permute-done.3.far_sum = f32[1,2048]{1,0:T(1,128)S(1)} collective-permute-done((f32[1,2048]{1,0:T(1,128)S(1)}, f32[1,2048]{1,0:T(1,128)S(1)}, u32[]{:S(2)}, u32[]{:S(2)}) %collective-permute-start.3) | collective-permute-done | bytes 8224 | tf_op jit(solution)/shard_map/ppermute | solution.py:230
  34.6 3.3 %shard_map.48 = (bf16[3,256,2048]{2,1,0:T(8,128)(2,1)S(1)}, f32[1,2048]{1,0:T(1,128)S(1)}, f32[3,256,256]{2,1,0:T(8,128)S(1)}, f32[1,256,256]{2,1,0:T(8,128)S(1)...) custom-call(s32[3]{0:T(128)S(1)} %pad_add_fusion.bits, bf16[256,2048]{1,0:T(8,128)(2,1)S(1)} %collective-permute-done.1.other, ...), custom_call_target="tpu_custom_call" | custom-call | flops 1024 | bytes 1024 | tf_op jit(solution)/shard_map/pallas_call | solution.py:243
  37.9 1.9 %collective-permute-start.4 = (f32[1,256,256]{2,1,0:T(8,128)S(1)}, f32[1,256,256]{2,1,0:T(8,128)S(1)}, u32[]{:S(2)}, u32[]{:S(2)}) collective-permute-start(f32[1,256,256]{2,1,0:T(8,128)S(1)} %get-tuple-element.36), channel_id=1, source_target_pairs={{4,5},{5,4},{8,9},{9,8},{6,7},{7,6},{10,11},{11,10},{20,21},{21,20... | collective-permute-start | bytes 786440 | tf_op jit(solution)/shard_map/ppermute | solution.py:211
  39.8 2.4 %collective-permute-start.5 = (f32[1,256,256]{2,1,0:T(8,128)S(1)}, f32[1,256,256]{2,1,0:T(8,128)S(1)}, u32[]{:S(2)}, u32[]{:S(2)}) collective-permute-start(f32[1,256,256]{2,1,0:T(8,128)S(1)} %get-tuple-element.37), channel_id=1, source_target_pairs={{4,5},{5,4},{8,9},{9,8},{6,7},{7,6},{10,11},{11,10},{20,21},{21,20... | collective-permute-start | bytes 786440 | tf_op jit(solution)/shard_map/ppermute | solution.py:211
  42.2 1.9 %collective-permute-start.6 = (f32[1,256,256]{2,1,0:T(8,128)S(1)}, f32[1,256,256]{2,1,0:T(8,128)S(1)}, u32[]{:S(2)}, u32[]{:S(2)}) collective-permute-start(f32[1,256,256]{2,1,0:T(8,128)S(1)} %get-tuple-element.38), channel_id=1, source_target_pairs={{4,5},{5,4},{8,9},{9,8},{6,7},{7,6},{10,11},{11,10},{20,21},{21,20... | collective-permute-start | bytes 786440 | tf_op jit(solution)/shard_map/ppermute | solution.py:211
  44.2 1.5 %collective-permute-done.6.rest_2_ = f32[1,256,256]{2,1,0:T(8,128)S(1)} collective-permute-done((f32[1,256,256]{2,1,0:T(8,128)S(1)}, f32[1,256,256]{2,1,0:T(8,128)S(1)}, u32[]{:S(2)}, u32[]{:S(2)}) %collective-permute-start.6) | collective-permute-done | bytes 262176 | tf_op jit(solution)/shard_map/ppermute | solution.py:211
  45.7 1.0 %shard_map.49 = (f32[256,256]{1,0:T(8,128)S(1)}, f32[256,256]{1,0:T(8,128)S(1)}, f32[256,256]{1,0:T(8,128)S(1)}, f32[256,256]{1,0:T(8,128)S(1)}, f32[256,256]{1,...) custom-call(s32[3]{0:T(128)S(1)} %pad_add_fusion.bits, s32[7,2,2]{2,1,0:T(2,128)S(1)} %copy-done.1, ...), custom_call_target="tpu_custom_call" | custom-call | flops 1024 | bytes 1024 | tf_op jit(solution)/shard_map/pallas_call | solution.py:185
  46.7 2.0 %collective-permute-start.10 = (f16[256,256]{1,0:T(8,128)(2,1)S(1)}, f16[256,256]{1,0:T(8,128)(2,1)S(1)}, u32[]{:S(2)}, u32[]{:S(2)}) collective-permute-start(f16[256,256]{1,0:T(8,128)(2,1)S(1)} %convert_element_type.70), channel_id=1, source_target_pairs={{4,5},{6,4},{10,10},{8,11},{20,21},{22,20},{26,26},{24,27}} | collective-permute-start | bytes 393224 | tf_op jit(solution)/shard_map/ppermute | solution.py:214
  48.8 1.3 %collective-permute-start.7 = (f16[256,256]{1,0:T(8,128)(2,1)S(1)}, f16[256,256]{1,0:T(8,128)(2,1)S(1)}, u32[]{:S(2)}, u32[]{:S(2)}) collective-permute-start(f16[256,256]{1,0:T(8,128)(2,1)S(1)} %convert_element_type.64), channel_id=1, source_target_pairs={{4,0},{5,2},{6,1},{7,6},{10,15},{11,13},{8,14},{9,9},{20,16},{21,1... | collective-permute-start | bytes 393224 | tf_op jit(solution)/shard_map/ppermute | solution.py:214
  50.1 1.3 %collective-permute-start.8 = (f16[256,256]{1,0:T(8,128)(2,1)S(1)}, f16[256,256]{1,0:T(8,128)(2,1)S(1)}, u32[]{:S(2)}, u32[]{:S(2)}) collective-permute-start(f16[256,256]{1,0:T(8,128)(2,1)S(1)} %convert_element_type.66), channel_id=1, source_target_pairs={{4,1},{5,6},{6,0},{7,2},{10,14},{11,9},{8,15},{9,13},{20,17},{21,2... | collective-permute-start | bytes 393224 | tf_op jit(solution)/shard_map/ppermute | solution.py:214
  52.1 1.4 %collective-permute-done.10 = f16[256,256]{1,0:T(8,128)(2,1)S(1)} collective-permute-done((f16[256,256]{1,0:T(8,128)(2,1)S(1)}, f16[256,256]{1,0:T(8,128)(2,1)S(1)}, u32[]{:S(2)}, u32[]{:S(2)}) %collective-permute-start.10) | collective-permute-done | bytes 131104 | tf_op jit(solution)/shard_map/ppermute | solution.py:214
  54.1 1.0 %collective-permute-done.far_edge = bf16[256,2048]{1,0:T(8,128)(2,1)S(1)} collective-permute-done((bf16[256,2048]{1,0:T(8,128)(2,1)S(1)}, bf16[256,2048]{1,0:T(8,128)(2,1)S(1)}, u32[]{:S(2)}, u32[]{:S(2)}) %collective-permute-start) | collective-permute-done | bytes 1048608 | tf_op jit(solution)/shard_map/ppermute | solution.py:232
  55.1 1.9 %shard_map.50 = (f32[2,256,256]{2,1,0:T(8,128)S(1)}, f32[2,256,256]{2,1,0:T(8,128)S(1)}, f32[256,256]{1,0:T(8,128)S(1)}, f32[256,256]{1,0:T(8,128)S(1)}, f32[256,256]{1,0:T(8,128)S(1)}) custom-call(s32[3]{0:T(128)S(1)} %pad_add_fusion.bits, ...), custom_call_target="tpu_custom_call", output_to_operand_aliasing={{2}: (4, {}), {3}: (5, {}), {4}: (6, {})} | custom-call | flops 1024 | bytes 1024 | tf_op jit(solution)/shard_map/pallas_call | solution.py:266
  57.0 7.9 %collective-permute-start.11 = (f32[2,256,256]{2,1,0:T(8,128)S(1)}, f32[2,256,256]{2,1,0:T(8,128)S(1)}, u32[]{:S(2)}, u32[]{:S(2)}) collective-permute-start(f32[2,256,256]{2,1,0:T(8,128)S(1)} %get-tuple-element.47), channel_id=1, source_target_pairs={{4,5},{5,4},{8,9},{9,8},{6,7},{7,6},{10,11},{11,10},{20,21},{21,20... | collective-permute-start | bytes 1572872 | tf_op jit(solution)/shard_map/ppermute | solution.py:211
  67.3 1.3 %collective-permute-start.12 = (f16[256,256]{1,0:T(8,128)(2,1)S(1)}, f16[256,256]{1,0:T(8,128)(2,1)S(1)}, u32[]{:S(2)}, u32[]{:S(2)}) collective-permute-start(f16[256,256]{1,0:T(8,128)(2,1)S(1)} %convert_element_type.72), channel_id=1, source_target_pairs={{4,12},{5,14},{6,13},{7,15},{10,3},{11,1},{8,2},{9,0},{20,28},{21,... | collective-permute-start | bytes 393224 | tf_op jit(solution)/shard_map/ppermute | solution.py:214
  68.7 1.3 %collective-permute-start.13 = (f16[256,256]{1,0:T(8,128)(2,1)S(1)}, f16[256,256]{1,0:T(8,128)(2,1)S(1)}, u32[]{:S(2)}, u32[]{:S(2)}) collective-permute-start(f16[256,256]{1,0:T(8,128)(2,1)S(1)} %convert_element_type.74), channel_id=1, source_target_pairs={{4,13},{5,15},{6,12},{7,14},{10,2},{11,0},{8,3},{9,1},{20,29},{21,... | collective-permute-start | bytes 393224 | tf_op jit(solution)/shard_map/ppermute | solution.py:214
  70.0 1.9 %collective-permute-start.14 = (f16[256,256]{1,0:T(8,128)(2,1)S(1)}, f16[256,256]{1,0:T(8,128)(2,1)S(1)}, u32[]{:S(2)}, u32[]{:S(2)}) collective-permute-start(f16[256,256]{1,0:T(8,128)(2,1)S(1)} %convert_element_type.76), channel_id=1, source_target_pairs={{4,3},{5,11},{6,7},{7,9},{10,12},{11,4},{8,8},{9,6},{20,19},{21,27... | collective-permute-start | bytes 393224 | tf_op jit(solution)/shard_map/ppermute | solution.py:214
  72.0 6.8 %collective-permute-start.15 = (f16[256,256]{1,0:T(8,128)(2,1)S(1)}, f16[256,256]{1,0:T(8,128)(2,1)S(1)}, u32[]{:S(2)}, u32[]{:S(2)}) collective-permute-start(f16[256,256]{1,0:T(8,128)(2,1)S(1)} %convert_element_type.78), channel_id=1, source_target_pairs={{4,7},{5,9},{6,3},{7,11},{10,8},{11,6},{8,12},{9,4},{20,23},{21,25... | collective-permute-start | bytes 393224 | tf_op jit(solution)/shard_map/ppermute | solution.py:214
  80.0 1.3 %collective-permute-done.15 = f16[256,256]{1,0:T(8,128)(2,1)S(1)} collective-permute-done((f16[256,256]{1,0:T(8,128)(2,1)S(1)}, f16[256,256]{1,0:T(8,128)(2,1)S(1)}, u32[]{:S(2)}, u32[]{:S(2)}) %collective-permute-start.15) | collective-permute-done | bytes 131104 | tf_op jit(solution)/shard_map/ppermute | solution.py:214
  (38 shorter events, 6.5 us)
Async XLA Ops:
  0.1 1.6 %copy-start = (bf16[256,4096]{1,0:T(8,128)(2,1)S(1)}, bf16[256,4096]{1,0:T(8,128)(2,1)}, u32[]{:S(2)}) copy-start(bf16[256,4096]{1,0:T(8,128)(2,1)} %values.1) | copy-start | bytes 6291460
  2.6 31.5 %collective-permute-start.1 = (bf16[256,2048]{1,0:T(8,128)(2,1)S(1)}, bf16[256,2048]{1,0:T(8,128)(2,1)S(1)}, u32[]{:S(2)}, u32[]{:S(2)}) collective-permute-start(bf16[256,2048]{1,0:T(8,128)(2,1)S(1)} %get-tuple-element.30), channel_id=1, source_target_pairs={{4,8},{8,4},{5,9},{9,5},{6,10},{10,6},{7,11},{11,7},{20,24},{24,20... | collective-permute-start | bytes 3145736 | tf_op jit(solution)/shard_map/ppermute | solution.py:229
  6.1 28.5 %collective-permute-start.2 = (bf16[256,2048]{1,0:T(8,128)(2,1)S(1)}, bf16[256,2048]{1,0:T(8,128)(2,1)S(1)}, u32[]{:S(2)}, u32[]{:S(2)}) collective-permute-start(bf16[256,2048]{1,0:T(8,128)(2,1)S(1)} %get-tuple-element.31.near), channel_id=1, source_target_pairs={{0,4},{12,8},{1,5},{13,9},{2,6},{14,10},{3,7},{15,11},{16,20},{28,... | collective-permute-start | bytes 3145736 | tf_op jit(solution)/shard_map/ppermute | solution.py:231
  7.4 26.7 %collective-permute-start.3 = (f32[1,2048]{1,0:T(1,128)S(1)}, f32[1,2048]{1,0:T(1,128)S(1)}, u32[]{:S(2)}, u32[]{:S(2)}) collective-permute-start(f32[1,2048]{1,0:T(1,128)S(1)} %get-tuple-element.32), channel_id=1, source_target_pairs={{0,8},{12,4},{1,9},{13,5},{2,10},{14,6},{3,11},{15,7},{16,24},{28,... | collective-permute-start | bytes 24584 | tf_op jit(solution)/shard_map/ppermute | solution.py:230
  8.7 46.4 %collective-permute-start = (bf16[256,2048]{1,0:T(8,128)(2,1)S(1)}, bf16[256,2048]{1,0:T(8,128)(2,1)S(1)}, u32[]{:S(2)}, u32[]{:S(2)}) collective-permute-start(bf16[256,2048]{1,0:T(8,128)(2,1)S(1)} %get-tuple-element.30), channel_id=1, source_target_pairs={{0,8},{12,4},{1,9},{13,5},{2,10},{14,6},{3,11},{15,7},{16,24},{28,... | collective-permute-start | bytes 3145736 | tf_op jit(solution)/shard_map/ppermute | solution.py:232
  34.6 11.1 %copy-start.1 = (s32[7,2,2]{2,1,0:T(2,128)S(1)}, s32[7,2,2]{2,1,0:T(2,128)}, u32[]{:S(2)}) copy-start(s32[7,2,2]{2,1,0:T(2,128)} %constant.22.clone.places) | copy-start | bytes 340
  37.9 6.3 %collective-permute-start.4 = (f32[1,256,256]{2,1,0:T(8,128)S(1)}, f32[1,256,256]{2,1,0:T(8,128)S(1)}, u32[]{:S(2)}, u32[]{:S(2)}) collective-permute-start(f32[1,256,256]{2,1,0:T(8,128)S(1)} %get-tuple-element.36), channel_id=1, source_target_pairs={{4,5},{5,4},{8,9},{9,8},{6,7},{7,6},{10,11},{11,10},{20,21},{21,20... | collective-permute-start | bytes 786440 | tf_op jit(solution)/shard_map/ppermute | solution.py:211
  39.8 4.4 %collective-permute-start.5 = (f32[1,256,256]{2,1,0:T(8,128)S(1)}, f32[1,256,256]{2,1,0:T(8,128)S(1)}, u32[]{:S(2)}, u32[]{:S(2)}) collective-permute-start(f32[1,256,256]{2,1,0:T(8,128)S(1)} %get-tuple-element.37), channel_id=1, source_target_pairs={{4,5},{5,4},{8,9},{9,8},{6,7},{7,6},{10,11},{11,10},{20,21},{21,20... | collective-permute-start | bytes 786440 | tf_op jit(solution)/shard_map/ppermute | solution.py:211
  42.2 3.4 %collective-permute-start.6 = (f32[1,256,256]{2,1,0:T(8,128)S(1)}, f32[1,256,256]{2,1,0:T(8,128)S(1)}, u32[]{:S(2)}, u32[]{:S(2)}) collective-permute-start(f32[1,256,256]{2,1,0:T(8,128)S(1)} %get-tuple-element.38), channel_id=1, source_target_pairs={{4,5},{5,4},{8,9},{9,8},{6,7},{7,6},{10,11},{11,10},{20,21},{21,20... | collective-permute-start | bytes 786440 | tf_op jit(solution)/shard_map/ppermute | solution.py:211
  46.7 6.9 %collective-permute-start.10 = (f16[256,256]{1,0:T(8,128)(2,1)S(1)}, f16[256,256]{1,0:T(8,128)(2,1)S(1)}, u32[]{:S(2)}, u32[]{:S(2)}) collective-permute-start(f16[256,256]{1,0:T(8,128)(2,1)S(1)} %convert_element_type.70), channel_id=1, source_target_pairs={{4,5},{6,4},{10,10},{8,11},{20,21},{22,20},{26,26},{24,27}} | collective-permute-start | bytes 393224 | tf_op jit(solution)/shard_map/ppermute | solution.py:214
  48.8 4.8 %collective-permute-start.7 = (f16[256,256]{1,0:T(8,128)(2,1)S(1)}, f16[256,256]{1,0:T(8,128)(2,1)S(1)}, u32[]{:S(2)}, u32[]{:S(2)}) collective-permute-start(f16[256,256]{1,0:T(8,128)(2,1)S(1)} %convert_element_type.64), channel_id=1, source_target_pairs={{4,0},{5,2},{6,1},{7,6},{10,15},{11,13},{8,14},{9,9},{20,16},{21,1... | collective-permute-start | bytes 393224 | tf_op jit(solution)/shard_map/ppermute | solution.py:214
  50.1 3.9 %collective-permute-start.8 = (f16[256,256]{1,0:T(8,128)(2,1)S(1)}, f16[256,256]{1,0:T(8,128)(2,1)S(1)}, u32[]{:S(2)}, u32[]{:S(2)}) collective-permute-start(f16[256,256]{1,0:T(8,128)(2,1)S(1)} %convert_element_type.66), channel_id=1, source_target_pairs={{4,1},{5,6},{6,0},{7,2},{10,14},{11,9},{8,15},{9,13},{20,17},{21,2... | collective-permute-start | bytes 393224 | tf_op jit(solution)/shard_map/ppermute | solution.py:214
  51.4 15.0 %copy-start.2 = (s32[4,2,2]{2,1,0:T(2,128)S(1)}, s32[4,2,2]{2,1,0:T(2,128)}, u32[]{:S(2)}) copy-start(s32[4,2,2]{2,1,0:T(2,128)} %constant.23.clone.places) | copy-start | bytes 196
  51.5 2.6 %collective-permute-start.9 = (f16[256,256]{1,0:T(8,128)(2,1)S(1)}, f16[256,256]{1,0:T(8,128)(2,1)S(1)}, u32[]{:S(2)}, u32[]{:S(2)}) collective-permute-start(f16[256,256]{1,0:T(8,128)(2,1)S(1)} %convert_element_type.68), channel_id=1, source_target_pairs={{4,4},{6,5},{10,11},{8,10},{20,20},{22,21},{26,27},{24,26}} | collective-permute-start | bytes 393224 | tf_op jit(solution)/shard_map/ppermute | solution.py:214
  57.0 9.4 %collective-permute-start.11 = (f32[2,256,256]{2,1,0:T(8,128)S(1)}, f32[2,256,256]{2,1,0:T(8,128)S(1)}, u32[]{:S(2)}, u32[]{:S(2)}) collective-permute-start(f32[2,256,256]{2,1,0:T(8,128)S(1)} %get-tuple-element.47), channel_id=1, source_target_pairs={{4,5},{5,4},{8,9},{9,8},{6,7},{7,6},{10,11},{11,10},{20,21},{21,20... | collective-permute-start | bytes 1572872 | tf_op jit(solution)/shard_map/ppermute | solution.py:211
  64.9 7.0 %collective-permute-start.16 = (f16[256,256]{1,0:T(8,128)(2,1)S(1)}, f16[256,256]{1,0:T(8,128)(2,1)S(1)}, u32[]{:S(2)}, u32[]{:S(2)}) collective-permute-start(f16[256,256]{1,0:T(8,128)(2,1)S(1)} %convert_element_type.80), channel_id=1, source_target_pairs={{5,10},{7,8},{11,5},{9,7},{21,26},{23,24},{27,21},{25,23}} | collective-permute-start | bytes 393224 | tf_op jit(solution)/shard_map/ppermute | solution.py:214
  65.6 13.9 %collective-permute-start.17 = (f16[256,256]{1,0:T(8,128)(2,1)S(1)}, f16[256,256]{1,0:T(8,128)(2,1)S(1)}, u32[]{:S(2)}, u32[]{:S(2)}) collective-permute-start(f16[256,256]{1,0:T(8,128)(2,1)S(1)} %convert_element_type.82), channel_id=1, source_target_pairs={{5,8},{7,10},{11,7},{9,5},{21,24},{23,26},{27,23},{25,21}} | collective-permute-start | bytes 393224 | tf_op jit(solution)/shard_map/ppermute | solution.py:214
  67.3 12.2 %collective-permute-start.12 = (f16[256,256]{1,0:T(8,128)(2,1)S(1)}, f16[256,256]{1,0:T(8,128)(2,1)S(1)}, u32[]{:S(2)}, u32[]{:S(2)}) collective-permute-start(f16[256,256]{1,0:T(8,128)(2,1)S(1)} %convert_element_type.72), channel_id=1, source_target_pairs={{4,12},{5,14},{6,13},{7,15},{10,3},{11,1},{8,2},{9,0},{20,28},{21,... | collective-permute-start | bytes 393224 | tf_op jit(solution)/shard_map/ppermute | solution.py:214
  68.7 10.8 %collective-permute-start.13 = (f16[256,256]{1,0:T(8,128)(2,1)S(1)}, f16[256,256]{1,0:T(8,128)(2,1)S(1)}, u32[]{:S(2)}, u32[]{:S(2)}) collective-permute-start(f16[256,256]{1,0:T(8,128)(2,1)S(1)} %convert_element_type.74), channel_id=1, source_target_pairs={{4,13},{5,15},{6,12},{7,14},{10,2},{11,0},{8,3},{9,1},{20,29},{21,... | collective-permute-start | bytes 393224 | tf_op jit(solution)/shard_map/ppermute | solution.py:214
  70.0 10.0 %collective-permute-start.14 = (f16[256,256]{1,0:T(8,128)(2,1)S(1)}, f16[256,256]{1,0:T(8,128)(2,1)S(1)}, u32[]{:S(2)}, u32[]{:S(2)}) collective-permute-start(f16[256,256]{1,0:T(8,128)(2,1)S(1)} %convert_element_type.76), channel_id=1, source_target_pairs={{4,3},{5,11},{6,7},{7,9},{10,12},{11,4},{8,8},{9,6},{20,19},{21,27... | collective-permute-start | bytes 393224 | tf_op jit(solution)/shard_map/ppermute | solution.py:214
  72.0 9.4 %collective-permute-start.15 = (f16[256,256]{1,0:T(8,128)(2,1)S(1)}, f16[256,256]{1,0:T(8,128)(2,1)S(1)}, u32[]{:S(2)}, u32[]{:S(2)}) collective-permute-start(f16[256,256]{1,0:T(8,128)(2,1)S(1)} %convert_element_type.78), channel_id=1, source_target_pairs={{4,7},{5,9},{6,3},{7,11},{10,8},{11,6},{8,12},{9,4},{20,23},{21,25... | collective-permute-start | bytes 393224 | tf_op jit(solution)/shard_map/ppermute | solution.py:214

commit v10 on v9

--- a/solution.py
+++ b/solution.py
@@ -34,14 +34,12 @@
 
 
 NEAR_ROUNDS = (
-    (((0, 0), (0, 1)), ((0, 2), (1, 2))),
-    (((0, 1), (0, 0)), ((1, 2), (0, 2))),
-    (((1, 0), (1, 1)), (None, None)),
-    (((1, 1), (1, 0)), (None, None)),
+    (((1, 0), (1, 1)), ((0, 2), (1, 2))),
+    (((1, 1), (1, 0)), ((1, 2), (0, 2))),
 )
 FAR_ROUNDS = (
-    ((None, None), ((2, 0), (2, 2))),
-    ((None, None), ((2, 2), (2, 0))),
+    (((0, 0), (0, 1)), ((2, 2), (2, 0))),
+    (((0, 1), (0, 0)), ((2, 0), (2, 2))),
 )
 LATE_ROUNDS = (
     (((1, 3), (0, 3)), ((2, 1), (2, 3))),
@@ -150,15 +148,27 @@
         send[...] = both[1 - bits[1], pl.ds(place, 1), :, :]
 
 
+def late_products(core, last, centred, out):
+    for place, (_, j) in enumerate(LATE_SUMS[core]):
+        out[place] = block_product(last[...], last[...] if j == 3 else centred[j])
+
+
 def late_kernel(bits, far_edge, mean, centred, *rest):
-    own, send = rest[len(rest) // 2 - 2 : len(rest) // 2]
-    last, both = rest[-2:]
+    last, send = rest[(len(rest) - 2) // 2 :][:2]
     last[...] = (far_edge[...].astype(jnp.float32) - mean[...]).astype(jnp.bfloat16)
     for core in (0, 1):
-        for place, (_, j) in enumerate(LATE_SUMS[core]):
-            both[core, place] = block_product(last[...], last[...] if j == 3 else centred[j])
-    own[...] = both[bits[1]]
-    send[...] = both[1 - bits[1]]
+
+        @pl.when(bits[1] != core)
+        def _():
+            late_products(core, last, centred, send)
+
+
+def keep_kernel(bits, last, centred, own):
+    for core in (0, 1):
+
+        @pl.when(bits[1] == core)
+        def _():
+            late_products(core, last, centred, own)
 
 
 def combine_kernel(flips, scale, pieces, spares, bits, places, own, *rest):
@@ -263,20 +273,24 @@
 
     late_blocks = shape_of((2, local_rows, local_rows), jnp.float32)
     handed = [summed] + far_blocks
-    own, other, summed, *far_blocks = pl.pallas_call(
+    last, other, summed, *far_blocks = pl.pallas_call(
         late_kernel,
-        out_shape=[late_blocks, late_blocks]
+        out_shape=[shape_of((local_rows, part), jnp.bfloat16), late_blocks]
         + [shape_of(value.shape, value.dtype) for value in handed],
         in_specs=[SMEM] + [VMEM] * 3 + [ANY] * len(handed),
         out_specs=[VMEM] * 2 + [ANY] * len(handed),
-        scratch_shapes=[
-            pltpu.VMEM((local_rows, part), jnp.bfloat16),
-            pltpu.VMEM((2,) + late_blocks.shape, jnp.float32),
-        ],
         input_output_aliases={4 + i: 2 + i for i in range(len(handed))},
         compiler_params=LIMIT,
         cost_estimate=BRIEF,
     )(bits, from_far_edge, mean, centred, *handed)
+    own = pl.pallas_call(
+        keep_kernel,
+        out_shape=late_blocks,
+        in_specs=[SMEM] + [VMEM] * 2,
+        out_specs=VMEM,
+        compiler_params=LIMIT,
+        cost_estimate=BRIEF,
+    )(bits, last, centred)
     other = swap(other)
     arrived = [send(value, blocks) for value, blocks in zip(far_blocks, FAR_ROUNDS)]
     places = held_place(LATE_HELD, LATE_ROUNDS)

time: 83.6 us -> 81.2 us (0.971)
  starting transfers between devices: 39.5 us -> 34.9 us
  waiting for transfers between devices: 30.5 us -> 32 us
    ppermute x4, starting transfers between devices: 14.1 us -> 8.17 us  [swap(): return lax.ppermute(value, ('row', 'half'), centres)]
    ppermute x10 -> x8, waiting for transfers between devices: 3.73 us -> 6.35 us  [send(): lax.ppermute(value.astype(jnp.float16), everyone, round_pairs(blocks))]
    ppermute x10 -> x8, starting transfers between devices: 18 us -> 19.4 us  [send(): lax.ppermute(value.astype(jnp.float16), everyone, round_pairs(blocks))]
    ppermute x1, waiting for transfers between devices: 0.99 us -> 0.01 us  [two_centres(): from_far_edge = lax.ppermute(far, 'row', to_far)]
    pallas_call x1 -> x2, Pallas kernels: 1.89 us -> 2.74 us  [the longest x1 1.45 us: two_centres(): pl.pallas_call(late_kernel, out_shape=[shape_of((local_rows, part), jnp.b...]
  transfers between devices with their start and end apart: 18 -> 16, of which waited for: 8 -> 5; matrix products, arithmetic and copies ran while one was open for 0% -> 0% of each run, Pallas kernels for 7% -> 9%
where the time goes in v10:
time: 81.2 us; the launch traced here: 79.8 us
  starting transfers between devices  34.9 us (43%)
  waiting for transfers between devices  32 us (39%)
  Pallas kernels  9.22 us (11%)
  local copies, waits for them, and re-layouts  1.61 us (2%)
  other arithmetic  1.09 us (1%)
  between operations  1.02 us (1%)
    ppermute x1, waiting for transfers between devices, two_centres(): from_sum = lax.ppermute(far_sum, 'row', to_far)  24.1 us
    ppermute x8, starting transfers between devices, send(): lax.ppermute(value.astype(jnp.float16), everyone, round_pairs(blocks))  19.4 us
    ppermute x4, starting transfers between devices, swap(): return lax.ppermute(value, ('row', 'half'), centres)  8.17 us
    ppermute x8, waiting for transfers between devices, send(): lax.ppermute(value.astype(jnp.float16), everyone, round_pairs(blocks))  6.35 us
    ppermute x1, starting transfers between devices, two_centres(): from_centre = lax.ppermute(far, 'row', to_centre)  3.48 us
    pallas_call x1, Pallas kernels, two_centres(): pl.pallas_call(early_kernel, out_shape=[shape_of((3, local_rows, part), j...  3.3 us
    pallas_call x2, Pallas kernels, combine(): pl.pallas_call(functools.partial(combine_kernel, flips, 1.0 / samples, le...  1.83 us
  transfers between devices with their start and end apart: 16, of which 5 were waited for; matrix products, arithmetic and copies ran while one was open for 0% of the time, Pallas kernels for 9%

profile of v10, /device:TPU:8, one launch (start us, length us, event | category | flops | bytes accessed | tf_op | source)
XLA Modules:
  0.0 79.8 jit_solution(9388007686173780523)
XLA Ops:
  0.1 1.6 %copy-done = bf16[256,4096]{1,0:T(8,128)(2,1)S(1)} copy-done((bf16[256,4096]{1,0:T(8,128)(2,1)S(1)}, bf16[256,4096]{1,0:T(8,128)(2,1)}, u32[]{:S(2)}) %copy-start) | copy-done | bytes 2097176
  2.6 3.5 %collective-permute-start.1 = (bf16[256,2048]{1,0:T(8,128)(2,1)S(1)}, bf16[256,2048]{1,0:T(8,128)(2,1)S(1)}, u32[]{:S(2)}, u32[]{:S(2)}) collective-permute-start(bf16[256,2048]{1,0:T(8,128)(2,1)S(1)} %get-tuple-element.28), channel_id=1, source_target_pairs={{4,8},{8,4},{5,9},{9,5},{6,10},{10,6},{7,11},{11,7},{20,24},{24,20... | collective-permute-start | bytes 3145736 | tf_op jit(solution)/shard_map/ppermute | solution.py:239
  6.1 1.3 %collective-permute-start.2 = (bf16[256,2048]{1,0:T(8,128)(2,1)S(1)}, bf16[256,2048]{1,0:T(8,128)(2,1)S(1)}, u32[]{:S(2)}, u32[]{:S(2)}) collective-permute-start(bf16[256,2048]{1,0:T(8,128)(2,1)S(1)} %get-tuple-element.29.near), channel_id=1, source_target_pairs={{0,4},{12,8},{1,5},{13,9},{2,6},{14,10},{3,7},{15,11},{16,20},{28,... | collective-permute-start | bytes 3145736 | tf_op jit(solution)/shard_map/ppermute | solution.py:241
  7.4 1.3 %collective-permute-start.3 = (f32[1,2048]{1,0:T(1,128)S(1)}, f32[1,2048]{1,0:T(1,128)S(1)}, u32[]{:S(2)}, u32[]{:S(2)}) collective-permute-start(f32[1,2048]{1,0:T(1,128)S(1)} %get-tuple-element.30), channel_id=1, source_target_pairs={{0,8},{12,4},{1,9},{13,5},{2,10},{14,6},{3,11},{15,7},{16,24},{28,... | collective-permute-start | bytes 24584 | tf_op jit(solution)/shard_map/ppermute | solution.py:240
  8.7 1.3 %collective-permute-start = (bf16[256,2048]{1,0:T(8,128)(2,1)S(1)}, bf16[256,2048]{1,0:T(8,128)(2,1)S(1)}, u32[]{:S(2)}, u32[]{:S(2)}) collective-permute-start(bf16[256,2048]{1,0:T(8,128)(2,1)S(1)} %get-tuple-element.28), channel_id=1, source_target_pairs={{0,8},{12,4},{1,9},{13,5},{2,10},{14,6},{3,11},{15,7},{16,24},{28,... | collective-permute-start | bytes 3145736 | tf_op jit(solution)/shard_map/ppermute | solution.py:242
  10.0 24.1 %collective-permute-done.3.far_sum = f32[1,2048]{1,0:T(1,128)S(1)} collective-permute-done((f32[1,2048]{1,0:T(1,128)S(1)}, f32[1,2048]{1,0:T(1,128)S(1)}, u32[]{:S(2)}, u32[]{:S(2)}) %collective-permute-start.3) | collective-permute-done | bytes 8224 | tf_op jit(solution)/shard_map/ppermute | solution.py:240
  34.6 3.3 %shard_map.48 = (bf16[3,256,2048]{2,1,0:T(8,128)(2,1)S(1)}, f32[1,2048]{1,0:T(1,128)S(1)}, f32[3,256,256]{2,1,0:T(8,128)S(1)}, f32[1,256,256]{2,1,0:T(8,128)S(1)...) custom-call(s32[3]{0:T(128)S(1)} %pad_add_fusion.bits, bf16[256,2048]{1,0:T(8,128)(2,1)S(1)} %collective-permute-done.1.other, ...), custom_call_target="tpu_custom_call" | custom-call | flops 1024 | bytes 1024 | tf_op jit(solution)/shard_map/pallas_call | solution.py:253
  37.9 1.9 %collective-permute-start.4 = (f32[1,256,256]{2,1,0:T(8,128)S(1)}, f32[1,256,256]{2,1,0:T(8,128)S(1)}, u32[]{:S(2)}, u32[]{:S(2)}) collective-permute-start(f32[1,256,256]{2,1,0:T(8,128)S(1)} %get-tuple-element.34), channel_id=1, source_target_pairs={{4,5},{5,4},{8,9},{9,8},{6,7},{7,6},{10,11},{11,10},{20,21},{21,20... | collective-permute-start | bytes 786440 | tf_op jit(solution)/shard_map/ppermute | solution.py:221
  39.8 2.4 %collective-permute-start.5 = (f32[1,256,256]{2,1,0:T(8,128)S(1)}, f32[1,256,256]{2,1,0:T(8,128)S(1)}, u32[]{:S(2)}, u32[]{:S(2)}) collective-permute-start(f32[1,256,256]{2,1,0:T(8,128)S(1)} %get-tuple-element.35), channel_id=1, source_target_pairs={{4,5},{5,4},{8,9},{9,8},{6,7},{7,6},{10,11},{11,10},{20,21},{21,20... | collective-permute-start | bytes 786440 | tf_op jit(solution)/shard_map/ppermute | solution.py:221
  42.2 1.9 %collective-permute-start.6 = (f32[1,256,256]{2,1,0:T(8,128)S(1)}, f32[1,256,256]{2,1,0:T(8,128)S(1)}, u32[]{:S(2)}, u32[]{:S(2)}) collective-permute-start(f32[1,256,256]{2,1,0:T(8,128)S(1)} %get-tuple-element.36), channel_id=1, source_target_pairs={{4,5},{5,4},{8,9},{9,8},{6,7},{7,6},{10,11},{11,10},{20,21},{21,20... | collective-permute-start | bytes 786440 | tf_op jit(solution)/shard_map/ppermute | solution.py:221
  44.2 1.5 %collective-permute-done.6.rest_2_ = f32[1,256,256]{2,1,0:T(8,128)S(1)} collective-permute-done((f32[1,256,256]{2,1,0:T(8,128)S(1)}, f32[1,256,256]{2,1,0:T(8,128)S(1)}, u32[]{:S(2)}, u32[]{:S(2)}) %collective-permute-start.6) | collective-permute-done | bytes 262176 | tf_op jit(solution)/shard_map/ppermute | solution.py:221
  45.7 0.9 %shard_map.49 = (f32[256,256]{1,0:T(8,128)S(1)}, f32[256,256]{1,0:T(8,128)S(1)}, f32[256,256]{1,0:T(8,128)S(1)}, f32[256,256]{1,0:T(8,128)S(1)}, f32[256,256]{1,0:T(8,128)S(1)}) custom-call(s32[3]{0:T(128)S(1)} %pad_add_fusion.bits, s32[5,2,2]{2,1,0:T(2,128)S(1)} %copy-done.1, f32[3,256,256]{2,1,0:T(8,128)S(1)} %get-tuple-element.33.own, ...), custom_call_target="tpu_custom_call" | custom-call | flops 1024 | bytes 1024 | tf_op jit(solution)/shard_map/pallas_call | solution.py:195
  47.3 3.3 %collective-permute-start.8 = (f16[256,256]{1,0:T(8,128)(2,1)S(1)}, f16[256,256]{1,0:T(8,128)(2,1)S(1)}, u32[]{:S(2)}, u32[]{:S(2)}) collective-permute-start(f16[256,256]{1,0:T(8,128)(2,1)S(1)} %convert_element_type.54), channel_id=1, source_target_pairs={{4,5},{5,6},{6,4},{7,2},{10,10},{11,9},{8,11},{9,13},{20,21},{21,2... | collective-permute-start | bytes 393224 | tf_op jit(solution)/shard_map/ppermute | solution.py:224
  50.7 4.5 %collective-permute-done.8 = f16[256,256]{1,0:T(8,128)(2,1)S(1)} collective-permute-done((f16[256,256]{1,0:T(8,128)(2,1)S(1)}, f16[256,256]{1,0:T(8,128)(2,1)S(1)}, u32[]{:S(2)}, u32[]{:S(2)}) %collective-permute-start.8) | collective-permute-done | bytes 131104 | tf_op jit(solution)/shard_map/ppermute | solution.py:224
  55.2 1.5 %shard_map.50 = (bf16[256,2048]{1,0:T(8,128)(2,1)S(1)}, f32[2,256,256]{2,1,0:T(8,128)S(1)}, f32[256,256]{1,0:T(8,128)S(1)}, f32[256,256]{1,0:T(8,128)S(1)}, f32[256,256]{1,0:T(8,128)S(1)}) custom-call(s32[3]{0:T(128)S(1)} %pad_add_fusion.bits, ...), custom_call_target="tpu_custom_call", output_to_operand_aliasing={{2}: (4, {}), {3}: (5, {}), {4}: (6, {})} | custom-call | flops 1024 | bytes 1024 | tf_op jit(solution)/shard_map/pallas_call | solution.py:276
  56.7 1.9 %collective-permute-start.9 = (f32[2,256,256]{2,1,0:T(8,128)S(1)}, f32[2,256,256]{2,1,0:T(8,128)S(1)}, u32[]{:S(2)}, u32[]{:S(2)}) collective-permute-start(f32[2,256,256]{2,1,0:T(8,128)S(1)} %get-tuple-element.43), channel_id=1, source_target_pairs={{4,5},{5,4},{8,9},{9,8},{6,7},{7,6},{10,11},{11,10},{20,21},{21,20... | collective-permute-start | bytes 1572872 | tf_op jit(solution)/shard_map/ppermute | solution.py:221
  58.7 1.3 %collective-permute-start.14 = (f16[256,256]{1,0:T(8,128)(2,1)S(1)}, f16[256,256]{1,0:T(8,128)(2,1)S(1)}, u32[]{:S(2)}, u32[]{:S(2)}) collective-permute-start(f16[256,256]{1,0:T(8,128)(2,1)S(1)} %convert_element_type.64), channel_id=1, source_target_pairs={{4,1},{5,8},{6,0},{7,10},{10,14},{11,7},{8,15},{9,5},{20,17},{21,2... | collective-permute-start | bytes 393224 | tf_op jit(solution)/shard_map/ppermute | solution.py:224
  60.0 1.3 %shard_map.51.own = f32[2,256,256]{2,1,0:T(8,128)S(1)} custom-call(s32[3]{0:T(128)S(1)} %pad_add_fusion.bits, bf16[256,2048]{1,0:T(8,128)(2,1)S(1)} %get-tuple-element.42.last, bf16[3,256,2048]{2,1,0:T(8,128)(2,1)S(1)} %get-tuple-element.32.centred), custom_call_target="tpu_custom_call" | custom-call | flops 1024 | bytes 1024 | tf_op jit(solution)/shard_map/pallas_call | solution.py:286
  61.3 1.3 %collective-permute-start.15 = (f16[256,256]{1,0:T(8,128)(2,1)S(1)}, f16[256,256]{1,0:T(8,128)(2,1)S(1)}, u32[]{:S(2)}, u32[]{:S(2)}) collective-permute-start(f16[256,256]{1,0:T(8,128)(2,1)S(1)} %convert_element_type.66), channel_id=1, source_target_pairs={{4,0},{5,10},{6,1},{7,8},{10,15},{11,5},{8,14},{9,7},{20,16},{21,2... | collective-permute-start | bytes 393224 | tf_op jit(solution)/shard_map/ppermute | solution.py:224
  63.5 1.3 %collective-permute-start.10 = (f16[256,256]{1,0:T(8,128)(2,1)S(1)}, f16[256,256]{1,0:T(8,128)(2,1)S(1)}, u32[]{:S(2)}, u32[]{:S(2)}) collective-permute-start(f16[256,256]{1,0:T(8,128)(2,1)S(1)} %convert_element_type.56), channel_id=1, source_target_pairs={{4,12},{5,14},{6,13},{7,15},{10,3},{11,1},{8,2},{9,0},{20,28},{21,... | collective-permute-start | bytes 393224 | tf_op jit(solution)/shard_map/ppermute | solution.py:224
  64.9 1.3 %collective-permute-start.11 = (f16[256,256]{1,0:T(8,128)(2,1)S(1)}, f16[256,256]{1,0:T(8,128)(2,1)S(1)}, u32[]{:S(2)}, u32[]{:S(2)}) collective-permute-start(f16[256,256]{1,0:T(8,128)(2,1)S(1)} %convert_element_type.58), channel_id=1, source_target_pairs={{4,13},{5,15},{6,12},{7,14},{10,2},{11,0},{8,3},{9,1},{20,29},{21,... | collective-permute-start | bytes 393224 | tf_op jit(solution)/shard_map/ppermute | solution.py:224
  66.2 1.9 %collective-permute-start.12 = (f16[256,256]{1,0:T(8,128)(2,1)S(1)}, f16[256,256]{1,0:T(8,128)(2,1)S(1)}, u32[]{:S(2)}, u32[]{:S(2)}) collective-permute-start(f16[256,256]{1,0:T(8,128)(2,1)S(1)} %convert_element_type.60), channel_id=1, source_target_pairs={{4,3},{5,11},{6,7},{7,9},{10,12},{11,4},{8,8},{9,6},{20,19},{21,27... | collective-permute-start | bytes 393224 | tf_op jit(solution)/shard_map/ppermute | solution.py:224
  68.2 8.3 %collective-permute-start.13 = (f16[256,256]{1,0:T(8,128)(2,1)S(1)}, f16[256,256]{1,0:T(8,128)(2,1)S(1)}, u32[]{:S(2)}, u32[]{:S(2)}) collective-permute-start(f16[256,256]{1,0:T(8,128)(2,1)S(1)} %convert_element_type.62), channel_id=1, source_target_pairs={{4,7},{5,9},{6,3},{7,11},{10,8},{11,6},{8,12},{9,4},{20,23},{21,25... | collective-permute-start | bytes 393224 | tf_op jit(solution)/shard_map/ppermute | solution.py:224
  77.3 1.7 %collective-permute-done.13 = f16[256,256]{1,0:T(8,128)(2,1)S(1)} collective-permute-done((f16[256,256]{1,0:T(8,128)(2,1)S(1)}, f16[256,256]{1,0:T(8,128)(2,1)S(1)}, u32[]{:S(2)}, u32[]{:S(2)}) %collective-permute-start.13) | collective-permute-done | bytes 131104 | tf_op jit(solution)/shard_map/ppermute | solution.py:224
  (33 shorter events, 4.1 us)
Async XLA Ops:
  0.1 1.6 %copy-start = (bf16[256,4096]{1,0:T(8,128)(2,1)S(1)}, bf16[256,4096]{1,0:T(8,128)(2,1)}, u32[]{:S(2)}) copy-start(bf16[256,4096]{1,0:T(8,128)(2,1)} %values.1) | copy-start | bytes 6291460
  2.6 31.5 %collective-permute-start.1 = (bf16[256,2048]{1,0:T(8,128)(2,1)S(1)}, bf16[256,2048]{1,0:T(8,128)(2,1)S(1)}, u32[]{:S(2)}, u32[]{:S(2)}) collective-permute-start(bf16[256,2048]{1,0:T(8,128)(2,1)S(1)} %get-tuple-element.28), channel_id=1, source_target_pairs={{4,8},{8,4},{5,9},{9,5},{6,10},{10,6},{7,11},{11,7},{20,24},{24,20... | collective-permute-start | bytes 3145736 | tf_op jit(solution)/shard_map/ppermute | solution.py:239
  6.1 28.5 %collective-permute-start.2 = (bf16[256,2048]{1,0:T(8,128)(2,1)S(1)}, bf16[256,2048]{1,0:T(8,128)(2,1)S(1)}, u32[]{:S(2)}, u32[]{:S(2)}) collective-permute-start(bf16[256,2048]{1,0:T(8,128)(2,1)S(1)} %get-tuple-element.29.near), channel_id=1, source_target_pairs={{0,4},{12,8},{1,5},{13,9},{2,6},{14,10},{3,7},{15,11},{16,20},{28,... | collective-permute-start | bytes 3145736 | tf_op jit(solution)/shard_map/ppermute | solution.py:241
  7.4 26.7 %collective-permute-start.3 = (f32[1,2048]{1,0:T(1,128)S(1)}, f32[1,2048]{1,0:T(1,128)S(1)}, u32[]{:S(2)}, u32[]{:S(2)}) collective-permute-start(f32[1,2048]{1,0:T(1,128)S(1)} %get-tuple-element.30), channel_id=1, source_target_pairs={{0,8},{12,4},{1,9},{13,5},{2,10},{14,6},{3,11},{15,7},{16,24},{28,... | collective-permute-start | bytes 24584 | tf_op jit(solution)/shard_map/ppermute | solution.py:240
  8.7 46.6 %collective-permute-start = (bf16[256,2048]{1,0:T(8,128)(2,1)S(1)}, bf16[256,2048]{1,0:T(8,128)(2,1)S(1)}, u32[]{:S(2)}, u32[]{:S(2)}) collective-permute-start(bf16[256,2048]{1,0:T(8,128)(2,1)S(1)} %get-tuple-element.28), channel_id=1, source_target_pairs={{0,8},{12,4},{1,9},{13,5},{2,10},{14,6},{3,11},{15,7},{16,24},{28,... | collective-permute-start | bytes 3145736 | tf_op jit(solution)/shard_map/ppermute | solution.py:242
  34.6 11.1 %copy-start.1 = (s32[5,2,2]{2,1,0:T(2,128)S(1)}, s32[5,2,2]{2,1,0:T(2,128)}, u32[]{:S(2)}) copy-start(s32[5,2,2]{2,1,0:T(2,128)} %constant.22.clone.places) | copy-start | bytes 244
  37.9 6.3 %collective-permute-start.4 = (f32[1,256,256]{2,1,0:T(8,128)S(1)}, f32[1,256,256]{2,1,0:T(8,128)S(1)}, u32[]{:S(2)}, u32[]{:S(2)}) collective-permute-start(f32[1,256,256]{2,1,0:T(8,128)S(1)} %get-tuple-element.34), channel_id=1, source_target_pairs={{4,5},{5,4},{8,9},{9,8},{6,7},{7,6},{10,11},{11,10},{20,21},{21,20... | collective-permute-start | bytes 786440 | tf_op jit(solution)/shard_map/ppermute | solution.py:221
  39.8 4.4 %collective-permute-start.5 = (f32[1,256,256]{2,1,0:T(8,128)S(1)}, f32[1,256,256]{2,1,0:T(8,128)S(1)}, u32[]{:S(2)}, u32[]{:S(2)}) collective-permute-start(f32[1,256,256]{2,1,0:T(8,128)S(1)} %get-tuple-element.35), channel_id=1, source_target_pairs={{4,5},{5,4},{8,9},{9,8},{6,7},{7,6},{10,11},{11,10},{20,21},{21,20... | collective-permute-start | bytes 786440 | tf_op jit(solution)/shard_map/ppermute | solution.py:221
  42.2 3.4 %collective-permute-start.6 = (f32[1,256,256]{2,1,0:T(8,128)S(1)}, f32[1,256,256]{2,1,0:T(8,128)S(1)}, u32[]{:S(2)}, u32[]{:S(2)}) collective-permute-start(f32[1,256,256]{2,1,0:T(8,128)S(1)} %get-tuple-element.36), channel_id=1, source_target_pairs={{4,5},{5,4},{8,9},{9,8},{6,7},{7,6},{10,11},{11,10},{20,21},{21,20... | collective-permute-start | bytes 786440 | tf_op jit(solution)/shard_map/ppermute | solution.py:221
  46.6 4.0 %collective-permute-start.7 = (f16[256,256]{1,0:T(8,128)(2,1)S(1)}, f16[256,256]{1,0:T(8,128)(2,1)S(1)}, u32[]{:S(2)}, u32[]{:S(2)}) collective-permute-start(f16[256,256]{1,0:T(8,128)(2,1)S(1)} %convert_element_type.52), channel_id=1, source_target_pairs={{4,4},{5,2},{6,5},{7,6},{10,11},{11,13},{8,10},{9,9},{20,20},{21,1... | collective-permute-start | bytes 393224 | tf_op jit(solution)/shard_map/ppermute | solution.py:224
  47.3 7.9 %collective-permute-start.8 = (f16[256,256]{1,0:T(8,128)(2,1)S(1)}, f16[256,256]{1,0:T(8,128)(2,1)S(1)}, u32[]{:S(2)}, u32[]{:S(2)}) collective-permute-start(f16[256,256]{1,0:T(8,128)(2,1)S(1)} %convert_element_type.54), channel_id=1, source_target_pairs={{4,5},{5,6},{6,4},{7,2},{10,10},{11,9},{8,11},{9,13},{20,21},{21,2... | collective-permute-start | bytes 393224 | tf_op jit(solution)/shard_map/ppermute | solution.py:224
  56.7 5.9 %copy-start.2 = (s32[4,2,2]{2,1,0:T(2,128)S(1)}, s32[4,2,2]{2,1,0:T(2,128)}, u32[]{:S(2)}) copy-start(s32[4,2,2]{2,1,0:T(2,128)} %constant.23.clone.places) | copy-start | bytes 196
  56.7 5.9 %collective-permute-start.9 = (f32[2,256,256]{2,1,0:T(8,128)S(1)}, f32[2,256,256]{2,1,0:T(8,128)S(1)}, u32[]{:S(2)}, u32[]{:S(2)}) collective-permute-start(f32[2,256,256]{2,1,0:T(8,128)S(1)} %get-tuple-element.43), channel_id=1, source_target_pairs={{4,5},{5,4},{8,9},{9,8},{6,7},{7,6},{10,11},{11,10},{20,21},{21,20... | collective-permute-start | bytes 1572872 | tf_op jit(solution)/shard_map/ppermute | solution.py:221
  58.7 9.5 %collective-permute-start.14 = (f16[256,256]{1,0:T(8,128)(2,1)S(1)}, f16[256,256]{1,0:T(8,128)(2,1)S(1)}, u32[]{:S(2)}, u32[]{:S(2)}) collective-permute-start(f16[256,256]{1,0:T(8,128)(2,1)S(1)} %convert_element_type.64), channel_id=1, source_target_pairs={{4,1},{5,8},{6,0},{7,10},{10,14},{11,7},{8,15},{9,5},{20,17},{21,2... | collective-permute-start | bytes 393224 | tf_op jit(solution)/shard_map/ppermute | solution.py:224
  61.3 15.9 %collective-permute-start.15 = (f16[256,256]{1,0:T(8,128)(2,1)S(1)}, f16[256,256]{1,0:T(8,128)(2,1)S(1)}, u32[]{:S(2)}, u32[]{:S(2)}) collective-permute-start(f16[256,256]{1,0:T(8,128)(2,1)S(1)} %convert_element_type.66), channel_id=1, source_target_pairs={{4,0},{5,10},{6,1},{7,8},{10,15},{11,5},{8,14},{9,7},{20,16},{21,2... | collective-permute-start | bytes 393224 | tf_op jit(solution)/shard_map/ppermute | solution.py:224
  63.5 13.6 %collective-permute-start.10 = (f16[256,256]{1,0:T(8,128)(2,1)S(1)}, f16[256,256]{1,0:T(8,128)(2,1)S(1)}, u32[]{:S(2)}, u32[]{:S(2)}) collective-permute-start(f16[256,256]{1,0:T(8,128)(2,1)S(1)} %convert_element_type.56), channel_id=1, source_target_pairs={{4,12},{5,14},{6,13},{7,15},{10,3},{11,1},{8,2},{9,0},{20,28},{21,... | collective-permute-start | bytes 393224 | tf_op jit(solution)/shard_map/ppermute | solution.py:224
  64.9 12.3 %collective-permute-start.11 = (f16[256,256]{1,0:T(8,128)(2,1)S(1)}, f16[256,256]{1,0:T(8,128)(2,1)S(1)}, u32[]{:S(2)}, u32[]{:S(2)}) collective-permute-start(f16[256,256]{1,0:T(8,128)(2,1)S(1)} %convert_element_type.58), channel_id=1, source_target_pairs={{4,13},{5,15},{6,12},{7,14},{10,2},{11,0},{8,3},{9,1},{20,29},{21,... | collective-permute-start | bytes 393224 | tf_op jit(solution)/shard_map/ppermute | solution.py:224
  66.2 11.1 %collective-permute-start.12 = (f16[256,256]{1,0:T(8,128)(2,1)S(1)}, f16[256,256]{1,0:T(8,128)(2,1)S(1)}, u32[]{:S(2)}, u32[]{:S(2)}) collective-permute-start(f16[256,256]{1,0:T(8,128)(2,1)S(1)} %convert_element_type.60), channel_id=1, source_target_pairs={{4,3},{5,11},{6,7},{7,9},{10,12},{11,4},{8,8},{9,6},{20,19},{21,27... | collective-permute-start | bytes 393224 | tf_op jit(solution)/shard_map/ppermute | solution.py:224
  68.2 10.8 %collective-permute-start.13 = (f16[256,256]{1,0:T(8,128)(2,1)S(1)}, f16[256,256]{1,0:T(8,128)(2,1)S(1)}, u32[]{:S(2)}, u32[]{:S(2)}) collective-permute-start(f16[256,256]{1,0:T(8,128)(2,1)S(1)} %convert_element_type.62), channel_id=1, source_target_pairs={{4,7},{5,9},{6,3},{7,11},{10,8},{11,6},{8,12},{9,4},{20,23},{21,25... | collective-permute-start | bytes 393224 | tf_op jit(solution)/shard_map/ppermute | solution.py:224

commit v11 on v10

--- a/solution.py
+++ b/solution.py
@@ -37,11 +37,11 @@
     (((1, 0), (1, 1)), ((0, 2), (1, 2))),
     (((1, 1), (1, 0)), ((1, 2), (0, 2))),
 )
-FAR_ROUNDS = (
+MIDDLE_ROUNDS = (
     (((0, 0), (0, 1)), ((2, 2), (2, 0))),
+)
+LATE_ROUNDS = (
     (((0, 1), (0, 0)), ((2, 0), (2, 2))),
-)
-LATE_ROUNDS = (
     (((1, 3), (0, 3)), ((2, 1), (2, 3))),
     (((0, 3), (1, 3)), ((2, 3), (2, 1))),
     (((3, 1), (3, 0)), ((3, 3), (3, 2))),
@@ -52,11 +52,10 @@
     ((0, 0), (0, 1), (1, 1), (1, 0), (1, 1)),
     ((2, 2), (2, 0), (2, 1), (0, 2), (1, 2)),
 )
-SPARE = 2
 LATE_SUMS = (((3, 0), (3, 1)), ((3, 2), (3, 3)))
 LATE_HELD = (
-    ((3, 0), (3, 1), (0, 3), (1, 3), (1, 1)),
-    ((3, 2), (3, 3), (2, 3), (3, 3), (2, 1)),
+    ((3, 0), (3, 1), (0, 3), (1, 3)) + EARLY_SUMS[0],
+    ((3, 2), (3, 3), (2, 3), (3, 3)) + EARLY_SUMS[1],
 )
 VMEM = pl.BlockSpec(memory_space=pltpu.VMEM)
 SMEM = pl.BlockSpec(memory_space=pltpu.SMEM)
@@ -265,15 +264,16 @@
         cost_estimate=BRIEF,
     )(bits, from_centre, from_edge, near, partial)
     others = [swap(other) for other in others]
-    places = held_place(EARLY_HELD, NEAR_ROUNDS + FAR_ROUNDS) + [[[SPARE] * 2] * 2]
-    *early, spare = combine(bits, own, others, (1, 2), (), EARLY_HELD, places, samples)
-    near_blocks, far_blocks = early[: len(NEAR_ROUNDS)], early[len(NEAR_ROUNDS) :]
+    places = held_place(EARLY_HELD, NEAR_ROUNDS + MIDDLE_ROUNDS)
+    places += [[[i] * 2] * 2 for i in range(3)]
+    early = list(combine(bits, own, others, (1, 2), (), EARLY_HELD, places, samples))
+    near_blocks, middle_blocks, spares = early[:2], early[2:3], early[3:]
     arrived = [send(value, blocks) for value, blocks in zip(near_blocks, NEAR_ROUNDS)]
     summed = sum(block.astype(jnp.float32) for block in arrived)
 
     late_blocks = shape_of((2, local_rows, local_rows), jnp.float32)
-    handed = [summed] + far_blocks
-    last, other, summed, *far_blocks = pl.pallas_call(
+    handed = [summed] + middle_blocks
+    last, other, summed, *middle_blocks = pl.pallas_call(
         late_kernel,
         out_shape=[shape_of((local_rows, part), jnp.bfloat16), late_blocks]
         + [shape_of(value.shape, value.dtype) for value in handed],
@@ -292,9 +292,9 @@
         cost_estimate=BRIEF,
     )(bits, last, centred)
     other = swap(other)
-    arrived = [send(value, blocks) for value, blocks in zip(far_blocks, FAR_ROUNDS)]
+    arrived = [send(value, blocks) for value, blocks in zip(middle_blocks, MIDDLE_ROUNDS)]
     places = held_place(LATE_HELD, LATE_ROUNDS)
-    late = combine(bits, own, [other], (0, 1), (spare,), LATE_HELD, places, samples)
+    late = combine(bits, own, [other], (0, 1), spares, LATE_HELD, places, samples)
     arrived += [send(value, blocks) for value, blocks in zip(late, LATE_ROUNDS)]
     summed = summed + sum(block.astype(jnp.float32) for block in reversed(arrived))
     return add_shift(summed, 1, shift, local_rows)

time: 81.2 us -> 81.3 us (level)
  the two profiles are of different devices: /device:TPU:8 before, /device:TPU:1 now
where the time goes in v11:
time: 81.3 us; the launch traced here: 80.8 us
  waiting for transfers between devices  47.3 us (58%)
  starting transfers between devices  20.5 us (25%)
  Pallas kernels  9.29 us (11%)
  local copies, waits for them, and re-layouts  1.61 us (2%)
  other arithmetic  1.09 us (1%)
  between operations  1.01 us (1%)
    ppermute x1, waiting for transfers between devices, two_centres(): from_sum = lax.ppermute(far_sum, 'row', to_far)  18.9 us
    ppermute x8, waiting for transfers between devices, send(): lax.ppermute(value.astype(jnp.float16), everyone, round_pairs(blocks))  14.2 us
    ppermute x1, waiting for transfers between devices, two_centres(): from_far_edge = lax.ppermute(far, 'row', to_far)  14.1 us
    ppermute x8, starting transfers between devices, send(): lax.ppermute(value.astype(jnp.float16), everyone, round_pairs(blocks))  7.83 us
    ppermute x1, starting transfers between devices, two_centres(): from_edge = lax.ppermute(near, 'row', to_own)  6.57 us
    pallas_call x1, Pallas kernels, two_centres(): pl.pallas_call(early_kernel, out_shape=[shape_of((3, local_rows, part), j...  3.3 us
    ppermute x4, starting transfers between devices, swap(): return lax.ppermute(value, ('row', 'half'), centres)  2.73 us
    pallas_call x2, Pallas kernels, combine(): pl.pallas_call(functools.partial(combine_kernel, flips, 1.0 / samples, le...  1.9 us
  transfers between devices with their start and end apart: 16, of which 6 were waited for; matrix products, arithmetic and copies ran while one was open for 0% of the time, Pallas kernels for 9%

profile of v11, /device:TPU:1, one launch (start us, length us, event | category | flops | bytes accessed | tf_op | source)
XLA Modules:
  0.0 80.8 jit_solution(10379880608682873675)
XLA Ops:
  0.1 1.6 %copy-done = bf16[256,4096]{1,0:T(8,128)(2,1)S(1)} copy-done((bf16[256,4096]{1,0:T(8,128)(2,1)S(1)}, bf16[256,4096]{1,0:T(8,128)(2,1)}, u32[]{:S(2)}) %copy-start) | copy-done | bytes 2097176
  1.7 0.9 %shard_map.46 = (bf16[256,2048]{1,0:T(8,128)(2,1)S(1)}, bf16[256,2048]{1,0:T(8,128)(2,1)S(1)}, f32[1,2048]{1,0:T(1,128)S(1)}) custom-call(s32[3]{0:T(128)S(1)} %pad_add_fusion.bits, bf16[256,4096]{1,0:T(8,128)(2,1)S(1)} %copy-done), custom_call_target="tpu_custom_call" | custom-call | flops 1024 | bytes 1024 | tf_op jit(solution)/shard_map/pallas_call | solution.py:225
  2.6 0.7 collective-permute-start.1
  3.3 6.6 %collective-permute-start.2 = (bf16[256,2048]{1,0:T(8,128)(2,1)S(1)}, bf16[256,2048]{1,0:T(8,128)(2,1)S(1)}, u32[]{:S(2)}, u32[]{:S(2)}) collective-permute-start(bf16[256,2048]{1,0:T(8,128)(2,1)S(1)} %get-tuple-element.30.near), channel_id=1, source_target_pairs={{0,4},{12,8},{1,5},{13,9},{2,6},{14,10},{3,7},{15,11},{16,20},{28,... | collective-permute-start | bytes 3145736 | tf_op jit(solution)/shard_map/ppermute | solution.py:240
  9.9 1.3 %collective-permute-start.3 = (f32[1,2048]{1,0:T(1,128)S(1)}, f32[1,2048]{1,0:T(1,128)S(1)}, u32[]{:S(2)}, u32[]{:S(2)}) collective-permute-start(f32[1,2048]{1,0:T(1,128)S(1)} %get-tuple-element.31), channel_id=1, source_target_pairs={{0,8},{12,4},{1,9},{13,5},{2,10},{14,6},{3,11},{15,7},{16,24},{28,... | collective-permute-start | bytes 24584 | tf_op jit(solution)/shard_map/ppermute | solution.py:239
  11.2 1.4 %collective-permute-start = (bf16[256,2048]{1,0:T(8,128)(2,1)S(1)}, bf16[256,2048]{1,0:T(8,128)(2,1)S(1)}, u32[]{:S(2)}, u32[]{:S(2)}) collective-permute-start(bf16[256,2048]{1,0:T(8,128)(2,1)S(1)} %get-tuple-element.29), channel_id=1, source_target_pairs={{0,8},{12,4},{1,9},{13,5},{2,10},{14,6},{3,11},{15,7},{16,24},{28,... | collective-permute-start | bytes 3145736 | tf_op jit(solution)/shard_map/ppermute | solution.py:241
  12.6 18.9 %collective-permute-done.3.far_sum = f32[1,2048]{1,0:T(1,128)S(1)} collective-permute-done((f32[1,2048]{1,0:T(1,128)S(1)}, f32[1,2048]{1,0:T(1,128)S(1)}, u32[]{:S(2)}, u32[]{:S(2)}) %collective-permute-start.3) | collective-permute-done | bytes 8224 | tf_op jit(solution)/shard_map/ppermute | solution.py:239
  32.0 3.3 %shard_map.48 = (bf16[3,256,2048]{2,1,0:T(8,128)(2,1)S(1)}, f32[1,2048]{1,0:T(1,128)S(1)}, f32[3,256,256]{2,1,0:T(8,128)S(1)}, f32[1,256,256]{2,1,0:T(8,128)S(1)...) custom-call(s32[3]{0:T(128)S(1)} %pad_add_fusion.bits, bf16[256,2048]{1,0:T(8,128)(2,1)S(1)} %collective-permute-done.1.other, ...), custom_call_target="tpu_custom_call" | custom-call | flops 1024 | bytes 1024 | tf_op jit(solution)/shard_map/pallas_call | solution.py:252
  36.7 0.7 collective-permute-start.6
  37.4 1.0 %shard_map.49 = (f32[256,256]{1,0:T(8,128)S(1)}, f32[256,256]{1,0:T(8,128)S(1)}, f32[256,256]{1,0:T(8,128)S(1)}, f32[256,256]{1,0:T(8,128)S(1)}, f32[256,256]{1,0:T(8,128)S(1)}, /*index=5*/f32[256,256]{1,0:T(8,128)S(1)}) custom-call(s32[3]{0:T(128)S(1)} %pad_add_fusion.bits, s32[6,2,2]{2,1,0:T(2,128)S(1)} %copy-done.1, ...), custom_call_target="tpu_custom_call" | custom-call | flops 1024 | bytes 1024 | tf_op jit(solution)/shard_map/pallas_call | solution.py:194
  39.8 14.1 %collective-permute-done.far_edge = bf16[256,2048]{1,0:T(8,128)(2,1)S(1)} collective-permute-done((bf16[256,2048]{1,0:T(8,128)(2,1)S(1)}, bf16[256,2048]{1,0:T(8,128)(2,1)S(1)}, u32[]{:S(2)}, u32[]{:S(2)}) %collective-permute-start) | collective-permute-done | bytes 1048608 | tf_op jit(solution)/shard_map/ppermute | solution.py:241
  54.0 1.5 %shard_map.50 = (bf16[256,2048]{1,0:T(8,128)(2,1)S(1)}, f32[2,256,256]{2,1,0:T(8,128)S(1)}, f32[256,256]{1,0:T(8,128)S(1)}, f32[256,256]{1,0:T(8,128)S(1)}) custom-call(s32[3]{0:T(128)S(1)} %pad_add_fusion.bits, bf16[256,2048]{1,0:T(8,128)(2,1)S(1)} %collective-permute-done.far_edge, ...), custom_call_target="tpu_custom_call", output_to_operand_aliasing={{2}: (4, {}), {3}: (5, {})} | custom-call | flops 1024 | bytes 1024 | tf_op jit(solution)/shard_map/pallas_call | solution.py:276
  55.4 0.7 collective-permute-start.9
  56.2 1.3 %collective-permute-start.15 = (f16[256,256]{1,0:T(8,128)(2,1)S(1)}, f16[256,256]{1,0:T(8,128)(2,1)S(1)}, u32[]{:S(2)}, u32[]{:S(2)}) collective-permute-start(f16[256,256]{1,0:T(8,128)(2,1)S(1)} %convert_element_type.66), channel_id=1, source_target_pairs={{4,0},{5,10},{6,1},{7,8},{10,15},{11,5},{8,14},{9,7},{20,16},{21,2... | collective-permute-start | bytes 393224 | tf_op jit(solution)/shard_map/ppermute | solution.py:223
  57.5 1.3 %shard_map.51.own = f32[2,256,256]{2,1,0:T(8,128)S(1)} custom-call(s32[3]{0:T(128)S(1)} %pad_add_fusion.bits, bf16[256,2048]{1,0:T(8,128)(2,1)S(1)} %get-tuple-element.42.last, bf16[3,256,2048]{2,1,0:T(8,128)(2,1)S(1)} %get-tuple-element.33.centred), custom_call_target="tpu_custom_call" | custom-call | flops 1024 | bytes 1024 | tf_op jit(solution)/shard_map/pallas_call | solution.py:286
  58.8 0.9 %shard_map.52 = (f32[256,256]{1,0:T(8,128)S(1)}, f32[256,256]{1,0:T(8,128)S(1)}, f32[256,256]{1,0:T(8,128)S(1)}, f32[256,256]{1,0:T(8,128)S(1)}, f32[256,256]{1,0:T(8,128)S(1)}) custom-call(s32[3]{0:T(128)S(1)} %pad_add_fusion.bits, s32[5,2,2]{2,1,0:T(2,128)S(1)} %copy-done.2, f32[2,256,256]{2,1,0:T(8,128)S(1)} %shard_map.51.own, ...), custom_call_target="tpu_custom_call" | custom-call | flops 1024 | bytes 1024 | tf_op jit(solution)/shard_map/pallas_call | solution.py:194
  59.7 1.3 %collective-permute-start.10 = (f16[256,256]{1,0:T(8,128)(2,1)S(1)}, f16[256,256]{1,0:T(8,128)(2,1)S(1)}, u32[]{:S(2)}, u32[]{:S(2)}) collective-permute-start(f16[256,256]{1,0:T(8,128)(2,1)S(1)} %convert_element_type.56), channel_id=1, source_target_pairs={{4,12},{5,14},{6,13},{7,15},{10,3},{11,1},{8,2},{9,0},{20,28},{21,... | collective-permute-start | bytes 393224 | tf_op jit(solution)/shard_map/ppermute | solution.py:223
  61.1 1.3 %collective-permute-start.11 = (f16[256,256]{1,0:T(8,128)(2,1)S(1)}, f16[256,256]{1,0:T(8,128)(2,1)S(1)}, u32[]{:S(2)}, u32[]{:S(2)}) collective-permute-start(f16[256,256]{1,0:T(8,128)(2,1)S(1)} %convert_element_type.58), channel_id=1, source_target_pairs={{4,13},{5,15},{6,12},{7,14},{10,2},{11,0},{8,3},{9,1},{20,29},{21,... | collective-permute-start | bytes 393224 | tf_op jit(solution)/shard_map/ppermute | solution.py:223
  63.8 2.4 %collective-permute-done.15 = f16[256,256]{1,0:T(8,128)(2,1)S(1)} collective-permute-done((f16[256,256]{1,0:T(8,128)(2,1)S(1)}, f16[256,256]{1,0:T(8,128)(2,1)S(1)}, u32[]{:S(2)}, u32[]{:S(2)}) %collective-permute-start.15) | collective-permute-done | bytes 131104 | tf_op jit(solution)/shard_map/ppermute | solution.py:223
  66.2 1.3 %collective-permute-start.14 = (f16[256,256]{1,0:T(8,128)(2,1)S(1)}, f16[256,256]{1,0:T(8,128)(2,1)S(1)}, u32[]{:S(2)}, u32[]{:S(2)}) collective-permute-start(f16[256,256]{1,0:T(8,128)(2,1)S(1)} %convert_element_type.64), channel_id=1, source_target_pairs={{4,1},{5,8},{6,0},{7,10},{10,14},{11,7},{8,15},{9,5},{20,17},{21,2... | collective-permute-start | bytes 393224 | tf_op jit(solution)/shard_map/ppermute | solution.py:223
  68.2 4.6 %collective-permute-done.10 = f16[256,256]{1,0:T(8,128)(2,1)S(1)} collective-permute-done((f16[256,256]{1,0:T(8,128)(2,1)S(1)}, f16[256,256]{1,0:T(8,128)(2,1)S(1)}, u32[]{:S(2)}, u32[]{:S(2)}) %collective-permute-start.10) | collective-permute-done | bytes 131104 | tf_op jit(solution)/shard_map/ppermute | solution.py:223
  72.8 2.2 %collective-permute-done.11 = f16[256,256]{1,0:T(8,128)(2,1)S(1)} collective-permute-done((f16[256,256]{1,0:T(8,128)(2,1)S(1)}, f16[256,256]{1,0:T(8,128)(2,1)S(1)}, u32[]{:S(2)}, u32[]{:S(2)}) %collective-permute-start.11) | collective-permute-done | bytes 131104 | tf_op jit(solution)/shard_map/ppermute | solution.py:223
  74.9 5.1 %collective-permute-done.14 = f16[256,256]{1,0:T(8,128)(2,1)S(1)} collective-permute-done((f16[256,256]{1,0:T(8,128)(2,1)S(1)}, f16[256,256]{1,0:T(8,128)(2,1)S(1)}, u32[]{:S(2)}, u32[]{:S(2)}) %collective-permute-start.14) | collective-permute-done | bytes 131104 | tf_op jit(solution)/shard_map/ppermute | solution.py:223
  80.0 0.8 %select_add_fusion = f32[256,256]{1,0:T(8,128)} fusion(f32[256,256]{1,0:T(8,128)S(1)} %get-tuple-element.41, f16[256,256]{1,0:T(8,128)(2,1)S(1)} %collective-permute-done.15, f16[256,256]{1,0:T(8,128)(2,1)S(1)} %collective-permute-done.14, f16[256,256]{1,0:T(8,128)(2,1)S(1)} %collective-permute-done.13, f16[256,256]{1,0:T(8,128)(2,1)S(1)} %collective-permute-done.12, ...), kind=kLoop, calls=%fused_computation | loop fusion | flops 983040 | bytes 1312772 | tf_op jit(solution)/shard_map/add | solution.py:21
  (33 shorter events, 4.8 us)
Async XLA Ops:
  0.1 1.6 %copy-start = (bf16[256,4096]{1,0:T(8,128)(2,1)S(1)}, bf16[256,4096]{1,0:T(8,128)(2,1)}, u32[]{:S(2)}) copy-start(bf16[256,4096]{1,0:T(8,128)(2,1)} %values.1) | copy-start | bytes 6291460
  2.6 28.9 %collective-permute-start.1 = (bf16[256,2048]{1,0:T(8,128)(2,1)S(1)}, bf16[256,2048]{1,0:T(8,128)(2,1)S(1)}, u32[]{:S(2)}, u32[]{:S(2)}) collective-permute-start(bf16[256,2048]{1,0:T(8,128)(2,1)S(1)} %get-tuple-element.29), channel_id=1, source_target_pairs={{4,8},{8,4},{5,9},{9,5},{6,10},{10,6},{7,11},{11,7},{20,24},{24,20... | collective-permute-start | bytes 3145736 | tf_op jit(solution)/shard_map/ppermute | solution.py:238
  3.3 28.7 %collective-permute-start.2 = (bf16[256,2048]{1,0:T(8,128)(2,1)S(1)}, bf16[256,2048]{1,0:T(8,128)(2,1)S(1)}, u32[]{:S(2)}, u32[]{:S(2)}) collective-permute-start(bf16[256,2048]{1,0:T(8,128)(2,1)S(1)} %get-tuple-element.30.near), channel_id=1, source_target_pairs={{0,4},{12,8},{1,5},{13,9},{2,6},{14,10},{3,7},{15,11},{16,20},{28,... | collective-permute-start | bytes 3145736 | tf_op jit(solution)/shard_map/ppermute | solution.py:240
  9.9 21.6 %collective-permute-start.3 = (f32[1,2048]{1,0:T(1,128)S(1)}, f32[1,2048]{1,0:T(1,128)S(1)}, u32[]{:S(2)}, u32[]{:S(2)}) collective-permute-start(f32[1,2048]{1,0:T(1,128)S(1)} %get-tuple-element.31), channel_id=1, source_target_pairs={{0,8},{12,4},{1,9},{13,5},{2,10},{14,6},{3,11},{15,7},{16,24},{28,... | collective-permute-start | bytes 24584 | tf_op jit(solution)/shard_map/ppermute | solution.py:239
  11.2 42.8 %collective-permute-start = (bf16[256,2048]{1,0:T(8,128)(2,1)S(1)}, bf16[256,2048]{1,0:T(8,128)(2,1)S(1)}, u32[]{:S(2)}, u32[]{:S(2)}) collective-permute-start(bf16[256,2048]{1,0:T(8,128)(2,1)S(1)} %get-tuple-element.29), channel_id=1, source_target_pairs={{0,8},{12,4},{1,9},{13,5},{2,10},{14,6},{3,11},{15,7},{16,24},{28,... | collective-permute-start | bytes 3145736 | tf_op jit(solution)/shard_map/ppermute | solution.py:241
  32.0 5.4 %copy-start.1 = (s32[6,2,2]{2,1,0:T(2,128)S(1)}, s32[6,2,2]{2,1,0:T(2,128)}, u32[]{:S(2)}) copy-start(s32[6,2,2]{2,1,0:T(2,128)} %constant.22.clone.places) | copy-start | bytes 292
  35.3 2.1 %collective-permute-start.4 = (f32[1,256,256]{2,1,0:T(8,128)S(1)}, f32[1,256,256]{2,1,0:T(8,128)S(1)}, u32[]{:S(2)}, u32[]{:S(2)}) collective-permute-start(f32[1,256,256]{2,1,0:T(8,128)S(1)} %get-tuple-element.35), channel_id=1, source_target_pairs={{4,5},{5,4},{8,9},{9,8},{6,7},{7,6},{10,11},{11,10},{20,21},{21,20... | collective-permute-start | bytes 786440 | tf_op jit(solution)/shard_map/ppermute | solution.py:220
  36.0 1.4 %collective-permute-start.5 = (f32[1,256,256]{2,1,0:T(8,128)S(1)}, f32[1,256,256]{2,1,0:T(8,128)S(1)}, u32[]{:S(2)}, u32[]{:S(2)}) collective-permute-start(f32[1,256,256]{2,1,0:T(8,128)S(1)} %get-tuple-element.36), channel_id=1, source_target_pairs={{4,5},{5,4},{8,9},{9,8},{6,7},{7,6},{10,11},{11,10},{20,21},{21,20... | collective-permute-start | bytes 786440 | tf_op jit(solution)/shard_map/ppermute | solution.py:220
  36.7 0.7 collective-permute-start.6
  38.4 1.4 %collective-permute-start.7 = (f16[256,256]{1,0:T(8,128)(2,1)S(1)}, f16[256,256]{1,0:T(8,128)(2,1)S(1)}, u32[]{:S(2)}, u32[]{:S(2)}) collective-permute-start(f16[256,256]{1,0:T(8,128)(2,1)S(1)} %convert_element_type.52), channel_id=1, source_target_pairs={{4,4},{5,2},{6,5},{7,6},{10,11},{11,13},{8,10},{9,9},{20,20},{21,1... | collective-permute-start | bytes 393224 | tf_op jit(solution)/shard_map/ppermute | solution.py:223
  39.1 0.7 collective-permute-start.8
  55.4 3.3 %copy-start.2 = (s32[5,2,2]{2,1,0:T(2,128)S(1)}, s32[5,2,2]{2,1,0:T(2,128)}, u32[]{:S(2)}) copy-start(s32[5,2,2]{2,1,0:T(2,128)} %constant.23.clone.places) | copy-start | bytes 244
  55.4 3.3 %collective-permute-start.9 = (f32[2,256,256]{2,1,0:T(8,128)S(1)}, f32[2,256,256]{2,1,0:T(8,128)S(1)}, u32[]{:S(2)}, u32[]{:S(2)}) collective-permute-start(f32[2,256,256]{2,1,0:T(8,128)S(1)} %get-tuple-element.43), channel_id=1, source_target_pairs={{4,5},{5,4},{8,9},{9,8},{6,7},{7,6},{10,11},{11,10},{20,21},{21,20... | collective-permute-start | bytes 1572872 | tf_op jit(solution)/shard_map/ppermute | solution.py:220
  56.2 10.0 %collective-permute-start.15 = (f16[256,256]{1,0:T(8,128)(2,1)S(1)}, f16[256,256]{1,0:T(8,128)(2,1)S(1)}, u32[]{:S(2)}, u32[]{:S(2)}) collective-permute-start(f16[256,256]{1,0:T(8,128)(2,1)S(1)} %convert_element_type.66), channel_id=1, source_target_pairs={{4,0},{5,10},{6,1},{7,8},{10,15},{11,5},{8,14},{9,7},{20,16},{21,2... | collective-permute-start | bytes 393224 | tf_op jit(solution)/shard_map/ppermute | solution.py:223
  59.7 13.0 %collective-permute-start.10 = (f16[256,256]{1,0:T(8,128)(2,1)S(1)}, f16[256,256]{1,0:T(8,128)(2,1)S(1)}, u32[]{:S(2)}, u32[]{:S(2)}) collective-permute-start(f16[256,256]{1,0:T(8,128)(2,1)S(1)} %convert_element_type.56), channel_id=1, source_target_pairs={{4,12},{5,14},{6,13},{7,15},{10,3},{11,1},{8,2},{9,0},{20,28},{21,... | collective-permute-start | bytes 393224 | tf_op jit(solution)/shard_map/ppermute | solution.py:223
  61.1 13.9 %collective-permute-start.11 = (f16[256,256]{1,0:T(8,128)(2,1)S(1)}, f16[256,256]{1,0:T(8,128)(2,1)S(1)}, u32[]{:S(2)}, u32[]{:S(2)}) collective-permute-start(f16[256,256]{1,0:T(8,128)(2,1)S(1)} %convert_element_type.58), channel_id=1, source_target_pairs={{4,13},{5,15},{6,12},{7,14},{10,2},{11,0},{8,3},{9,1},{20,29},{21,... | collective-permute-start | bytes 393224 | tf_op jit(solution)/shard_map/ppermute | solution.py:223
  62.4 12.5 %collective-permute-start.12 = (f16[256,256]{1,0:T(8,128)(2,1)S(1)}, f16[256,256]{1,0:T(8,128)(2,1)S(1)}, u32[]{:S(2)}, u32[]{:S(2)}) collective-permute-start(f16[256,256]{1,0:T(8,128)(2,1)S(1)} %convert_element_type.60), channel_id=1, source_target_pairs={{4,3},{5,11},{6,7},{7,9},{10,12},{11,4},{8,8},{9,6},{20,19},{21,27... | collective-permute-start | bytes 393224 | tf_op jit(solution)/shard_map/ppermute | solution.py:223
  63.1 11.8 %collective-permute-start.13 = (f16[256,256]{1,0:T(8,128)(2,1)S(1)}, f16[256,256]{1,0:T(8,128)(2,1)S(1)}, u32[]{:S(2)}, u32[]{:S(2)}) collective-permute-start(f16[256,256]{1,0:T(8,128)(2,1)S(1)} %convert_element_type.62), channel_id=1, source_target_pairs={{4,7},{5,9},{6,3},{7,11},{10,8},{11,6},{8,12},{9,4},{20,23},{21,25... | collective-permute-start | bytes 393224 | tf_op jit(solution)/shard_map/ppermute | solution.py:223
  66.2 13.8 %collective-permute-start.14 = (f16[256,256]{1,0:T(8,128)(2,1)S(1)}, f16[256,256]{1,0:T(8,128)(2,1)S(1)}, u32[]{:S(2)}, u32[]{:S(2)}) collective-permute-start(f16[256,256]{1,0:T(8,128)(2,1)S(1)} %convert_element_type.64), channel_id=1, source_target_pairs={{4,1},{5,8},{6,0},{7,10},{10,14},{11,7},{8,15},{9,5},{20,17},{21,2... | collective-permute-start | bytes 393224 | tf_op jit(solution)/shard_map/ppermute | solution.py:223

commit v12 on v10

--- a/solution.py
+++ b/solution.py
@@ -34,28 +34,28 @@
 
 
 NEAR_ROUNDS = (
-    (((1, 0), (1, 1)), ((0, 2), (1, 2))),
-    (((1, 1), (1, 0)), ((1, 2), (0, 2))),
+    (((1, 1), (0, 2)), ((1, 0), (1, 2))),
+    (((0, 2), (1, 1)), ((1, 2), (1, 0))),
 )
 FAR_ROUNDS = (
-    (((0, 0), (0, 1)), ((2, 2), (2, 0))),
-    (((0, 1), (0, 0)), ((2, 0), (2, 2))),
+    (((2, 0), (0, 0)), ((0, 1), (2, 2))),
+    (((0, 0), (2, 0)), ((2, 2), (0, 1))),
 )
 LATE_ROUNDS = (
-    (((1, 3), (0, 3)), ((2, 1), (2, 3))),
-    (((0, 3), (1, 3)), ((2, 3), (2, 1))),
-    (((3, 1), (3, 0)), ((3, 3), (3, 2))),
-    (((3, 0), (3, 1)), ((3, 2), (3, 3))),
-)
-EARLY_SUMS = (((0, 0), (0, 1), (1, 1)), ((2, 2), (2, 0), (2, 1)))
+    (((1, 3), (0, 3)), ((3, 3), (3, 2))),
+    (((3, 1), (3, 0)), ((2, 1), (2, 3))),
+    (((0, 3), (1, 3)), ((3, 2), (3, 3))),
+    (((3, 0), (3, 1)), ((2, 3), (2, 1))),
+)
+EARLY_SUMS = (((1, 1), (2, 0), (0, 0)), ((2, 2), (0, 1), (2, 1)))
 EARLY_HELD = (
-    ((0, 0), (0, 1), (1, 1), (1, 0), (1, 1)),
-    ((2, 2), (2, 0), (2, 1), (0, 2), (1, 2)),
+    ((1, 1), (2, 0), (0, 0), (0, 2), (0, 0)),
+    ((2, 2), (0, 1), (2, 1), (1, 0), (1, 2)),
 )
 SPARE = 2
 LATE_SUMS = (((3, 0), (3, 1)), ((3, 2), (3, 3)))
 LATE_HELD = (
-    ((3, 0), (3, 1), (0, 3), (1, 3), (1, 1)),
+    ((3, 0), (3, 1), (0, 3), (1, 3), (0, 0)),
     ((3, 2), (3, 3), (2, 3), (3, 3), (2, 1)),
 )
 VMEM = pl.BlockSpec(memory_space=pltpu.VMEM)

time: 81.2 us -> 85.1 us (1.048)
  the two profiles are of different devices: /device:TPU:8 before, /device:TPU:0 now
where the time goes in v12:
time: 85.1 us; the launch traced here: 84.6 us
  waiting for transfers between devices  50 us (59%)
  starting transfers between devices  21.7 us (25%)
  Pallas kernels  9.22 us (11%)
  local copies, waits for them, and re-layouts  1.61 us (2%)
  other arithmetic  1.09 us (1%)
  between operations  1.01 us (1%)
    ppermute x1, waiting for transfers between devices, two_centres(): from_sum = lax.ppermute(far_sum, 'row', to_far)  21 us
    ppermute x8, waiting for transfers between devices, send(): lax.ppermute(value.astype(jnp.float16), everyone, round_pairs(blocks))  16.3 us
    ppermute x1, waiting for transfers between devices, two_centres(): from_far_edge = lax.ppermute(far, 'row', to_far)  12.7 us
    ppermute x8, starting transfers between devices, send(): lax.ppermute(value.astype(jnp.float16), everyone, round_pairs(blocks))  7.83 us
    ppermute x1, starting transfers between devices, two_centres(): from_edge = lax.ppermute(near, 'row', to_own)  7.75 us
    pallas_call x1, Pallas kernels, two_centres(): pl.pallas_call(early_kernel, out_shape=[shape_of((3, local_rows, part), j...  3.3 us
    ppermute x4, starting transfers between devices, swap(): return lax.ppermute(value, ('row', 'half'), centres)  2.73 us
    pallas_call x2, Pallas kernels, combine(): pl.pallas_call(functools.partial(combine_kernel, flips, 1.0 / samples, le...  1.83 us
  transfers between devices with their start and end apart: 16, of which 6 were waited for; matrix products, arithmetic and copies ran while one was open for 0% of the time, Pallas kernels for 8%

profile of v12, /device:TPU:0, one launch (start us, length us, event | category | flops | bytes accessed | tf_op | source)
XLA Modules:
  0.0 84.6 jit_solution(11897588255857876497)
XLA Ops:
  0.1 1.6 %copy-done = bf16[256,4096]{1,0:T(8,128)(2,1)S(1)} copy-done((bf16[256,4096]{1,0:T(8,128)(2,1)S(1)}, bf16[256,4096]{1,0:T(8,128)(2,1)}, u32[]{:S(2)}) %copy-start) | copy-done | bytes 2097176
  1.7 0.9 %shard_map.46 = (bf16[256,2048]{1,0:T(8,128)(2,1)S(1)}, bf16[256,2048]{1,0:T(8,128)(2,1)S(1)}, f32[1,2048]{1,0:T(1,128)S(1)}) custom-call(s32[3]{0:T(128)S(1)} %pad_add_fusion.bits, bf16[256,4096]{1,0:T(8,128)(2,1)S(1)} %copy-done), custom_call_target="tpu_custom_call" | custom-call | flops 1024 | bytes 1024 | tf_op jit(solution)/shard_map/pallas_call | solution.py:226
  2.6 0.7 collective-permute-start.1
  3.3 7.8 %collective-permute-start.2 = (bf16[256,2048]{1,0:T(8,128)(2,1)S(1)}, bf16[256,2048]{1,0:T(8,128)(2,1)S(1)}, u32[]{:S(2)}, u32[]{:S(2)}) collective-permute-start(bf16[256,2048]{1,0:T(8,128)(2,1)S(1)} %get-tuple-element.29.near), channel_id=1, source_target_pairs={{0,4},{12,8},{1,5},{13,9},{2,6},{14,10},{3,7},{15,11},{16,20},{28,... | collective-permute-start | bytes 3145736 | tf_op jit(solution)/shard_map/ppermute | solution.py:241
  11.1 1.3 %collective-permute-start.3 = (f32[1,2048]{1,0:T(1,128)S(1)}, f32[1,2048]{1,0:T(1,128)S(1)}, u32[]{:S(2)}, u32[]{:S(2)}) collective-permute-start(f32[1,2048]{1,0:T(1,128)S(1)} %get-tuple-element.30), channel_id=1, source_target_pairs={{0,8},{12,4},{1,9},{13,5},{2,10},{14,6},{3,11},{15,7},{16,24},{28,... | collective-permute-start | bytes 24584 | tf_op jit(solution)/shard_map/ppermute | solution.py:240
  12.4 1.4 %collective-permute-start = (bf16[256,2048]{1,0:T(8,128)(2,1)S(1)}, bf16[256,2048]{1,0:T(8,128)(2,1)S(1)}, u32[]{:S(2)}, u32[]{:S(2)}) collective-permute-start(bf16[256,2048]{1,0:T(8,128)(2,1)S(1)} %get-tuple-element.28), channel_id=1, source_target_pairs={{0,8},{12,4},{1,9},{13,5},{2,10},{14,6},{3,11},{15,7},{16,24},{28,... | collective-permute-start | bytes 3145736 | tf_op jit(solution)/shard_map/ppermute | solution.py:242
  13.7 21.0 %collective-permute-done.3.far_sum = f32[1,2048]{1,0:T(1,128)S(1)} collective-permute-done((f32[1,2048]{1,0:T(1,128)S(1)}, f32[1,2048]{1,0:T(1,128)S(1)}, u32[]{:S(2)}, u32[]{:S(2)}) %collective-permute-start.3) | collective-permute-done | bytes 8224 | tf_op jit(solution)/shard_map/ppermute | solution.py:240
  35.3 3.3 %shard_map.48 = (bf16[3,256,2048]{2,1,0:T(8,128)(2,1)S(1)}, f32[1,2048]{1,0:T(1,128)S(1)}, f32[3,256,256]{2,1,0:T(8,128)S(1)}, f32[1,256,256]{2,1,0:T(8,128)S(1)...) custom-call(s32[3]{0:T(128)S(1)} %pad_add_fusion.bits, bf16[256,2048]{1,0:T(8,128)(2,1)S(1)} %collective-permute-done.1.other, ...), custom_call_target="tpu_custom_call" | custom-call | flops 1024 | bytes 1024 | tf_op jit(solution)/shard_map/pallas_call | solution.py:253
  39.2 0.7 collective-permute-start.5
  40.7 0.9 %shard_map.49 = (f32[256,256]{1,0:T(8,128)S(1)}, f32[256,256]{1,0:T(8,128)S(1)}, f32[256,256]{1,0:T(8,128)S(1)}, f32[256,256]{1,0:T(8,128)S(1)}, f32[256,256]{1,0:T(8,128)S(1)}) custom-call(s32[3]{0:T(128)S(1)} %pad_add_fusion.bits, s32[5,2,2]{2,1,0:T(2,128)S(1)} %copy-done.1, f32[3,256,256]{2,1,0:T(8,128)S(1)} %get-tuple-element.33.own, ...), custom_call_target="tpu_custom_call" | custom-call | flops 1024 | bytes 1024 | tf_op jit(solution)/shard_map/pallas_call | solution.py:195
  43.1 12.7 %collective-permute-done.far_edge = bf16[256,2048]{1,0:T(8,128)(2,1)S(1)} collective-permute-done((bf16[256,2048]{1,0:T(8,128)(2,1)S(1)}, bf16[256,2048]{1,0:T(8,128)(2,1)S(1)}, u32[]{:S(2)}, u32[]{:S(2)}) %collective-permute-start) | collective-permute-done | bytes 1048608 | tf_op jit(solution)/shard_map/ppermute | solution.py:242
  55.8 1.4 %shard_map.50 = (bf16[256,2048]{1,0:T(8,128)(2,1)S(1)}, f32[2,256,256]{2,1,0:T(8,128)S(1)}, f32[256,256]{1,0:T(8,128)S(1)}, f32[256,256]{1,0:T(8,128)S(1)}, f32[256,256]{1,0:T(8,128)S(1)}) custom-call(s32[3]{0:T(128)S(1)} %pad_add_fusion.bits, ...), custom_call_target="tpu_custom_call", output_to_operand_aliasing={{2}: (4, {}), {3}: (5, {}), {4}: (6, {})} | custom-call | flops 1024 | bytes 1024 | tf_op jit(solution)/shard_map/pallas_call | solution.py:276
  57.2 0.7 collective-permute-start.9
  58.0 1.3 %collective-permute-start.14 = (f16[256,256]{1,0:T(8,128)(2,1)S(1)}, f16[256,256]{1,0:T(8,128)(2,1)S(1)}, u32[]{:S(2)}, u32[]{:S(2)}) collective-permute-start(f16[256,256]{1,0:T(8,128)(2,1)S(1)} %convert_element_type.64), channel_id=1, source_target_pairs={{4,0},{5,10},{6,8},{7,1},{10,15},{11,5},{8,7},{9,14},{20,16},{21,2... | collective-permute-start | bytes 393224 | tf_op jit(solution)/shard_map/ppermute | solution.py:224
  59.3 1.3 %shard_map.51.own = f32[2,256,256]{2,1,0:T(8,128)S(1)} custom-call(s32[3]{0:T(128)S(1)} %pad_add_fusion.bits, bf16[256,2048]{1,0:T(8,128)(2,1)S(1)} %get-tuple-element.42.last, bf16[3,256,2048]{2,1,0:T(8,128)(2,1)S(1)} %get-tuple-element.32.centred), custom_call_target="tpu_custom_call" | custom-call | flops 1024 | bytes 1024 | tf_op jit(solution)/shard_map/pallas_call | solution.py:286
  60.6 1.3 %collective-permute-start.15 = (f16[256,256]{1,0:T(8,128)(2,1)S(1)}, f16[256,256]{1,0:T(8,128)(2,1)S(1)}, u32[]{:S(2)}, u32[]{:S(2)}) collective-permute-start(f16[256,256]{1,0:T(8,128)(2,1)S(1)} %convert_element_type.66), channel_id=1, source_target_pairs={{4,8},{5,1},{6,0},{7,10},{10,7},{11,14},{8,15},{9,5},{20,24},{21,1... | collective-permute-start | bytes 393224 | tf_op jit(solution)/shard_map/ppermute | solution.py:224
  61.9 0.9 %shard_map.52 = (f32[256,256]{1,0:T(8,128)S(1)}, f32[256,256]{1,0:T(8,128)S(1)}, f32[256,256]{1,0:T(8,128)S(1)}, f32[256,256]{1,0:T(8,128)S(1)}) custom-call(s32[3]{0:T(128)S(1)} %pad_add_fusion.bits, s32[4,2,2]{2,1,0:T(2,128)S(1)} %copy-done.2, f32[2,256,256]{2,1,0:T(8,128)S(1)} %shard_map.51.own, f32[2,256,256]{2,1,0:T(8,128)S(1)} %collective-permute-done.9.rest_0_, ...), custom_call_target="tpu_custom_call" | custom-call | flops 1024 | bytes 1024 | tf_op jit(solution)/shard_map/pallas_call | solution.py:195
  63.5 1.3 %collective-permute-start.11 = (f16[256,256]{1,0:T(8,128)(2,1)S(1)}, f16[256,256]{1,0:T(8,128)(2,1)S(1)}, u32[]{:S(2)}, u32[]{:S(2)}) collective-permute-start(f16[256,256]{1,0:T(8,128)(2,1)S(1)} %convert_element_type.58), channel_id=1, source_target_pairs={{4,3},{5,14},{6,7},{7,15},{10,12},{11,1},{8,8},{9,0},{20,19},{21,3... | collective-permute-start | bytes 393224 | tf_op jit(solution)/shard_map/ppermute | solution.py:224
  65.6 1.4 %collective-permute-done.14 = f16[256,256]{1,0:T(8,128)(2,1)S(1)} collective-permute-done((f16[256,256]{1,0:T(8,128)(2,1)S(1)}, f16[256,256]{1,0:T(8,128)(2,1)S(1)}, u32[]{:S(2)}, u32[]{:S(2)}) %collective-permute-start.14) | collective-permute-done | bytes 131104 | tf_op jit(solution)/shard_map/ppermute | solution.py:224
  67.0 1.3 %collective-permute-start.13 = (f16[256,256]{1,0:T(8,128)(2,1)S(1)}, f16[256,256]{1,0:T(8,128)(2,1)S(1)}, u32[]{:S(2)}, u32[]{:S(2)}) collective-permute-start(f16[256,256]{1,0:T(8,128)(2,1)S(1)} %convert_element_type.62), channel_id=1, source_target_pairs={{4,7},{5,15},{6,3},{7,14},{10,8},{11,0},{8,12},{9,1},{20,23},{21,3... | collective-permute-start | bytes 393224 | tf_op jit(solution)/shard_map/ppermute | solution.py:224
  68.9 2.6 %collective-permute-done.15 = f16[256,256]{1,0:T(8,128)(2,1)S(1)} collective-permute-done((f16[256,256]{1,0:T(8,128)(2,1)S(1)}, f16[256,256]{1,0:T(8,128)(2,1)S(1)}, u32[]{:S(2)}, u32[]{:S(2)}) %collective-permute-start.15) | collective-permute-done | bytes 131104 | tf_op jit(solution)/shard_map/ppermute | solution.py:224
  71.5 7.2 %collective-permute-done.11 = f16[256,256]{1,0:T(8,128)(2,1)S(1)} collective-permute-done((f16[256,256]{1,0:T(8,128)(2,1)S(1)}, f16[256,256]{1,0:T(8,128)(2,1)S(1)}, u32[]{:S(2)}, u32[]{:S(2)}) %collective-permute-start.11) | collective-permute-done | bytes 131104 | tf_op jit(solution)/shard_map/ppermute | solution.py:224
  78.7 5.1 %collective-permute-done.13 = f16[256,256]{1,0:T(8,128)(2,1)S(1)} collective-permute-done((f16[256,256]{1,0:T(8,128)(2,1)S(1)}, f16[256,256]{1,0:T(8,128)(2,1)S(1)}, u32[]{:S(2)}, u32[]{:S(2)}) %collective-permute-start.13) | collective-permute-done | bytes 131104 | tf_op jit(solution)/shard_map/ppermute | solution.py:224
  83.8 0.8 select_add_fusion
  (33 shorter events, 4.8 us)
Async XLA Ops:
  0.1 1.6 %copy-start = (bf16[256,4096]{1,0:T(8,128)(2,1)S(1)}, bf16[256,4096]{1,0:T(8,128)(2,1)}, u32[]{:S(2)}) copy-start(bf16[256,4096]{1,0:T(8,128)(2,1)} %values.1) | copy-start | bytes 6291460
  2.6 32.2 %collective-permute-start.1 = (bf16[256,2048]{1,0:T(8,128)(2,1)S(1)}, bf16[256,2048]{1,0:T(8,128)(2,1)S(1)}, u32[]{:S(2)}, u32[]{:S(2)}) collective-permute-start(bf16[256,2048]{1,0:T(8,128)(2,1)S(1)} %get-tuple-element.28), channel_id=1, source_target_pairs={{4,8},{8,4},{5,9},{9,5},{6,10},{10,6},{7,11},{11,7},{20,24},{24,20... | collective-permute-start | bytes 3145736 | tf_op jit(solution)/shard_map/ppermute | solution.py:239
  3.3 31.9 %collective-permute-start.2 = (bf16[256,2048]{1,0:T(8,128)(2,1)S(1)}, bf16[256,2048]{1,0:T(8,128)(2,1)S(1)}, u32[]{:S(2)}, u32[]{:S(2)}) collective-permute-start(bf16[256,2048]{1,0:T(8,128)(2,1)S(1)} %get-tuple-element.29.near), channel_id=1, source_target_pairs={{0,4},{12,8},{1,5},{13,9},{2,6},{14,10},{3,7},{15,11},{16,20},{28,... | collective-permute-start | bytes 3145736 | tf_op jit(solution)/shard_map/ppermute | solution.py:241
  11.1 23.7 %collective-permute-start.3 = (f32[1,2048]{1,0:T(1,128)S(1)}, f32[1,2048]{1,0:T(1,128)S(1)}, u32[]{:S(2)}, u32[]{:S(2)}) collective-permute-start(f32[1,2048]{1,0:T(1,128)S(1)} %get-tuple-element.30), channel_id=1, source_target_pairs={{0,8},{12,4},{1,9},{13,5},{2,10},{14,6},{3,11},{15,7},{16,24},{28,... | collective-permute-start | bytes 24584 | tf_op jit(solution)/shard_map/ppermute | solution.py:240
  12.4 43.4 %collective-permute-start = (bf16[256,2048]{1,0:T(8,128)(2,1)S(1)}, bf16[256,2048]{1,0:T(8,128)(2,1)S(1)}, u32[]{:S(2)}, u32[]{:S(2)}) collective-permute-start(bf16[256,2048]{1,0:T(8,128)(2,1)S(1)} %get-tuple-element.28), channel_id=1, source_target_pairs={{0,8},{12,4},{1,9},{13,5},{2,10},{14,6},{3,11},{15,7},{16,24},{28,... | collective-permute-start | bytes 3145736 | tf_op jit(solution)/shard_map/ppermute | solution.py:242
  35.2 5.4 %copy-start.1 = (s32[5,2,2]{2,1,0:T(2,128)S(1)}, s32[5,2,2]{2,1,0:T(2,128)}, u32[]{:S(2)}) copy-start(s32[5,2,2]{2,1,0:T(2,128)} %constant.22.clone.places) | copy-start | bytes 244
  38.6 2.1 %collective-permute-start.4 = (f32[1,256,256]{2,1,0:T(8,128)S(1)}, f32[1,256,256]{2,1,0:T(8,128)S(1)}, u32[]{:S(2)}, u32[]{:S(2)}) collective-permute-start(f32[1,256,256]{2,1,0:T(8,128)S(1)} %get-tuple-element.34), channel_id=1, source_target_pairs={{4,5},{5,4},{8,9},{9,8},{6,7},{7,6},{10,11},{11,10},{20,21},{21,20... | collective-permute-start | bytes 786440 | tf_op jit(solution)/shard_map/ppermute | solution.py:221
  39.2 1.4 %collective-permute-start.5 = (f32[1,256,256]{2,1,0:T(8,128)S(1)}, f32[1,256,256]{2,1,0:T(8,128)S(1)}, u32[]{:S(2)}, u32[]{:S(2)}) collective-permute-start(f32[1,256,256]{2,1,0:T(8,128)S(1)} %get-tuple-element.35), channel_id=1, source_target_pairs={{4,5},{5,4},{8,9},{9,8},{6,7},{7,6},{10,11},{11,10},{20,21},{21,20... | collective-permute-start | bytes 786440 | tf_op jit(solution)/shard_map/ppermute | solution.py:221
  39.9 0.7 collective-permute-start.6
  41.6 1.4 %collective-permute-start.7 = (f16[256,256]{1,0:T(8,128)(2,1)S(1)}, f16[256,256]{1,0:T(8,128)(2,1)S(1)}, u32[]{:S(2)}, u32[]{:S(2)}) collective-permute-start(f16[256,256]{1,0:T(8,128)(2,1)S(1)} %convert_element_type.52), channel_id=1, source_target_pairs={{4,5},{5,4},{6,2},{7,6},{10,10},{11,11},{8,13},{9,9},{20,21},{21,2... | collective-permute-start | bytes 393224 | tf_op jit(solution)/shard_map/ppermute | solution.py:224
  42.3 0.7 collective-permute-start.8
  57.2 4.7 %copy-start.2 = (s32[4,2,2]{2,1,0:T(2,128)S(1)}, s32[4,2,2]{2,1,0:T(2,128)}, u32[]{:S(2)}) copy-start(s32[4,2,2]{2,1,0:T(2,128)} %constant.23.clone.places) | copy-start | bytes 196
  57.2 4.6 %collective-permute-start.9 = (f32[2,256,256]{2,1,0:T(8,128)S(1)}, f32[2,256,256]{2,1,0:T(8,128)S(1)}, u32[]{:S(2)}, u32[]{:S(2)}) collective-permute-start(f32[2,256,256]{2,1,0:T(8,128)S(1)} %get-tuple-element.43), channel_id=1, source_target_pairs={{4,5},{5,4},{8,9},{9,8},{6,7},{7,6},{10,11},{11,10},{20,21},{21,20... | collective-permute-start | bytes 1572872 | tf_op jit(solution)/shard_map/ppermute | solution.py:221
  58.0 9.0 %collective-permute-start.14 = (f16[256,256]{1,0:T(8,128)(2,1)S(1)}, f16[256,256]{1,0:T(8,128)(2,1)S(1)}, u32[]{:S(2)}, u32[]{:S(2)}) collective-permute-start(f16[256,256]{1,0:T(8,128)(2,1)S(1)} %convert_element_type.64), channel_id=1, source_target_pairs={{4,0},{5,10},{6,8},{7,1},{10,15},{11,5},{8,7},{9,14},{20,16},{21,2... | collective-permute-start | bytes 393224 | tf_op jit(solution)/shard_map/ppermute | solution.py:224
  60.6 10.9 %collective-permute-start.15 = (f16[256,256]{1,0:T(8,128)(2,1)S(1)}, f16[256,256]{1,0:T(8,128)(2,1)S(1)}, u32[]{:S(2)}, u32[]{:S(2)}) collective-permute-start(f16[256,256]{1,0:T(8,128)(2,1)S(1)} %convert_element_type.66), channel_id=1, source_target_pairs={{4,8},{5,1},{6,0},{7,10},{10,7},{11,14},{8,15},{9,5},{20,24},{21,1... | collective-permute-start | bytes 393224 | tf_op jit(solution)/shard_map/ppermute | solution.py:224
  62.8 8.7 %collective-permute-start.10 = (f16[256,256]{1,0:T(8,128)(2,1)S(1)}, f16[256,256]{1,0:T(8,128)(2,1)S(1)}, u32[]{:S(2)}, u32[]{:S(2)}) collective-permute-start(f16[256,256]{1,0:T(8,128)(2,1)S(1)} %convert_element_type.56), channel_id=1, source_target_pairs={{4,12},{5,11},{6,13},{7,9},{10,3},{11,4},{8,2},{9,6},{20,28},{21,2... | collective-permute-start | bytes 393224 | tf_op jit(solution)/shard_map/ppermute | solution.py:224
  63.5 15.2 %collective-permute-start.11 = (f16[256,256]{1,0:T(8,128)(2,1)S(1)}, f16[256,256]{1,0:T(8,128)(2,1)S(1)}, u32[]{:S(2)}, u32[]{:S(2)}) collective-permute-start(f16[256,256]{1,0:T(8,128)(2,1)S(1)} %convert_element_type.58), channel_id=1, source_target_pairs={{4,3},{5,14},{6,7},{7,15},{10,12},{11,1},{8,8},{9,0},{20,19},{21,3... | collective-permute-start | bytes 393224 | tf_op jit(solution)/shard_map/ppermute | solution.py:224
  64.9 13.8 %collective-permute-start.12 = (f16[256,256]{1,0:T(8,128)(2,1)S(1)}, f16[256,256]{1,0:T(8,128)(2,1)S(1)}, u32[]{:S(2)}, u32[]{:S(2)}) collective-permute-start(f16[256,256]{1,0:T(8,128)(2,1)S(1)} %convert_element_type.60), channel_id=1, source_target_pairs={{4,13},{5,9},{6,12},{7,11},{10,2},{11,6},{8,3},{9,4},{20,29},{21,2... | collective-permute-start | bytes 393224 | tf_op jit(solution)/shard_map/ppermute | solution.py:224
  67.0 16.8 %collective-permute-start.13 = (f16[256,256]{1,0:T(8,128)(2,1)S(1)}, f16[256,256]{1,0:T(8,128)(2,1)S(1)}, u32[]{:S(2)}, u32[]{:S(2)}) collective-permute-start(f16[256,256]{1,0:T(8,128)(2,1)S(1)} %convert_element_type.62), channel_id=1, source_target_pairs={{4,7},{5,15},{6,3},{7,14},{10,8},{11,0},{8,12},{9,1},{20,23},{21,3... | collective-permute-start | bytes 393224 | tf_op jit(solution)/shard_map/ppermute | solution.py:224

commit v13 on v10

--- a/solution.py
+++ b/solution.py
@@ -150,7 +150,8 @@
 
 def late_products(core, last, centred, out):
     for place, (_, j) in enumerate(LATE_SUMS[core]):
-        out[place] = block_product(last[...], last[...] if j == 3 else centred[j])
+        product = block_product(last[...], last[...] if j == 3 else centred[j])
+        out[place] = product * (1.0 / (4 * last.shape[0]))
 
 
 def late_kernel(bits, far_edge, mean, centred, *rest):
@@ -291,10 +292,10 @@
         compiler_params=LIMIT,
         cost_estimate=BRIEF,
     )(bits, last, centred)
-    other = swap(other)
+    other = swap(other.astype(jnp.float16)).astype(jnp.float32)
     arrived = [send(value, blocks) for value, blocks in zip(far_blocks, FAR_ROUNDS)]
     places = held_place(LATE_HELD, LATE_ROUNDS)
-    late = combine(bits, own, [other], (0, 1), (spare,), LATE_HELD, places, samples)
+    late = combine(bits, own, [other], (0, 1), (spare,), LATE_HELD, places, 1)
     arrived += [send(value, blocks) for value, blocks in zip(late, LATE_ROUNDS)]
     summed = summed + sum(block.astype(jnp.float32) for block in reversed(arrived))
     return add_shift(summed, 1, shift, local_rows)

time: 81.2 us -> 81.3 us (level)
  transfers between devices with their start and end apart: 16 -> 16, of which waited for: 5 -> 4; matrix products, arithmetic and copies ran while one was open for 0% -> 0% of each run, Pallas kernels for 9% -> 9%
where the time goes in v13:
time: 81.3 us; the launch traced here: 79.9 us
  starting transfers between devices  34.9 us (43%)
  waiting for transfers between devices  32 us (39%)
  Pallas kernels  9.22 us (11%)
  local copies, waits for them, and re-layouts  1.61 us (2%)
  other arithmetic  1.16 us (1%)
  between operations  1.04 us (1%)
    ppermute x1, waiting for transfers between devices, two_centres(): from_sum = lax.ppermute(far_sum, 'row', to_far)  24.1 us
    ppermute x8, starting transfers between devices, send(): lax.ppermute(value.astype(jnp.float16), everyone, round_pairs(blocks))  19.4 us
    ppermute x4, starting transfers between devices, swap(): return lax.ppermute(value, ('row', 'half'), centres)  8.17 us
    ppermute x8, waiting for transfers between devices, send(): lax.ppermute(value.astype(jnp.float16), everyone, round_pairs(blocks))  6.35 us
    ppermute x1, starting transfers between devices, two_centres(): from_centre = lax.ppermute(far, 'row', to_centre)  3.48 us
    pallas_call x1, Pallas kernels, two_centres(): pl.pallas_call(early_kernel, out_shape=[shape_of((3, local_rows, part), j...  3.3 us
    pallas_call x2, Pallas kernels, combine(): pl.pallas_call(functools.partial(combine_kernel, flips, 1.0 / samples, le...  1.83 us
  transfers between devices with their start and end apart: 16, of which 4 were waited for; matrix products, arithmetic and copies ran while one was open for 0% of the time, Pallas kernels for 9%

profile of v13, /device:TPU:8, one launch (start us, length us, event | category | flops | bytes accessed | tf_op | source)
XLA Modules:
  0.0 79.9 jit_solution(9982391935985965891)
XLA Ops:
  0.1 1.6 %copy-done = bf16[256,4096]{1,0:T(8,128)(2,1)S(1)} copy-done((bf16[256,4096]{1,0:T(8,128)(2,1)S(1)}, bf16[256,4096]{1,0:T(8,128)(2,1)}, u32[]{:S(2)}) %copy-start) | copy-done | bytes 2097176
  2.6 3.5 %collective-permute-start.1 = (bf16[256,2048]{1,0:T(8,128)(2,1)S(1)}, bf16[256,2048]{1,0:T(8,128)(2,1)S(1)}, u32[]{:S(2)}, u32[]{:S(2)}) collective-permute-start(bf16[256,2048]{1,0:T(8,128)(2,1)S(1)} %get-tuple-element.28), channel_id=1, source_target_pairs={{4,8},{8,4},{5,9},{9,5},{6,10},{10,6},{7,11},{11,7},{20,24},{24,20... | collective-permute-start | bytes 3145736 | tf_op jit(solution)/shard_map/ppermute | solution.py:240
  6.1 1.3 %collective-permute-start.2 = (bf16[256,2048]{1,0:T(8,128)(2,1)S(1)}, bf16[256,2048]{1,0:T(8,128)(2,1)S(1)}, u32[]{:S(2)}, u32[]{:S(2)}) collective-permute-start(bf16[256,2048]{1,0:T(8,128)(2,1)S(1)} %get-tuple-element.29.near), channel_id=1, source_target_pairs={{0,4},{12,8},{1,5},{13,9},{2,6},{14,10},{3,7},{15,11},{16,20},{28,... | collective-permute-start | bytes 3145736 | tf_op jit(solution)/shard_map/ppermute | solution.py:242
  7.4 1.3 %collective-permute-start.3 = (f32[1,2048]{1,0:T(1,128)S(1)}, f32[1,2048]{1,0:T(1,128)S(1)}, u32[]{:S(2)}, u32[]{:S(2)}) collective-permute-start(f32[1,2048]{1,0:T(1,128)S(1)} %get-tuple-element.30), channel_id=1, source_target_pairs={{0,8},{12,4},{1,9},{13,5},{2,10},{14,6},{3,11},{15,7},{16,24},{28,... | collective-permute-start | bytes 24584 | tf_op jit(solution)/shard_map/ppermute | solution.py:241
  8.7 1.3 %collective-permute-start = (bf16[256,2048]{1,0:T(8,128)(2,1)S(1)}, bf16[256,2048]{1,0:T(8,128)(2,1)S(1)}, u32[]{:S(2)}, u32[]{:S(2)}) collective-permute-start(bf16[256,2048]{1,0:T(8,128)(2,1)S(1)} %get-tuple-element.28), channel_id=1, source_target_pairs={{0,8},{12,4},{1,9},{13,5},{2,10},{14,6},{3,11},{15,7},{16,24},{28,... | collective-permute-start | bytes 3145736 | tf_op jit(solution)/shard_map/ppermute | solution.py:243
  10.0 24.1 %collective-permute-done.3.far_sum = f32[1,2048]{1,0:T(1,128)S(1)} collective-permute-done((f32[1,2048]{1,0:T(1,128)S(1)}, f32[1,2048]{1,0:T(1,128)S(1)}, u32[]{:S(2)}, u32[]{:S(2)}) %collective-permute-start.3) | collective-permute-done | bytes 8224 | tf_op jit(solution)/shard_map/ppermute | solution.py:241
  34.6 3.3 %shard_map.48 = (bf16[3,256,2048]{2,1,0:T(8,128)(2,1)S(1)}, f32[1,2048]{1,0:T(1,128)S(1)}, f32[3,256,256]{2,1,0:T(8,128)S(1)}, f32[1,256,256]{2,1,0:T(8,128)S(1)...) custom-call(s32[3]{0:T(128)S(1)} %pad_add_fusion.bits, bf16[256,2048]{1,0:T(8,128)(2,1)S(1)} %collective-permute-done.1.other, ...), custom_call_target="tpu_custom_call" | custom-call | flops 1024 | bytes 1024 | tf_op jit(solution)/shard_map/pallas_call | solution.py:254
  37.9 1.9 %collective-permute-start.4 = (f32[1,256,256]{2,1,0:T(8,128)S(1)}, f32[1,256,256]{2,1,0:T(8,128)S(1)}, u32[]{:S(2)}, u32[]{:S(2)}) collective-permute-start(f32[1,256,256]{2,1,0:T(8,128)S(1)} %get-tuple-element.34), channel_id=1, source_target_pairs={{4,5},{5,4},{8,9},{9,8},{6,7},{7,6},{10,11},{11,10},{20,21},{21,20... | collective-permute-start | bytes 786440 | tf_op jit(solution)/shard_map/ppermute | solution.py:222
  39.8 2.4 %collective-permute-start.5 = (f32[1,256,256]{2,1,0:T(8,128)S(1)}, f32[1,256,256]{2,1,0:T(8,128)S(1)}, u32[]{:S(2)}, u32[]{:S(2)}) collective-permute-start(f32[1,256,256]{2,1,0:T(8,128)S(1)} %get-tuple-element.35), channel_id=1, source_target_pairs={{4,5},{5,4},{8,9},{9,8},{6,7},{7,6},{10,11},{11,10},{20,21},{21,20... | collective-permute-start | bytes 786440 | tf_op jit(solution)/shard_map/ppermute | solution.py:222
  42.2 1.9 %collective-permute-start.6 = (f32[1,256,256]{2,1,0:T(8,128)S(1)}, f32[1,256,256]{2,1,0:T(8,128)S(1)}, u32[]{:S(2)}, u32[]{:S(2)}) collective-permute-start(f32[1,256,256]{2,1,0:T(8,128)S(1)} %get-tuple-element.36), channel_id=1, source_target_pairs={{4,5},{5,4},{8,9},{9,8},{6,7},{7,6},{10,11},{11,10},{20,21},{21,20... | collective-permute-start | bytes 786440 | tf_op jit(solution)/shard_map/ppermute | solution.py:222
  44.2 1.5 %collective-permute-done.6.rest_2_ = f32[1,256,256]{2,1,0:T(8,128)S(1)} collective-permute-done((f32[1,256,256]{2,1,0:T(8,128)S(1)}, f32[1,256,256]{2,1,0:T(8,128)S(1)}, u32[]{:S(2)}, u32[]{:S(2)}) %collective-permute-start.6) | collective-permute-done | bytes 262176 | tf_op jit(solution)/shard_map/ppermute | solution.py:222
  45.7 0.9 %shard_map.49 = (f32[256,256]{1,0:T(8,128)S(1)}, f32[256,256]{1,0:T(8,128)S(1)}, f32[256,256]{1,0:T(8,128)S(1)}, f32[256,256]{1,0:T(8,128)S(1)}, f32[256,256]{1,0:T(8,128)S(1)}) custom-call(s32[3]{0:T(128)S(1)} %pad_add_fusion.bits, s32[5,2,2]{2,1,0:T(2,128)S(1)} %copy-done.1, f32[3,256,256]{2,1,0:T(8,128)S(1)} %get-tuple-element.33.own, ...), custom_call_target="tpu_custom_call" | custom-call | flops 1024 | bytes 1024 | tf_op jit(solution)/shard_map/pallas_call | solution.py:196
  47.3 3.3 %collective-permute-start.8 = (f16[256,256]{1,0:T(8,128)(2,1)S(1)}, f16[256,256]{1,0:T(8,128)(2,1)S(1)}, u32[]{:S(2)}, u32[]{:S(2)}) collective-permute-start(f16[256,256]{1,0:T(8,128)(2,1)S(1)} %convert_element_type.60), channel_id=1, source_target_pairs={{4,5},{5,6},{6,4},{7,2},{10,10},{11,9},{8,11},{9,13},{20,21},{21,2... | collective-permute-start | bytes 393224 | tf_op jit(solution)/shard_map/ppermute | solution.py:225
  50.7 4.5 %collective-permute-done.8 = f16[256,256]{1,0:T(8,128)(2,1)S(1)} collective-permute-done((f16[256,256]{1,0:T(8,128)(2,1)S(1)}, f16[256,256]{1,0:T(8,128)(2,1)S(1)}, u32[]{:S(2)}, u32[]{:S(2)}) %collective-permute-start.8) | collective-permute-done | bytes 131104 | tf_op jit(solution)/shard_map/ppermute | solution.py:225
  55.2 1.5 %shard_map.50 = (bf16[256,2048]{1,0:T(8,128)(2,1)S(1)}, f32[2,256,256]{2,1,0:T(8,128)S(1)}, f32[256,256]{1,0:T(8,128)S(1)}, f32[256,256]{1,0:T(8,128)S(1)}, f32[256,256]{1,0:T(8,128)S(1)}) custom-call(s32[3]{0:T(128)S(1)} %pad_add_fusion.bits, ...), custom_call_target="tpu_custom_call", output_to_operand_aliasing={{2}: (4, {}), {3}: (5, {}), {4}: (6, {})} | custom-call | flops 1024 | bytes 1024 | tf_op jit(solution)/shard_map/pallas_call | solution.py:277
  56.8 1.9 %collective-permute-start.9 = (f16[2,256,256]{2,1,0:T(8,128)(2,1)S(1)}, f16[2,256,256]{2,1,0:T(8,128)(2,1)S(1)}, u32[]{:S(2)}, u32[]{:S(2)}) collective-permute-start(f16[2,256,256]{2,1,0:T(8,128)(2,1)S(1)} %convert_element_type.62), channel_id=1, source_target_pairs={{4,5},{5,4},{8,9},{9,8},{6,7},{7,6},{10,11},{11,10},{20,21},{21,20... | collective-permute-start | bytes 786440 | tf_op jit(solution)/shard_map/ppermute | solution.py:222
  58.7 1.3 %collective-permute-start.14 = (f16[256,256]{1,0:T(8,128)(2,1)S(1)}, f16[256,256]{1,0:T(8,128)(2,1)S(1)}, u32[]{:S(2)}, u32[]{:S(2)}) collective-permute-start(f16[256,256]{1,0:T(8,128)(2,1)S(1)} %convert_element_type.72), channel_id=1, source_target_pairs={{4,1},{5,8},{6,0},{7,10},{10,14},{11,7},{8,15},{9,5},{20,17},{21,2... | collective-permute-start | bytes 393224 | tf_op jit(solution)/shard_map/ppermute | solution.py:225
  60.0 1.3 %shard_map.51.own = f32[2,256,256]{2,1,0:T(8,128)S(1)} custom-call(s32[3]{0:T(128)S(1)} %pad_add_fusion.bits, bf16[256,2048]{1,0:T(8,128)(2,1)S(1)} %get-tuple-element.42.last, bf16[3,256,2048]{2,1,0:T(8,128)(2,1)S(1)} %get-tuple-element.32.centred), custom_call_target="tpu_custom_call" | custom-call | flops 1024 | bytes 1024 | tf_op jit(solution)/shard_map/pallas_call | solution.py:287
  61.3 1.3 %collective-permute-start.15 = (f16[256,256]{1,0:T(8,128)(2,1)S(1)}, f16[256,256]{1,0:T(8,128)(2,1)S(1)}, u32[]{:S(2)}, u32[]{:S(2)}) collective-permute-start(f16[256,256]{1,0:T(8,128)(2,1)S(1)} %convert_element_type.74), channel_id=1, source_target_pairs={{4,0},{5,10},{6,1},{7,8},{10,15},{11,5},{8,14},{9,7},{20,16},{21,2... | collective-permute-start | bytes 393224 | tf_op jit(solution)/shard_map/ppermute | solution.py:225
  63.6 1.3 %collective-permute-start.10 = (f16[256,256]{1,0:T(8,128)(2,1)S(1)}, f16[256,256]{1,0:T(8,128)(2,1)S(1)}, u32[]{:S(2)}, u32[]{:S(2)}) collective-permute-start(f16[256,256]{1,0:T(8,128)(2,1)S(1)} %convert_element_type.64), channel_id=1, source_target_pairs={{4,12},{5,14},{6,13},{7,15},{10,3},{11,1},{8,2},{9,0},{20,28},{21,... | collective-permute-start | bytes 393224 | tf_op jit(solution)/shard_map/ppermute | solution.py:225
  65.0 1.3 %collective-permute-start.11 = (f16[256,256]{1,0:T(8,128)(2,1)S(1)}, f16[256,256]{1,0:T(8,128)(2,1)S(1)}, u32[]{:S(2)}, u32[]{:S(2)}) collective-permute-start(f16[256,256]{1,0:T(8,128)(2,1)S(1)} %convert_element_type.66), channel_id=1, source_target_pairs={{4,13},{5,15},{6,12},{7,14},{10,2},{11,0},{8,3},{9,1},{20,29},{21,... | collective-permute-start | bytes 393224 | tf_op jit(solution)/shard_map/ppermute | solution.py:225
  66.3 1.9 %collective-permute-start.12 = (f16[256,256]{1,0:T(8,128)(2,1)S(1)}, f16[256,256]{1,0:T(8,128)(2,1)S(1)}, u32[]{:S(2)}, u32[]{:S(2)}) collective-permute-start(f16[256,256]{1,0:T(8,128)(2,1)S(1)} %convert_element_type.68), channel_id=1, source_target_pairs={{4,3},{5,11},{6,7},{7,9},{10,12},{11,4},{8,8},{9,6},{20,19},{21,27... | collective-permute-start | bytes 393224 | tf_op jit(solution)/shard_map/ppermute | solution.py:225
  68.3 8.3 %collective-permute-start.13 = (f16[256,256]{1,0:T(8,128)(2,1)S(1)}, f16[256,256]{1,0:T(8,128)(2,1)S(1)}, u32[]{:S(2)}, u32[]{:S(2)}) collective-permute-start(f16[256,256]{1,0:T(8,128)(2,1)S(1)} %convert_element_type.70), channel_id=1, source_target_pairs={{4,7},{5,9},{6,3},{7,11},{10,8},{11,6},{8,12},{9,4},{20,23},{21,25... | collective-permute-start | bytes 393224 | tf_op jit(solution)/shard_map/ppermute | solution.py:225
  77.3 1.7 %collective-permute-done.13 = f16[256,256]{1,0:T(8,128)(2,1)S(1)} collective-permute-done((f16[256,256]{1,0:T(8,128)(2,1)S(1)}, f16[256,256]{1,0:T(8,128)(2,1)S(1)}, u32[]{:S(2)}, u32[]{:S(2)}) %collective-permute-start.13) | collective-permute-done | bytes 131104 | tf_op jit(solution)/shard_map/ppermute | solution.py:225
  (35 shorter events, 4.2 us)
Async XLA Ops:
  0.1 1.6 %copy-start = (bf16[256,4096]{1,0:T(8,128)(2,1)S(1)}, bf16[256,4096]{1,0:T(8,128)(2,1)}, u32[]{:S(2)}) copy-start(bf16[256,4096]{1,0:T(8,128)(2,1)} %values.1) | copy-start | bytes 6291460
  2.6 31.5 %collective-permute-start.1 = (bf16[256,2048]{1,0:T(8,128)(2,1)S(1)}, bf16[256,2048]{1,0:T(8,128)(2,1)S(1)}, u32[]{:S(2)}, u32[]{:S(2)}) collective-permute-start(bf16[256,2048]{1,0:T(8,128)(2,1)S(1)} %get-tuple-element.28), channel_id=1, source_target_pairs={{4,8},{8,4},{5,9},{9,5},{6,10},{10,6},{7,11},{11,7},{20,24},{24,20... | collective-permute-start | bytes 3145736 | tf_op jit(solution)/shard_map/ppermute | solution.py:240
  6.1 28.5 %collective-permute-start.2 = (bf16[256,2048]{1,0:T(8,128)(2,1)S(1)}, bf16[256,2048]{1,0:T(8,128)(2,1)S(1)}, u32[]{:S(2)}, u32[]{:S(2)}) collective-permute-start(bf16[256,2048]{1,0:T(8,128)(2,1)S(1)} %get-tuple-element.29.near), channel_id=1, source_target_pairs={{0,4},{12,8},{1,5},{13,9},{2,6},{14,10},{3,7},{15,11},{16,20},{28,... | collective-permute-start | bytes 3145736 | tf_op jit(solution)/shard_map/ppermute | solution.py:242
  7.4 26.7 %collective-permute-start.3 = (f32[1,2048]{1,0:T(1,128)S(1)}, f32[1,2048]{1,0:T(1,128)S(1)}, u32[]{:S(2)}, u32[]{:S(2)}) collective-permute-start(f32[1,2048]{1,0:T(1,128)S(1)} %get-tuple-element.30), channel_id=1, source_target_pairs={{0,8},{12,4},{1,9},{13,5},{2,10},{14,6},{3,11},{15,7},{16,24},{28,... | collective-permute-start | bytes 24584 | tf_op jit(solution)/shard_map/ppermute | solution.py:241
  8.7 46.6 %collective-permute-start = (bf16[256,2048]{1,0:T(8,128)(2,1)S(1)}, bf16[256,2048]{1,0:T(8,128)(2,1)S(1)}, u32[]{:S(2)}, u32[]{:S(2)}) collective-permute-start(bf16[256,2048]{1,0:T(8,128)(2,1)S(1)} %get-tuple-element.28), channel_id=1, source_target_pairs={{0,8},{12,4},{1,9},{13,5},{2,10},{14,6},{3,11},{15,7},{16,24},{28,... | collective-permute-start | bytes 3145736 | tf_op jit(solution)/shard_map/ppermute | solution.py:243
  34.6 11.1 %copy-start.1 = (s32[5,2,2]{2,1,0:T(2,128)S(1)}, s32[5,2,2]{2,1,0:T(2,128)}, u32[]{:S(2)}) copy-start(s32[5,2,2]{2,1,0:T(2,128)} %constant.22.clone.places) | copy-start | bytes 244
  37.9 6.3 %collective-permute-start.4 = (f32[1,256,256]{2,1,0:T(8,128)S(1)}, f32[1,256,256]{2,1,0:T(8,128)S(1)}, u32[]{:S(2)}, u32[]{:S(2)}) collective-permute-start(f32[1,256,256]{2,1,0:T(8,128)S(1)} %get-tuple-element.34), channel_id=1, source_target_pairs={{4,5},{5,4},{8,9},{9,8},{6,7},{7,6},{10,11},{11,10},{20,21},{21,20... | collective-permute-start | bytes 786440 | tf_op jit(solution)/shard_map/ppermute | solution.py:222
  39.8 4.4 %collective-permute-start.5 = (f32[1,256,256]{2,1,0:T(8,128)S(1)}, f32[1,256,256]{2,1,0:T(8,128)S(1)}, u32[]{:S(2)}, u32[]{:S(2)}) collective-permute-start(f32[1,256,256]{2,1,0:T(8,128)S(1)} %get-tuple-element.35), channel_id=1, source_target_pairs={{4,5},{5,4},{8,9},{9,8},{6,7},{7,6},{10,11},{11,10},{20,21},{21,20... | collective-permute-start | bytes 786440 | tf_op jit(solution)/shard_map/ppermute | solution.py:222
  42.2 3.4 %collective-permute-start.6 = (f32[1,256,256]{2,1,0:T(8,128)S(1)}, f32[1,256,256]{2,1,0:T(8,128)S(1)}, u32[]{:S(2)}, u32[]{:S(2)}) collective-permute-start(f32[1,256,256]{2,1,0:T(8,128)S(1)} %get-tuple-element.36), channel_id=1, source_target_pairs={{4,5},{5,4},{8,9},{9,8},{6,7},{7,6},{10,11},{11,10},{20,21},{21,20... | collective-permute-start | bytes 786440 | tf_op jit(solution)/shard_map/ppermute | solution.py:222
  46.6 4.0 %collective-permute-start.7 = (f16[256,256]{1,0:T(8,128)(2,1)S(1)}, f16[256,256]{1,0:T(8,128)(2,1)S(1)}, u32[]{:S(2)}, u32[]{:S(2)}) collective-permute-start(f16[256,256]{1,0:T(8,128)(2,1)S(1)} %convert_element_type.58), channel_id=1, source_target_pairs={{4,4},{5,2},{6,5},{7,6},{10,11},{11,13},{8,10},{9,9},{20,20},{21,1... | collective-permute-start | bytes 393224 | tf_op jit(solution)/shard_map/ppermute | solution.py:225
  47.3 7.9 %collective-permute-start.8 = (f16[256,256]{1,0:T(8,128)(2,1)S(1)}, f16[256,256]{1,0:T(8,128)(2,1)S(1)}, u32[]{:S(2)}, u32[]{:S(2)}) collective-permute-start(f16[256,256]{1,0:T(8,128)(2,1)S(1)} %convert_element_type.60), channel_id=1, source_target_pairs={{4,5},{5,6},{6,4},{7,2},{10,10},{11,9},{8,11},{9,13},{20,21},{21,2... | collective-permute-start | bytes 393224 | tf_op jit(solution)/shard_map/ppermute | solution.py:225
  56.8 5.9 %collective-permute-start.9 = (f16[2,256,256]{2,1,0:T(8,128)(2,1)S(1)}, f16[2,256,256]{2,1,0:T(8,128)(2,1)S(1)}, u32[]{:S(2)}, u32[]{:S(2)}) collective-permute-start(f16[2,256,256]{2,1,0:T(8,128)(2,1)S(1)} %convert_element_type.62), channel_id=1, source_target_pairs={{4,5},{5,4},{8,9},{9,8},{6,7},{7,6},{10,11},{11,10},{20,21},{21,20... | collective-permute-start | bytes 786440 | tf_op jit(solution)/shard_map/ppermute | solution.py:222
  58.7 4.0 %copy-start.2 = (s32[4,2,2]{2,1,0:T(2,128)S(1)}, s32[4,2,2]{2,1,0:T(2,128)}, u32[]{:S(2)}) copy-start(s32[4,2,2]{2,1,0:T(2,128)} %constant.23.clone.places) | copy-start | bytes 196
  58.7 9.5 %collective-permute-start.14 = (f16[256,256]{1,0:T(8,128)(2,1)S(1)}, f16[256,256]{1,0:T(8,128)(2,1)S(1)}, u32[]{:S(2)}, u32[]{:S(2)}) collective-permute-start(f16[256,256]{1,0:T(8,128)(2,1)S(1)} %convert_element_type.72), channel_id=1, source_target_pairs={{4,1},{5,8},{6,0},{7,10},{10,14},{11,7},{8,15},{9,5},{20,17},{21,2... | collective-permute-start | bytes 393224 | tf_op jit(solution)/shard_map/ppermute | solution.py:225
  61.3 15.9 %collective-permute-start.15 = (f16[256,256]{1,0:T(8,128)(2,1)S(1)}, f16[256,256]{1,0:T(8,128)(2,1)S(1)}, u32[]{:S(2)}, u32[]{:S(2)}) collective-permute-start(f16[256,256]{1,0:T(8,128)(2,1)S(1)} %convert_element_type.74), channel_id=1, source_target_pairs={{4,0},{5,10},{6,1},{7,8},{10,15},{11,5},{8,14},{9,7},{20,16},{21,2... | collective-permute-start | bytes 393224 | tf_op jit(solution)/shard_map/ppermute | solution.py:225
  63.6 13.6 %collective-permute-start.10 = (f16[256,256]{1,0:T(8,128)(2,1)S(1)}, f16[256,256]{1,0:T(8,128)(2,1)S(1)}, u32[]{:S(2)}, u32[]{:S(2)}) collective-permute-start(f16[256,256]{1,0:T(8,128)(2,1)S(1)} %convert_element_type.64), channel_id=1, source_target_pairs={{4,12},{5,14},{6,13},{7,15},{10,3},{11,1},{8,2},{9,0},{20,28},{21,... | collective-permute-start | bytes 393224 | tf_op jit(solution)/shard_map/ppermute | solution.py:225
  65.0 12.3 %collective-permute-start.11 = (f16[256,256]{1,0:T(8,128)(2,1)S(1)}, f16[256,256]{1,0:T(8,128)(2,1)S(1)}, u32[]{:S(2)}, u32[]{:S(2)}) collective-permute-start(f16[256,256]{1,0:T(8,128)(2,1)S(1)} %convert_element_type.66), channel_id=1, source_target_pairs={{4,13},{5,15},{6,12},{7,14},{10,2},{11,0},{8,3},{9,1},{20,29},{21,... | collective-permute-start | bytes 393224 | tf_op jit(solution)/shard_map/ppermute | solution.py:225
  66.3 11.0 %collective-permute-start.12 = (f16[256,256]{1,0:T(8,128)(2,1)S(1)}, f16[256,256]{1,0:T(8,128)(2,1)S(1)}, u32[]{:S(2)}, u32[]{:S(2)}) collective-permute-start(f16[256,256]{1,0:T(8,128)(2,1)S(1)} %convert_element_type.68), channel_id=1, source_target_pairs={{4,3},{5,11},{6,7},{7,9},{10,12},{11,4},{8,8},{9,6},{20,19},{21,27... | collective-permute-start | bytes 393224 | tf_op jit(solution)/shard_map/ppermute | solution.py:225
  68.3 10.8 %collective-permute-start.13 = (f16[256,256]{1,0:T(8,128)(2,1)S(1)}, f16[256,256]{1,0:T(8,128)(2,1)S(1)}, u32[]{:S(2)}, u32[]{:S(2)}) collective-permute-start(f16[256,256]{1,0:T(8,128)(2,1)S(1)} %convert_element_type.70), channel_id=1, source_target_pairs={{4,7},{5,9},{6,3},{7,11},{10,8},{11,6},{8,12},{9,4},{20,23},{21,25... | collective-permute-start | bytes 393224 | tf_op jit(solution)/shard_map/ppermute | solution.py:225

commit v14 on v11

--- a/solution.py
+++ b/solution.py
@@ -34,23 +34,24 @@
 
 
 NEAR_ROUNDS = (
-    (((1, 0), (1, 1)), ((0, 2), (1, 2))),
-    (((1, 1), (1, 0)), ((1, 2), (0, 2))),
-)
-MIDDLE_ROUNDS = (
-    (((0, 0), (0, 1)), ((2, 2), (2, 0))),
+    (((1, 1), (0, 2)), ((1, 0), (1, 2))),
+    (((0, 2), (1, 1)), ((1, 2), (1, 0))),
+)
+EDGE_ROUNDS = (
+    (((0, 0), None), (None, (0, 1))),
+    ((None, (0, 0)), ((0, 1), None)),
 )
 LATE_ROUNDS = (
-    (((0, 1), (0, 0)), ((2, 0), (2, 2))),
-    (((1, 3), (0, 3)), ((2, 1), (2, 3))),
-    (((0, 3), (1, 3)), ((2, 3), (2, 1))),
-    (((3, 1), (3, 0)), ((3, 3), (3, 2))),
+    (((0, 3), (1, 3)), ((2, 2), (2, 3))),
+    (((1, 3), (0, 3)), ((2, 1), (2, 2))),
+    (((2, 0), (3, 0)), ((2, 3), (2, 1))),
+    (((3, 1), (2, 0)), ((3, 3), (3, 2))),
     (((3, 0), (3, 1)), ((3, 2), (3, 3))),
 )
-EARLY_SUMS = (((0, 0), (0, 1), (1, 1)), ((2, 2), (2, 0), (2, 1)))
+EARLY_SUMS = (((1, 1), (2, 0), (0, 0)), ((2, 1), (0, 1), (2, 2)))
 EARLY_HELD = (
-    ((0, 0), (0, 1), (1, 1), (1, 0), (1, 1)),
-    ((2, 2), (2, 0), (2, 1), (0, 2), (1, 2)),
+    ((1, 1), (2, 0), (0, 0), (1, 1), (0, 2)),
+    ((2, 1), (0, 1), (2, 2), (1, 2), (1, 0)),
 )
 LATE_SUMS = (((3, 0), (3, 1)), ((3, 2), (3, 3)))
 LATE_HELD = (
@@ -264,16 +265,16 @@
         cost_estimate=BRIEF,
     )(bits, from_centre, from_edge, near, partial)
     others = [swap(other) for other in others]
-    places = held_place(EARLY_HELD, NEAR_ROUNDS + MIDDLE_ROUNDS)
+    places = held_place(EARLY_HELD, NEAR_ROUNDS + EDGE_ROUNDS)
     places += [[[i] * 2] * 2 for i in range(3)]
-    early = list(combine(bits, own, others, (1, 2), (), EARLY_HELD, places, samples))
-    near_blocks, middle_blocks, spares = early[:2], early[2:3], early[3:]
+    early = list(combine(bits, own, others, (0, 1), (), EARLY_HELD, places, samples))
+    near_blocks, edge_blocks, spares = early[:2], early[2:4], early[4:]
     arrived = [send(value, blocks) for value, blocks in zip(near_blocks, NEAR_ROUNDS)]
     summed = sum(block.astype(jnp.float32) for block in arrived)
 
     late_blocks = shape_of((2, local_rows, local_rows), jnp.float32)
-    handed = [summed] + middle_blocks
-    last, other, summed, *middle_blocks = pl.pallas_call(
+    handed = [summed] + edge_blocks
+    last, other, summed, *edge_blocks = pl.pallas_call(
         late_kernel,
         out_shape=[shape_of((local_rows, part), jnp.bfloat16), late_blocks]
         + [shape_of(value.shape, value.dtype) for value in handed],
@@ -292,7 +293,7 @@
         cost_estimate=BRIEF,
     )(bits, last, centred)
     other = swap(other)
-    arrived = [send(value, blocks) for value, blocks in zip(middle_blocks, MIDDLE_ROUNDS)]
+    arrived = [send(value, blocks) for value, blocks in zip(edge_blocks, EDGE_ROUNDS)]
     places = held_place(LATE_HELD, LATE_ROUNDS)
     late = combine(bits, own, [other], (0, 1), spares, LATE_HELD, places, samples)
     arrived += [send(value, blocks) for value, blocks in zip(late, LATE_ROUNDS)]

time: 81.3 us -> 82.6 us (1.016)
  the two profiles are of different devices: /device:TPU:1 before, /device:TPU:9 now
where the time goes in v14:
time: 82.6 us; the launch traced here: 82.1 us
  starting transfers between devices  38.4 us (46%)
  waiting for transfers between devices  30.6 us (37%)
  Pallas kernels  9.32 us (11%)
  local copies, waits for them, and re-layouts  1.61 us (2%)
  other arithmetic  1.13 us (1%)
  between operations  1.04 us (1%)
    ppermute x1, waiting for transfers between devices, two_centres(): from_sum = lax.ppermute(far_sum, 'row', to_far)  21.5 us
    ppermute x9, starting transfers between devices, send(): lax.ppermute(value.astype(jnp.float16), everyone, round_pairs(blocks))  19.4 us
    ppermute x4, starting transfers between devices, swap(): return lax.ppermute(value, ('row', 'half'), centres)  12 us
    ppermute x9, waiting for transfers between devices, send(): lax.ppermute(value.astype(jnp.float16), everyone, round_pairs(blocks))  7.97 us
    pallas_call x1, Pallas kernels, two_centres(): pl.pallas_call(early_kernel, out_shape=[shape_of((3, local_rows, part), j...  3.3 us
    ppermute x1, starting transfers between devices, two_centres(): from_centre = lax.ppermute(far, 'row', to_centre)  3.2 us
    pallas_call x2, Pallas kernels, combine(): pl.pallas_call(functools.partial(combine_kernel, flips, 1.0 / samples, le...  1.93 us
  transfers between devices with their start and end apart: 17, of which 4 were waited for; matrix products, arithmetic and copies ran while one was open for 0% of the time, Pallas kernels for 8%

profile of v14, /device:TPU:9, one launch (start us, length us, event | category | flops | bytes accessed | tf_op | source)
XLA Modules:
  0.0 82.1 jit_solution(9908156456546955129)
XLA Ops:
  0.1 1.6 %copy-done = bf16[256,4096]{1,0:T(8,128)(2,1)S(1)} copy-done((bf16[256,4096]{1,0:T(8,128)(2,1)S(1)}, bf16[256,4096]{1,0:T(8,128)(2,1)}, u32[]{:S(2)}) %copy-start) | copy-done | bytes 2097176
  2.6 3.2 %collective-permute-start.1 = (bf16[256,2048]{1,0:T(8,128)(2,1)S(1)}, bf16[256,2048]{1,0:T(8,128)(2,1)S(1)}, u32[]{:S(2)}, u32[]{:S(2)}) collective-permute-start(bf16[256,2048]{1,0:T(8,128)(2,1)S(1)} %get-tuple-element.31), channel_id=1, source_target_pairs={{4,8},{8,4},{5,9},{9,5},{6,10},{10,6},{7,11},{11,7},{20,24},{24,20... | collective-permute-start | bytes 3145736 | tf_op jit(solution)/shard_map/ppermute | solution.py:239
  5.8 1.3 %collective-permute-start.2 = (bf16[256,2048]{1,0:T(8,128)(2,1)S(1)}, bf16[256,2048]{1,0:T(8,128)(2,1)S(1)}, u32[]{:S(2)}, u32[]{:S(2)}) collective-permute-start(bf16[256,2048]{1,0:T(8,128)(2,1)S(1)} %get-tuple-element.32.near), channel_id=1, source_target_pairs={{0,4},{12,8},{1,5},{13,9},{2,6},{14,10},{3,7},{15,11},{16,20},{28,... | collective-permute-start | bytes 3145736 | tf_op jit(solution)/shard_map/ppermute | solution.py:241
  7.1 1.3 %collective-permute-start.3 = (f32[1,2048]{1,0:T(1,128)S(1)}, f32[1,2048]{1,0:T(1,128)S(1)}, u32[]{:S(2)}, u32[]{:S(2)}) collective-permute-start(f32[1,2048]{1,0:T(1,128)S(1)} %get-tuple-element.33), channel_id=1, source_target_pairs={{0,8},{12,4},{1,9},{13,5},{2,10},{14,6},{3,11},{15,7},{16,24},{28,... | collective-permute-start | bytes 24584 | tf_op jit(solution)/shard_map/ppermute | solution.py:240
  8.4 1.3 %collective-permute-start = (bf16[256,2048]{1,0:T(8,128)(2,1)S(1)}, bf16[256,2048]{1,0:T(8,128)(2,1)S(1)}, u32[]{:S(2)}, u32[]{:S(2)}) collective-permute-start(bf16[256,2048]{1,0:T(8,128)(2,1)S(1)} %get-tuple-element.31), channel_id=1, source_target_pairs={{0,8},{12,4},{1,9},{13,5},{2,10},{14,6},{3,11},{15,7},{16,24},{28,... | collective-permute-start | bytes 3145736 | tf_op jit(solution)/shard_map/ppermute | solution.py:242
  9.7 21.5 %collective-permute-done.3.far_sum = f32[1,2048]{1,0:T(1,128)S(1)} collective-permute-done((f32[1,2048]{1,0:T(1,128)S(1)}, f32[1,2048]{1,0:T(1,128)S(1)}, u32[]{:S(2)}, u32[]{:S(2)}) %collective-permute-start.3) | collective-permute-done | bytes 8224 | tf_op jit(solution)/shard_map/ppermute | solution.py:240
  31.6 3.3 %shard_map.48 = (bf16[3,256,2048]{2,1,0:T(8,128)(2,1)S(1)}, f32[1,2048]{1,0:T(1,128)S(1)}, f32[3,256,256]{2,1,0:T(8,128)S(1)}, f32[1,256,256]{2,1,0:T(8,128)S(1)...) custom-call(s32[3]{0:T(128)S(1)} %pad_add_fusion.bits, bf16[256,2048]{1,0:T(8,128)(2,1)S(1)} %collective-permute-done.1.other, ...), custom_call_target="tpu_custom_call" | custom-call | flops 1024 | bytes 1024 | tf_op jit(solution)/shard_map/pallas_call | solution.py:253
  35.0 5.5 %collective-permute-start.4 = (f32[1,256,256]{2,1,0:T(8,128)S(1)}, f32[1,256,256]{2,1,0:T(8,128)S(1)}, u32[]{:S(2)}, u32[]{:S(2)}) collective-permute-start(f32[1,256,256]{2,1,0:T(8,128)S(1)} %get-tuple-element.37), channel_id=1, source_target_pairs={{4,5},{5,4},{8,9},{9,8},{6,7},{7,6},{10,11},{11,10},{20,21},{21,20... | collective-permute-start | bytes 786440 | tf_op jit(solution)/shard_map/ppermute | solution.py:221
  40.5 1.9 %collective-permute-start.5 = (f32[1,256,256]{2,1,0:T(8,128)S(1)}, f32[1,256,256]{2,1,0:T(8,128)S(1)}, u32[]{:S(2)}, u32[]{:S(2)}) collective-permute-start(f32[1,256,256]{2,1,0:T(8,128)S(1)} %get-tuple-element.38), channel_id=1, source_target_pairs={{4,5},{5,4},{8,9},{9,8},{6,7},{7,6},{10,11},{11,10},{20,21},{21,20... | collective-permute-start | bytes 786440 | tf_op jit(solution)/shard_map/ppermute | solution.py:221
  42.4 2.4 %collective-permute-start.6 = (f32[1,256,256]{2,1,0:T(8,128)S(1)}, f32[1,256,256]{2,1,0:T(8,128)S(1)}, u32[]{:S(2)}, u32[]{:S(2)}) collective-permute-start(f32[1,256,256]{2,1,0:T(8,128)S(1)} %get-tuple-element.39), channel_id=1, source_target_pairs={{4,5},{5,4},{8,9},{9,8},{6,7},{7,6},{10,11},{11,10},{20,21},{21,20... | collective-permute-start | bytes 786440 | tf_op jit(solution)/shard_map/ppermute | solution.py:221
  44.9 1.1 %collective-permute-done.6.rest_2_ = f32[1,256,256]{2,1,0:T(8,128)S(1)} collective-permute-done((f32[1,256,256]{2,1,0:T(8,128)S(1)}, f32[1,256,256]{2,1,0:T(8,128)S(1)}, u32[]{:S(2)}, u32[]{:S(2)}) %collective-permute-start.6) | collective-permute-done | bytes 262176 | tf_op jit(solution)/shard_map/ppermute | solution.py:221
  47.0 2.3 %collective-permute-start.7 = (f16[256,256]{1,0:T(8,128)(2,1)S(1)}, f16[256,256]{1,0:T(8,128)(2,1)S(1)}, u32[]{:S(2)}, u32[]{:S(2)}) collective-permute-start(f16[256,256]{1,0:T(8,128)(2,1)S(1)} %convert_element_type.58), channel_id=1, source_target_pairs={{4,5},{5,4},{6,2},{7,6},{10,10},{11,11},{8,13},{9,9},{20,21},{21,2... | collective-permute-start | bytes 393224 | tf_op jit(solution)/shard_map/ppermute | solution.py:224
  49.3 3.0 %collective-permute-start.8 = (f16[256,256]{1,0:T(8,128)(2,1)S(1)}, f16[256,256]{1,0:T(8,128)(2,1)S(1)}, u32[]{:S(2)}, u32[]{:S(2)}) collective-permute-start(f16[256,256]{1,0:T(8,128)(2,1)S(1)} %convert_element_type.60), channel_id=1, source_target_pairs={{4,2},{5,6},{6,5},{7,4},{10,13},{11,9},{8,10},{9,11},{20,18},{21,2... | collective-permute-start | bytes 393224 | tf_op jit(solution)/shard_map/ppermute | solution.py:224
  52.4 4.1 %collective-permute-done.8 = f16[256,256]{1,0:T(8,128)(2,1)S(1)} collective-permute-done((f16[256,256]{1,0:T(8,128)(2,1)S(1)}, f16[256,256]{1,0:T(8,128)(2,1)S(1)}, u32[]{:S(2)}, u32[]{:S(2)}) %collective-permute-start.8) | collective-permute-done | bytes 131104 | tf_op jit(solution)/shard_map/ppermute | solution.py:224
  56.5 1.5 %shard_map.50 = (bf16[256,2048]{1,0:T(8,128)(2,1)S(1)}, f32[2,256,256]{2,1,0:T(8,128)S(1)}, f32[256,256]{1,0:T(8,128)S(1)}, f32[256,256]{1,0:T(8,128)S(1)}, f32[256,256]{1,0:T(8,128)S(1)}) custom-call(s32[3]{0:T(128)S(1)} %pad_add_fusion.bits, ...), custom_call_target="tpu_custom_call", output_to_operand_aliasing={{2}: (4, {}), {3}: (5, {}), {4}: (6, {})} | custom-call | flops 1024 | bytes 1024 | tf_op jit(solution)/shard_map/pallas_call | solution.py:277
  58.0 2.1 %collective-permute-start.9 = (f32[2,256,256]{2,1,0:T(8,128)S(1)}, f32[2,256,256]{2,1,0:T(8,128)S(1)}, u32[]{:S(2)}, u32[]{:S(2)}) collective-permute-start(f32[2,256,256]{2,1,0:T(8,128)S(1)} %get-tuple-element.46), channel_id=1, source_target_pairs={{4,5},{5,4},{8,9},{9,8},{6,7},{7,6},{10,11},{11,10},{20,21},{21,20... | collective-permute-start | bytes 1572872 | tf_op jit(solution)/shard_map/ppermute | solution.py:221
  60.2 1.3 %collective-permute-start.15 = (f16[256,256]{1,0:T(8,128)(2,1)S(1)}, f16[256,256]{1,0:T(8,128)(2,1)S(1)}, u32[]{:S(2)}, u32[]{:S(2)}) collective-permute-start(f16[256,256]{1,0:T(8,128)(2,1)S(1)} %convert_element_type.72), channel_id=1, source_target_pairs={{5,1},{6,0},{11,14},{8,15},{21,17},{22,16},{27,30},{24,31}} | collective-permute-start | bytes 393224 | tf_op jit(solution)/shard_map/ppermute | solution.py:224
  62.2 1.3 %shard_map.51.own = f32[2,256,256]{2,1,0:T(8,128)S(1)} custom-call(s32[3]{0:T(128)S(1)} %pad_add_fusion.bits, bf16[256,2048]{1,0:T(8,128)(2,1)S(1)} %get-tuple-element.45.last, bf16[3,256,2048]{2,1,0:T(8,128)(2,1)S(1)} %get-tuple-element.35.centred), custom_call_target="tpu_custom_call" | custom-call | flops 1024 | bytes 1024 | tf_op jit(solution)/shard_map/pallas_call | solution.py:287
  64.4 1.3 %collective-permute-start.10 = (f16[256,256]{1,0:T(8,128)(2,1)S(1)}, f16[256,256]{1,0:T(8,128)(2,1)S(1)}, u32[]{:S(2)}, u32[]{:S(2)}) collective-permute-start(f16[256,256]{1,0:T(8,128)(2,1)S(1)} %convert_element_type.62), channel_id=1, source_target_pairs={{4,12},{5,14},{6,13},{7,15},{10,3},{11,1},{8,2},{9,0},{20,28},{21,... | collective-permute-start | bytes 393224 | tf_op jit(solution)/shard_map/ppermute | solution.py:224
  65.8 1.3 %collective-permute-start.11 = (f16[256,256]{1,0:T(8,128)(2,1)S(1)}, f16[256,256]{1,0:T(8,128)(2,1)S(1)}, u32[]{:S(2)}, u32[]{:S(2)}) collective-permute-start(f16[256,256]{1,0:T(8,128)(2,1)S(1)} %convert_element_type.64), channel_id=1, source_target_pairs={{4,13},{5,15},{6,8},{7,14},{10,2},{11,0},{8,7},{9,1},{20,29},{21,3... | collective-permute-start | bytes 393224 | tf_op jit(solution)/shard_map/ppermute | solution.py:224
  67.1 3.2 %collective-permute-start.12 = (f16[256,256]{1,0:T(8,128)(2,1)S(1)}, f16[256,256]{1,0:T(8,128)(2,1)S(1)}, u32[]{:S(2)}, u32[]{:S(2)}) collective-permute-start(f16[256,256]{1,0:T(8,128)(2,1)S(1)} %convert_element_type.66), channel_id=1, source_target_pairs={{4,8},{5,11},{6,12},{7,9},{10,7},{11,4},{8,3},{9,6},{20,24},{21,27... | collective-permute-start | bytes 393224 | tf_op jit(solution)/shard_map/ppermute | solution.py:224
  70.3 4.3 %collective-permute-start.13 = (f16[256,256]{1,0:T(8,128)(2,1)S(1)}, f16[256,256]{1,0:T(8,128)(2,1)S(1)}, u32[]{:S(2)}, u32[]{:S(2)}) collective-permute-start(f16[256,256]{1,0:T(8,128)(2,1)S(1)} %convert_element_type.68), channel_id=1, source_target_pairs={{4,7},{5,9},{6,3},{7,10},{10,8},{11,6},{8,12},{9,5},{20,23},{21,25... | collective-permute-start | bytes 393224 | tf_op jit(solution)/shard_map/ppermute | solution.py:224
  74.6 2.1 %collective-permute-start.14 = (f16[256,256]{1,0:T(8,128)(2,1)S(1)}, f16[256,256]{1,0:T(8,128)(2,1)S(1)}, u32[]{:S(2)}, u32[]{:S(2)}) collective-permute-start(f16[256,256]{1,0:T(8,128)(2,1)S(1)} %convert_element_type.70), channel_id=1, source_target_pairs={{4,3},{5,10},{6,7},{7,11},{10,12},{11,5},{8,8},{9,4},{20,19},{21,2... | collective-permute-start | bytes 393224 | tf_op jit(solution)/shard_map/ppermute | solution.py:224
  77.4 3.8 %collective-permute-done.14 = f16[256,256]{1,0:T(8,128)(2,1)S(1)} collective-permute-done((f16[256,256]{1,0:T(8,128)(2,1)S(1)}, f16[256,256]{1,0:T(8,128)(2,1)S(1)}, u32[]{:S(2)}, u32[]{:S(2)}) %collective-permute-start.14) | collective-permute-done | bytes 131104 | tf_op jit(solution)/shard_map/ppermute | solution.py:224
  (36 shorter events, 5.1 us)
Async XLA Ops:
  0.1 1.6 %copy-start = (bf16[256,4096]{1,0:T(8,128)(2,1)S(1)}, bf16[256,4096]{1,0:T(8,128)(2,1)}, u32[]{:S(2)}) copy-start(bf16[256,4096]{1,0:T(8,128)(2,1)} %values.1) | copy-start | bytes 6291460
  2.6 28.6 %collective-permute-start.1 = (bf16[256,2048]{1,0:T(8,128)(2,1)S(1)}, bf16[256,2048]{1,0:T(8,128)(2,1)S(1)}, u32[]{:S(2)}, u32[]{:S(2)}) collective-permute-start(bf16[256,2048]{1,0:T(8,128)(2,1)S(1)} %get-tuple-element.31), channel_id=1, source_target_pairs={{4,8},{8,4},{5,9},{9,5},{6,10},{10,6},{7,11},{11,7},{20,24},{24,20... | collective-permute-start | bytes 3145736 | tf_op jit(solution)/shard_map/ppermute | solution.py:239
  5.8 25.9 %collective-permute-start.2 = (bf16[256,2048]{1,0:T(8,128)(2,1)S(1)}, bf16[256,2048]{1,0:T(8,128)(2,1)S(1)}, u32[]{:S(2)}, u32[]{:S(2)}) collective-permute-start(bf16[256,2048]{1,0:T(8,128)(2,1)S(1)} %get-tuple-element.32.near), channel_id=1, source_target_pairs={{0,4},{12,8},{1,5},{13,9},{2,6},{14,10},{3,7},{15,11},{16,20},{28,... | collective-permute-start | bytes 3145736 | tf_op jit(solution)/shard_map/ppermute | solution.py:241
  7.1 24.1 %collective-permute-start.3 = (f32[1,2048]{1,0:T(1,128)S(1)}, f32[1,2048]{1,0:T(1,128)S(1)}, u32[]{:S(2)}, u32[]{:S(2)}) collective-permute-start(f32[1,2048]{1,0:T(1,128)S(1)} %get-tuple-element.33), channel_id=1, source_target_pairs={{0,8},{12,4},{1,9},{13,5},{2,10},{14,6},{3,11},{15,7},{16,24},{28,... | collective-permute-start | bytes 24584 | tf_op jit(solution)/shard_map/ppermute | solution.py:240
  8.4 48.1 %collective-permute-start = (bf16[256,2048]{1,0:T(8,128)(2,1)S(1)}, bf16[256,2048]{1,0:T(8,128)(2,1)S(1)}, u32[]{:S(2)}, u32[]{:S(2)}) collective-permute-start(bf16[256,2048]{1,0:T(8,128)(2,1)S(1)} %get-tuple-element.31), channel_id=1, source_target_pairs={{0,8},{12,4},{1,9},{13,5},{2,10},{14,6},{3,11},{15,7},{16,24},{28,... | collective-permute-start | bytes 3145736 | tf_op jit(solution)/shard_map/ppermute | solution.py:242
  31.6 14.4 %copy-start.1 = (s32[7,2,2]{2,1,0:T(2,128)S(1)}, s32[7,2,2]{2,1,0:T(2,128)}, u32[]{:S(2)}) copy-start(s32[7,2,2]{2,1,0:T(2,128)} %constant.22.clone.places) | copy-start | bytes 340
  35.0 9.9 %collective-permute-start.4 = (f32[1,256,256]{2,1,0:T(8,128)S(1)}, f32[1,256,256]{2,1,0:T(8,128)S(1)}, u32[]{:S(2)}, u32[]{:S(2)}) collective-permute-start(f32[1,256,256]{2,1,0:T(8,128)S(1)} %get-tuple-element.37), channel_id=1, source_target_pairs={{4,5},{5,4},{8,9},{9,8},{6,7},{7,6},{10,11},{11,10},{20,21},{21,20... | collective-permute-start | bytes 786440 | tf_op jit(solution)/shard_map/ppermute | solution.py:221
  40.5 4.4 %collective-permute-start.5 = (f32[1,256,256]{2,1,0:T(8,128)S(1)}, f32[1,256,256]{2,1,0:T(8,128)S(1)}, u32[]{:S(2)}, u32[]{:S(2)}) collective-permute-start(f32[1,256,256]{2,1,0:T(8,128)S(1)} %get-tuple-element.38), channel_id=1, source_target_pairs={{4,5},{5,4},{8,9},{9,8},{6,7},{7,6},{10,11},{11,10},{20,21},{21,20... | collective-permute-start | bytes 786440 | tf_op jit(solution)/shard_map/ppermute | solution.py:221
  42.4 3.6 %collective-permute-start.6 = (f32[1,256,256]{2,1,0:T(8,128)S(1)}, f32[1,256,256]{2,1,0:T(8,128)S(1)}, u32[]{:S(2)}, u32[]{:S(2)}) collective-permute-start(f32[1,256,256]{2,1,0:T(8,128)S(1)} %get-tuple-element.39), channel_id=1, source_target_pairs={{4,5},{5,4},{8,9},{9,8},{6,7},{7,6},{10,11},{11,10},{20,21},{21,20... | collective-permute-start | bytes 786440 | tf_op jit(solution)/shard_map/ppermute | solution.py:221
  47.0 5.3 %collective-permute-start.7 = (f16[256,256]{1,0:T(8,128)(2,1)S(1)}, f16[256,256]{1,0:T(8,128)(2,1)S(1)}, u32[]{:S(2)}, u32[]{:S(2)}) collective-permute-start(f16[256,256]{1,0:T(8,128)(2,1)S(1)} %convert_element_type.58), channel_id=1, source_target_pairs={{4,5},{5,4},{6,2},{7,6},{10,10},{11,11},{8,13},{9,9},{20,21},{21,2... | collective-permute-start | bytes 393224 | tf_op jit(solution)/shard_map/ppermute | solution.py:224
  49.3 7.2 %collective-permute-start.8 = (f16[256,256]{1,0:T(8,128)(2,1)S(1)}, f16[256,256]{1,0:T(8,128)(2,1)S(1)}, u32[]{:S(2)}, u32[]{:S(2)}) collective-permute-start(f16[256,256]{1,0:T(8,128)(2,1)S(1)} %convert_element_type.60), channel_id=1, source_target_pairs={{4,2},{5,6},{6,5},{7,4},{10,13},{11,9},{8,10},{9,11},{20,18},{21,2... | collective-permute-start | bytes 393224 | tf_op jit(solution)/shard_map/ppermute | solution.py:224
  58.0 5.5 %copy-start.2 = (s32[5,2,2]{2,1,0:T(2,128)S(1)}, s32[5,2,2]{2,1,0:T(2,128)}, u32[]{:S(2)}) copy-start(s32[5,2,2]{2,1,0:T(2,128)} %constant.23.clone.places) | copy-start | bytes 244
  58.0 5.5 %collective-permute-start.9 = (f32[2,256,256]{2,1,0:T(8,128)S(1)}, f32[2,256,256]{2,1,0:T(8,128)S(1)}, u32[]{:S(2)}, u32[]{:S(2)}) collective-permute-start(f32[2,256,256]{2,1,0:T(8,128)S(1)} %get-tuple-element.46), channel_id=1, source_target_pairs={{4,5},{5,4},{8,9},{9,8},{6,7},{7,6},{10,11},{11,10},{20,21},{21,20... | collective-permute-start | bytes 1572872 | tf_op jit(solution)/shard_map/ppermute | solution.py:221
  60.2 10.2 %collective-permute-start.15 = (f16[256,256]{1,0:T(8,128)(2,1)S(1)}, f16[256,256]{1,0:T(8,128)(2,1)S(1)}, u32[]{:S(2)}, u32[]{:S(2)}) collective-permute-start(f16[256,256]{1,0:T(8,128)(2,1)S(1)} %convert_element_type.72), channel_id=1, source_target_pairs={{5,1},{6,0},{11,14},{8,15},{21,17},{22,16},{27,30},{24,31}} | collective-permute-start | bytes 393224 | tf_op jit(solution)/shard_map/ppermute | solution.py:224
  61.5 13.2 %collective-permute-start.16 = (f16[256,256]{1,0:T(8,128)(2,1)S(1)}, f16[256,256]{1,0:T(8,128)(2,1)S(1)}, u32[]{:S(2)}, u32[]{:S(2)}) collective-permute-start(f16[256,256]{1,0:T(8,128)(2,1)S(1)} %convert_element_type.74), channel_id=1, source_target_pairs={{4,0},{7,1},{10,15},{9,14},{20,16},{23,17},{26,31},{25,30}} | collective-permute-start | bytes 393224 | tf_op jit(solution)/shard_map/ppermute | solution.py:224
  64.4 13.0 %collective-permute-start.10 = (f16[256,256]{1,0:T(8,128)(2,1)S(1)}, f16[256,256]{1,0:T(8,128)(2,1)S(1)}, u32[]{:S(2)}, u32[]{:S(2)}) collective-permute-start(f16[256,256]{1,0:T(8,128)(2,1)S(1)} %convert_element_type.62), channel_id=1, source_target_pairs={{4,12},{5,14},{6,13},{7,15},{10,3},{11,1},{8,2},{9,0},{20,28},{21,... | collective-permute-start | bytes 393224 | tf_op jit(solution)/shard_map/ppermute | solution.py:224
  65.8 11.6 %collective-permute-start.11 = (f16[256,256]{1,0:T(8,128)(2,1)S(1)}, f16[256,256]{1,0:T(8,128)(2,1)S(1)}, u32[]{:S(2)}, u32[]{:S(2)}) collective-permute-start(f16[256,256]{1,0:T(8,128)(2,1)S(1)} %convert_element_type.64), channel_id=1, source_target_pairs={{4,13},{5,15},{6,8},{7,14},{10,2},{11,0},{8,7},{9,1},{20,29},{21,3... | collective-permute-start | bytes 393224 | tf_op jit(solution)/shard_map/ppermute | solution.py:224
  67.1 10.3 %collective-permute-start.12 = (f16[256,256]{1,0:T(8,128)(2,1)S(1)}, f16[256,256]{1,0:T(8,128)(2,1)S(1)}, u32[]{:S(2)}, u32[]{:S(2)}) collective-permute-start(f16[256,256]{1,0:T(8,128)(2,1)S(1)} %convert_element_type.66), channel_id=1, source_target_pairs={{4,8},{5,11},{6,12},{7,9},{10,7},{11,4},{8,3},{9,6},{20,24},{21,27... | collective-permute-start | bytes 393224 | tf_op jit(solution)/shard_map/ppermute | solution.py:224
  70.3 7.1 %collective-permute-start.13 = (f16[256,256]{1,0:T(8,128)(2,1)S(1)}, f16[256,256]{1,0:T(8,128)(2,1)S(1)}, u32[]{:S(2)}, u32[]{:S(2)}) collective-permute-start(f16[256,256]{1,0:T(8,128)(2,1)S(1)} %convert_element_type.68), channel_id=1, source_target_pairs={{4,7},{5,9},{6,3},{7,10},{10,8},{11,6},{8,12},{9,5},{20,23},{21,25... | collective-permute-start | bytes 393224 | tf_op jit(solution)/shard_map/ppermute | solution.py:224
  74.6 6.6 %collective-permute-start.14 = (f16[256,256]{1,0:T(8,128)(2,1)S(1)}, f16[256,256]{1,0:T(8,128)(2,1)S(1)}, u32[]{:S(2)}, u32[]{:S(2)}) collective-permute-start(f16[256,256]{1,0:T(8,128)(2,1)S(1)} %convert_element_type.70), channel_id=1, source_target_pairs={{4,3},{5,10},{6,7},{7,11},{10,12},{11,5},{8,8},{9,4},{20,19},{21,2... | collective-permute-start | bytes 393224 | tf_op jit(solution)/shard_map/ppermute | solution.py:224

commit v15 on v10

--- a/solution.py
+++ b/solution.py
@@ -154,21 +154,15 @@
 
 
 def late_kernel(bits, far_edge, mean, centred, *rest):
-    last, send = rest[(len(rest) - 2) // 2 :][:2]
+    own, send = rest[(len(rest) - 3) // 2 :][:2]
+    last = rest[-1]
     last[...] = (far_edge[...].astype(jnp.float32) - mean[...]).astype(jnp.bfloat16)
-    for core in (0, 1):
-
-        @pl.when(bits[1] != core)
-        def _():
-            late_products(core, last, centred, send)
-
-
-def keep_kernel(bits, last, centred, own):
     for core in (0, 1):
 
         @pl.when(bits[1] == core)
         def _():
             late_products(core, last, centred, own)
+            late_products(1 - core, last, centred, send)
 
 
 def combine_kernel(flips, scale, pieces, spares, bits, places, own, *rest):
@@ -273,24 +267,17 @@
 
     late_blocks = shape_of((2, local_rows, local_rows), jnp.float32)
     handed = [summed] + far_blocks
-    last, other, summed, *far_blocks = pl.pallas_call(
+    own, other, summed, *far_blocks = pl.pallas_call(
         late_kernel,
-        out_shape=[shape_of((local_rows, part), jnp.bfloat16), late_blocks]
+        out_shape=[late_blocks, late_blocks]
         + [shape_of(value.shape, value.dtype) for value in handed],
         in_specs=[SMEM] + [VMEM] * 3 + [ANY] * len(handed),
         out_specs=[VMEM] * 2 + [ANY] * len(handed),
+        scratch_shapes=[pltpu.VMEM((local_rows, part), jnp.bfloat16)],
         input_output_aliases={4 + i: 2 + i for i in range(len(handed))},
         compiler_params=LIMIT,
         cost_estimate=BRIEF,
     )(bits, from_far_edge, mean, centred, *handed)
-    own = pl.pallas_call(
-        keep_kernel,
-        out_shape=late_blocks,
-        in_specs=[SMEM] + [VMEM] * 2,
-        out_specs=VMEM,
-        compiler_params=LIMIT,
-        cost_estimate=BRIEF,
-    )(bits, last, centred)
     other = swap(other)
     arrived = [send(value, blocks) for value, blocks in zip(far_blocks, FAR_ROUNDS)]
     places = held_place(LATE_HELD, LATE_ROUNDS)

time: 81.2 us -> 80.5 us (level)
    pallas_call x2 -> x1, Pallas kernels: 2.74 us -> 2 us  [two_centres(): pl.pallas_call(late_kernel, out_shape=[late_blocks, late_blocks] + [shape...]
  transfers between devices with their start and end apart: 16 -> 16, of which waited for: 5 -> 5; matrix products, arithmetic and copies ran while one was open for 0% -> 0% of each run, Pallas kernels for 9% -> 7%
where the time goes in v15:
time: 80.5 us; the launch traced here: 79 us
  starting transfers between devices  34.9 us (43%)
  waiting for transfers between devices  32 us (40%)
  Pallas kernels  8.48 us (11%)
  local copies, waits for them, and re-layouts  1.61 us (2%)
  other arithmetic  1.09 us (1%)
  between operations  1.01 us (1%)
    ppermute x1, waiting for transfers between devices, two_centres(): from_sum = lax.ppermute(far_sum, 'row', to_far)  24.1 us
    ppermute x8, starting transfers between devices, send(): lax.ppermute(value.astype(jnp.float16), everyone, round_pairs(blocks))  19.4 us
    ppermute x4, starting transfers between devices, swap(): return lax.ppermute(value, ('row', 'half'), centres)  8.17 us
    ppermute x8, waiting for transfers between devices, send(): lax.ppermute(value.astype(jnp.float16), everyone, round_pairs(blocks))  6.35 us
    ppermute x1, starting transfers between devices, two_centres(): from_centre = lax.ppermute(far, 'row', to_centre)  3.48 us
    pallas_call x1, Pallas kernels, two_centres(): pl.pallas_call(early_kernel, out_shape=[shape_of((3, local_rows, part), j...  3.3 us
    pallas_call x1, Pallas kernels, two_centres(): pl.pallas_call(late_kernel, out_shape=[late_blocks, late_blocks] + [shape...  2 us
    pallas_call x2, Pallas kernels, combine(): pl.pallas_call(functools.partial(combine_kernel, flips, 1.0 / samples, le...  1.83 us
  transfers between devices with their start and end apart: 16, of which 5 were waited for; matrix products, arithmetic and copies ran while one was open for 0% of the time, Pallas kernels for 7%

profile of v15, /device:TPU:8, one launch (start us, length us, event | category | flops | bytes accessed | tf_op | source)
XLA Modules:
  0.0 79.0 jit_solution(14624932357739738309)
XLA Ops:
  0.1 1.6 %copy-done = bf16[256,4096]{1,0:T(8,128)(2,1)S(1)} copy-done((bf16[256,4096]{1,0:T(8,128)(2,1)S(1)}, bf16[256,4096]{1,0:T(8,128)(2,1)}, u32[]{:S(2)}) %copy-start) | copy-done | bytes 2097176
  2.6 3.5 %collective-permute-start.1 = (bf16[256,2048]{1,0:T(8,128)(2,1)S(1)}, bf16[256,2048]{1,0:T(8,128)(2,1)S(1)}, u32[]{:S(2)}, u32[]{:S(2)}) collective-permute-start(bf16[256,2048]{1,0:T(8,128)(2,1)S(1)} %get-tuple-element.28), channel_id=1, source_target_pairs={{4,8},{8,4},{5,9},{9,5},{6,10},{10,6},{7,11},{11,7},{20,24},{24,20... | collective-permute-start | bytes 3145736 | tf_op jit(solution)/shard_map/ppermute | solution.py:233
  6.1 1.3 %collective-permute-start.2 = (bf16[256,2048]{1,0:T(8,128)(2,1)S(1)}, bf16[256,2048]{1,0:T(8,128)(2,1)S(1)}, u32[]{:S(2)}, u32[]{:S(2)}) collective-permute-start(bf16[256,2048]{1,0:T(8,128)(2,1)S(1)} %get-tuple-element.29.near), channel_id=1, source_target_pairs={{0,4},{12,8},{1,5},{13,9},{2,6},{14,10},{3,7},{15,11},{16,20},{28,... | collective-permute-start | bytes 3145736 | tf_op jit(solution)/shard_map/ppermute | solution.py:235
  7.4 1.3 %collective-permute-start.3 = (f32[1,2048]{1,0:T(1,128)S(1)}, f32[1,2048]{1,0:T(1,128)S(1)}, u32[]{:S(2)}, u32[]{:S(2)}) collective-permute-start(f32[1,2048]{1,0:T(1,128)S(1)} %get-tuple-element.30), channel_id=1, source_target_pairs={{0,8},{12,4},{1,9},{13,5},{2,10},{14,6},{3,11},{15,7},{16,24},{28,... | collective-permute-start | bytes 24584 | tf_op jit(solution)/shard_map/ppermute | solution.py:234
  8.7 1.3 %collective-permute-start = (bf16[256,2048]{1,0:T(8,128)(2,1)S(1)}, bf16[256,2048]{1,0:T(8,128)(2,1)S(1)}, u32[]{:S(2)}, u32[]{:S(2)}) collective-permute-start(bf16[256,2048]{1,0:T(8,128)(2,1)S(1)} %get-tuple-element.28), channel_id=1, source_target_pairs={{0,8},{12,4},{1,9},{13,5},{2,10},{14,6},{3,11},{15,7},{16,24},{28,... | collective-permute-start | bytes 3145736 | tf_op jit(solution)/shard_map/ppermute | solution.py:236
  10.0 24.1 %collective-permute-done.3.far_sum = f32[1,2048]{1,0:T(1,128)S(1)} collective-permute-done((f32[1,2048]{1,0:T(1,128)S(1)}, f32[1,2048]{1,0:T(1,128)S(1)}, u32[]{:S(2)}, u32[]{:S(2)}) %collective-permute-start.3) | collective-permute-done | bytes 8224 | tf_op jit(solution)/shard_map/ppermute | solution.py:234
  34.6 3.3 %shard_map.48 = (bf16[3,256,2048]{2,1,0:T(8,128)(2,1)S(1)}, f32[1,2048]{1,0:T(1,128)S(1)}, f32[3,256,256]{2,1,0:T(8,128)S(1)}, f32[1,256,256]{2,1,0:T(8,128)S(1)...) custom-call(s32[3]{0:T(128)S(1)} %pad_add_fusion.bits, bf16[256,2048]{1,0:T(8,128)(2,1)S(1)} %collective-permute-done.1.other, ...), custom_call_target="tpu_custom_call" | custom-call | flops 1024 | bytes 1024 | tf_op jit(solution)/shard_map/pallas_call | solution.py:247
  37.9 1.9 %collective-permute-start.4 = (f32[1,256,256]{2,1,0:T(8,128)S(1)}, f32[1,256,256]{2,1,0:T(8,128)S(1)}, u32[]{:S(2)}, u32[]{:S(2)}) collective-permute-start(f32[1,256,256]{2,1,0:T(8,128)S(1)} %get-tuple-element.34), channel_id=1, source_target_pairs={{4,5},{5,4},{8,9},{9,8},{6,7},{7,6},{10,11},{11,10},{20,21},{21,20... | collective-permute-start | bytes 786440 | tf_op jit(solution)/shard_map/ppermute | solution.py:215
  39.8 2.4 %collective-permute-start.5 = (f32[1,256,256]{2,1,0:T(8,128)S(1)}, f32[1,256,256]{2,1,0:T(8,128)S(1)}, u32[]{:S(2)}, u32[]{:S(2)}) collective-permute-start(f32[1,256,256]{2,1,0:T(8,128)S(1)} %get-tuple-element.35), channel_id=1, source_target_pairs={{4,5},{5,4},{8,9},{9,8},{6,7},{7,6},{10,11},{11,10},{20,21},{21,20... | collective-permute-start | bytes 786440 | tf_op jit(solution)/shard_map/ppermute | solution.py:215
  42.2 1.9 %collective-permute-start.6 = (f32[1,256,256]{2,1,0:T(8,128)S(1)}, f32[1,256,256]{2,1,0:T(8,128)S(1)}, u32[]{:S(2)}, u32[]{:S(2)}) collective-permute-start(f32[1,256,256]{2,1,0:T(8,128)S(1)} %get-tuple-element.36), channel_id=1, source_target_pairs={{4,5},{5,4},{8,9},{9,8},{6,7},{7,6},{10,11},{11,10},{20,21},{21,20... | collective-permute-start | bytes 786440 | tf_op jit(solution)/shard_map/ppermute | solution.py:215
  44.2 1.5 %collective-permute-done.6.rest_2_ = f32[1,256,256]{2,1,0:T(8,128)S(1)} collective-permute-done((f32[1,256,256]{2,1,0:T(8,128)S(1)}, f32[1,256,256]{2,1,0:T(8,128)S(1)}, u32[]{:S(2)}, u32[]{:S(2)}) %collective-permute-start.6) | collective-permute-done | bytes 262176 | tf_op jit(solution)/shard_map/ppermute | solution.py:215
  45.7 0.9 %shard_map.49 = (f32[256,256]{1,0:T(8,128)S(1)}, f32[256,256]{1,0:T(8,128)S(1)}, f32[256,256]{1,0:T(8,128)S(1)}, f32[256,256]{1,0:T(8,128)S(1)}, f32[256,256]{1,0:T(8,128)S(1)}) custom-call(s32[3]{0:T(128)S(1)} %pad_add_fusion.bits, s32[5,2,2]{2,1,0:T(2,128)S(1)} %copy-done.1, f32[3,256,256]{2,1,0:T(8,128)S(1)} %get-tuple-element.33.own, ...), custom_call_target="tpu_custom_call" | custom-call | flops 1024 | bytes 1024 | tf_op jit(solution)/shard_map/pallas_call | solution.py:189
  47.4 3.3 %collective-permute-start.8 = (f16[256,256]{1,0:T(8,128)(2,1)S(1)}, f16[256,256]{1,0:T(8,128)(2,1)S(1)}, u32[]{:S(2)}, u32[]{:S(2)}) collective-permute-start(f16[256,256]{1,0:T(8,128)(2,1)S(1)} %convert_element_type.54), channel_id=1, source_target_pairs={{4,5},{5,6},{6,4},{7,2},{10,10},{11,9},{8,11},{9,13},{20,21},{21,2... | collective-permute-start | bytes 393224 | tf_op jit(solution)/shard_map/ppermute | solution.py:218
  50.7 4.5 %collective-permute-done.8 = f16[256,256]{1,0:T(8,128)(2,1)S(1)} collective-permute-done((f16[256,256]{1,0:T(8,128)(2,1)S(1)}, f16[256,256]{1,0:T(8,128)(2,1)S(1)}, u32[]{:S(2)}, u32[]{:S(2)}) %collective-permute-start.8) | collective-permute-done | bytes 131104 | tf_op jit(solution)/shard_map/ppermute | solution.py:218
  55.3 2.0 %shard_map.50 = (f32[2,256,256]{2,1,0:T(8,128)S(1)}, f32[2,256,256]{2,1,0:T(8,128)S(1)}, f32[256,256]{1,0:T(8,128)S(1)}, f32[256,256]{1,0:T(8,128)S(1)}, f32[256,256]{1,0:T(8,128)S(1)}) custom-call(s32[3]{0:T(128)S(1)} %pad_add_fusion.bits, ...), custom_call_target="tpu_custom_call", output_to_operand_aliasing={{2}: (4, {}), {3}: (5, {}), {4}: (6, {})} | custom-call | flops 1024 | bytes 1024 | tf_op jit(solution)/shard_map/pallas_call | solution.py:270
  57.3 1.9 %collective-permute-start.9 = (f32[2,256,256]{2,1,0:T(8,128)S(1)}, f32[2,256,256]{2,1,0:T(8,128)S(1)}, u32[]{:S(2)}, u32[]{:S(2)}) collective-permute-start(f32[2,256,256]{2,1,0:T(8,128)S(1)} %get-tuple-element.43), channel_id=1, source_target_pairs={{4,5},{5,4},{8,9},{9,8},{6,7},{7,6},{10,11},{11,10},{20,21},{21,20... | collective-permute-start | bytes 1572872 | tf_op jit(solution)/shard_map/ppermute | solution.py:215
  59.2 1.3 %collective-permute-start.14 = (f16[256,256]{1,0:T(8,128)(2,1)S(1)}, f16[256,256]{1,0:T(8,128)(2,1)S(1)}, u32[]{:S(2)}, u32[]{:S(2)}) collective-permute-start(f16[256,256]{1,0:T(8,128)(2,1)S(1)} %convert_element_type.64), channel_id=1, source_target_pairs={{4,1},{5,8},{6,0},{7,10},{10,14},{11,7},{8,15},{9,5},{20,17},{21,2... | collective-permute-start | bytes 393224 | tf_op jit(solution)/shard_map/ppermute | solution.py:218
  60.5 1.3 %collective-permute-start.15 = (f16[256,256]{1,0:T(8,128)(2,1)S(1)}, f16[256,256]{1,0:T(8,128)(2,1)S(1)}, u32[]{:S(2)}, u32[]{:S(2)}) collective-permute-start(f16[256,256]{1,0:T(8,128)(2,1)S(1)} %convert_element_type.66), channel_id=1, source_target_pairs={{4,0},{5,10},{6,1},{7,8},{10,15},{11,5},{8,14},{9,7},{20,16},{21,2... | collective-permute-start | bytes 393224 | tf_op jit(solution)/shard_map/ppermute | solution.py:218
  61.9 0.9 %shard_map.51 = (f32[256,256]{1,0:T(8,128)S(1)}, f32[256,256]{1,0:T(8,128)S(1)}, f32[256,256]{1,0:T(8,128)S(1)}, f32[256,256]{1,0:T(8,128)S(1)}) custom-call(s32[3]{0:T(128)S(1)} %pad_add_fusion.bits, s32[4,2,2]{2,1,0:T(2,128)S(1)} %copy-done.2, f32[2,256,256]{2,1,0:T(8,128)S(1)} %get-tuple-element.42.own, ...), custom_call_target="tpu_custom_call" | custom-call | flops 1024 | bytes 1024 | tf_op jit(solution)/shard_map/pallas_call | solution.py:189
  62.8 1.3 %collective-permute-start.10 = (f16[256,256]{1,0:T(8,128)(2,1)S(1)}, f16[256,256]{1,0:T(8,128)(2,1)S(1)}, u32[]{:S(2)}, u32[]{:S(2)}) collective-permute-start(f16[256,256]{1,0:T(8,128)(2,1)S(1)} %convert_element_type.56), channel_id=1, source_target_pairs={{4,12},{5,14},{6,13},{7,15},{10,3},{11,1},{8,2},{9,0},{20,28},{21,... | collective-permute-start | bytes 393224 | tf_op jit(solution)/shard_map/ppermute | solution.py:218
  64.1 1.3 %collective-permute-start.11 = (f16[256,256]{1,0:T(8,128)(2,1)S(1)}, f16[256,256]{1,0:T(8,128)(2,1)S(1)}, u32[]{:S(2)}, u32[]{:S(2)}) collective-permute-start(f16[256,256]{1,0:T(8,128)(2,1)S(1)} %convert_element_type.58), channel_id=1, source_target_pairs={{4,13},{5,15},{6,12},{7,14},{10,2},{11,0},{8,3},{9,1},{20,29},{21,... | collective-permute-start | bytes 393224 | tf_op jit(solution)/shard_map/ppermute | solution.py:218
  65.5 1.9 %collective-permute-start.12 = (f16[256,256]{1,0:T(8,128)(2,1)S(1)}, f16[256,256]{1,0:T(8,128)(2,1)S(1)}, u32[]{:S(2)}, u32[]{:S(2)}) collective-permute-start(f16[256,256]{1,0:T(8,128)(2,1)S(1)} %convert_element_type.60), channel_id=1, source_target_pairs={{4,3},{5,11},{6,7},{7,9},{10,12},{11,4},{8,8},{9,6},{20,19},{21,27... | collective-permute-start | bytes 393224 | tf_op jit(solution)/shard_map/ppermute | solution.py:218
  67.4 8.3 %collective-permute-start.13 = (f16[256,256]{1,0:T(8,128)(2,1)S(1)}, f16[256,256]{1,0:T(8,128)(2,1)S(1)}, u32[]{:S(2)}, u32[]{:S(2)}) collective-permute-start(f16[256,256]{1,0:T(8,128)(2,1)S(1)} %convert_element_type.62), channel_id=1, source_target_pairs={{4,7},{5,9},{6,3},{7,11},{10,8},{11,6},{8,12},{9,4},{20,23},{21,25... | collective-permute-start | bytes 393224 | tf_op jit(solution)/shard_map/ppermute | solution.py:218
  76.5 1.7 %collective-permute-done.13 = f16[256,256]{1,0:T(8,128)(2,1)S(1)} collective-permute-done((f16[256,256]{1,0:T(8,128)(2,1)S(1)}, f16[256,256]{1,0:T(8,128)(2,1)S(1)}, u32[]{:S(2)}, u32[]{:S(2)}) %collective-permute-start.13) | collective-permute-done | bytes 131104 | tf_op jit(solution)/shard_map/ppermute | solution.py:218
  (32 shorter events, 3.3 us)
Async XLA Ops:
  0.1 1.6 %copy-start = (bf16[256,4096]{1,0:T(8,128)(2,1)S(1)}, bf16[256,4096]{1,0:T(8,128)(2,1)}, u32[]{:S(2)}) copy-start(bf16[256,4096]{1,0:T(8,128)(2,1)} %values.1) | copy-start | bytes 6291460
  2.6 31.5 %collective-permute-start.1 = (bf16[256,2048]{1,0:T(8,128)(2,1)S(1)}, bf16[256,2048]{1,0:T(8,128)(2,1)S(1)}, u32[]{:S(2)}, u32[]{:S(2)}) collective-permute-start(bf16[256,2048]{1,0:T(8,128)(2,1)S(1)} %get-tuple-element.28), channel_id=1, source_target_pairs={{4,8},{8,4},{5,9},{9,5},{6,10},{10,6},{7,11},{11,7},{20,24},{24,20... | collective-permute-start | bytes 3145736 | tf_op jit(solution)/shard_map/ppermute | solution.py:233
  6.1 28.5 %collective-permute-start.2 = (bf16[256,2048]{1,0:T(8,128)(2,1)S(1)}, bf16[256,2048]{1,0:T(8,128)(2,1)S(1)}, u32[]{:S(2)}, u32[]{:S(2)}) collective-permute-start(bf16[256,2048]{1,0:T(8,128)(2,1)S(1)} %get-tuple-element.29.near), channel_id=1, source_target_pairs={{0,4},{12,8},{1,5},{13,9},{2,6},{14,10},{3,7},{15,11},{16,20},{28,... | collective-permute-start | bytes 3145736 | tf_op jit(solution)/shard_map/ppermute | solution.py:235
  7.4 26.7 %collective-permute-start.3 = (f32[1,2048]{1,0:T(1,128)S(1)}, f32[1,2048]{1,0:T(1,128)S(1)}, u32[]{:S(2)}, u32[]{:S(2)}) collective-permute-start(f32[1,2048]{1,0:T(1,128)S(1)} %get-tuple-element.30), channel_id=1, source_target_pairs={{0,8},{12,4},{1,9},{13,5},{2,10},{14,6},{3,11},{15,7},{16,24},{28,... | collective-permute-start | bytes 24584 | tf_op jit(solution)/shard_map/ppermute | solution.py:234
  8.7 46.6 %collective-permute-start = (bf16[256,2048]{1,0:T(8,128)(2,1)S(1)}, bf16[256,2048]{1,0:T(8,128)(2,1)S(1)}, u32[]{:S(2)}, u32[]{:S(2)}) collective-permute-start(bf16[256,2048]{1,0:T(8,128)(2,1)S(1)} %get-tuple-element.28), channel_id=1, source_target_pairs={{0,8},{12,4},{1,9},{13,5},{2,10},{14,6},{3,11},{15,7},{16,24},{28,... | collective-permute-start | bytes 3145736 | tf_op jit(solution)/shard_map/ppermute | solution.py:236
  34.6 11.1 %copy-start.1 = (s32[5,2,2]{2,1,0:T(2,128)S(1)}, s32[5,2,2]{2,1,0:T(2,128)}, u32[]{:S(2)}) copy-start(s32[5,2,2]{2,1,0:T(2,128)} %constant.22.clone.places) | copy-start | bytes 244
  37.9 6.3 %collective-permute-start.4 = (f32[1,256,256]{2,1,0:T(8,128)S(1)}, f32[1,256,256]{2,1,0:T(8,128)S(1)}, u32[]{:S(2)}, u32[]{:S(2)}) collective-permute-start(f32[1,256,256]{2,1,0:T(8,128)S(1)} %get-tuple-element.34), channel_id=1, source_target_pairs={{4,5},{5,4},{8,9},{9,8},{6,7},{7,6},{10,11},{11,10},{20,21},{21,20... | collective-permute-start | bytes 786440 | tf_op jit(solution)/shard_map/ppermute | solution.py:215
  39.8 4.4 %collective-permute-start.5 = (f32[1,256,256]{2,1,0:T(8,128)S(1)}, f32[1,256,256]{2,1,0:T(8,128)S(1)}, u32[]{:S(2)}, u32[]{:S(2)}) collective-permute-start(f32[1,256,256]{2,1,0:T(8,128)S(1)} %get-tuple-element.35), channel_id=1, source_target_pairs={{4,5},{5,4},{8,9},{9,8},{6,7},{7,6},{10,11},{11,10},{20,21},{21,20... | collective-permute-start | bytes 786440 | tf_op jit(solution)/shard_map/ppermute | solution.py:215
  42.2 3.4 %collective-permute-start.6 = (f32[1,256,256]{2,1,0:T(8,128)S(1)}, f32[1,256,256]{2,1,0:T(8,128)S(1)}, u32[]{:S(2)}, u32[]{:S(2)}) collective-permute-start(f32[1,256,256]{2,1,0:T(8,128)S(1)} %get-tuple-element.36), channel_id=1, source_target_pairs={{4,5},{5,4},{8,9},{9,8},{6,7},{7,6},{10,11},{11,10},{20,21},{21,20... | collective-permute-start | bytes 786440 | tf_op jit(solution)/shard_map/ppermute | solution.py:215
  46.6 4.0 %collective-permute-start.7 = (f16[256,256]{1,0:T(8,128)(2,1)S(1)}, f16[256,256]{1,0:T(8,128)(2,1)S(1)}, u32[]{:S(2)}, u32[]{:S(2)}) collective-permute-start(f16[256,256]{1,0:T(8,128)(2,1)S(1)} %convert_element_type.52), channel_id=1, source_target_pairs={{4,4},{5,2},{6,5},{7,6},{10,11},{11,13},{8,10},{9,9},{20,20},{21,1... | collective-permute-start | bytes 393224 | tf_op jit(solution)/shard_map/ppermute | solution.py:218
  47.3 14.5 %copy-start.2 = (s32[4,2,2]{2,1,0:T(2,128)S(1)}, s32[4,2,2]{2,1,0:T(2,128)}, u32[]{:S(2)}) copy-start(s32[4,2,2]{2,1,0:T(2,128)} %constant.23.clone.places) | copy-start | bytes 196
  47.4 7.9 %collective-permute-start.8 = (f16[256,256]{1,0:T(8,128)(2,1)S(1)}, f16[256,256]{1,0:T(8,128)(2,1)S(1)}, u32[]{:S(2)}, u32[]{:S(2)}) collective-permute-start(f16[256,256]{1,0:T(8,128)(2,1)S(1)} %convert_element_type.54), channel_id=1, source_target_pairs={{4,5},{5,6},{6,4},{7,2},{10,10},{11,9},{8,11},{9,13},{20,21},{21,2... | collective-permute-start | bytes 393224 | tf_op jit(solution)/shard_map/ppermute | solution.py:218
  57.3 4.6 %collective-permute-start.9 = (f32[2,256,256]{2,1,0:T(8,128)S(1)}, f32[2,256,256]{2,1,0:T(8,128)S(1)}, u32[]{:S(2)}, u32[]{:S(2)}) collective-permute-start(f32[2,256,256]{2,1,0:T(8,128)S(1)} %get-tuple-element.43), channel_id=1, source_target_pairs={{4,5},{5,4},{8,9},{9,8},{6,7},{7,6},{10,11},{11,10},{20,21},{21,20... | collective-permute-start | bytes 1572872 | tf_op jit(solution)/shard_map/ppermute | solution.py:215
  59.2 8.2 %collective-permute-start.14 = (f16[256,256]{1,0:T(8,128)(2,1)S(1)}, f16[256,256]{1,0:T(8,128)(2,1)S(1)}, u32[]{:S(2)}, u32[]{:S(2)}) collective-permute-start(f16[256,256]{1,0:T(8,128)(2,1)S(1)} %convert_element_type.64), channel_id=1, source_target_pairs={{4,1},{5,8},{6,0},{7,10},{10,14},{11,7},{8,15},{9,5},{20,17},{21,2... | collective-permute-start | bytes 393224 | tf_op jit(solution)/shard_map/ppermute | solution.py:218
  60.5 15.8 %collective-permute-start.15 = (f16[256,256]{1,0:T(8,128)(2,1)S(1)}, f16[256,256]{1,0:T(8,128)(2,1)S(1)}, u32[]{:S(2)}, u32[]{:S(2)}) collective-permute-start(f16[256,256]{1,0:T(8,128)(2,1)S(1)} %convert_element_type.66), channel_id=1, source_target_pairs={{4,0},{5,10},{6,1},{7,8},{10,15},{11,5},{8,14},{9,7},{20,16},{21,2... | collective-permute-start | bytes 393224 | tf_op jit(solution)/shard_map/ppermute | solution.py:218
  62.8 13.6 %collective-permute-start.10 = (f16[256,256]{1,0:T(8,128)(2,1)S(1)}, f16[256,256]{1,0:T(8,128)(2,1)S(1)}, u32[]{:S(2)}, u32[]{:S(2)}) collective-permute-start(f16[256,256]{1,0:T(8,128)(2,1)S(1)} %convert_element_type.56), channel_id=1, source_target_pairs={{4,12},{5,14},{6,13},{7,15},{10,3},{11,1},{8,2},{9,0},{20,28},{21,... | collective-permute-start | bytes 393224 | tf_op jit(solution)/shard_map/ppermute | solution.py:218
  64.1 12.3 %collective-permute-start.11 = (f16[256,256]{1,0:T(8,128)(2,1)S(1)}, f16[256,256]{1,0:T(8,128)(2,1)S(1)}, u32[]{:S(2)}, u32[]{:S(2)}) collective-permute-start(f16[256,256]{1,0:T(8,128)(2,1)S(1)} %convert_element_type.58), channel_id=1, source_target_pairs={{4,13},{5,15},{6,12},{7,14},{10,2},{11,0},{8,3},{9,1},{20,29},{21,... | collective-permute-start | bytes 393224 | tf_op jit(solution)/shard_map/ppermute | solution.py:218
  65.5 11.1 %collective-permute-start.12 = (f16[256,256]{1,0:T(8,128)(2,1)S(1)}, f16[256,256]{1,0:T(8,128)(2,1)S(1)}, u32[]{:S(2)}, u32[]{:S(2)}) collective-permute-start(f16[256,256]{1,0:T(8,128)(2,1)S(1)} %convert_element_type.60), channel_id=1, source_target_pairs={{4,3},{5,11},{6,7},{7,9},{10,12},{11,4},{8,8},{9,6},{20,19},{21,27... | collective-permute-start | bytes 393224 | tf_op jit(solution)/shard_map/ppermute | solution.py:218
  67.4 10.8 %collective-permute-start.13 = (f16[256,256]{1,0:T(8,128)(2,1)S(1)}, f16[256,256]{1,0:T(8,128)(2,1)S(1)}, u32[]{:S(2)}, u32[]{:S(2)}) collective-permute-start(f16[256,256]{1,0:T(8,128)(2,1)S(1)} %convert_element_type.62), channel_id=1, source_target_pairs={{4,7},{5,9},{6,3},{7,11},{10,8},{11,6},{8,12},{9,4},{20,23},{21,25... | collective-permute-start | bytes 393224 | tf_op jit(solution)/shard_map/ppermute | solution.py:218

commit v16 on v15

--- a/solution.py
+++ b/solution.py
@@ -42,10 +42,10 @@
     (((0, 1), (0, 0)), ((2, 0), (2, 2))),
 )
 LATE_ROUNDS = (
+    (((3, 0), (3, 1)), ((3, 2), (3, 3))),
+    (((3, 1), (3, 0)), ((3, 3), (3, 2))),
+    (((0, 3), (1, 3)), ((2, 3), (2, 1))),
     (((1, 3), (0, 3)), ((2, 1), (2, 3))),
-    (((0, 3), (1, 3)), ((2, 3), (2, 1))),
-    (((3, 1), (3, 0)), ((3, 3), (3, 2))),
-    (((3, 0), (3, 1)), ((3, 2), (3, 3))),
 )
 EARLY_SUMS = (((0, 0), (0, 1), (1, 1)), ((2, 2), (2, 0), (2, 1)))
 EARLY_HELD = (
@@ -125,8 +125,7 @@
         partial[:, columns] = far_sum[:, columns] + jnp.sum(rows, axis=0, keepdims=True)
 
 
-def early_kernel(bits, other, edge, near, partial, centred, mean, own, *rest):
-    sends, both = rest[:-1], rest[-1]
+def early_kernel(bits, other, edge, near, partial, centred, mean, own, send, both):
     rows, part = near.shape
     step = 512
 
@@ -142,15 +141,15 @@
 
     for core in (0, 1):
         for place, (i, j) in enumerate(EARLY_SUMS[core]):
-            both[core, place] = block_product(centred[i], centred[j])
+            both[core, place] = block_product(centred[i], centred[j]) * (1.0 / (4 * rows))
     own[...] = both[bits[1]]
-    for place, send in enumerate(sends):
-        send[...] = both[1 - bits[1], pl.ds(place, 1), :, :]
+    send[...] = both[1 - bits[1]]
 
 
 def late_products(core, last, centred, out):
     for place, (_, j) in enumerate(LATE_SUMS[core]):
-        out[place] = block_product(last[...], last[...] if j == 3 else centred[j])
+        product = block_product(last[...], last[...] if j == 3 else centred[j])
+        out[place] = product * (1.0 / (4 * last.shape[0]))
 
 
 def late_kernel(bits, far_edge, mean, centred, *rest):
@@ -165,13 +164,13 @@
             late_products(1 - core, last, centred, send)
 
 
-def combine_kernel(flips, scale, pieces, spares, bits, places, own, *rest):
+def combine_kernel(flips, pieces, spares, bits, places, own, *rest):
     others, spare = rest[:pieces], rest[pieces : pieces + spares]
     outs, held = rest[pieces + spares : -1], rest[-1]
     count = own.shape[0]
     for i in range(count):
         other = others[0][i] if pieces == 1 else others[i][0]
-        held[i] = (own[i] + other) * scale
+        held[i] = own[i] + other
     for n, i in enumerate(flips):
         held[count + n] = held[i].T
     for i in range(spares):
@@ -184,10 +183,10 @@
     return jax.ShapeDtypeStruct(shape, dtype)
 
 
-def combine(bits, own, others, flips, spares, held, places, samples):
+def combine(bits, own, others, flips, spares, held, places):
     rows = own.shape[1]
     return pl.pallas_call(
-        functools.partial(combine_kernel, flips, 1.0 / samples, len(others), len(spares)),
+        functools.partial(combine_kernel, flips, len(others), len(spares)),
         out_shape=[shape_of((rows, rows), jnp.float32)] * len(places),
         in_specs=[SMEM, SMEM] + [VMEM] * (1 + len(others) + len(spares)),
         out_specs=[VMEM] * len(places),
@@ -199,7 +198,6 @@
 
 def two_centres(log_derivs, shift):
     local_rows, local_params = log_derivs.shape
-    samples = local_rows * 4
     part = local_params // 2
     everyone = ("row", "col", "half")
     row, col, half = (lax.axis_index(name) for name in everyone)
@@ -212,7 +210,8 @@
     centres = [(r * 2 + h, r * 2 + 1 - h) for r in (1, 2) for h in (0, 1)]
 
     def swap(value):
-        return lax.ppermute(value, ("row", "half"), centres)
+        narrow = lax.ppermute(value.astype(jnp.float16), ("row", "half"), centres)
+        return narrow.astype(jnp.float32)
 
     def send(value, blocks):
         return lax.ppermute(value.astype(jnp.float16), everyone, round_pairs(blocks))
@@ -244,23 +243,23 @@
         cost_estimate=LONG,
     )(from_centre, near, from_sum)
     early_blocks = (3, local_rows, local_rows)
-    centred, mean, own, *others = pl.pallas_call(
+    centred, mean, own, other = pl.pallas_call(
         early_kernel,
         out_shape=[
             shape_of((3, local_rows, part), jnp.bfloat16),
             shape_of((1, part), jnp.float32),
             shape_of(early_blocks, jnp.float32),
-        ]
-        + [shape_of((1, local_rows, local_rows), jnp.float32)] * 3,
+            shape_of(early_blocks, jnp.float32),
+        ],
         in_specs=[SMEM] + [VMEM] * 4,
-        out_specs=[VMEM] * 6,
+        out_specs=[VMEM] * 4,
         scratch_shapes=[pltpu.VMEM((2,) + early_blocks, jnp.float32)],
         compiler_params=LIMIT,
         cost_estimate=BRIEF,
     )(bits, from_centre, from_edge, near, partial)
-    others = [swap(other) for other in others]
+    others = [swap(other)]
     places = held_place(EARLY_HELD, NEAR_ROUNDS + FAR_ROUNDS) + [[[SPARE] * 2] * 2]
-    *early, spare = combine(bits, own, others, (1, 2), (), EARLY_HELD, places, samples)
+    *early, spare = combine(bits, own, others, (1, 2), (), EARLY_HELD, places)
     near_blocks, far_blocks = early[: len(NEAR_ROUNDS)], early[len(NEAR_ROUNDS) :]
     arrived = [send(value, blocks) for value, blocks in zip(near_blocks, NEAR_ROUNDS)]
     summed = sum(block.astype(jnp.float32) for block in arrived)
@@ -281,7 +280,7 @@
     other = swap(other)
     arrived = [send(value, blocks) for value, blocks in zip(far_blocks, FAR_ROUNDS)]
     places = held_place(LATE_HELD, LATE_ROUNDS)
-    late = combine(bits, own, [other], (0, 1), (spare,), LATE_HELD, places, samples)
+    late = combine(bits, own, [other], (0, 1), (spare,), LATE_HELD, places)
     arrived += [send(value, blocks) for value, blocks in zip(late, LATE_ROUNDS)]
     summed = summed + sum(block.astype(jnp.float32) for block in reversed(arrived))
     return add_shift(summed, 1, shift, local_rows)

time: 80.5 us -> 79.8 us (level); the launches traced: 79 us -> 79.4 us
  waiting for transfers between devices: 32 us -> 38.8 us
  starting transfers between devices: 34.9 us -> 28.2 us
    ppermute x4 -> x2, starting transfers between devices: 8.17 us -> 3.84 us  [swap(): narrow = lax.ppermute(value.astype(jnp.float16), ('row', 'half'), centres)]
    ppermute x1, waiting for transfers between devices: 0.01 us -> 3.89 us  [two_centres(): from_far_edge = lax.ppermute(far, 'row', to_far)]
    ppermute x8, waiting for transfers between devices: 6.35 us -> 9.11 us  [send(): lax.ppermute(value.astype(jnp.float16), everyone, round_pairs(blocks))]
    ppermute x8, starting transfers between devices: 19.4 us -> 17 us  [send(): lax.ppermute(value.astype(jnp.float16), everyone, round_pairs(blocks))]
    ppermute x4 -> x2, waiting for transfers between devices: 1.49 us -> 1.69 us  [swap(): narrow = lax.ppermute(value.astype(jnp.float16), ('row', 'half'), centres)]
  transfers between devices with their start and end apart: 16 -> 14, of which waited for: 5 -> 6; matrix products, arithmetic and copies ran while one was open for 0% -> 0% of each run, Pallas kernels for 7% -> 7%
where the time goes in v16:
time: 79.8 us; the launch traced here: 79.4 us
  waiting for transfers between devices  38.8 us (49%)
  starting transfers between devices  28.2 us (35%)
  Pallas kernels  8.47 us (11%)
  local copies, waits for them, and re-layouts  1.6 us (2%)
  other arithmetic  1.29 us (2%)
  between operations  1 us (1%)
    ppermute x1, waiting for transfers between devices, two_centres(): from_sum = lax.ppermute(far_sum, 'row', to_far)  24.1 us
    ppermute x8, starting transfers between devices, send(): lax.ppermute(value.astype(jnp.float16), everyone, round_pairs(blocks))  17 us
    ppermute x8, waiting for transfers between devices, send(): lax.ppermute(value.astype(jnp.float16), everyone, round_pairs(blocks))  9.11 us
    ppermute x1, waiting for transfers between devices, two_centres(): from_far_edge = lax.ppermute(far, 'row', to_far)  3.89 us
    ppermute x2, starting transfers between devices, swap(): narrow = lax.ppermute(value.astype(jnp.float16), ('row', 'half'), centres)  3.84 us
    ppermute x1, starting transfers between devices, two_centres(): from_centre = lax.ppermute(far, 'row', to_centre)  3.48 us
    pallas_call x1, Pallas kernels, two_centres(): pl.pallas_call(early_kernel, out_shape=[shape_of((3, local_rows, part), j...  3.31 us
    pallas_call x1, Pallas kernels, two_centres(): pl.pallas_call(late_kernel, out_shape=[late_blocks, late_blocks] + [shape...  2 us
  transfers between devices with their start and end apart: 14, of which 6 were waited for; matrix products, arithmetic and copies ran while one was open for 0% of the time, Pallas kernels for 7%

profile of v16, /device:TPU:8, one launch (start us, length us, event | category | flops | bytes accessed | tf_op | source)
XLA Modules:
  0.0 79.4 jit_solution(94871730464858568)
XLA Ops:
  0.1 1.6 %copy-done = bf16[256,4096]{1,0:T(8,128)(2,1)S(1)} copy-done((bf16[256,4096]{1,0:T(8,128)(2,1)S(1)}, bf16[256,4096]{1,0:T(8,128)(2,1)}, u32[]{:S(2)}) %copy-start) | copy-done | bytes 2097176
  2.6 3.5 %collective-permute-start.1 = (bf16[256,2048]{1,0:T(8,128)(2,1)S(1)}, bf16[256,2048]{1,0:T(8,128)(2,1)S(1)}, u32[]{:S(2)}, u32[]{:S(2)}) collective-permute-start(bf16[256,2048]{1,0:T(8,128)(2,1)S(1)} %get-tuple-element.26), channel_id=1, source_target_pairs={{4,8},{8,4},{5,9},{9,5},{6,10},{10,6},{7,11},{11,7},{20,24},{24,20... | collective-permute-start | bytes 3145736 | tf_op jit(solution)/shard_map/ppermute | solution.py:232
  6.1 1.3 %collective-permute-start.2 = (bf16[256,2048]{1,0:T(8,128)(2,1)S(1)}, bf16[256,2048]{1,0:T(8,128)(2,1)S(1)}, u32[]{:S(2)}, u32[]{:S(2)}) collective-permute-start(bf16[256,2048]{1,0:T(8,128)(2,1)S(1)} %get-tuple-element.27.near), channel_id=1, source_target_pairs={{0,4},{12,8},{1,5},{13,9},{2,6},{14,10},{3,7},{15,11},{16,20},{28,... | collective-permute-start | bytes 3145736 | tf_op jit(solution)/shard_map/ppermute | solution.py:234
  7.4 1.3 %collective-permute-start.3 = (f32[1,2048]{1,0:T(1,128)S(1)}, f32[1,2048]{1,0:T(1,128)S(1)}, u32[]{:S(2)}, u32[]{:S(2)}) collective-permute-start(f32[1,2048]{1,0:T(1,128)S(1)} %get-tuple-element.28), channel_id=1, source_target_pairs={{0,8},{12,4},{1,9},{13,5},{2,10},{14,6},{3,11},{15,7},{16,24},{28,... | collective-permute-start | bytes 24584 | tf_op jit(solution)/shard_map/ppermute | solution.py:233
  8.7 1.3 %collective-permute-start = (bf16[256,2048]{1,0:T(8,128)(2,1)S(1)}, bf16[256,2048]{1,0:T(8,128)(2,1)S(1)}, u32[]{:S(2)}, u32[]{:S(2)}) collective-permute-start(bf16[256,2048]{1,0:T(8,128)(2,1)S(1)} %get-tuple-element.26), channel_id=1, source_target_pairs={{0,8},{12,4},{1,9},{13,5},{2,10},{14,6},{3,11},{15,7},{16,24},{28,... | collective-permute-start | bytes 3145736 | tf_op jit(solution)/shard_map/ppermute | solution.py:235
  10.0 24.1 %collective-permute-done.3.far_sum = f32[1,2048]{1,0:T(1,128)S(1)} collective-permute-done((f32[1,2048]{1,0:T(1,128)S(1)}, f32[1,2048]{1,0:T(1,128)S(1)}, u32[]{:S(2)}, u32[]{:S(2)}) %collective-permute-start.3) | collective-permute-done | bytes 8224 | tf_op jit(solution)/shard_map/ppermute | solution.py:233
  34.6 3.3 %shard_map.48 = (bf16[3,256,2048]{2,1,0:T(8,128)(2,1)S(1)}, f32[1,2048]{1,0:T(1,128)S(1)}, f32[3,256,256]{2,1,0:T(8,128)S(1)}, f32[3,256,256]{2,1,0:T(8,128)S(1)}) custom-call(s32[3]{0:T(128)S(1)} %pad_add_fusion.bits, bf16[256,2048]{1,0:T(8,128)(2,1)S(1)} %collective-permute-done.1.other, bf16[256,2048]{1,0:T(8,128)(2,1)S(1)} %collective-permute-done.2.edge, ...), custom_call_target="tpu_custom_call" | custom-call | flops 1024 | bytes 1024 | tf_op jit(solution)/shard_map/pallas_call | solution.py:246
  38.0 1.9 %collective-permute-start.4 = (f16[3,256,256]{2,1,0:T(8,128)(2,1)S(1)}, f16[3,256,256]{2,1,0:T(8,128)(2,1)S(1)}, u32[]{:S(2)}, u32[]{:S(2)}) collective-permute-start(f16[3,256,256]{2,1,0:T(8,128)(2,1)S(1)} %convert_element_type.64), channel_id=1, source_target_pairs={{4,5},{5,4},{8,9},{9,8},{6,7},{7,6},{10,11},{11,10},{20,21},{21,20... | collective-permute-start | bytes 1179656 | tf_op jit(solution)/shard_map/ppermute | solution.py:213
  39.9 1.7 %collective-permute-done.4 = f16[3,256,256]{2,1,0:T(8,128)(2,1)S(1)} collective-permute-done((f16[3,256,256]{2,1,0:T(8,128)(2,1)S(1)}, f16[3,256,256]{2,1,0:T(8,128)(2,1)S(1)}, u32[]{:S(2)}, u32[]{:S(2)}) %collective-permute-start.4) | collective-permute-done | bytes 393248 | tf_op jit(solution)/shard_map/ppermute | solution.py:213
  41.7 0.9 %shard_map.49 = (f32[256,256]{1,0:T(8,128)S(1)}, f32[256,256]{1,0:T(8,128)S(1)}, f32[256,256]{1,0:T(8,128)S(1)}, f32[256,256]{1,0:T(8,128)S(1)}, f32[256,256]{1,0:T(8,128)S(1)}) custom-call(s32[3]{0:T(128)S(1)} %pad_add_fusion.bits, s32[5,2,2]{2,1,0:T(2,128)S(1)} %copy-done.1, f32[3,256,256]{2,1,0:T(8,128)S(1)} %get-tuple-element.31.own, ...), custom_call_target="tpu_custom_call" | custom-call | flops 1024 | bytes 1024 | tf_op jit(solution)/shard_map/pallas_call | solution.py:188
  43.3 3.3 %collective-permute-start.6 = (f16[256,256]{1,0:T(8,128)(2,1)S(1)}, f16[256,256]{1,0:T(8,128)(2,1)S(1)}, u32[]{:S(2)}, u32[]{:S(2)}) collective-permute-start(f16[256,256]{1,0:T(8,128)(2,1)S(1)} %convert_element_type.68), channel_id=1, source_target_pairs={{4,5},{5,6},{6,4},{7,2},{10,10},{11,9},{8,11},{9,13},{20,21},{21,2... | collective-permute-start | bytes 393224 | tf_op jit(solution)/shard_map/ppermute | solution.py:217
  46.6 4.5 %collective-permute-done.6 = f16[256,256]{1,0:T(8,128)(2,1)S(1)} collective-permute-done((f16[256,256]{1,0:T(8,128)(2,1)S(1)}, f16[256,256]{1,0:T(8,128)(2,1)S(1)}, u32[]{:S(2)}, u32[]{:S(2)}) %collective-permute-start.6) | collective-permute-done | bytes 131104 | tf_op jit(solution)/shard_map/ppermute | solution.py:217
  51.2 3.9 %collective-permute-done.far_edge = bf16[256,2048]{1,0:T(8,128)(2,1)S(1)} collective-permute-done((bf16[256,2048]{1,0:T(8,128)(2,1)S(1)}, bf16[256,2048]{1,0:T(8,128)(2,1)S(1)}, u32[]{:S(2)}, u32[]{:S(2)}) %collective-permute-start) | collective-permute-done | bytes 1048608 | tf_op jit(solution)/shard_map/ppermute | solution.py:235
  55.1 2.0 %shard_map.50 = (f32[2,256,256]{2,1,0:T(8,128)S(1)}, f32[2,256,256]{2,1,0:T(8,128)S(1)}, f32[256,256]{1,0:T(8,128)S(1)}, f32[256,256]{1,0:T(8,128)S(1)}, f32[256,256]{1,0:T(8,128)S(1)}) custom-call(s32[3]{0:T(128)S(1)} %pad_add_fusion.bits, ...), custom_call_target="tpu_custom_call", output_to_operand_aliasing={{2}: (4, {}), {3}: (5, {}), {4}: (6, {})} | custom-call | flops 1024 | bytes 1024 | tf_op jit(solution)/shard_map/pallas_call | solution.py:269
  57.2 1.9 %collective-permute-start.7 = (f16[2,256,256]{2,1,0:T(8,128)(2,1)S(1)}, f16[2,256,256]{2,1,0:T(8,128)(2,1)S(1)}, u32[]{:S(2)}, u32[]{:S(2)}) collective-permute-start(f16[2,256,256]{2,1,0:T(8,128)(2,1)S(1)} %convert_element_type.70), channel_id=1, source_target_pairs={{4,5},{5,4},{8,9},{9,8},{6,7},{7,6},{10,11},{11,10},{20,21},{21,20... | collective-permute-start | bytes 786440 | tf_op jit(solution)/shard_map/ppermute | solution.py:213
  59.1 1.3 %collective-permute-start.12 = (f16[256,256]{1,0:T(8,128)(2,1)S(1)}, f16[256,256]{1,0:T(8,128)(2,1)S(1)}, u32[]{:S(2)}, u32[]{:S(2)}) collective-permute-start(f16[256,256]{1,0:T(8,128)(2,1)S(1)} %convert_element_type.80), channel_id=1, source_target_pairs={{4,1},{5,8},{6,0},{7,10},{10,14},{11,7},{8,15},{9,5},{20,17},{21,2... | collective-permute-start | bytes 393224 | tf_op jit(solution)/shard_map/ppermute | solution.py:217
  60.5 1.3 %collective-permute-start.13 = (f16[256,256]{1,0:T(8,128)(2,1)S(1)}, f16[256,256]{1,0:T(8,128)(2,1)S(1)}, u32[]{:S(2)}, u32[]{:S(2)}) collective-permute-start(f16[256,256]{1,0:T(8,128)(2,1)S(1)} %convert_element_type.82), channel_id=1, source_target_pairs={{4,0},{5,10},{6,1},{7,8},{10,15},{11,5},{8,14},{9,7},{20,16},{21,2... | collective-permute-start | bytes 393224 | tf_op jit(solution)/shard_map/ppermute | solution.py:217
  61.8 0.9 %shard_map.51 = (f32[256,256]{1,0:T(8,128)S(1)}, f32[256,256]{1,0:T(8,128)S(1)}, f32[256,256]{1,0:T(8,128)S(1)}, f32[256,256]{1,0:T(8,128)S(1)}) custom-call(s32[3]{0:T(128)S(1)} %pad_add_fusion.bits, s32[4,2,2]{2,1,0:T(2,128)S(1)} %copy-done.2, f32[2,256,256]{2,1,0:T(8,128)S(1)} %get-tuple-element.38.own, f32[2,256,256]{2,1,0:T(8,128)S(1)} %convert_element_type.71.rest_0_, ...), custom_call_target="tpu_custom_call" | custom-call | flops 1024 | bytes 1024 | tf_op jit(solution)/shard_map/pallas_call | solution.py:188
  62.8 1.3 %collective-permute-start.10 = (f16[256,256]{1,0:T(8,128)(2,1)S(1)}, f16[256,256]{1,0:T(8,128)(2,1)S(1)}, u32[]{:S(2)}, u32[]{:S(2)}) collective-permute-start(f16[256,256]{1,0:T(8,128)(2,1)S(1)} %convert_element_type.76), channel_id=1, source_target_pairs={{4,13},{5,15},{6,12},{7,14},{10,2},{11,0},{8,3},{9,1},{20,29},{21,... | collective-permute-start | bytes 393224 | tf_op jit(solution)/shard_map/ppermute | solution.py:217
  64.1 1.3 %collective-permute-start.11 = (f16[256,256]{1,0:T(8,128)(2,1)S(1)}, f16[256,256]{1,0:T(8,128)(2,1)S(1)}, u32[]{:S(2)}, u32[]{:S(2)}) collective-permute-start(f16[256,256]{1,0:T(8,128)(2,1)S(1)} %convert_element_type.78), channel_id=1, source_target_pairs={{4,12},{5,14},{6,13},{7,15},{10,3},{11,1},{8,2},{9,0},{20,28},{21,... | collective-permute-start | bytes 393224 | tf_op jit(solution)/shard_map/ppermute | solution.py:217
  65.4 5.9 %collective-permute-start.8 = (f16[256,256]{1,0:T(8,128)(2,1)S(1)}, f16[256,256]{1,0:T(8,128)(2,1)S(1)}, u32[]{:S(2)}, u32[]{:S(2)}) collective-permute-start(f16[256,256]{1,0:T(8,128)(2,1)S(1)} %convert_element_type.72), channel_id=1, source_target_pairs={{4,7},{5,9},{6,3},{7,11},{10,8},{11,6},{8,12},{9,4},{20,23},{21,25... | collective-permute-start | bytes 393224 | tf_op jit(solution)/shard_map/ppermute | solution.py:217
  71.4 1.9 %collective-permute-start.9 = (f16[256,256]{1,0:T(8,128)(2,1)S(1)}, f16[256,256]{1,0:T(8,128)(2,1)S(1)}, u32[]{:S(2)}, u32[]{:S(2)}) collective-permute-start(f16[256,256]{1,0:T(8,128)(2,1)S(1)} %convert_element_type.74), channel_id=1, source_target_pairs={{4,3},{5,11},{6,7},{7,9},{10,12},{11,4},{8,8},{9,6},{20,19},{21,27... | collective-permute-start | bytes 393224 | tf_op jit(solution)/shard_map/ppermute | solution.py:217
  74.0 2.6 %collective-permute-done.8 = f16[256,256]{1,0:T(8,128)(2,1)S(1)} collective-permute-done((f16[256,256]{1,0:T(8,128)(2,1)S(1)}, f16[256,256]{1,0:T(8,128)(2,1)S(1)}, u32[]{:S(2)}, u32[]{:S(2)}) %collective-permute-start.8) | collective-permute-done | bytes 131104 | tf_op jit(solution)/shard_map/ppermute | solution.py:217
  76.6 2.0 %collective-permute-done.9 = f16[256,256]{1,0:T(8,128)(2,1)S(1)} collective-permute-done((f16[256,256]{1,0:T(8,128)(2,1)S(1)}, f16[256,256]{1,0:T(8,128)(2,1)S(1)}, u32[]{:S(2)}, u32[]{:S(2)}) %collective-permute-start.9) | collective-permute-done | bytes 131104 | tf_op jit(solution)/shard_map/ppermute | solution.py:217
  (32 shorter events, 3.3 us)
Async XLA Ops:
  0.1 1.6 %copy-start = (bf16[256,4096]{1,0:T(8,128)(2,1)S(1)}, bf16[256,4096]{1,0:T(8,128)(2,1)}, u32[]{:S(2)}) copy-start(bf16[256,4096]{1,0:T(8,128)(2,1)} %values.1) | copy-start | bytes 6291460
  2.6 31.5 %collective-permute-start.1 = (bf16[256,2048]{1,0:T(8,128)(2,1)S(1)}, bf16[256,2048]{1,0:T(8,128)(2,1)S(1)}, u32[]{:S(2)}, u32[]{:S(2)}) collective-permute-start(bf16[256,2048]{1,0:T(8,128)(2,1)S(1)} %get-tuple-element.26), channel_id=1, source_target_pairs={{4,8},{8,4},{5,9},{9,5},{6,10},{10,6},{7,11},{11,7},{20,24},{24,20... | collective-permute-start | bytes 3145736 | tf_op jit(solution)/shard_map/ppermute | solution.py:232
  6.1 28.5 %collective-permute-start.2 = (bf16[256,2048]{1,0:T(8,128)(2,1)S(1)}, bf16[256,2048]{1,0:T(8,128)(2,1)S(1)}, u32[]{:S(2)}, u32[]{:S(2)}) collective-permute-start(bf16[256,2048]{1,0:T(8,128)(2,1)S(1)} %get-tuple-element.27.near), channel_id=1, source_target_pairs={{0,4},{12,8},{1,5},{13,9},{2,6},{14,10},{3,7},{15,11},{16,20},{28,... | collective-permute-start | bytes 3145736 | tf_op jit(solution)/shard_map/ppermute | solution.py:234
  7.4 26.7 %collective-permute-start.3 = (f32[1,2048]{1,0:T(1,128)S(1)}, f32[1,2048]{1,0:T(1,128)S(1)}, u32[]{:S(2)}, u32[]{:S(2)}) collective-permute-start(f32[1,2048]{1,0:T(1,128)S(1)} %get-tuple-element.28), channel_id=1, source_target_pairs={{0,8},{12,4},{1,9},{13,5},{2,10},{14,6},{3,11},{15,7},{16,24},{28,... | collective-permute-start | bytes 24584 | tf_op jit(solution)/shard_map/ppermute | solution.py:233
  8.7 46.4 %collective-permute-start = (bf16[256,2048]{1,0:T(8,128)(2,1)S(1)}, bf16[256,2048]{1,0:T(8,128)(2,1)S(1)}, u32[]{:S(2)}, u32[]{:S(2)}) collective-permute-start(bf16[256,2048]{1,0:T(8,128)(2,1)S(1)} %get-tuple-element.26), channel_id=1, source_target_pairs={{0,8},{12,4},{1,9},{13,5},{2,10},{14,6},{3,11},{15,7},{16,24},{28,... | collective-permute-start | bytes 3145736 | tf_op jit(solution)/shard_map/ppermute | solution.py:235
  34.6 7.1 %copy-start.1 = (s32[5,2,2]{2,1,0:T(2,128)S(1)}, s32[5,2,2]{2,1,0:T(2,128)}, u32[]{:S(2)}) copy-start(s32[5,2,2]{2,1,0:T(2,128)} %constant.22.clone.places) | copy-start | bytes 244
  38.0 3.6 %collective-permute-start.4 = (f16[3,256,256]{2,1,0:T(8,128)(2,1)S(1)}, f16[3,256,256]{2,1,0:T(8,128)(2,1)S(1)}, u32[]{:S(2)}, u32[]{:S(2)}) collective-permute-start(f16[3,256,256]{2,1,0:T(8,128)(2,1)S(1)} %convert_element_type.64), channel_id=1, source_target_pairs={{4,5},{5,4},{8,9},{9,8},{6,7},{7,6},{10,11},{11,10},{20,21},{21,20... | collective-permute-start | bytes 1179656 | tf_op jit(solution)/shard_map/ppermute | solution.py:213
  42.6 4.0 %collective-permute-start.5 = (f16[256,256]{1,0:T(8,128)(2,1)S(1)}, f16[256,256]{1,0:T(8,128)(2,1)S(1)}, u32[]{:S(2)}, u32[]{:S(2)}) collective-permute-start(f16[256,256]{1,0:T(8,128)(2,1)S(1)} %convert_element_type.66), channel_id=1, source_target_pairs={{4,4},{5,2},{6,5},{7,6},{10,11},{11,13},{8,10},{9,9},{20,20},{21,1... | collective-permute-start | bytes 393224 | tf_op jit(solution)/shard_map/ppermute | solution.py:217
  43.3 7.9 %collective-permute-start.6 = (f16[256,256]{1,0:T(8,128)(2,1)S(1)}, f16[256,256]{1,0:T(8,128)(2,1)S(1)}, u32[]{:S(2)}, u32[]{:S(2)}) collective-permute-start(f16[256,256]{1,0:T(8,128)(2,1)S(1)} %convert_element_type.68), channel_id=1, source_target_pairs={{4,5},{5,6},{6,4},{7,2},{10,10},{11,9},{8,11},{9,13},{20,21},{21,2... | collective-permute-start | bytes 393224 | tf_op jit(solution)/shard_map/ppermute | solution.py:217
  55.1 6.7 %copy-start.2 = (s32[4,2,2]{2,1,0:T(2,128)S(1)}, s32[4,2,2]{2,1,0:T(2,128)}, u32[]{:S(2)}) copy-start(s32[4,2,2]{2,1,0:T(2,128)} %constant.23.clone.places) | copy-start | bytes 196
  57.2 4.6 %collective-permute-start.7 = (f16[2,256,256]{2,1,0:T(8,128)(2,1)S(1)}, f16[2,256,256]{2,1,0:T(8,128)(2,1)S(1)}, u32[]{:S(2)}, u32[]{:S(2)}) collective-permute-start(f16[2,256,256]{2,1,0:T(8,128)(2,1)S(1)} %convert_element_type.70), channel_id=1, source_target_pairs={{4,5},{5,4},{8,9},{9,8},{6,7},{7,6},{10,11},{11,10},{20,21},{21,20... | collective-permute-start | bytes 786440 | tf_op jit(solution)/shard_map/ppermute | solution.py:213
  59.1 12.3 %collective-permute-start.12 = (f16[256,256]{1,0:T(8,128)(2,1)S(1)}, f16[256,256]{1,0:T(8,128)(2,1)S(1)}, u32[]{:S(2)}, u32[]{:S(2)}) collective-permute-start(f16[256,256]{1,0:T(8,128)(2,1)S(1)} %convert_element_type.80), channel_id=1, source_target_pairs={{4,1},{5,8},{6,0},{7,10},{10,14},{11,7},{8,15},{9,5},{20,17},{21,2... | collective-permute-start | bytes 393224 | tf_op jit(solution)/shard_map/ppermute | solution.py:217
  60.5 13.5 %collective-permute-start.13 = (f16[256,256]{1,0:T(8,128)(2,1)S(1)}, f16[256,256]{1,0:T(8,128)(2,1)S(1)}, u32[]{:S(2)}, u32[]{:S(2)}) collective-permute-start(f16[256,256]{1,0:T(8,128)(2,1)S(1)} %convert_element_type.82), channel_id=1, source_target_pairs={{4,0},{5,10},{6,1},{7,8},{10,15},{11,5},{8,14},{9,7},{20,16},{21,2... | collective-permute-start | bytes 393224 | tf_op jit(solution)/shard_map/ppermute | solution.py:217
  62.8 11.2 %collective-permute-start.10 = (f16[256,256]{1,0:T(8,128)(2,1)S(1)}, f16[256,256]{1,0:T(8,128)(2,1)S(1)}, u32[]{:S(2)}, u32[]{:S(2)}) collective-permute-start(f16[256,256]{1,0:T(8,128)(2,1)S(1)} %convert_element_type.76), channel_id=1, source_target_pairs={{4,13},{5,15},{6,12},{7,14},{10,2},{11,0},{8,3},{9,1},{20,29},{21,... | collective-permute-start | bytes 393224 | tf_op jit(solution)/shard_map/ppermute | solution.py:217
  64.1 9.9 %collective-permute-start.11 = (f16[256,256]{1,0:T(8,128)(2,1)S(1)}, f16[256,256]{1,0:T(8,128)(2,1)S(1)}, u32[]{:S(2)}, u32[]{:S(2)}) collective-permute-start(f16[256,256]{1,0:T(8,128)(2,1)S(1)} %convert_element_type.78), channel_id=1, source_target_pairs={{4,12},{5,14},{6,13},{7,15},{10,3},{11,1},{8,2},{9,0},{20,28},{21,... | collective-permute-start | bytes 393224 | tf_op jit(solution)/shard_map/ppermute | solution.py:217
  65.4 11.2 %collective-permute-start.8 = (f16[256,256]{1,0:T(8,128)(2,1)S(1)}, f16[256,256]{1,0:T(8,128)(2,1)S(1)}, u32[]{:S(2)}, u32[]{:S(2)}) collective-permute-start(f16[256,256]{1,0:T(8,128)(2,1)S(1)} %convert_element_type.72), channel_id=1, source_target_pairs={{4,7},{5,9},{6,3},{7,11},{10,8},{11,6},{8,12},{9,4},{20,23},{21,25... | collective-permute-start | bytes 393224 | tf_op jit(solution)/shard_map/ppermute | solution.py:217
  71.4 7.2 %collective-permute-start.9 = (f16[256,256]{1,0:T(8,128)(2,1)S(1)}, f16[256,256]{1,0:T(8,128)(2,1)S(1)}, u32[]{:S(2)}, u32[]{:S(2)}) collective-permute-start(f16[256,256]{1,0:T(8,128)(2,1)S(1)} %convert_element_type.74), channel_id=1, source_target_pairs={{4,3},{5,11},{6,7},{7,9},{10,12},{11,4},{8,8},{9,6},{20,19},{21,27... | collective-permute-start | bytes 393224 | tf_op jit(solution)/shard_map/ppermute | solution.py:217

commit v17 on v16

--- a/solution.py
+++ b/solution.py
@@ -36,9 +36,10 @@
 NEAR_ROUNDS = (
     (((1, 0), (1, 1)), ((0, 2), (1, 2))),
     (((1, 1), (1, 0)), ((1, 2), (0, 2))),
+    (((0, 0), (0, 1)), (None, None)),
 )
 FAR_ROUNDS = (
-    (((0, 0), (0, 1)), ((2, 2), (2, 0))),
+    ((None, None), ((2, 2), (2, 0))),
     (((0, 1), (0, 0)), ((2, 0), (2, 2))),
 )
 LATE_ROUNDS = (

time: 79.8 us -> 80.6 us (1.010); the launches traced: 79.4 us -> 79 us
  waiting for transfers between devices: 38.8 us -> 34.7 us
  starting transfers between devices: 28.2 us -> 31.8 us
    ppermute x8 -> x9, waiting for transfers between devices: 9.11 us -> 5.01 us  [send(): lax.ppermute(value.astype(jnp.float16), everyone, round_pairs(blocks))]
    ppermute x8 -> x9, starting transfers between devices: 17 us -> 20.6 us  [send(): lax.ppermute(value.astype(jnp.float16), everyone, round_pairs(blocks))]
  transfers between devices with their start and end apart: 14 -> 15, of which waited for: 6 -> 5; matrix products, arithmetic and copies ran while one was open for 0% -> 0% of each run, Pallas kernels for 7% -> 7%
where the time goes in v17:
time: 80.6 us; the launch traced here: 79 us
  waiting for transfers between devices  34.7 us (43%)
  starting transfers between devices  31.8 us (39%)
  Pallas kernels  8.51 us (11%)
  local copies, waits for them, and re-layouts  1.6 us (2%)
  other arithmetic  1.34 us (2%)
  between operations  1.02 us (1%)
    ppermute x1, waiting for transfers between devices, two_centres(): from_sum = lax.ppermute(far_sum, 'row', to_far)  24.1 us
    ppermute x9, starting transfers between devices, send(): lax.ppermute(value.astype(jnp.float16), everyone, round_pairs(blocks))  20.6 us
    ppermute x9, waiting for transfers between devices, send(): lax.ppermute(value.astype(jnp.float16), everyone, round_pairs(blocks))  5.01 us
    ppermute x2, starting transfers between devices, swap(): narrow = lax.ppermute(value.astype(jnp.float16), ('row', 'half'), centres)  3.84 us
    ppermute x1, waiting for transfers between devices, two_centres(): from_far_edge = lax.ppermute(far, 'row', to_far)  3.82 us
    ppermute x1, starting transfers between devices, two_centres(): from_centre = lax.ppermute(far, 'row', to_centre)  3.48 us
    pallas_call x1, Pallas kernels, two_centres(): pl.pallas_call(early_kernel, out_shape=[shape_of((3, local_rows, part), j...  3.31 us
    pallas_call x1, Pallas kernels, two_centres(): pl.pallas_call(late_kernel, out_shape=[late_blocks, late_blocks] + [shape...  2 us
  transfers between devices with their start and end apart: 15, of which 5 were waited for; matrix products, arithmetic and copies ran while one was open for 0% of the time, Pallas kernels for 7%

profile of v17, /device:TPU:8, one launch (start us, length us, event | category | flops | bytes accessed | tf_op | source)
XLA Modules:
  0.0 79.0 jit_solution(5169873972714497031)
XLA Ops:
  0.1 1.6 %copy-done = bf16[256,4096]{1,0:T(8,128)(2,1)S(1)} copy-done((bf16[256,4096]{1,0:T(8,128)(2,1)S(1)}, bf16[256,4096]{1,0:T(8,128)(2,1)}, u32[]{:S(2)}) %copy-start) | copy-done | bytes 2097176
  1.7 0.9 %shard_map.46 = (bf16[256,2048]{1,0:T(8,128)(2,1)S(1)}, bf16[256,2048]{1,0:T(8,128)(2,1)S(1)}, f32[1,2048]{1,0:T(1,128)S(1)}) custom-call(s32[3]{0:T(128)S(1)} %pad_add_fusion.bits, bf16[256,4096]{1,0:T(8,128)(2,1)S(1)} %copy-done), custom_call_target="tpu_custom_call" | custom-call | flops 1024 | bytes 1024 | tf_op jit(solution)/shard_map/pallas_call | solution.py:220
  2.6 3.5 %collective-permute-start.1 = (bf16[256,2048]{1,0:T(8,128)(2,1)S(1)}, bf16[256,2048]{1,0:T(8,128)(2,1)S(1)}, u32[]{:S(2)}, u32[]{:S(2)}) collective-permute-start(bf16[256,2048]{1,0:T(8,128)(2,1)S(1)} %get-tuple-element.27), channel_id=1, source_target_pairs={{4,8},{8,4},{5,9},{9,5},{6,10},{10,6},{7,11},{11,7},{20,24},{24,20... | collective-permute-start | bytes 3145736 | tf_op jit(solution)/shard_map/ppermute | solution.py:233
  6.1 1.3 %collective-permute-start.2 = (bf16[256,2048]{1,0:T(8,128)(2,1)S(1)}, bf16[256,2048]{1,0:T(8,128)(2,1)S(1)}, u32[]{:S(2)}, u32[]{:S(2)}) collective-permute-start(bf16[256,2048]{1,0:T(8,128)(2,1)S(1)} %get-tuple-element.28.near), channel_id=1, source_target_pairs={{0,4},{12,8},{1,5},{13,9},{2,6},{14,10},{3,7},{15,11},{16,20},{28,... | collective-permute-start | bytes 3145736 | tf_op jit(solution)/shard_map/ppermute | solution.py:235
  7.4 1.3 %collective-permute-start.3 = (f32[1,2048]{1,0:T(1,128)S(1)}, f32[1,2048]{1,0:T(1,128)S(1)}, u32[]{:S(2)}, u32[]{:S(2)}) collective-permute-start(f32[1,2048]{1,0:T(1,128)S(1)} %get-tuple-element.29), channel_id=1, source_target_pairs={{0,8},{12,4},{1,9},{13,5},{2,10},{14,6},{3,11},{15,7},{16,24},{28,... | collective-permute-start | bytes 24584 | tf_op jit(solution)/shard_map/ppermute | solution.py:234
  8.7 1.3 %collective-permute-start = (bf16[256,2048]{1,0:T(8,128)(2,1)S(1)}, bf16[256,2048]{1,0:T(8,128)(2,1)S(1)}, u32[]{:S(2)}, u32[]{:S(2)}) collective-permute-start(bf16[256,2048]{1,0:T(8,128)(2,1)S(1)} %get-tuple-element.27), channel_id=1, source_target_pairs={{0,8},{12,4},{1,9},{13,5},{2,10},{14,6},{3,11},{15,7},{16,24},{28,... | collective-permute-start | bytes 3145736 | tf_op jit(solution)/shard_map/ppermute | solution.py:236
  10.0 24.1 %collective-permute-done.3.far_sum = f32[1,2048]{1,0:T(1,128)S(1)} collective-permute-done((f32[1,2048]{1,0:T(1,128)S(1)}, f32[1,2048]{1,0:T(1,128)S(1)}, u32[]{:S(2)}, u32[]{:S(2)}) %collective-permute-start.3) | collective-permute-done | bytes 8224 | tf_op jit(solution)/shard_map/ppermute | solution.py:234
  34.6 3.3 %shard_map.48 = (bf16[3,256,2048]{2,1,0:T(8,128)(2,1)S(1)}, f32[1,2048]{1,0:T(1,128)S(1)}, f32[3,256,256]{2,1,0:T(8,128)S(1)}, f32[3,256,256]{2,1,0:T(8,128)S(1)}) custom-call(s32[3]{0:T(128)S(1)} %pad_add_fusion.bits, bf16[256,2048]{1,0:T(8,128)(2,1)S(1)} %collective-permute-done.1.other, bf16[256,2048]{1,0:T(8,128)(2,1)S(1)} %collective-permute-done.2.edge, ...), custom_call_target="tpu_custom_call" | custom-call | flops 1024 | bytes 1024 | tf_op jit(solution)/shard_map/pallas_call | solution.py:247
  38.0 1.9 %collective-permute-start.4 = (f16[3,256,256]{2,1,0:T(8,128)(2,1)S(1)}, f16[3,256,256]{2,1,0:T(8,128)(2,1)S(1)}, u32[]{:S(2)}, u32[]{:S(2)}) collective-permute-start(f16[3,256,256]{2,1,0:T(8,128)(2,1)S(1)} %convert_element_type.70), channel_id=1, source_target_pairs={{4,5},{5,4},{8,9},{9,8},{6,7},{7,6},{10,11},{11,10},{20,21},{21,20... | collective-permute-start | bytes 1179656 | tf_op jit(solution)/shard_map/ppermute | solution.py:214
  39.9 1.7 %collective-permute-done.4 = f16[3,256,256]{2,1,0:T(8,128)(2,1)S(1)} collective-permute-done((f16[3,256,256]{2,1,0:T(8,128)(2,1)S(1)}, f16[3,256,256]{2,1,0:T(8,128)(2,1)S(1)}, u32[]{:S(2)}, u32[]{:S(2)}) %collective-permute-start.4) | collective-permute-done | bytes 393248 | tf_op jit(solution)/shard_map/ppermute | solution.py:214
  41.7 1.0 %shard_map.49 = (f32[256,256]{1,0:T(8,128)S(1)}, f32[256,256]{1,0:T(8,128)S(1)}, f32[256,256]{1,0:T(8,128)S(1)}, f32[256,256]{1,0:T(8,128)S(1)}, f32[256,256]{1,0:T(8,128)S(1)}, /*index=5*/f32[256,256]{1,0:T(8,128)S(1)}) custom-call(s32[3]{0:T(128)S(1)} %pad_add_fusion.bits, s32[6,2,2]{2,1,0:T(2,128)S(1)} %copy-done.1, ...), custom_call_target="tpu_custom_call" | custom-call | flops 1024 | bytes 1024 | tf_op jit(solution)/shard_map/pallas_call | solution.py:189
  43.4 3.3 %collective-permute-start.6 = (f16[256,256]{1,0:T(8,128)(2,1)S(1)}, f16[256,256]{1,0:T(8,128)(2,1)S(1)}, u32[]{:S(2)}, u32[]{:S(2)}) collective-permute-start(f16[256,256]{1,0:T(8,128)(2,1)S(1)} %convert_element_type.74), channel_id=1, source_target_pairs={{4,5},{5,6},{6,4},{7,2},{10,10},{11,9},{8,11},{9,13},{20,21},{21,2... | collective-permute-start | bytes 393224 | tf_op jit(solution)/shard_map/ppermute | solution.py:218
  46.7 1.3 %collective-permute-start.7 = (f16[256,256]{1,0:T(8,128)(2,1)S(1)}, f16[256,256]{1,0:T(8,128)(2,1)S(1)}, u32[]{:S(2)}, u32[]{:S(2)}) collective-permute-start(f16[256,256]{1,0:T(8,128)(2,1)S(1)} %convert_element_type.76), channel_id=1, source_target_pairs={{4,0},{6,1},{10,15},{8,14},{20,16},{22,17},{26,31},{24,30}} | collective-permute-start | bytes 393224 | tf_op jit(solution)/shard_map/ppermute | solution.py:218
  48.0 3.2 %collective-permute-done.6 = f16[256,256]{1,0:T(8,128)(2,1)S(1)} collective-permute-done((f16[256,256]{1,0:T(8,128)(2,1)S(1)}, f16[256,256]{1,0:T(8,128)(2,1)S(1)}, u32[]{:S(2)}, u32[]{:S(2)}) %collective-permute-start.6) | collective-permute-done | bytes 131104 | tf_op jit(solution)/shard_map/ppermute | solution.py:218
  51.3 3.8 %collective-permute-done.far_edge = bf16[256,2048]{1,0:T(8,128)(2,1)S(1)} collective-permute-done((bf16[256,2048]{1,0:T(8,128)(2,1)S(1)}, bf16[256,2048]{1,0:T(8,128)(2,1)S(1)}, u32[]{:S(2)}, u32[]{:S(2)}) %collective-permute-start) | collective-permute-done | bytes 1048608 | tf_op jit(solution)/shard_map/ppermute | solution.py:236
  55.1 2.0 %shard_map.50 = (f32[2,256,256]{2,1,0:T(8,128)S(1)}, f32[2,256,256]{2,1,0:T(8,128)S(1)}, f32[256,256]{1,0:T(8,128)S(1)}, f32[256,256]{1,0:T(8,128)S(1)}, f32[256,256]{1,0:T(8,128)S(1)}) custom-call(s32[3]{0:T(128)S(1)} %pad_add_fusion.bits, ...), custom_call_target="tpu_custom_call", output_to_operand_aliasing={{2}: (4, {}), {3}: (5, {}), {4}: (6, {})} | custom-call | flops 1024 | bytes 1024 | tf_op jit(solution)/shard_map/pallas_call | solution.py:270
  57.2 1.9 %collective-permute-start.8 = (f16[2,256,256]{2,1,0:T(8,128)(2,1)S(1)}, f16[2,256,256]{2,1,0:T(8,128)(2,1)S(1)}, u32[]{:S(2)}, u32[]{:S(2)}) collective-permute-start(f16[2,256,256]{2,1,0:T(8,128)(2,1)S(1)} %convert_element_type.78), channel_id=1, source_target_pairs={{4,5},{5,4},{8,9},{9,8},{6,7},{7,6},{10,11},{11,10},{20,21},{21,20... | collective-permute-start | bytes 786440 | tf_op jit(solution)/shard_map/ppermute | solution.py:214
  59.1 1.3 %collective-permute-start.13 = (f16[256,256]{1,0:T(8,128)(2,1)S(1)}, f16[256,256]{1,0:T(8,128)(2,1)S(1)}, u32[]{:S(2)}, u32[]{:S(2)}) collective-permute-start(f16[256,256]{1,0:T(8,128)(2,1)S(1)} %convert_element_type.88), channel_id=1, source_target_pairs={{4,1},{5,8},{6,0},{7,10},{10,14},{11,7},{8,15},{9,5},{20,17},{21,2... | collective-permute-start | bytes 393224 | tf_op jit(solution)/shard_map/ppermute | solution.py:218
  61.2 0.9 %shard_map.51 = (f32[256,256]{1,0:T(8,128)S(1)}, f32[256,256]{1,0:T(8,128)S(1)}, f32[256,256]{1,0:T(8,128)S(1)}, f32[256,256]{1,0:T(8,128)S(1)}) custom-call(s32[3]{0:T(128)S(1)} %pad_add_fusion.bits, s32[4,2,2]{2,1,0:T(2,128)S(1)} %copy-done.2, f32[2,256,256]{2,1,0:T(8,128)S(1)} %get-tuple-element.40.own, f32[2,256,256]{2,1,0:T(8,128)S(1)} %convert_element_type.79.rest_0_, ...), custom_call_target="tpu_custom_call" | custom-call | flops 1024 | bytes 1024 | tf_op jit(solution)/shard_map/pallas_call | solution.py:189
  62.1 1.9 %collective-permute-start.10 = (f16[256,256]{1,0:T(8,128)(2,1)S(1)}, f16[256,256]{1,0:T(8,128)(2,1)S(1)}, u32[]{:S(2)}, u32[]{:S(2)}) collective-permute-start(f16[256,256]{1,0:T(8,128)(2,1)S(1)} %convert_element_type.82), channel_id=1, source_target_pairs={{4,3},{5,11},{6,7},{7,9},{10,12},{11,4},{8,8},{9,6},{20,19},{21,27... | collective-permute-start | bytes 393224 | tf_op jit(solution)/shard_map/ppermute | solution.py:218
  64.1 1.3 %collective-permute-start.11 = (f16[256,256]{1,0:T(8,128)(2,1)S(1)}, f16[256,256]{1,0:T(8,128)(2,1)S(1)}, u32[]{:S(2)}, u32[]{:S(2)}) collective-permute-start(f16[256,256]{1,0:T(8,128)(2,1)S(1)} %convert_element_type.84), channel_id=1, source_target_pairs={{4,13},{5,15},{6,12},{7,14},{10,2},{11,0},{8,3},{9,1},{20,29},{21,... | collective-permute-start | bytes 393224 | tf_op jit(solution)/shard_map/ppermute | solution.py:218
  65.4 1.3 %collective-permute-start.12 = (f16[256,256]{1,0:T(8,128)(2,1)S(1)}, f16[256,256]{1,0:T(8,128)(2,1)S(1)}, u32[]{:S(2)}, u32[]{:S(2)}) collective-permute-start(f16[256,256]{1,0:T(8,128)(2,1)S(1)} %convert_element_type.86), channel_id=1, source_target_pairs={{4,12},{5,14},{6,13},{7,15},{10,3},{11,1},{8,2},{9,0},{20,28},{21,... | collective-permute-start | bytes 393224 | tf_op jit(solution)/shard_map/ppermute | solution.py:218
  66.7 8.9 %collective-permute-start.9 = (f16[256,256]{1,0:T(8,128)(2,1)S(1)}, f16[256,256]{1,0:T(8,128)(2,1)S(1)}, u32[]{:S(2)}, u32[]{:S(2)}) collective-permute-start(f16[256,256]{1,0:T(8,128)(2,1)S(1)} %convert_element_type.80), channel_id=1, source_target_pairs={{4,7},{5,9},{6,3},{7,11},{10,8},{11,6},{8,12},{9,4},{20,23},{21,25... | collective-permute-start | bytes 393224 | tf_op jit(solution)/shard_map/ppermute | solution.py:218
  76.4 1.8 %collective-permute-done.9 = f16[256,256]{1,0:T(8,128)(2,1)S(1)} collective-permute-done((f16[256,256]{1,0:T(8,128)(2,1)S(1)}, f16[256,256]{1,0:T(8,128)(2,1)S(1)}, u32[]{:S(2)}, u32[]{:S(2)}) %collective-permute-start.9) | collective-permute-done | bytes 131104 | tf_op jit(solution)/shard_map/ppermute | solution.py:218
  (35 shorter events, 3.2 us)
Async XLA Ops:
  0.1 1.6 %copy-start = (bf16[256,4096]{1,0:T(8,128)(2,1)S(1)}, bf16[256,4096]{1,0:T(8,128)(2,1)}, u32[]{:S(2)}) copy-start(bf16[256,4096]{1,0:T(8,128)(2,1)} %values.1) | copy-start | bytes 6291460
  2.6 31.5 %collective-permute-start.1 = (bf16[256,2048]{1,0:T(8,128)(2,1)S(1)}, bf16[256,2048]{1,0:T(8,128)(2,1)S(1)}, u32[]{:S(2)}, u32[]{:S(2)}) collective-permute-start(bf16[256,2048]{1,0:T(8,128)(2,1)S(1)} %get-tuple-element.27), channel_id=1, source_target_pairs={{4,8},{8,4},{5,9},{9,5},{6,10},{10,6},{7,11},{11,7},{20,24},{24,20... | collective-permute-start | bytes 3145736 | tf_op jit(solution)/shard_map/ppermute | solution.py:233
  6.1 28.5 %collective-permute-start.2 = (bf16[256,2048]{1,0:T(8,128)(2,1)S(1)}, bf16[256,2048]{1,0:T(8,128)(2,1)S(1)}, u32[]{:S(2)}, u32[]{:S(2)}) collective-permute-start(bf16[256,2048]{1,0:T(8,128)(2,1)S(1)} %get-tuple-element.28.near), channel_id=1, source_target_pairs={{0,4},{12,8},{1,5},{13,9},{2,6},{14,10},{3,7},{15,11},{16,20},{28,... | collective-permute-start | bytes 3145736 | tf_op jit(solution)/shard_map/ppermute | solution.py:235
  7.4 26.7 %collective-permute-start.3 = (f32[1,2048]{1,0:T(1,128)S(1)}, f32[1,2048]{1,0:T(1,128)S(1)}, u32[]{:S(2)}, u32[]{:S(2)}) collective-permute-start(f32[1,2048]{1,0:T(1,128)S(1)} %get-tuple-element.29), channel_id=1, source_target_pairs={{0,8},{12,4},{1,9},{13,5},{2,10},{14,6},{3,11},{15,7},{16,24},{28,... | collective-permute-start | bytes 24584 | tf_op jit(solution)/shard_map/ppermute | solution.py:234
  8.7 46.4 %collective-permute-start = (bf16[256,2048]{1,0:T(8,128)(2,1)S(1)}, bf16[256,2048]{1,0:T(8,128)(2,1)S(1)}, u32[]{:S(2)}, u32[]{:S(2)}) collective-permute-start(bf16[256,2048]{1,0:T(8,128)(2,1)S(1)} %get-tuple-element.27), channel_id=1, source_target_pairs={{0,8},{12,4},{1,9},{13,5},{2,10},{14,6},{3,11},{15,7},{16,24},{28,... | collective-permute-start | bytes 3145736 | tf_op jit(solution)/shard_map/ppermute | solution.py:236
  34.6 7.1 %copy-start.1 = (s32[6,2,2]{2,1,0:T(2,128)S(1)}, s32[6,2,2]{2,1,0:T(2,128)}, u32[]{:S(2)}) copy-start(s32[6,2,2]{2,1,0:T(2,128)} %constant.22.clone.places) | copy-start | bytes 292
  38.0 3.6 %collective-permute-start.4 = (f16[3,256,256]{2,1,0:T(8,128)(2,1)S(1)}, f16[3,256,256]{2,1,0:T(8,128)(2,1)S(1)}, u32[]{:S(2)}, u32[]{:S(2)}) collective-permute-start(f16[3,256,256]{2,1,0:T(8,128)(2,1)S(1)} %convert_element_type.70), channel_id=1, source_target_pairs={{4,5},{5,4},{8,9},{9,8},{6,7},{7,6},{10,11},{11,10},{20,21},{21,20... | collective-permute-start | bytes 1179656 | tf_op jit(solution)/shard_map/ppermute | solution.py:214
  42.7 5.3 %collective-permute-start.5 = (f16[256,256]{1,0:T(8,128)(2,1)S(1)}, f16[256,256]{1,0:T(8,128)(2,1)S(1)}, u32[]{:S(2)}, u32[]{:S(2)}) collective-permute-start(f16[256,256]{1,0:T(8,128)(2,1)S(1)} %convert_element_type.72), channel_id=1, source_target_pairs={{4,4},{5,2},{6,5},{7,6},{10,11},{11,13},{8,10},{9,9},{20,20},{21,1... | collective-permute-start | bytes 393224 | tf_op jit(solution)/shard_map/ppermute | solution.py:218
  43.4 7.9 %collective-permute-start.6 = (f16[256,256]{1,0:T(8,128)(2,1)S(1)}, f16[256,256]{1,0:T(8,128)(2,1)S(1)}, u32[]{:S(2)}, u32[]{:S(2)}) collective-permute-start(f16[256,256]{1,0:T(8,128)(2,1)S(1)} %convert_element_type.74), channel_id=1, source_target_pairs={{4,5},{5,6},{6,4},{7,2},{10,10},{11,9},{8,11},{9,13},{20,21},{21,2... | collective-permute-start | bytes 393224 | tf_op jit(solution)/shard_map/ppermute | solution.py:218
  46.7 4.5 %collective-permute-start.7 = (f16[256,256]{1,0:T(8,128)(2,1)S(1)}, f16[256,256]{1,0:T(8,128)(2,1)S(1)}, u32[]{:S(2)}, u32[]{:S(2)}) collective-permute-start(f16[256,256]{1,0:T(8,128)(2,1)S(1)} %convert_element_type.76), channel_id=1, source_target_pairs={{4,0},{6,1},{10,15},{8,14},{20,16},{22,17},{26,31},{24,30}} | collective-permute-start | bytes 393224 | tf_op jit(solution)/shard_map/ppermute | solution.py:218
  55.1 6.1 %copy-start.2 = (s32[4,2,2]{2,1,0:T(2,128)S(1)}, s32[4,2,2]{2,1,0:T(2,128)}, u32[]{:S(2)}) copy-start(s32[4,2,2]{2,1,0:T(2,128)} %constant.23.clone.places) | copy-start | bytes 196
  57.2 4.0 %collective-permute-start.8 = (f16[2,256,256]{2,1,0:T(8,128)(2,1)S(1)}, f16[2,256,256]{2,1,0:T(8,128)(2,1)S(1)}, u32[]{:S(2)}, u32[]{:S(2)}) collective-permute-start(f16[2,256,256]{2,1,0:T(8,128)(2,1)S(1)} %convert_element_type.78), channel_id=1, source_target_pairs={{4,5},{5,4},{8,9},{9,8},{6,7},{7,6},{10,11},{11,10},{20,21},{21,20... | collective-permute-start | bytes 786440 | tf_op jit(solution)/shard_map/ppermute | solution.py:214
  59.1 7.6 %collective-permute-start.13 = (f16[256,256]{1,0:T(8,128)(2,1)S(1)}, f16[256,256]{1,0:T(8,128)(2,1)S(1)}, u32[]{:S(2)}, u32[]{:S(2)}) collective-permute-start(f16[256,256]{1,0:T(8,128)(2,1)S(1)} %convert_element_type.88), channel_id=1, source_target_pairs={{4,1},{5,8},{6,0},{7,10},{10,14},{11,7},{8,15},{9,5},{20,17},{21,2... | collective-permute-start | bytes 393224 | tf_op jit(solution)/shard_map/ppermute | solution.py:218
  60.5 15.9 %collective-permute-start.14 = (f16[256,256]{1,0:T(8,128)(2,1)S(1)}, f16[256,256]{1,0:T(8,128)(2,1)S(1)}, u32[]{:S(2)}, u32[]{:S(2)}) collective-permute-start(f16[256,256]{1,0:T(8,128)(2,1)S(1)} %convert_element_type.90), channel_id=1, source_target_pairs={{5,10},{7,8},{11,5},{9,7},{21,26},{23,24},{27,21},{25,23}} | collective-permute-start | bytes 393224 | tf_op jit(solution)/shard_map/ppermute | solution.py:218
  62.1 14.2 %collective-permute-start.10 = (f16[256,256]{1,0:T(8,128)(2,1)S(1)}, f16[256,256]{1,0:T(8,128)(2,1)S(1)}, u32[]{:S(2)}, u32[]{:S(2)}) collective-permute-start(f16[256,256]{1,0:T(8,128)(2,1)S(1)} %convert_element_type.82), channel_id=1, source_target_pairs={{4,3},{5,11},{6,7},{7,9},{10,12},{11,4},{8,8},{9,6},{20,19},{21,27... | collective-permute-start | bytes 393224 | tf_op jit(solution)/shard_map/ppermute | solution.py:218
  64.1 12.3 %collective-permute-start.11 = (f16[256,256]{1,0:T(8,128)(2,1)S(1)}, f16[256,256]{1,0:T(8,128)(2,1)S(1)}, u32[]{:S(2)}, u32[]{:S(2)}) collective-permute-start(f16[256,256]{1,0:T(8,128)(2,1)S(1)} %convert_element_type.84), channel_id=1, source_target_pairs={{4,13},{5,15},{6,12},{7,14},{10,2},{11,0},{8,3},{9,1},{20,29},{21,... | collective-permute-start | bytes 393224 | tf_op jit(solution)/shard_map/ppermute | solution.py:218
  65.4 11.0 %collective-permute-start.12 = (f16[256,256]{1,0:T(8,128)(2,1)S(1)}, f16[256,256]{1,0:T(8,128)(2,1)S(1)}, u32[]{:S(2)}, u32[]{:S(2)}) collective-permute-start(f16[256,256]{1,0:T(8,128)(2,1)S(1)} %convert_element_type.86), channel_id=1, source_target_pairs={{4,12},{5,14},{6,13},{7,15},{10,3},{11,1},{8,2},{9,0},{20,28},{21,... | collective-permute-start | bytes 393224 | tf_op jit(solution)/shard_map/ppermute | solution.py:218
  66.7 11.4 %collective-permute-start.9 = (f16[256,256]{1,0:T(8,128)(2,1)S(1)}, f16[256,256]{1,0:T(8,128)(2,1)S(1)}, u32[]{:S(2)}, u32[]{:S(2)}) collective-permute-start(f16[256,256]{1,0:T(8,128)(2,1)S(1)} %convert_element_type.80), channel_id=1, source_target_pairs={{4,7},{5,9},{6,3},{7,11},{10,8},{11,6},{8,12},{9,4},{20,23},{21,25... | collective-permute-start | bytes 393224 | tf_op jit(solution)/shard_map/ppermute | solution.py:218

commit v18 on v17

--- a/solution.py
+++ b/solution.py
@@ -43,10 +43,10 @@
     (((0, 1), (0, 0)), ((2, 0), (2, 2))),
 )
 LATE_ROUNDS = (
+    (((1, 3), (0, 3)), ((2, 1), (2, 3))),
     (((3, 0), (3, 1)), ((3, 2), (3, 3))),
     (((3, 1), (3, 0)), ((3, 3), (3, 2))),
     (((0, 3), (1, 3)), ((2, 3), (2, 1))),
-    (((1, 3), (0, 3)), ((2, 1), (2, 3))),
 )
 EARLY_SUMS = (((0, 0), (0, 1), (1, 1)), ((2, 2), (2, 0), (2, 1)))
 EARLY_HELD = (

time: 80.6 us -> 79.8 us (0.990); the launches traced: 79 us -> 79.4 us
  waiting for transfers between devices: 34.7 us -> 37.4 us
  starting transfers between devices: 31.8 us -> 29.5 us
    ppermute x9, waiting for transfers between devices: 5.01 us -> 7.78 us  [send(): lax.ppermute(value.astype(jnp.float16), everyone, round_pairs(blocks))]
    ppermute x9, starting transfers between devices: 20.6 us -> 18.3 us  [send(): lax.ppermute(value.astype(jnp.float16), everyone, round_pairs(blocks))]
  transfers between devices with their start and end apart: 15 -> 15, of which waited for: 5 -> 6; matrix products, arithmetic and copies ran while one was open for 0% -> 0% of each run, Pallas kernels for 7% -> 7%
where the time goes in v18:
time: 79.8 us; the launch traced here: 79.4 us
  waiting for transfers between devices  37.4 us (47%)
  starting transfers between devices  29.5 us (37%)
  Pallas kernels  8.51 us (11%)
  local copies, waits for them, and re-layouts  1.6 us (2%)
  other arithmetic  1.34 us (2%)
  between operations  1.02 us (1%)
    ppermute x1, waiting for transfers between devices, two_centres(): from_sum = lax.ppermute(far_sum, 'row', to_far)  24.1 us
    ppermute x9, starting transfers between devices, send(): lax.ppermute(value.astype(jnp.float16), everyone, round_pairs(blocks))  18.3 us
    ppermute x9, waiting for transfers between devices, send(): lax.ppermute(value.astype(jnp.float16), everyone, round_pairs(blocks))  7.78 us
    ppermute x2, starting transfers between devices, swap(): narrow = lax.ppermute(value.astype(jnp.float16), ('row', 'half'), centres)  3.84 us
    ppermute x1, waiting for transfers between devices, two_centres(): from_far_edge = lax.ppermute(far, 'row', to_far)  3.82 us
    ppermute x1, starting transfers between devices, two_centres(): from_centre = lax.ppermute(far, 'row', to_centre)  3.48 us
    pallas_call x1, Pallas kernels, two_centres(): pl.pallas_call(early_kernel, out_shape=[shape_of((3, local_rows, part), j...  3.31 us
    pallas_call x1, Pallas kernels, two_centres(): pl.pallas_call(late_kernel, out_shape=[late_blocks, late_blocks] + [shape...  2 us
  transfers between devices with their start and end apart: 15, of which 6 were waited for; matrix products, arithmetic and copies ran while one was open for 0% of the time, Pallas kernels for 7%

profile of v18, /device:TPU:8, one launch (start us, length us, event | category | flops | bytes accessed | tf_op | source)
XLA Modules:
  0.0 79.4 jit_solution(1260884020259962433)
XLA Ops:
  0.1 1.6 %copy-done = bf16[256,4096]{1,0:T(8,128)(2,1)S(1)} copy-done((bf16[256,4096]{1,0:T(8,128)(2,1)S(1)}, bf16[256,4096]{1,0:T(8,128)(2,1)}, u32[]{:S(2)}) %copy-start) | copy-done | bytes 2097176
  2.6 3.5 %collective-permute-start.1 = (bf16[256,2048]{1,0:T(8,128)(2,1)S(1)}, bf16[256,2048]{1,0:T(8,128)(2,1)S(1)}, u32[]{:S(2)}, u32[]{:S(2)}) collective-permute-start(bf16[256,2048]{1,0:T(8,128)(2,1)S(1)} %get-tuple-element.27), channel_id=1, source_target_pairs={{4,8},{8,4},{5,9},{9,5},{6,10},{10,6},{7,11},{11,7},{20,24},{24,20... | collective-permute-start | bytes 3145736 | tf_op jit(solution)/shard_map/ppermute | solution.py:233
  6.1 1.3 %collective-permute-start.2 = (bf16[256,2048]{1,0:T(8,128)(2,1)S(1)}, bf16[256,2048]{1,0:T(8,128)(2,1)S(1)}, u32[]{:S(2)}, u32[]{:S(2)}) collective-permute-start(bf16[256,2048]{1,0:T(8,128)(2,1)S(1)} %get-tuple-element.28.near), channel_id=1, source_target_pairs={{0,4},{12,8},{1,5},{13,9},{2,6},{14,10},{3,7},{15,11},{16,20},{28,... | collective-permute-start | bytes 3145736 | tf_op jit(solution)/shard_map/ppermute | solution.py:235
  7.4 1.3 %collective-permute-start.3 = (f32[1,2048]{1,0:T(1,128)S(1)}, f32[1,2048]{1,0:T(1,128)S(1)}, u32[]{:S(2)}, u32[]{:S(2)}) collective-permute-start(f32[1,2048]{1,0:T(1,128)S(1)} %get-tuple-element.29), channel_id=1, source_target_pairs={{0,8},{12,4},{1,9},{13,5},{2,10},{14,6},{3,11},{15,7},{16,24},{28,... | collective-permute-start | bytes 24584 | tf_op jit(solution)/shard_map/ppermute | solution.py:234
  8.7 1.3 %collective-permute-start = (bf16[256,2048]{1,0:T(8,128)(2,1)S(1)}, bf16[256,2048]{1,0:T(8,128)(2,1)S(1)}, u32[]{:S(2)}, u32[]{:S(2)}) collective-permute-start(bf16[256,2048]{1,0:T(8,128)(2,1)S(1)} %get-tuple-element.27), channel_id=1, source_target_pairs={{0,8},{12,4},{1,9},{13,5},{2,10},{14,6},{3,11},{15,7},{16,24},{28,... | collective-permute-start | bytes 3145736 | tf_op jit(solution)/shard_map/ppermute | solution.py:236
  10.0 24.1 %collective-permute-done.3.far_sum = f32[1,2048]{1,0:T(1,128)S(1)} collective-permute-done((f32[1,2048]{1,0:T(1,128)S(1)}, f32[1,2048]{1,0:T(1,128)S(1)}, u32[]{:S(2)}, u32[]{:S(2)}) %collective-permute-start.3) | collective-permute-done | bytes 8224 | tf_op jit(solution)/shard_map/ppermute | solution.py:234
  34.6 3.3 %shard_map.48 = (bf16[3,256,2048]{2,1,0:T(8,128)(2,1)S(1)}, f32[1,2048]{1,0:T(1,128)S(1)}, f32[3,256,256]{2,1,0:T(8,128)S(1)}, f32[3,256,256]{2,1,0:T(8,128)S(1)}) custom-call(s32[3]{0:T(128)S(1)} %pad_add_fusion.bits, bf16[256,2048]{1,0:T(8,128)(2,1)S(1)} %collective-permute-done.1.other, bf16[256,2048]{1,0:T(8,128)(2,1)S(1)} %collective-permute-done.2.edge, ...), custom_call_target="tpu_custom_call" | custom-call | flops 1024 | bytes 1024 | tf_op jit(solution)/shard_map/pallas_call | solution.py:247
  38.0 1.9 %collective-permute-start.4 = (f16[3,256,256]{2,1,0:T(8,128)(2,1)S(1)}, f16[3,256,256]{2,1,0:T(8,128)(2,1)S(1)}, u32[]{:S(2)}, u32[]{:S(2)}) collective-permute-start(f16[3,256,256]{2,1,0:T(8,128)(2,1)S(1)} %convert_element_type.70), channel_id=1, source_target_pairs={{4,5},{5,4},{8,9},{9,8},{6,7},{7,6},{10,11},{11,10},{20,21},{21,20... | collective-permute-start | bytes 1179656 | tf_op jit(solution)/shard_map/ppermute | solution.py:214
  39.9 1.7 %collective-permute-done.4 = f16[3,256,256]{2,1,0:T(8,128)(2,1)S(1)} collective-permute-done((f16[3,256,256]{2,1,0:T(8,128)(2,1)S(1)}, f16[3,256,256]{2,1,0:T(8,128)(2,1)S(1)}, u32[]{:S(2)}, u32[]{:S(2)}) %collective-permute-start.4) | collective-permute-done | bytes 393248 | tf_op jit(solution)/shard_map/ppermute | solution.py:214
  41.7 1.0 %shard_map.49 = (f32[256,256]{1,0:T(8,128)S(1)}, f32[256,256]{1,0:T(8,128)S(1)}, f32[256,256]{1,0:T(8,128)S(1)}, f32[256,256]{1,0:T(8,128)S(1)}, f32[256,256]{1,0:T(8,128)S(1)}, /*index=5*/f32[256,256]{1,0:T(8,128)S(1)}) custom-call(s32[3]{0:T(128)S(1)} %pad_add_fusion.bits, s32[6,2,2]{2,1,0:T(2,128)S(1)} %copy-done.1, ...), custom_call_target="tpu_custom_call" | custom-call | flops 1024 | bytes 1024 | tf_op jit(solution)/shard_map/pallas_call | solution.py:189
  43.4 3.3 %collective-permute-start.6 = (f16[256,256]{1,0:T(8,128)(2,1)S(1)}, f16[256,256]{1,0:T(8,128)(2,1)S(1)}, u32[]{:S(2)}, u32[]{:S(2)}) collective-permute-start(f16[256,256]{1,0:T(8,128)(2,1)S(1)} %convert_element_type.74), channel_id=1, source_target_pairs={{4,5},{5,6},{6,4},{7,2},{10,10},{11,9},{8,11},{9,13},{20,21},{21,2... | collective-permute-start | bytes 393224 | tf_op jit(solution)/shard_map/ppermute | solution.py:218
  46.7 1.3 %collective-permute-start.7 = (f16[256,256]{1,0:T(8,128)(2,1)S(1)}, f16[256,256]{1,0:T(8,128)(2,1)S(1)}, u32[]{:S(2)}, u32[]{:S(2)}) collective-permute-start(f16[256,256]{1,0:T(8,128)(2,1)S(1)} %convert_element_type.76), channel_id=1, source_target_pairs={{4,0},{6,1},{10,15},{8,14},{20,16},{22,17},{26,31},{24,30}} | collective-permute-start | bytes 393224 | tf_op jit(solution)/shard_map/ppermute | solution.py:218
  48.0 3.2 %collective-permute-done.6 = f16[256,256]{1,0:T(8,128)(2,1)S(1)} collective-permute-done((f16[256,256]{1,0:T(8,128)(2,1)S(1)}, f16[256,256]{1,0:T(8,128)(2,1)S(1)}, u32[]{:S(2)}, u32[]{:S(2)}) %collective-permute-start.6) | collective-permute-done | bytes 131104 | tf_op jit(solution)/shard_map/ppermute | solution.py:218
  51.3 3.8 %collective-permute-done.far_edge = bf16[256,2048]{1,0:T(8,128)(2,1)S(1)} collective-permute-done((bf16[256,2048]{1,0:T(8,128)(2,1)S(1)}, bf16[256,2048]{1,0:T(8,128)(2,1)S(1)}, u32[]{:S(2)}, u32[]{:S(2)}) %collective-permute-start) | collective-permute-done | bytes 1048608 | tf_op jit(solution)/shard_map/ppermute | solution.py:236
  55.1 2.0 %shard_map.50 = (f32[2,256,256]{2,1,0:T(8,128)S(1)}, f32[2,256,256]{2,1,0:T(8,128)S(1)}, f32[256,256]{1,0:T(8,128)S(1)}, f32[256,256]{1,0:T(8,128)S(1)}, f32[256,256]{1,0:T(8,128)S(1)}) custom-call(s32[3]{0:T(128)S(1)} %pad_add_fusion.bits, ...), custom_call_target="tpu_custom_call", output_to_operand_aliasing={{2}: (4, {}), {3}: (5, {}), {4}: (6, {})} | custom-call | flops 1024 | bytes 1024 | tf_op jit(solution)/shard_map/pallas_call | solution.py:270
  57.2 1.9 %collective-permute-start.8 = (f16[2,256,256]{2,1,0:T(8,128)(2,1)S(1)}, f16[2,256,256]{2,1,0:T(8,128)(2,1)S(1)}, u32[]{:S(2)}, u32[]{:S(2)}) collective-permute-start(f16[2,256,256]{2,1,0:T(8,128)(2,1)S(1)} %convert_element_type.78), channel_id=1, source_target_pairs={{4,5},{5,4},{8,9},{9,8},{6,7},{7,6},{10,11},{11,10},{20,21},{21,20... | collective-permute-start | bytes 786440 | tf_op jit(solution)/shard_map/ppermute | solution.py:214
  59.1 1.3 %collective-permute-start.13 = (f16[256,256]{1,0:T(8,128)(2,1)S(1)}, f16[256,256]{1,0:T(8,128)(2,1)S(1)}, u32[]{:S(2)}, u32[]{:S(2)}) collective-permute-start(f16[256,256]{1,0:T(8,128)(2,1)S(1)} %convert_element_type.88), channel_id=1, source_target_pairs={{4,1},{5,8},{6,0},{7,10},{10,14},{11,7},{8,15},{9,5},{20,17},{21,2... | collective-permute-start | bytes 393224 | tf_op jit(solution)/shard_map/ppermute | solution.py:218
  61.2 0.9 %shard_map.51 = (f32[256,256]{1,0:T(8,128)S(1)}, f32[256,256]{1,0:T(8,128)S(1)}, f32[256,256]{1,0:T(8,128)S(1)}, f32[256,256]{1,0:T(8,128)S(1)}) custom-call(s32[3]{0:T(128)S(1)} %pad_add_fusion.bits, s32[4,2,2]{2,1,0:T(2,128)S(1)} %copy-done.2, f32[2,256,256]{2,1,0:T(8,128)S(1)} %get-tuple-element.40.own, f32[2,256,256]{2,1,0:T(8,128)S(1)} %convert_element_type.79.rest_0_, ...), custom_call_target="tpu_custom_call" | custom-call | flops 1024 | bytes 1024 | tf_op jit(solution)/shard_map/pallas_call | solution.py:189
  62.1 1.3 %collective-permute-start.10 = (f16[256,256]{1,0:T(8,128)(2,1)S(1)}, f16[256,256]{1,0:T(8,128)(2,1)S(1)}, u32[]{:S(2)}, u32[]{:S(2)}) collective-permute-start(f16[256,256]{1,0:T(8,128)(2,1)S(1)} %convert_element_type.82), channel_id=1, source_target_pairs={{4,13},{5,15},{6,12},{7,14},{10,2},{11,0},{8,3},{9,1},{20,29},{21,... | collective-permute-start | bytes 393224 | tf_op jit(solution)/shard_map/ppermute | solution.py:218
  63.5 1.3 %collective-permute-start.11 = (f16[256,256]{1,0:T(8,128)(2,1)S(1)}, f16[256,256]{1,0:T(8,128)(2,1)S(1)}, u32[]{:S(2)}, u32[]{:S(2)}) collective-permute-start(f16[256,256]{1,0:T(8,128)(2,1)S(1)} %convert_element_type.84), channel_id=1, source_target_pairs={{4,12},{5,14},{6,13},{7,15},{10,3},{11,1},{8,2},{9,0},{20,28},{21,... | collective-permute-start | bytes 393224 | tf_op jit(solution)/shard_map/ppermute | solution.py:218
  64.8 6.6 %collective-permute-start.12 = (f16[256,256]{1,0:T(8,128)(2,1)S(1)}, f16[256,256]{1,0:T(8,128)(2,1)S(1)}, u32[]{:S(2)}, u32[]{:S(2)}) collective-permute-start(f16[256,256]{1,0:T(8,128)(2,1)S(1)} %convert_element_type.86), channel_id=1, source_target_pairs={{4,7},{5,9},{6,3},{7,11},{10,8},{11,6},{8,12},{9,4},{20,23},{21,25... | collective-permute-start | bytes 393224 | tf_op jit(solution)/shard_map/ppermute | solution.py:218
  71.4 1.9 %collective-permute-start.9 = (f16[256,256]{1,0:T(8,128)(2,1)S(1)}, f16[256,256]{1,0:T(8,128)(2,1)S(1)}, u32[]{:S(2)}, u32[]{:S(2)}) collective-permute-start(f16[256,256]{1,0:T(8,128)(2,1)S(1)} %convert_element_type.80), channel_id=1, source_target_pairs={{4,3},{5,11},{6,7},{7,9},{10,12},{11,4},{8,8},{9,6},{20,19},{21,27... | collective-permute-start | bytes 393224 | tf_op jit(solution)/shard_map/ppermute | solution.py:218
  74.0 2.2 %collective-permute-done.12 = f16[256,256]{1,0:T(8,128)(2,1)S(1)} collective-permute-done((f16[256,256]{1,0:T(8,128)(2,1)S(1)}, f16[256,256]{1,0:T(8,128)(2,1)S(1)}, u32[]{:S(2)}, u32[]{:S(2)}) %collective-permute-start.12) | collective-permute-done | bytes 131104 | tf_op jit(solution)/shard_map/ppermute | solution.py:218
  76.2 2.4 %collective-permute-done.9 = f16[256,256]{1,0:T(8,128)(2,1)S(1)} collective-permute-done((f16[256,256]{1,0:T(8,128)(2,1)S(1)}, f16[256,256]{1,0:T(8,128)(2,1)S(1)}, u32[]{:S(2)}, u32[]{:S(2)}) %collective-permute-start.9) | collective-permute-done | bytes 131104 | tf_op jit(solution)/shard_map/ppermute | solution.py:218
  (35 shorter events, 4.1 us)
Async XLA Ops:
  0.1 1.6 %copy-start = (bf16[256,4096]{1,0:T(8,128)(2,1)S(1)}, bf16[256,4096]{1,0:T(8,128)(2,1)}, u32[]{:S(2)}) copy-start(bf16[256,4096]{1,0:T(8,128)(2,1)} %values.1) | copy-start | bytes 6291460
  2.6 31.5 %collective-permute-start.1 = (bf16[256,2048]{1,0:T(8,128)(2,1)S(1)}, bf16[256,2048]{1,0:T(8,128)(2,1)S(1)}, u32[]{:S(2)}, u32[]{:S(2)}) collective-permute-start(bf16[256,2048]{1,0:T(8,128)(2,1)S(1)} %get-tuple-element.27), channel_id=1, source_target_pairs={{4,8},{8,4},{5,9},{9,5},{6,10},{10,6},{7,11},{11,7},{20,24},{24,20... | collective-permute-start | bytes 3145736 | tf_op jit(solution)/shard_map/ppermute | solution.py:233
  6.1 28.5 %collective-permute-start.2 = (bf16[256,2048]{1,0:T(8,128)(2,1)S(1)}, bf16[256,2048]{1,0:T(8,128)(2,1)S(1)}, u32[]{:S(2)}, u32[]{:S(2)}) collective-permute-start(bf16[256,2048]{1,0:T(8,128)(2,1)S(1)} %get-tuple-element.28.near), channel_id=1, source_target_pairs={{0,4},{12,8},{1,5},{13,9},{2,6},{14,10},{3,7},{15,11},{16,20},{28,... | collective-permute-start | bytes 3145736 | tf_op jit(solution)/shard_map/ppermute | solution.py:235
  7.4 26.7 %collective-permute-start.3 = (f32[1,2048]{1,0:T(1,128)S(1)}, f32[1,2048]{1,0:T(1,128)S(1)}, u32[]{:S(2)}, u32[]{:S(2)}) collective-permute-start(f32[1,2048]{1,0:T(1,128)S(1)} %get-tuple-element.29), channel_id=1, source_target_pairs={{0,8},{12,4},{1,9},{13,5},{2,10},{14,6},{3,11},{15,7},{16,24},{28,... | collective-permute-start | bytes 24584 | tf_op jit(solution)/shard_map/ppermute | solution.py:234
  8.7 46.4 %collective-permute-start = (bf16[256,2048]{1,0:T(8,128)(2,1)S(1)}, bf16[256,2048]{1,0:T(8,128)(2,1)S(1)}, u32[]{:S(2)}, u32[]{:S(2)}) collective-permute-start(bf16[256,2048]{1,0:T(8,128)(2,1)S(1)} %get-tuple-element.27), channel_id=1, source_target_pairs={{0,8},{12,4},{1,9},{13,5},{2,10},{14,6},{3,11},{15,7},{16,24},{28,... | collective-permute-start | bytes 3145736 | tf_op jit(solution)/shard_map/ppermute | solution.py:236
  34.6 7.1 %copy-start.1 = (s32[6,2,2]{2,1,0:T(2,128)S(1)}, s32[6,2,2]{2,1,0:T(2,128)}, u32[]{:S(2)}) copy-start(s32[6,2,2]{2,1,0:T(2,128)} %constant.22.clone.places) | copy-start | bytes 292
  38.0 3.6 %collective-permute-start.4 = (f16[3,256,256]{2,1,0:T(8,128)(2,1)S(1)}, f16[3,256,256]{2,1,0:T(8,128)(2,1)S(1)}, u32[]{:S(2)}, u32[]{:S(2)}) collective-permute-start(f16[3,256,256]{2,1,0:T(8,128)(2,1)S(1)} %convert_element_type.70), channel_id=1, source_target_pairs={{4,5},{5,4},{8,9},{9,8},{6,7},{7,6},{10,11},{11,10},{20,21},{21,20... | collective-permute-start | bytes 1179656 | tf_op jit(solution)/shard_map/ppermute | solution.py:214
  42.7 5.3 %collective-permute-start.5 = (f16[256,256]{1,0:T(8,128)(2,1)S(1)}, f16[256,256]{1,0:T(8,128)(2,1)S(1)}, u32[]{:S(2)}, u32[]{:S(2)}) collective-permute-start(f16[256,256]{1,0:T(8,128)(2,1)S(1)} %convert_element_type.72), channel_id=1, source_target_pairs={{4,4},{5,2},{6,5},{7,6},{10,11},{11,13},{8,10},{9,9},{20,20},{21,1... | collective-permute-start | bytes 393224 | tf_op jit(solution)/shard_map/ppermute | solution.py:218
  43.4 7.9 %collective-permute-start.6 = (f16[256,256]{1,0:T(8,128)(2,1)S(1)}, f16[256,256]{1,0:T(8,128)(2,1)S(1)}, u32[]{:S(2)}, u32[]{:S(2)}) collective-permute-start(f16[256,256]{1,0:T(8,128)(2,1)S(1)} %convert_element_type.74), channel_id=1, source_target_pairs={{4,5},{5,6},{6,4},{7,2},{10,10},{11,9},{8,11},{9,13},{20,21},{21,2... | collective-permute-start | bytes 393224 | tf_op jit(solution)/shard_map/ppermute | solution.py:218
  46.7 4.5 %collective-permute-start.7 = (f16[256,256]{1,0:T(8,128)(2,1)S(1)}, f16[256,256]{1,0:T(8,128)(2,1)S(1)}, u32[]{:S(2)}, u32[]{:S(2)}) collective-permute-start(f16[256,256]{1,0:T(8,128)(2,1)S(1)} %convert_element_type.76), channel_id=1, source_target_pairs={{4,0},{6,1},{10,15},{8,14},{20,16},{22,17},{26,31},{24,30}} | collective-permute-start | bytes 393224 | tf_op jit(solution)/shard_map/ppermute | solution.py:218
  55.1 6.1 %copy-start.2 = (s32[4,2,2]{2,1,0:T(2,128)S(1)}, s32[4,2,2]{2,1,0:T(2,128)}, u32[]{:S(2)}) copy-start(s32[4,2,2]{2,1,0:T(2,128)} %constant.23.clone.places) | copy-start | bytes 196
  57.2 4.0 %collective-permute-start.8 = (f16[2,256,256]{2,1,0:T(8,128)(2,1)S(1)}, f16[2,256,256]{2,1,0:T(8,128)(2,1)S(1)}, u32[]{:S(2)}, u32[]{:S(2)}) collective-permute-start(f16[2,256,256]{2,1,0:T(8,128)(2,1)S(1)} %convert_element_type.78), channel_id=1, source_target_pairs={{4,5},{5,4},{8,9},{9,8},{6,7},{7,6},{10,11},{11,10},{20,21},{21,20... | collective-permute-start | bytes 786440 | tf_op jit(solution)/shard_map/ppermute | solution.py:214
  59.1 12.3 %collective-permute-start.13 = (f16[256,256]{1,0:T(8,128)(2,1)S(1)}, f16[256,256]{1,0:T(8,128)(2,1)S(1)}, u32[]{:S(2)}, u32[]{:S(2)}) collective-permute-start(f16[256,256]{1,0:T(8,128)(2,1)S(1)} %convert_element_type.88), channel_id=1, source_target_pairs={{4,1},{5,8},{6,0},{7,10},{10,14},{11,7},{8,15},{9,5},{20,17},{21,2... | collective-permute-start | bytes 393224 | tf_op jit(solution)/shard_map/ppermute | solution.py:218
  60.5 13.5 %collective-permute-start.14 = (f16[256,256]{1,0:T(8,128)(2,1)S(1)}, f16[256,256]{1,0:T(8,128)(2,1)S(1)}, u32[]{:S(2)}, u32[]{:S(2)}) collective-permute-start(f16[256,256]{1,0:T(8,128)(2,1)S(1)} %convert_element_type.90), channel_id=1, source_target_pairs={{5,10},{7,8},{11,5},{9,7},{21,26},{23,24},{27,21},{25,23}} | collective-permute-start | bytes 393224 | tf_op jit(solution)/shard_map/ppermute | solution.py:218
  62.1 11.9 %collective-permute-start.10 = (f16[256,256]{1,0:T(8,128)(2,1)S(1)}, f16[256,256]{1,0:T(8,128)(2,1)S(1)}, u32[]{:S(2)}, u32[]{:S(2)}) collective-permute-start(f16[256,256]{1,0:T(8,128)(2,1)S(1)} %convert_element_type.82), channel_id=1, source_target_pairs={{4,13},{5,15},{6,12},{7,14},{10,2},{11,0},{8,3},{9,1},{20,29},{21,... | collective-permute-start | bytes 393224 | tf_op jit(solution)/shard_map/ppermute | solution.py:218
  63.5 10.6 %collective-permute-start.11 = (f16[256,256]{1,0:T(8,128)(2,1)S(1)}, f16[256,256]{1,0:T(8,128)(2,1)S(1)}, u32[]{:S(2)}, u32[]{:S(2)}) collective-permute-start(f16[256,256]{1,0:T(8,128)(2,1)S(1)} %convert_element_type.84), channel_id=1, source_target_pairs={{4,12},{5,14},{6,13},{7,15},{10,3},{11,1},{8,2},{9,0},{20,28},{21,... | collective-permute-start | bytes 393224 | tf_op jit(solution)/shard_map/ppermute | solution.py:218
  64.8 11.4 %collective-permute-start.12 = (f16[256,256]{1,0:T(8,128)(2,1)S(1)}, f16[256,256]{1,0:T(8,128)(2,1)S(1)}, u32[]{:S(2)}, u32[]{:S(2)}) collective-permute-start(f16[256,256]{1,0:T(8,128)(2,1)S(1)} %convert_element_type.86), channel_id=1, source_target_pairs={{4,7},{5,9},{6,3},{7,11},{10,8},{11,6},{8,12},{9,4},{20,23},{21,25... | collective-permute-start | bytes 393224 | tf_op jit(solution)/shard_map/ppermute | solution.py:218
  71.4 7.2 %collective-permute-start.9 = (f16[256,256]{1,0:T(8,128)(2,1)S(1)}, f16[256,256]{1,0:T(8,128)(2,1)S(1)}, u32[]{:S(2)}, u32[]{:S(2)}) collective-permute-start(f16[256,256]{1,0:T(8,128)(2,1)S(1)} %convert_element_type.80), channel_id=1, source_target_pairs={{4,3},{5,11},{6,7},{7,9},{10,12},{11,4},{8,8},{9,6},{20,19},{21,27... | collective-permute-start | bytes 393224 | tf_op jit(solution)/shard_map/ppermute | solution.py:218

commit v19 on v16

--- a/solution.py
+++ b/solution.py
@@ -226,7 +226,7 @@
         in_specs=[SMEM, ANY],
         out_specs=[VMEM] * 3,
         scratch_shapes=[pltpu.SemaphoreType.DMA((2,))],
-        compiler_params=LIMIT,
+        compiler_params=pltpu.CompilerParams(vmem_limit_bytes=57 * 2**20),
         cost_estimate=BRIEF,
     )(bits, log_derivs)
     from_centre = lax.ppermute(far, "row", to_centre)

time: 79.8 us -> 81.7 us (1.024)
  Pallas kernels: 8.47 us -> 11.1 us
  waiting for transfers between devices: 38.8 us -> 37.1 us
    pallas_call x1, Pallas kernels: 0.89 us -> 3.55 us  [two_centres(): pl.pallas_call(split_kernel, out_shape=[shape_of((local_rows, part), jnp....]
    ppermute x1, waiting for transfers between devices: 3.89 us -> 1.93 us  [two_centres(): from_far_edge = lax.ppermute(far, 'row', to_far)]
    unnamed x6 -> x10, local copies, waits for them, and re-layouts: 1.6 us -> 1.97 us
where the time goes in v19:
time: 81.7 us; the launch traced here: 81.2 us
  waiting for transfers between devices  37.1 us (45%)
  starting transfers between devices  28.2 us (35%)
  Pallas kernels  11.1 us (14%)
  local copies, waits for them, and re-layouts  1.97 us (2%)
  other arithmetic  1.83 us (2%)
  between operations  1.02 us (1%)
    ppermute x1, waiting for transfers between devices, two_centres(): from_sum = lax.ppermute(far_sum, 'row', to_far)  24.3 us
    ppermute x8, starting transfers between devices, send(): lax.ppermute(value.astype(jnp.float16), everyone, round_pairs(blocks))  17 us
    ppermute x8, waiting for transfers between devices, send(): lax.ppermute(value.astype(jnp.float16), everyone, round_pairs(blocks))  9.11 us
    ppermute x2, starting transfers between devices, swap(): narrow = lax.ppermute(value.astype(jnp.float16), ('row', 'half'), centres)  3.84 us
    pallas_call x1, Pallas kernels, two_centres(): pl.pallas_call(split_kernel, out_shape=[shape_of((local_rows, part), jnp....  3.55 us
    ppermute x1, starting transfers between devices, two_centres(): from_centre = lax.ppermute(far, 'row', to_centre)  3.48 us
    pallas_call x1, Pallas kernels, two_centres(): pl.pallas_call(early_kernel, out_shape=[shape_of((3, local_rows, part), j...  3.3 us
    pallas_call x1, Pallas kernels, two_centres(): pl.pallas_call(late_kernel, out_shape=[late_blocks, late_blocks] + [shape...  2 us
  transfers between devices with their start and end apart: 14, of which 6 were waited for; matrix products, arithmetic and copies ran while one was open for 0% of the time, Pallas kernels for 7%

profile of v19, /device:TPU:8, one launch (start us, length us, event | category | flops | bytes accessed | tf_op | source)
XLA Modules:
  0.0 81.2 jit_solution(7292917338582900509)
XLA Ops:
  0.6 3.6 %shard_map.46 = (bf16[256,2048]{1,0:T(8,128)(2,1)}, bf16[256,2048]{1,0:T(8,128)(2,1)}, f32[1,2048]{1,0:T(1,128)}) custom-call(s32[3]{0:T(128)} %pad_add_fusion.bits, bf16[256,4096]{1,0:T(8,128)(2,1)} %values.1), custom_call_target="tpu_custom_call" | custom-call | flops 1024 | bytes 1024 | tf_op jit(solution)/shard_map/pallas_call | solution.py:219
  4.2 3.5 %collective-permute-start.1 = (bf16[256,2048]{1,0:T(8,128)(2,1)}, bf16[256,2048]{1,0:T(8,128)(2,1)S(1)}, u32[]{:S(2)}, u32[]{:S(2)}) collective-permute-start(bf16[256,2048]{1,0:T(8,128)(2,1)} %get-tuple-element.26), channel_id=1, source_target_pairs={{4,8},{8,4},{5,9},{9,5},{6,10},{10,6},{7,11},{11,7},{20,24},{24,20... | collective-permute-start | bytes 3145736 | tf_op jit(solution)/shard_map/ppermute | solution.py:232
  7.7 1.3 %collective-permute-start.2 = (bf16[256,2048]{1,0:T(8,128)(2,1)}, bf16[256,2048]{1,0:T(8,128)(2,1)S(1)}, u32[]{:S(2)}, u32[]{:S(2)}) collective-permute-start(bf16[256,2048]{1,0:T(8,128)(2,1)} %get-tuple-element.27.near), channel_id=1, source_target_pairs={{0,4},{12,8},{1,5},{13,9},{2,6},{14,10},{3,7},{15,11},{16,20},{28,... | collective-permute-start | bytes 3145736 | tf_op jit(solution)/shard_map/ppermute | solution.py:234
  9.0 1.3 %collective-permute-start.3 = (f32[1,2048]{1,0:T(1,128)}, f32[1,2048]{1,0:T(1,128)S(1)}, u32[]{:S(2)}, u32[]{:S(2)}) collective-permute-start(f32[1,2048]{1,0:T(1,128)} %get-tuple-element.28), channel_id=1, source_target_pairs={{0,8},{12,4},{1,9},{13,5},{2,10},{14,6},{3,11},{15,7},{16,24},{28,... | collective-permute-start | bytes 24584 | tf_op jit(solution)/shard_map/ppermute | solution.py:233
  10.3 1.3 %collective-permute-start = (bf16[256,2048]{1,0:T(8,128)(2,1)}, bf16[256,2048]{1,0:T(8,128)(2,1)S(1)}, u32[]{:S(2)}, u32[]{:S(2)}) collective-permute-start(bf16[256,2048]{1,0:T(8,128)(2,1)} %get-tuple-element.26), channel_id=1, source_target_pairs={{0,8},{12,4},{1,9},{13,5},{2,10},{14,6},{3,11},{15,7},{16,24},{28,... | collective-permute-start | bytes 3145736 | tf_op jit(solution)/shard_map/ppermute | solution.py:235
  11.6 24.3 %collective-permute-done.3.far_sum = f32[1,2048]{1,0:T(1,128)S(1)} collective-permute-done((f32[1,2048]{1,0:T(1,128)}, f32[1,2048]{1,0:T(1,128)S(1)}, u32[]{:S(2)}, u32[]{:S(2)}) %collective-permute-start.3) | collective-permute-done | bytes 8224 | tf_op jit(solution)/shard_map/ppermute | solution.py:233
  35.9 1.2 %copy-done = bf16[256,2048]{1,0:T(8,128)(2,1)S(1)} copy-done((bf16[256,2048]{1,0:T(8,128)(2,1)S(1)}, bf16[256,2048]{1,0:T(8,128)(2,1)}, u32[]{:S(2)}) %copy-start) | copy-done | bytes 1048600
  38.4 3.3 %shard_map.48 = (bf16[3,256,2048]{2,1,0:T(8,128)(2,1)S(1)}, f32[1,2048]{1,0:T(1,128)S(1)}, f32[3,256,256]{2,1,0:T(8,128)S(1)}, f32[3,256,256]{2,1,0:T(8,128)S(1)}) custom-call(s32[3]{0:T(128)S(1)} %copy-done.2, bf16[256,2048]{1,0:T(8,128)(2,1)S(1)} %collective-permute-done.1.other, bf16[256,2048]{1,0:T(8,128)(2,1)S(1)} %collective-permute-done.2.edge, ...), custom_call_target="tpu_custom_call" | custom-call | flops 1024 | bytes 1024 | tf_op jit(solution)/shard_map/pallas_call | solution.py:246
  41.7 1.9 %collective-permute-start.4 = (f16[3,256,256]{2,1,0:T(8,128)(2,1)S(1)}, f16[3,256,256]{2,1,0:T(8,128)(2,1)S(1)}, u32[]{:S(2)}, u32[]{:S(2)}) collective-permute-start(f16[3,256,256]{2,1,0:T(8,128)(2,1)S(1)} %convert_element_type.64), channel_id=1, source_target_pairs={{4,5},{5,4},{8,9},{9,8},{6,7},{7,6},{10,11},{11,10},{20,21},{21,20... | collective-permute-start | bytes 1179656 | tf_op jit(solution)/shard_map/ppermute | solution.py:213
  43.7 1.7 %collective-permute-done.4 = f16[3,256,256]{2,1,0:T(8,128)(2,1)S(1)} collective-permute-done((f16[3,256,256]{2,1,0:T(8,128)(2,1)S(1)}, f16[3,256,256]{2,1,0:T(8,128)(2,1)S(1)}, u32[]{:S(2)}, u32[]{:S(2)}) %collective-permute-start.4) | collective-permute-done | bytes 393248 | tf_op jit(solution)/shard_map/ppermute | solution.py:213
  45.4 0.9 %shard_map.49 = (f32[256,256]{1,0:T(8,128)S(1)}, f32[256,256]{1,0:T(8,128)S(1)}, f32[256,256]{1,0:T(8,128)S(1)}, f32[256,256]{1,0:T(8,128)S(1)}, f32[256,256]{1,0:T(8,128)S(1)}) custom-call(s32[3]{0:T(128)S(1)} %copy-done.2, s32[5,2,2]{2,1,0:T(2,128)S(1)} %copy-done.3, f32[3,256,256]{2,1,0:T(8,128)S(1)} %get-tuple-element.31.own, ...), custom_call_target="tpu_custom_call" | custom-call | flops 1024 | bytes 1024 | tf_op jit(solution)/shard_map/pallas_call | solution.py:188
  47.1 3.3 %collective-permute-start.6 = (f16[256,256]{1,0:T(8,128)(2,1)S(1)}, f16[256,256]{1,0:T(8,128)(2,1)S(1)}, u32[]{:S(2)}, u32[]{:S(2)}) collective-permute-start(f16[256,256]{1,0:T(8,128)(2,1)S(1)} %convert_element_type.68), channel_id=1, source_target_pairs={{4,5},{5,6},{6,4},{7,2},{10,10},{11,9},{8,11},{9,13},{20,21},{21,2... | collective-permute-start | bytes 393224 | tf_op jit(solution)/shard_map/ppermute | solution.py:217
  50.4 4.5 %collective-permute-done.6 = f16[256,256]{1,0:T(8,128)(2,1)S(1)} collective-permute-done((f16[256,256]{1,0:T(8,128)(2,1)S(1)}, f16[256,256]{1,0:T(8,128)(2,1)S(1)}, u32[]{:S(2)}, u32[]{:S(2)}) %collective-permute-start.6) | collective-permute-done | bytes 131104 | tf_op jit(solution)/shard_map/ppermute | solution.py:217
  55.0 1.9 %collective-permute-done.far_edge = bf16[256,2048]{1,0:T(8,128)(2,1)S(1)} collective-permute-done((bf16[256,2048]{1,0:T(8,128)(2,1)}, bf16[256,2048]{1,0:T(8,128)(2,1)S(1)}, u32[]{:S(2)}, u32[]{:S(2)}) %collective-permute-start) | collective-permute-done | bytes 1048608 | tf_op jit(solution)/shard_map/ppermute | solution.py:235
  56.9 2.0 %shard_map.50 = (f32[2,256,256]{2,1,0:T(8,128)S(1)}, f32[2,256,256]{2,1,0:T(8,128)S(1)}, f32[256,256]{1,0:T(8,128)S(1)}, f32[256,256]{1,0:T(8,128)S(1)}, f32[256,256]{1,0:T(8,128)S(1)}) custom-call(s32[3]{0:T(128)S(1)} %copy-done.2, bf16[256,2048]{1,0:T(8,128)(2,1)S(1)} %collective-permute-done.far_edge, ...), custom_call_target="tpu_custom_call", output_to_operand_aliasing={{2}: (4, {}), {3}: (5, {}), {4}: (6, {})} | custom-call | flops 1024 | bytes 1024 | tf_op jit(solution)/shard_map/pallas_call | solution.py:269
  59.0 1.9 %collective-permute-start.7 = (f16[2,256,256]{2,1,0:T(8,128)(2,1)S(1)}, f16[2,256,256]{2,1,0:T(8,128)(2,1)S(1)}, u32[]{:S(2)}, u32[]{:S(2)}) collective-permute-start(f16[2,256,256]{2,1,0:T(8,128)(2,1)S(1)} %convert_element_type.70), channel_id=1, source_target_pairs={{4,5},{5,4},{8,9},{9,8},{6,7},{7,6},{10,11},{11,10},{20,21},{21,20... | collective-permute-start | bytes 786440 | tf_op jit(solution)/shard_map/ppermute | solution.py:213
  60.9 1.3 %collective-permute-start.12 = (f16[256,256]{1,0:T(8,128)(2,1)S(1)}, f16[256,256]{1,0:T(8,128)(2,1)S(1)}, u32[]{:S(2)}, u32[]{:S(2)}) collective-permute-start(f16[256,256]{1,0:T(8,128)(2,1)S(1)} %convert_element_type.80), channel_id=1, source_target_pairs={{4,1},{5,8},{6,0},{7,10},{10,14},{11,7},{8,15},{9,5},{20,17},{21,2... | collective-permute-start | bytes 393224 | tf_op jit(solution)/shard_map/ppermute | solution.py:217
  62.3 1.3 %collective-permute-start.13 = (f16[256,256]{1,0:T(8,128)(2,1)S(1)}, f16[256,256]{1,0:T(8,128)(2,1)S(1)}, u32[]{:S(2)}, u32[]{:S(2)}) collective-permute-start(f16[256,256]{1,0:T(8,128)(2,1)S(1)} %convert_element_type.82), channel_id=1, source_target_pairs={{4,0},{5,10},{6,1},{7,8},{10,15},{11,5},{8,14},{9,7},{20,16},{21,2... | collective-permute-start | bytes 393224 | tf_op jit(solution)/shard_map/ppermute | solution.py:217
  64.6 1.3 %collective-permute-start.10 = (f16[256,256]{1,0:T(8,128)(2,1)S(1)}, f16[256,256]{1,0:T(8,128)(2,1)S(1)}, u32[]{:S(2)}, u32[]{:S(2)}) collective-permute-start(f16[256,256]{1,0:T(8,128)(2,1)S(1)} %convert_element_type.76), channel_id=1, source_target_pairs={{4,13},{5,15},{6,12},{7,14},{10,2},{11,0},{8,3},{9,1},{20,29},{21,... | collective-permute-start | bytes 393224 | tf_op jit(solution)/shard_map/ppermute | solution.py:217
  65.9 1.3 %collective-permute-start.11 = (f16[256,256]{1,0:T(8,128)(2,1)S(1)}, f16[256,256]{1,0:T(8,128)(2,1)S(1)}, u32[]{:S(2)}, u32[]{:S(2)}) collective-permute-start(f16[256,256]{1,0:T(8,128)(2,1)S(1)} %convert_element_type.78), channel_id=1, source_target_pairs={{4,12},{5,14},{6,13},{7,15},{10,3},{11,1},{8,2},{9,0},{20,28},{21,... | collective-permute-start | bytes 393224 | tf_op jit(solution)/shard_map/ppermute | solution.py:217
  67.2 5.9 %collective-permute-start.8 = (f16[256,256]{1,0:T(8,128)(2,1)S(1)}, f16[256,256]{1,0:T(8,128)(2,1)S(1)}, u32[]{:S(2)}, u32[]{:S(2)}) collective-permute-start(f16[256,256]{1,0:T(8,128)(2,1)S(1)} %convert_element_type.72), channel_id=1, source_target_pairs={{4,7},{5,9},{6,3},{7,11},{10,8},{11,6},{8,12},{9,4},{20,23},{21,25... | collective-permute-start | bytes 393224 | tf_op jit(solution)/shard_map/ppermute | solution.py:217
  73.2 1.9 %collective-permute-start.9 = (f16[256,256]{1,0:T(8,128)(2,1)S(1)}, f16[256,256]{1,0:T(8,128)(2,1)S(1)}, u32[]{:S(2)}, u32[]{:S(2)}) collective-permute-start(f16[256,256]{1,0:T(8,128)(2,1)S(1)} %convert_element_type.74), channel_id=1, source_target_pairs={{4,3},{5,11},{6,7},{7,9},{10,12},{11,4},{8,8},{9,6},{20,19},{21,27... | collective-permute-start | bytes 393224 | tf_op jit(solution)/shard_map/ppermute | solution.py:217
  75.8 2.6 %collective-permute-done.8 = f16[256,256]{1,0:T(8,128)(2,1)S(1)} collective-permute-done((f16[256,256]{1,0:T(8,128)(2,1)S(1)}, f16[256,256]{1,0:T(8,128)(2,1)S(1)}, u32[]{:S(2)}, u32[]{:S(2)}) %collective-permute-start.8) | collective-permute-done | bytes 131104 | tf_op jit(solution)/shard_map/ppermute | solution.py:217
  78.4 2.0 %collective-permute-done.9 = f16[256,256]{1,0:T(8,128)(2,1)S(1)} collective-permute-done((f16[256,256]{1,0:T(8,128)(2,1)S(1)}, f16[256,256]{1,0:T(8,128)(2,1)S(1)}, u32[]{:S(2)}, u32[]{:S(2)}) %collective-permute-start.9) | collective-permute-done | bytes 131104 | tf_op jit(solution)/shard_map/ppermute | solution.py:217
  (36 shorter events, 4.6 us)
Async XLA Ops:
  4.2 31.7 %collective-permute-start.1 = (bf16[256,2048]{1,0:T(8,128)(2,1)}, bf16[256,2048]{1,0:T(8,128)(2,1)S(1)}, u32[]{:S(2)}, u32[]{:S(2)}) collective-permute-start(bf16[256,2048]{1,0:T(8,128)(2,1)} %get-tuple-element.26), channel_id=1, source_target_pairs={{4,8},{8,4},{5,9},{9,5},{6,10},{10,6},{7,11},{11,7},{20,24},{24,20... | collective-permute-start | bytes 3145736 | tf_op jit(solution)/shard_map/ppermute | solution.py:232
  7.7 30.0 %collective-permute-start.2 = (bf16[256,2048]{1,0:T(8,128)(2,1)}, bf16[256,2048]{1,0:T(8,128)(2,1)S(1)}, u32[]{:S(2)}, u32[]{:S(2)}) collective-permute-start(bf16[256,2048]{1,0:T(8,128)(2,1)} %get-tuple-element.27.near), channel_id=1, source_target_pairs={{0,4},{12,8},{1,5},{13,9},{2,6},{14,10},{3,7},{15,11},{16,20},{28,... | collective-permute-start | bytes 3145736 | tf_op jit(solution)/shard_map/ppermute | solution.py:234
  9.0 28.7 %copy-start.2 = (s32[3]{0:T(128)S(1)}, s32[3]{0:T(128)}, u32[]{:S(2)}) copy-start(s32[3]{0:T(128)} %pad_add_fusion.bits) | copy-start | bytes 40
  9.0 26.9 %collective-permute-start.3 = (f32[1,2048]{1,0:T(1,128)}, f32[1,2048]{1,0:T(1,128)S(1)}, u32[]{:S(2)}, u32[]{:S(2)}) collective-permute-start(f32[1,2048]{1,0:T(1,128)} %get-tuple-element.28), channel_id=1, source_target_pairs={{0,8},{12,4},{1,9},{13,5},{2,10},{14,6},{3,11},{15,7},{16,24},{28,... | collective-permute-start | bytes 24584 | tf_op jit(solution)/shard_map/ppermute | solution.py:233
  10.3 46.6 %collective-permute-start = (bf16[256,2048]{1,0:T(8,128)(2,1)}, bf16[256,2048]{1,0:T(8,128)(2,1)S(1)}, u32[]{:S(2)}, u32[]{:S(2)}) collective-permute-start(bf16[256,2048]{1,0:T(8,128)(2,1)} %get-tuple-element.26), channel_id=1, source_target_pairs={{0,8},{12,4},{1,9},{13,5},{2,10},{14,6},{3,11},{15,7},{16,24},{28,... | collective-permute-start | bytes 3145736 | tf_op jit(solution)/shard_map/ppermute | solution.py:235
  35.9 1.2 %copy-start = (bf16[256,2048]{1,0:T(8,128)(2,1)S(1)}, bf16[256,2048]{1,0:T(8,128)(2,1)}, u32[]{:S(2)}) copy-start(bf16[256,2048]{1,0:T(8,128)(2,1)} %get-tuple-element.27.near) | copy-start | bytes 3145732
  37.1 1.2 %copy-start.1 = (bf16[256,2048]{1,0:T(8,128)(2,1)S(1)}, bf16[256,2048]{1,0:T(8,128)(2,1)}, u32[]{:S(2)}) copy-start(bf16[256,2048]{1,0:T(8,128)(2,1)} %get-tuple-element.27.near) | copy-start | bytes 3145732
  37.6 7.8 %copy-start.3 = (s32[5,2,2]{2,1,0:T(2,128)S(1)}, s32[5,2,2]{2,1,0:T(2,128)}, u32[]{:S(2)}) copy-start(s32[5,2,2]{2,1,0:T(2,128)} %constant.22.clone.places) | copy-start | bytes 244
  41.7 3.6 %collective-permute-start.4 = (f16[3,256,256]{2,1,0:T(8,128)(2,1)S(1)}, f16[3,256,256]{2,1,0:T(8,128)(2,1)S(1)}, u32[]{:S(2)}, u32[]{:S(2)}) collective-permute-start(f16[3,256,256]{2,1,0:T(8,128)(2,1)S(1)} %convert_element_type.64), channel_id=1, source_target_pairs={{4,5},{5,4},{8,9},{9,8},{6,7},{7,6},{10,11},{11,10},{20,21},{21,20... | collective-permute-start | bytes 1179656 | tf_op jit(solution)/shard_map/ppermute | solution.py:213
  46.4 4.0 %collective-permute-start.5 = (f16[256,256]{1,0:T(8,128)(2,1)S(1)}, f16[256,256]{1,0:T(8,128)(2,1)S(1)}, u32[]{:S(2)}, u32[]{:S(2)}) collective-permute-start(f16[256,256]{1,0:T(8,128)(2,1)S(1)} %convert_element_type.66), channel_id=1, source_target_pairs={{4,4},{5,2},{6,5},{7,6},{10,11},{11,13},{8,10},{9,9},{20,20},{21,1... | collective-permute-start | bytes 393224 | tf_op jit(solution)/shard_map/ppermute | solution.py:217
  47.1 7.9 %collective-permute-start.6 = (f16[256,256]{1,0:T(8,128)(2,1)S(1)}, f16[256,256]{1,0:T(8,128)(2,1)S(1)}, u32[]{:S(2)}, u32[]{:S(2)}) collective-permute-start(f16[256,256]{1,0:T(8,128)(2,1)S(1)} %convert_element_type.68), channel_id=1, source_target_pairs={{4,5},{5,6},{6,4},{7,2},{10,10},{11,9},{8,11},{9,13},{20,21},{21,2... | collective-permute-start | bytes 393224 | tf_op jit(solution)/shard_map/ppermute | solution.py:217
  56.9 6.7 %copy-start.4 = (s32[4,2,2]{2,1,0:T(2,128)S(1)}, s32[4,2,2]{2,1,0:T(2,128)}, u32[]{:S(2)}) copy-start(s32[4,2,2]{2,1,0:T(2,128)} %constant.23.clone.places) | copy-start | bytes 196
  59.0 4.6 %collective-permute-start.7 = (f16[2,256,256]{2,1,0:T(8,128)(2,1)S(1)}, f16[2,256,256]{2,1,0:T(8,128)(2,1)S(1)}, u32[]{:S(2)}, u32[]{:S(2)}) collective-permute-start(f16[2,256,256]{2,1,0:T(8,128)(2,1)S(1)} %convert_element_type.70), channel_id=1, source_target_pairs={{4,5},{5,4},{8,9},{9,8},{6,7},{7,6},{10,11},{11,10},{20,21},{21,20... | collective-permute-start | bytes 786440 | tf_op jit(solution)/shard_map/ppermute | solution.py:213
  60.9 12.3 %collective-permute-start.12 = (f16[256,256]{1,0:T(8,128)(2,1)S(1)}, f16[256,256]{1,0:T(8,128)(2,1)S(1)}, u32[]{:S(2)}, u32[]{:S(2)}) collective-permute-start(f16[256,256]{1,0:T(8,128)(2,1)S(1)} %convert_element_type.80), channel_id=1, source_target_pairs={{4,1},{5,8},{6,0},{7,10},{10,14},{11,7},{8,15},{9,5},{20,17},{21,2... | collective-permute-start | bytes 393224 | tf_op jit(solution)/shard_map/ppermute | solution.py:217
  62.3 13.5 %collective-permute-start.13 = (f16[256,256]{1,0:T(8,128)(2,1)S(1)}, f16[256,256]{1,0:T(8,128)(2,1)S(1)}, u32[]{:S(2)}, u32[]{:S(2)}) collective-permute-start(f16[256,256]{1,0:T(8,128)(2,1)S(1)} %convert_element_type.82), channel_id=1, source_target_pairs={{4,0},{5,10},{6,1},{7,8},{10,15},{11,5},{8,14},{9,7},{20,16},{21,2... | collective-permute-start | bytes 393224 | tf_op jit(solution)/shard_map/ppermute | solution.py:217
  64.6 11.2 %collective-permute-start.10 = (f16[256,256]{1,0:T(8,128)(2,1)S(1)}, f16[256,256]{1,0:T(8,128)(2,1)S(1)}, u32[]{:S(2)}, u32[]{:S(2)}) collective-permute-start(f16[256,256]{1,0:T(8,128)(2,1)S(1)} %convert_element_type.76), channel_id=1, source_target_pairs={{4,13},{5,15},{6,12},{7,14},{10,2},{11,0},{8,3},{9,1},{20,29},{21,... | collective-permute-start | bytes 393224 | tf_op jit(solution)/shard_map/ppermute | solution.py:217
  65.9 9.9 %collective-permute-start.11 = (f16[256,256]{1,0:T(8,128)(2,1)S(1)}, f16[256,256]{1,0:T(8,128)(2,1)S(1)}, u32[]{:S(2)}, u32[]{:S(2)}) collective-permute-start(f16[256,256]{1,0:T(8,128)(2,1)S(1)} %convert_element_type.78), channel_id=1, source_target_pairs={{4,12},{5,14},{6,13},{7,15},{10,3},{11,1},{8,2},{9,0},{20,28},{21,... | collective-permute-start | bytes 393224 | tf_op jit(solution)/shard_map/ppermute | solution.py:217
  67.2 11.2 %collective-permute-start.8 = (f16[256,256]{1,0:T(8,128)(2,1)S(1)}, f16[256,256]{1,0:T(8,128)(2,1)S(1)}, u32[]{:S(2)}, u32[]{:S(2)}) collective-permute-start(f16[256,256]{1,0:T(8,128)(2,1)S(1)} %convert_element_type.72), channel_id=1, source_target_pairs={{4,7},{5,9},{6,3},{7,11},{10,8},{11,6},{8,12},{9,4},{20,23},{21,25... | collective-permute-start | bytes 393224 | tf_op jit(solution)/shard_map/ppermute | solution.py:217
  73.2 7.2 %collective-permute-start.9 = (f16[256,256]{1,0:T(8,128)(2,1)S(1)}, f16[256,256]{1,0:T(8,128)(2,1)S(1)}, u32[]{:S(2)}, u32[]{:S(2)}) collective-permute-start(f16[256,256]{1,0:T(8,128)(2,1)S(1)} %convert_element_type.74), channel_id=1, source_target_pairs={{4,3},{5,11},{6,7},{7,9},{10,12},{11,4},{8,8},{9,6},{20,19},{21,27... | collective-permute-start | bytes 393224 | tf_op jit(solution)/shard_map/ppermute | solution.py:217

commit v20 on v16

--- a/solution.py
+++ b/solution.py
@@ -38,8 +38,8 @@
     (((1, 1), (1, 0)), ((1, 2), (0, 2))),
 )
 FAR_ROUNDS = (
+    (((0, 1), (0, 0)), ((2, 0), (2, 2))),
     (((0, 0), (0, 1)), ((2, 2), (2, 0))),
-    (((0, 1), (0, 0)), ((2, 0), (2, 2))),
 )
 LATE_ROUNDS = (
     (((3, 0), (3, 1)), ((3, 2), (3, 3))),

time: 79.8 us -> 79.8 us (level)
  no operation moved by 1% of the time
where the time goes in v20:
time: 79.8 us; the launch traced here: 79.4 us
  waiting for transfers between devices  38.8 us (49%)
  starting transfers between devices  28.2 us (35%)
  Pallas kernels  8.47 us (11%)
  local copies, waits for them, and re-layouts  1.6 us (2%)
  other arithmetic  1.29 us (2%)
  between operations  1 us (1%)
    ppermute x1, waiting for transfers between devices, two_centres(): from_sum = lax.ppermute(far_sum, 'row', to_far)  24.1 us
    ppermute x8, starting transfers between devices, send(): lax.ppermute(value.astype(jnp.float16), everyone, round_pairs(blocks))  17 us
    ppermute x8, waiting for transfers between devices, send(): lax.ppermute(value.astype(jnp.float16), everyone, round_pairs(blocks))  9.11 us
    ppermute x1, waiting for transfers between devices, two_centres(): from_far_edge = lax.ppermute(far, 'row', to_far)  3.89 us
    ppermute x2, starting transfers between devices, swap(): narrow = lax.ppermute(value.astype(jnp.float16), ('row', 'half'), centres)  3.84 us
    ppermute x1, starting transfers between devices, two_centres(): from_centre = lax.ppermute(far, 'row', to_centre)  3.48 us
    pallas_call x1, Pallas kernels, two_centres(): pl.pallas_call(early_kernel, out_shape=[shape_of((3, local_rows, part), j...  3.31 us
    pallas_call x1, Pallas kernels, two_centres(): pl.pallas_call(late_kernel, out_shape=[late_blocks, late_blocks] + [shape...  2 us
  transfers between devices with their start and end apart: 14, of which 6 were waited for; matrix products, arithmetic and copies ran while one was open for 0% of the time, Pallas kernels for 7%

profile of v20, /device:TPU:8, one launch (start us, length us, event | category | flops | bytes accessed | tf_op | source)
XLA Modules:
  0.0 79.4 jit_solution(11774382916048881036)
XLA Ops:
  0.1 1.6 %copy-done = bf16[256,4096]{1,0:T(8,128)(2,1)S(1)} copy-done((bf16[256,4096]{1,0:T(8,128)(2,1)S(1)}, bf16[256,4096]{1,0:T(8,128)(2,1)}, u32[]{:S(2)}) %copy-start) | copy-done | bytes 2097176
  2.6 3.5 %collective-permute-start.1 = (bf16[256,2048]{1,0:T(8,128)(2,1)S(1)}, bf16[256,2048]{1,0:T(8,128)(2,1)S(1)}, u32[]{:S(2)}, u32[]{:S(2)}) collective-permute-start(bf16[256,2048]{1,0:T(8,128)(2,1)S(1)} %get-tuple-element.26), channel_id=1, source_target_pairs={{4,8},{8,4},{5,9},{9,5},{6,10},{10,6},{7,11},{11,7},{20,24},{24,20... | collective-permute-start | bytes 3145736 | tf_op jit(solution)/shard_map/ppermute | solution.py:232
  6.1 1.3 %collective-permute-start.2 = (bf16[256,2048]{1,0:T(8,128)(2,1)S(1)}, bf16[256,2048]{1,0:T(8,128)(2,1)S(1)}, u32[]{:S(2)}, u32[]{:S(2)}) collective-permute-start(bf16[256,2048]{1,0:T(8,128)(2,1)S(1)} %get-tuple-element.27.near), channel_id=1, source_target_pairs={{0,4},{12,8},{1,5},{13,9},{2,6},{14,10},{3,7},{15,11},{16,20},{28,... | collective-permute-start | bytes 3145736 | tf_op jit(solution)/shard_map/ppermute | solution.py:234
  7.4 1.3 %collective-permute-start.3 = (f32[1,2048]{1,0:T(1,128)S(1)}, f32[1,2048]{1,0:T(1,128)S(1)}, u32[]{:S(2)}, u32[]{:S(2)}) collective-permute-start(f32[1,2048]{1,0:T(1,128)S(1)} %get-tuple-element.28), channel_id=1, source_target_pairs={{0,8},{12,4},{1,9},{13,5},{2,10},{14,6},{3,11},{15,7},{16,24},{28,... | collective-permute-start | bytes 24584 | tf_op jit(solution)/shard_map/ppermute | solution.py:233
  8.7 1.3 %collective-permute-start = (bf16[256,2048]{1,0:T(8,128)(2,1)S(1)}, bf16[256,2048]{1,0:T(8,128)(2,1)S(1)}, u32[]{:S(2)}, u32[]{:S(2)}) collective-permute-start(bf16[256,2048]{1,0:T(8,128)(2,1)S(1)} %get-tuple-element.26), channel_id=1, source_target_pairs={{0,8},{12,4},{1,9},{13,5},{2,10},{14,6},{3,11},{15,7},{16,24},{28,... | collective-permute-start | bytes 3145736 | tf_op jit(solution)/shard_map/ppermute | solution.py:235
  10.0 24.1 %collective-permute-done.3.far_sum = f32[1,2048]{1,0:T(1,128)S(1)} collective-permute-done((f32[1,2048]{1,0:T(1,128)S(1)}, f32[1,2048]{1,0:T(1,128)S(1)}, u32[]{:S(2)}, u32[]{:S(2)}) %collective-permute-start.3) | collective-permute-done | bytes 8224 | tf_op jit(solution)/shard_map/ppermute | solution.py:233
  34.6 3.3 %shard_map.48 = (bf16[3,256,2048]{2,1,0:T(8,128)(2,1)S(1)}, f32[1,2048]{1,0:T(1,128)S(1)}, f32[3,256,256]{2,1,0:T(8,128)S(1)}, f32[3,256,256]{2,1,0:T(8,128)S(1)}) custom-call(s32[3]{0:T(128)S(1)} %pad_add_fusion.bits, bf16[256,2048]{1,0:T(8,128)(2,1)S(1)} %collective-permute-done.1.other, bf16[256,2048]{1,0:T(8,128)(2,1)S(1)} %collective-permute-done.2.edge, ...), custom_call_target="tpu_custom_call" | custom-call | flops 1024 | bytes 1024 | tf_op jit(solution)/shard_map/pallas_call | solution.py:246
  38.0 1.9 %collective-permute-start.4 = (f16[3,256,256]{2,1,0:T(8,128)(2,1)S(1)}, f16[3,256,256]{2,1,0:T(8,128)(2,1)S(1)}, u32[]{:S(2)}, u32[]{:S(2)}) collective-permute-start(f16[3,256,256]{2,1,0:T(8,128)(2,1)S(1)} %convert_element_type.64), channel_id=1, source_target_pairs={{4,5},{5,4},{8,9},{9,8},{6,7},{7,6},{10,11},{11,10},{20,21},{21,20... | collective-permute-start | bytes 1179656 | tf_op jit(solution)/shard_map/ppermute | solution.py:213
  39.9 1.7 %collective-permute-done.4 = f16[3,256,256]{2,1,0:T(8,128)(2,1)S(1)} collective-permute-done((f16[3,256,256]{2,1,0:T(8,128)(2,1)S(1)}, f16[3,256,256]{2,1,0:T(8,128)(2,1)S(1)}, u32[]{:S(2)}, u32[]{:S(2)}) %collective-permute-start.4) | collective-permute-done | bytes 393248 | tf_op jit(solution)/shard_map/ppermute | solution.py:213
  41.7 0.9 %shard_map.49 = (f32[256,256]{1,0:T(8,128)S(1)}, f32[256,256]{1,0:T(8,128)S(1)}, f32[256,256]{1,0:T(8,128)S(1)}, f32[256,256]{1,0:T(8,128)S(1)}, f32[256,256]{1,0:T(8,128)S(1)}) custom-call(s32[3]{0:T(128)S(1)} %pad_add_fusion.bits, s32[5,2,2]{2,1,0:T(2,128)S(1)} %copy-done.1, f32[3,256,256]{2,1,0:T(8,128)S(1)} %get-tuple-element.31.own, ...), custom_call_target="tpu_custom_call" | custom-call | flops 1024 | bytes 1024 | tf_op jit(solution)/shard_map/pallas_call | solution.py:188
  43.3 3.3 %collective-permute-start.6 = (f16[256,256]{1,0:T(8,128)(2,1)S(1)}, f16[256,256]{1,0:T(8,128)(2,1)S(1)}, u32[]{:S(2)}, u32[]{:S(2)}) collective-permute-start(f16[256,256]{1,0:T(8,128)(2,1)S(1)} %convert_element_type.68), channel_id=1, source_target_pairs={{4,5},{5,6},{6,4},{7,2},{10,10},{11,9},{8,11},{9,13},{20,21},{21,2... | collective-permute-start | bytes 393224 | tf_op jit(solution)/shard_map/ppermute | solution.py:217
  46.6 4.5 %collective-permute-done.6 = f16[256,256]{1,0:T(8,128)(2,1)S(1)} collective-permute-done((f16[256,256]{1,0:T(8,128)(2,1)S(1)}, f16[256,256]{1,0:T(8,128)(2,1)S(1)}, u32[]{:S(2)}, u32[]{:S(2)}) %collective-permute-start.6) | collective-permute-done | bytes 131104 | tf_op jit(solution)/shard_map/ppermute | solution.py:217
  51.2 3.9 %collective-permute-done.far_edge = bf16[256,2048]{1,0:T(8,128)(2,1)S(1)} collective-permute-done((bf16[256,2048]{1,0:T(8,128)(2,1)S(1)}, bf16[256,2048]{1,0:T(8,128)(2,1)S(1)}, u32[]{:S(2)}, u32[]{:S(2)}) %collective-permute-start) | collective-permute-done | bytes 1048608 | tf_op jit(solution)/shard_map/ppermute | solution.py:235
  55.1 2.0 %shard_map.50 = (f32[2,256,256]{2,1,0:T(8,128)S(1)}, f32[2,256,256]{2,1,0:T(8,128)S(1)}, f32[256,256]{1,0:T(8,128)S(1)}, f32[256,256]{1,0:T(8,128)S(1)}, f32[256,256]{1,0:T(8,128)S(1)}) custom-call(s32[3]{0:T(128)S(1)} %pad_add_fusion.bits, ...), custom_call_target="tpu_custom_call", output_to_operand_aliasing={{2}: (4, {}), {3}: (5, {}), {4}: (6, {})} | custom-call | flops 1024 | bytes 1024 | tf_op jit(solution)/shard_map/pallas_call | solution.py:269
  57.2 1.9 %collective-permute-start.7 = (f16[2,256,256]{2,1,0:T(8,128)(2,1)S(1)}, f16[2,256,256]{2,1,0:T(8,128)(2,1)S(1)}, u32[]{:S(2)}, u32[]{:S(2)}) collective-permute-start(f16[2,256,256]{2,1,0:T(8,128)(2,1)S(1)} %convert_element_type.70), channel_id=1, source_target_pairs={{4,5},{5,4},{8,9},{9,8},{6,7},{7,6},{10,11},{11,10},{20,21},{21,20... | collective-permute-start | bytes 786440 | tf_op jit(solution)/shard_map/ppermute | solution.py:213
  59.1 1.3 %collective-permute-start.12 = (f16[256,256]{1,0:T(8,128)(2,1)S(1)}, f16[256,256]{1,0:T(8,128)(2,1)S(1)}, u32[]{:S(2)}, u32[]{:S(2)}) collective-permute-start(f16[256,256]{1,0:T(8,128)(2,1)S(1)} %convert_element_type.80), channel_id=1, source_target_pairs={{4,0},{5,10},{6,1},{7,8},{10,15},{11,5},{8,14},{9,7},{20,16},{21,2... | collective-permute-start | bytes 393224 | tf_op jit(solution)/shard_map/ppermute | solution.py:217
  60.5 1.3 %collective-permute-start.13 = (f16[256,256]{1,0:T(8,128)(2,1)S(1)}, f16[256,256]{1,0:T(8,128)(2,1)S(1)}, u32[]{:S(2)}, u32[]{:S(2)}) collective-permute-start(f16[256,256]{1,0:T(8,128)(2,1)S(1)} %convert_element_type.82), channel_id=1, source_target_pairs={{4,1},{5,8},{6,0},{7,10},{10,14},{11,7},{8,15},{9,5},{20,17},{21,2... | collective-permute-start | bytes 393224 | tf_op jit(solution)/shard_map/ppermute | solution.py:217
  61.8 0.9 %shard_map.51 = (f32[256,256]{1,0:T(8,128)S(1)}, f32[256,256]{1,0:T(8,128)S(1)}, f32[256,256]{1,0:T(8,128)S(1)}, f32[256,256]{1,0:T(8,128)S(1)}) custom-call(s32[3]{0:T(128)S(1)} %pad_add_fusion.bits, s32[4,2,2]{2,1,0:T(2,128)S(1)} %copy-done.2, f32[2,256,256]{2,1,0:T(8,128)S(1)} %get-tuple-element.38.own, f32[2,256,256]{2,1,0:T(8,128)S(1)} %convert_element_type.71.rest_0_, ...), custom_call_target="tpu_custom_call" | custom-call | flops 1024 | bytes 1024 | tf_op jit(solution)/shard_map/pallas_call | solution.py:188
  62.8 1.3 %collective-permute-start.10 = (f16[256,256]{1,0:T(8,128)(2,1)S(1)}, f16[256,256]{1,0:T(8,128)(2,1)S(1)}, u32[]{:S(2)}, u32[]{:S(2)}) collective-permute-start(f16[256,256]{1,0:T(8,128)(2,1)S(1)} %convert_element_type.76), channel_id=1, source_target_pairs={{4,13},{5,15},{6,12},{7,14},{10,2},{11,0},{8,3},{9,1},{20,29},{21,... | collective-permute-start | bytes 393224 | tf_op jit(solution)/shard_map/ppermute | solution.py:217
  64.1 1.3 %collective-permute-start.11 = (f16[256,256]{1,0:T(8,128)(2,1)S(1)}, f16[256,256]{1,0:T(8,128)(2,1)S(1)}, u32[]{:S(2)}, u32[]{:S(2)}) collective-permute-start(f16[256,256]{1,0:T(8,128)(2,1)S(1)} %convert_element_type.78), channel_id=1, source_target_pairs={{4,12},{5,14},{6,13},{7,15},{10,3},{11,1},{8,2},{9,0},{20,28},{21,... | collective-permute-start | bytes 393224 | tf_op jit(solution)/shard_map/ppermute | solution.py:217
  65.4 5.9 %collective-permute-start.8 = (f16[256,256]{1,0:T(8,128)(2,1)S(1)}, f16[256,256]{1,0:T(8,128)(2,1)S(1)}, u32[]{:S(2)}, u32[]{:S(2)}) collective-permute-start(f16[256,256]{1,0:T(8,128)(2,1)S(1)} %convert_element_type.72), channel_id=1, source_target_pairs={{4,7},{5,9},{6,3},{7,11},{10,8},{11,6},{8,12},{9,4},{20,23},{21,25... | collective-permute-start | bytes 393224 | tf_op jit(solution)/shard_map/ppermute | solution.py:217
  71.4 1.9 %collective-permute-start.9 = (f16[256,256]{1,0:T(8,128)(2,1)S(1)}, f16[256,256]{1,0:T(8,128)(2,1)S(1)}, u32[]{:S(2)}, u32[]{:S(2)}) collective-permute-start(f16[256,256]{1,0:T(8,128)(2,1)S(1)} %convert_element_type.74), channel_id=1, source_target_pairs={{4,3},{5,11},{6,7},{7,9},{10,12},{11,4},{8,8},{9,6},{20,19},{21,27... | collective-permute-start | bytes 393224 | tf_op jit(solution)/shard_map/ppermute | solution.py:217
  74.0 2.6 %collective-permute-done.8 = f16[256,256]{1,0:T(8,128)(2,1)S(1)} collective-permute-done((f16[256,256]{1,0:T(8,128)(2,1)S(1)}, f16[256,256]{1,0:T(8,128)(2,1)S(1)}, u32[]{:S(2)}, u32[]{:S(2)}) %collective-permute-start.8) | collective-permute-done | bytes 131104 | tf_op jit(solution)/shard_map/ppermute | solution.py:217
  76.6 2.0 %collective-permute-done.9 = f16[256,256]{1,0:T(8,128)(2,1)S(1)} collective-permute-done((f16[256,256]{1,0:T(8,128)(2,1)S(1)}, f16[256,256]{1,0:T(8,128)(2,1)S(1)}, u32[]{:S(2)}, u32[]{:S(2)}) %collective-permute-start.9) | collective-permute-done | bytes 131104 | tf_op jit(solution)/shard_map/ppermute | solution.py:217
  (32 shorter events, 3.3 us)
Async XLA Ops:
  0.1 1.6 %copy-start = (bf16[256,4096]{1,0:T(8,128)(2,1)S(1)}, bf16[256,4096]{1,0:T(8,128)(2,1)}, u32[]{:S(2)}) copy-start(bf16[256,4096]{1,0:T(8,128)(2,1)} %values.1) | copy-start | bytes 6291460
  2.6 31.5 %collective-permute-start.1 = (bf16[256,2048]{1,0:T(8,128)(2,1)S(1)}, bf16[256,2048]{1,0:T(8,128)(2,1)S(1)}, u32[]{:S(2)}, u32[]{:S(2)}) collective-permute-start(bf16[256,2048]{1,0:T(8,128)(2,1)S(1)} %get-tuple-element.26), channel_id=1, source_target_pairs={{4,8},{8,4},{5,9},{9,5},{6,10},{10,6},{7,11},{11,7},{20,24},{24,20... | collective-permute-start | bytes 3145736 | tf_op jit(solution)/shard_map/ppermute | solution.py:232
  6.1 28.5 %collective-permute-start.2 = (bf16[256,2048]{1,0:T(8,128)(2,1)S(1)}, bf16[256,2048]{1,0:T(8,128)(2,1)S(1)}, u32[]{:S(2)}, u32[]{:S(2)}) collective-permute-start(bf16[256,2048]{1,0:T(8,128)(2,1)S(1)} %get-tuple-element.27.near), channel_id=1, source_target_pairs={{0,4},{12,8},{1,5},{13,9},{2,6},{14,10},{3,7},{15,11},{16,20},{28,... | collective-permute-start | bytes 3145736 | tf_op jit(solution)/shard_map/ppermute | solution.py:234
  7.4 26.7 %collective-permute-start.3 = (f32[1,2048]{1,0:T(1,128)S(1)}, f32[1,2048]{1,0:T(1,128)S(1)}, u32[]{:S(2)}, u32[]{:S(2)}) collective-permute-start(f32[1,2048]{1,0:T(1,128)S(1)} %get-tuple-element.28), channel_id=1, source_target_pairs={{0,8},{12,4},{1,9},{13,5},{2,10},{14,6},{3,11},{15,7},{16,24},{28,... | collective-permute-start | bytes 24584 | tf_op jit(solution)/shard_map/ppermute | solution.py:233
  8.7 46.4 %collective-permute-start = (bf16[256,2048]{1,0:T(8,128)(2,1)S(1)}, bf16[256,2048]{1,0:T(8,128)(2,1)S(1)}, u32[]{:S(2)}, u32[]{:S(2)}) collective-permute-start(bf16[256,2048]{1,0:T(8,128)(2,1)S(1)} %get-tuple-element.26), channel_id=1, source_target_pairs={{0,8},{12,4},{1,9},{13,5},{2,10},{14,6},{3,11},{15,7},{16,24},{28,... | collective-permute-start | bytes 3145736 | tf_op jit(solution)/shard_map/ppermute | solution.py:235
  34.6 7.1 %copy-start.1 = (s32[5,2,2]{2,1,0:T(2,128)S(1)}, s32[5,2,2]{2,1,0:T(2,128)}, u32[]{:S(2)}) copy-start(s32[5,2,2]{2,1,0:T(2,128)} %constant.22.clone.places) | copy-start | bytes 244
  38.0 3.6 %collective-permute-start.4 = (f16[3,256,256]{2,1,0:T(8,128)(2,1)S(1)}, f16[3,256,256]{2,1,0:T(8,128)(2,1)S(1)}, u32[]{:S(2)}, u32[]{:S(2)}) collective-permute-start(f16[3,256,256]{2,1,0:T(8,128)(2,1)S(1)} %convert_element_type.64), channel_id=1, source_target_pairs={{4,5},{5,4},{8,9},{9,8},{6,7},{7,6},{10,11},{11,10},{20,21},{21,20... | collective-permute-start | bytes 1179656 | tf_op jit(solution)/shard_map/ppermute | solution.py:213
  42.6 4.0 %collective-permute-start.5 = (f16[256,256]{1,0:T(8,128)(2,1)S(1)}, f16[256,256]{1,0:T(8,128)(2,1)S(1)}, u32[]{:S(2)}, u32[]{:S(2)}) collective-permute-start(f16[256,256]{1,0:T(8,128)(2,1)S(1)} %convert_element_type.66), channel_id=1, source_target_pairs={{4,4},{5,2},{6,5},{7,6},{10,11},{11,13},{8,10},{9,9},{20,20},{21,1... | collective-permute-start | bytes 393224 | tf_op jit(solution)/shard_map/ppermute | solution.py:217
  43.3 7.9 %collective-permute-start.6 = (f16[256,256]{1,0:T(8,128)(2,1)S(1)}, f16[256,256]{1,0:T(8,128)(2,1)S(1)}, u32[]{:S(2)}, u32[]{:S(2)}) collective-permute-start(f16[256,256]{1,0:T(8,128)(2,1)S(1)} %convert_element_type.68), channel_id=1, source_target_pairs={{4,5},{5,6},{6,4},{7,2},{10,10},{11,9},{8,11},{9,13},{20,21},{21,2... | collective-permute-start | bytes 393224 | tf_op jit(solution)/shard_map/ppermute | solution.py:217
  55.1 6.7 %copy-start.2 = (s32[4,2,2]{2,1,0:T(2,128)S(1)}, s32[4,2,2]{2,1,0:T(2,128)}, u32[]{:S(2)}) copy-start(s32[4,2,2]{2,1,0:T(2,128)} %constant.23.clone.places) | copy-start | bytes 196
  57.2 4.6 %collective-permute-start.7 = (f16[2,256,256]{2,1,0:T(8,128)(2,1)S(1)}, f16[2,256,256]{2,1,0:T(8,128)(2,1)S(1)}, u32[]{:S(2)}, u32[]{:S(2)}) collective-permute-start(f16[2,256,256]{2,1,0:T(8,128)(2,1)S(1)} %convert_element_type.70), channel_id=1, source_target_pairs={{4,5},{5,4},{8,9},{9,8},{6,7},{7,6},{10,11},{11,10},{20,21},{21,20... | collective-permute-start | bytes 786440 | tf_op jit(solution)/shard_map/ppermute | solution.py:213
  59.1 12.3 %collective-permute-start.12 = (f16[256,256]{1,0:T(8,128)(2,1)S(1)}, f16[256,256]{1,0:T(8,128)(2,1)S(1)}, u32[]{:S(2)}, u32[]{:S(2)}) collective-permute-start(f16[256,256]{1,0:T(8,128)(2,1)S(1)} %convert_element_type.80), channel_id=1, source_target_pairs={{4,0},{5,10},{6,1},{7,8},{10,15},{11,5},{8,14},{9,7},{20,16},{21,2... | collective-permute-start | bytes 393224 | tf_op jit(solution)/shard_map/ppermute | solution.py:217
  60.5 13.5 %collective-permute-start.13 = (f16[256,256]{1,0:T(8,128)(2,1)S(1)}, f16[256,256]{1,0:T(8,128)(2,1)S(1)}, u32[]{:S(2)}, u32[]{:S(2)}) collective-permute-start(f16[256,256]{1,0:T(8,128)(2,1)S(1)} %convert_element_type.82), channel_id=1, source_target_pairs={{4,1},{5,8},{6,0},{7,10},{10,14},{11,7},{8,15},{9,5},{20,17},{21,2... | collective-permute-start | bytes 393224 | tf_op jit(solution)/shard_map/ppermute | solution.py:217
  62.8 11.2 %collective-permute-start.10 = (f16[256,256]{1,0:T(8,128)(2,1)S(1)}, f16[256,256]{1,0:T(8,128)(2,1)S(1)}, u32[]{:S(2)}, u32[]{:S(2)}) collective-permute-start(f16[256,256]{1,0:T(8,128)(2,1)S(1)} %convert_element_type.76), channel_id=1, source_target_pairs={{4,13},{5,15},{6,12},{7,14},{10,2},{11,0},{8,3},{9,1},{20,29},{21,... | collective-permute-start | bytes 393224 | tf_op jit(solution)/shard_map/ppermute | solution.py:217
  64.1 9.9 %collective-permute-start.11 = (f16[256,256]{1,0:T(8,128)(2,1)S(1)}, f16[256,256]{1,0:T(8,128)(2,1)S(1)}, u32[]{:S(2)}, u32[]{:S(2)}) collective-permute-start(f16[256,256]{1,0:T(8,128)(2,1)S(1)} %convert_element_type.78), channel_id=1, source_target_pairs={{4,12},{5,14},{6,13},{7,15},{10,3},{11,1},{8,2},{9,0},{20,28},{21,... | collective-permute-start | bytes 393224 | tf_op jit(solution)/shard_map/ppermute | solution.py:217
  65.4 11.2 %collective-permute-start.8 = (f16[256,256]{1,0:T(8,128)(2,1)S(1)}, f16[256,256]{1,0:T(8,128)(2,1)S(1)}, u32[]{:S(2)}, u32[]{:S(2)}) collective-permute-start(f16[256,256]{1,0:T(8,128)(2,1)S(1)} %convert_element_type.72), channel_id=1, source_target_pairs={{4,7},{5,9},{6,3},{7,11},{10,8},{11,6},{8,12},{9,4},{20,23},{21,25... | collective-permute-start | bytes 393224 | tf_op jit(solution)/shard_map/ppermute | solution.py:217
  71.4 7.2 %collective-permute-start.9 = (f16[256,256]{1,0:T(8,128)(2,1)S(1)}, f16[256,256]{1,0:T(8,128)(2,1)S(1)}, u32[]{:S(2)}, u32[]{:S(2)}) collective-permute-start(f16[256,256]{1,0:T(8,128)(2,1)S(1)} %convert_element_type.74), channel_id=1, source_target_pairs={{4,3},{5,11},{6,7},{7,9},{10,12},{11,4},{8,8},{9,6},{20,19},{21,27... | collective-permute-start | bytes 393224 | tf_op jit(solution)/shard_map/ppermute | solution.py:217
